TPU v7x, 256 devices: a whole 4x4x8 slice. The times are simulated.
256 devices in a mesh: section: 16 (over x, z_lo), dp: 16 (over z_hi, y, core).
Axes of the slice: x: 4, y: 4, z: 8 (z_hi: 2, z_lo: 4; z = z_hi * 4 + z_lo), core: 2. Of those that a mesh axis runs over, the one named last changes fastest.
Arguments:
- stream_in: bfloat16 [4096, 2048], P('dp'), may hold values from -6 to 6
- sample_ids: int32 [16, 8], P('dp'), may hold values from 0 to 31
- epoch_buffer: bfloat16 [16, 512, 32, 2048], P('section', 'dp'), may hold values from -8 to 8
- layer_weight: bfloat16 [16, 2048, 2048], P('section', 'dp'), may hold values from -0.125 to 0.125
- top_cotangent: bfloat16 [4096, 2048], P('dp'), may hold values from -6 to 6
Outputs:
- decoded: bfloat16 [16, 4096, 2048], P('section', 'dp')
- weight_grad: float32 [16, 2048, 2048], P('section', 'dp')
Inputs may be any that keep to these rules, and one draw needn't show every extreme that they name: `sample_ids`: an entry of the replica's own pool of 32 samples.
All inputs are finite; a program needn't handle non-finite values.
Results may differ from a plain program's by a relative error of at most 0.035.
Values may be sent and summed in bfloat16 or wider, within the bound.
No kernel may reach another device: no remote copies, remote signals or barrier semaphores. Data moves between devices by JAX's collectives and lax.ppermute only.
A program may use at most 128 MiB of HBM per device.

v0:
```python
import jax
import jax.numpy as jnp
from jax import lax
from jax.sharding import PartitionSpec as P

epsilon = 1e-05


def from_behind(value, axis, steps):
    count = lax.axis_size(axis)
    leading, last = (max(0, -steps), min(count, count - steps))
    return lax.ppermute(value, axis, [(source, source + steps) for source in range(leading, last)])


def normalize(values):
    return values * lax.rsqrt(jnp.mean(values * values, axis=-1, keepdims=True) + epsilon)


def encode(output_rows, base_rows):
    bound_rows = 2.0 * jnp.sqrt(
        jnp.mean(output_rows * output_rows, axis=-1, keepdims=True) + epsilon
    )
    delta_rows = jnp.clip(output_rows - base_rows, -bound_rows, bound_rows).astype(jnp.bfloat16)
    return (base_rows + delta_rows.astype(jnp.float32)).astype(jnp.bfloat16)


def local(stream_in, sample_ids, epoch_buffer, layer_weight, top_cotangent):
    sections = lax.axis_size("section")
    position = lax.axis_index("section")
    weight = lax.all_gather(layer_weight[0], "dp", axis=0, tiled=True)
    micro = sample_ids.shape[1]
    tokens_block = epoch_buffer.shape[2]
    width = stream_in.shape[1]
    group = 1
    blocks = micro // group
    block_rows = group * tokens_block
    base_all = jnp.take(epoch_buffer[0], sample_ids[0], axis=0)
    first_blocks = stream_in.reshape(blocks, block_rows, width)
    top_blocks = top_cotangent.reshape(blocks, block_rows, width)
    blank = jnp.zeros((block_rows, width), jnp.bfloat16)
    storage = jnp.zeros((blocks, block_rows, width), jnp.bfloat16)
    steps_total = jnp.arange(blocks + sections - 1, dtype=jnp.int32)

    def forward_step(carry, step_index):
        message, saved, decoded = carry
        block_index = step_index - position
        active_flag = (block_index >= 0) & (block_index < blocks)
        picked = jnp.clip(block_index, 0, blocks - 1)
        first_rows = lax.dynamic_index_in_dim(first_blocks, picked, 0, keepdims=False)
        incoming = jnp.where(position == 0, first_rows, message)

        def run_layer(operands):
            saved_rows, decoded_rows = operands
            values = incoming.astype(jnp.float32)
            normed = normalize(values).astype(jnp.bfloat16)
            output_rows = values + jnp.dot(normed, weight, preferred_element_type=jnp.float32)
            base_rows = lax.dynamic_index_in_dim(base_all, picked, 0, keepdims=False).astype(
                jnp.float32
            )
            encoded = encode(output_rows, base_rows)
            saved_rows = lax.dynamic_update_index_in_dim(saved_rows, incoming, picked, 0)
            decoded_rows = lax.dynamic_update_index_in_dim(decoded_rows, encoded, picked, 0)
            return (encoded, saved_rows, decoded_rows)

        def skip_layer(operands):
            return (blank, operands[0], operands[1])

        outgoing, saved, decoded = lax.cond(active_flag, run_layer, skip_layer, (saved, decoded))
        message = from_behind(outgoing, "section", 1)
        return ((message, saved, decoded), None)

    forward_state, leftover = lax.scan(forward_step, (blank, storage, storage), steps_total)
    saved = forward_state[1]
    decoded = forward_state[2]

    def backward_step(carry, step_index):
        message, cot_blocks = carry
        block_index = step_index - (sections - 1 - position)
        active_flag = (block_index >= 0) & (block_index < blocks)
        picked = jnp.clip(block_index, 0, blocks - 1)
        top_rows = lax.dynamic_index_in_dim(top_blocks, picked, 0, keepdims=False)
        incoming = jnp.where(position == sections - 1, top_rows, message)

        def run_back(cot_rows):
            values = lax.dynamic_index_in_dim(saved, picked, 0, keepdims=False).astype(jnp.float32)
            backward_rows = lax.dot_general(
                incoming, weight, (((1,), (1,)), ((), ())), preferred_element_type=jnp.float32
            )
            through = jax.vjp(normalize, values)[1](backward_rows)[0]
            sending = (incoming.astype(jnp.float32) + through).astype(jnp.bfloat16)
            return (sending, lax.dynamic_update_index_in_dim(cot_rows, incoming, picked, 0))

        def skip_back(cot_rows):
            return (blank, cot_rows)

        outgoing, cot_blocks = lax.cond(active_flag, run_back, skip_back, cot_blocks)
        message = from_behind(outgoing, "section", -1)
        return ((message, cot_blocks), None)

    backward_state, remains = lax.scan(backward_step, (blank, storage), steps_total)
    cot_all = backward_state[1].reshape(-1, width)
    normed_all = normalize(saved.reshape(-1, width).astype(jnp.float32)).astype(jnp.bfloat16)
    gradient = lax.psum_scatter(
        lax.dot_general(
            normed_all, cot_all, (((0,), (0,)), ((), ())), preferred_element_type=jnp.float32
        ).astype(jnp.bfloat16),
        "dp",
        scatter_dimension=0,
        tiled=True,
    ).astype(jnp.float32)
    return (decoded.reshape(1, -1, width), gradient[None])


def solution(mesh):
    in_specs = (
        P("dp", None),
        P("dp", None),
        P("section", "dp", None, None),
        P("section", "dp", None),
        P("dp", None),
    )
    out_specs = (P("section", "dp", None), P("section", "dp", None))
    return jax.shard_map(local, mesh=mesh, in_specs=in_specs, out_specs=out_specs, check_vma=False)
```

profile of v0, /device:TPU:96, one launch (start us, length us, event | category | flops | bytes accessed | tf_op | source)
XLA Modules:
  0.0 976.5 jit_solution(17282705051662248052)
XLA Ops:
  12.3 103.5 %all-gather.3.cloned.1.call-done = bf16[1,2048,2048]{2,1,0:T(8,128)(2,1)} async-done(((bf16[1,128,2048]{2,1,0:T(8,128)(2,1)}), bf16[1,2048,2048]{2,1,0:T(8,128)(2,1)}) %all-gather.3.cloned.1.call-update) | async-done | bytes 8388624 | tf_op jit(solution)/shard_map/all_gather | solution.py:30
  116.0 316.5 %while.32 = (s32[]{:T(128)}, bf16[32,2048]{1,0:T(8,128)(2,1)S(1)}, bf16[8,32,2048]{2,1,0:T(8,128)(2,1)S(1)}, bf16[8,32,2048]{2,1,0:T(8,128)(2,1)S(1)}, s32[23]{0...) while((s32[]{:T(128)}, bf16[32,2048]{1,0:T(8,128)(2,1)S(1)}, ...), condition=%wide.region_5.6_spmd, body=%wide.region_0.5_spmd.sunk | while | flops 269746368 | bytes 10619104 | solution.py:72
  117.3 8.3 collective-permute-start
  130.1 7.1 collective-permute-start
  141.0 7.1 collective-permute-start
  148.1 12.8 %collective-permute-done = bf16[32,2048]{1,0:T(8,128)(2,1)S(1)} collective-permute-done((bf16[32,2048]{1,0:T(8,128)(2,1)S(1)}, bf16[32,2048]{1,0:T(8,128)(2,1)S(1)}, u32[]{:S(2)}, u32[]{:S(2)}) %collective-permute-start) | collective-permute-done | bytes 131104 | tf_op jit(solution)/shard_map/while/body/eval_jaxpr/ppermute | solution.py:12
  215.0 7.1 collective-permute-start
  249.4 7.1 collective-permute-start
  283.8 7.1 collective-permute-start
  294.7 13.4 %collective-permute-start = (bf16[32,2048]{1,0:T(8,128)(2,1)S(1)}, bf16[32,2048]{1,0:T(8,128)(2,1)S(1)}, u32[]{:S(2)}, u32[]{:S(2)}) collective-permute-start(bf16[32,2048]{1,0:T(8,128)(2,1)S(1)} %get-tuple-element.538), channel_id=1, source_target_pairs={{0,16},{16,32},{32,48},{48,64},{64,80},{80,96},{96,112},{112,128},... | collective-permute-start | bytes 393224 | tf_op jit(solution)/shard_map/while/body/eval_jaxpr/ppermute | solution.py:12
  311.9 7.1 collective-permute-start
  322.8 7.1 collective-permute-start
  333.6 7.1 collective-permute-start
  377.5 7.1 collective-permute-start
  389.6 7.1 collective-permute-start
  400.9 7.1 collective-permute-start
  411.8 7.1 collective-permute-start
  422.8 7.1 collective-permute-start
  433.4 387.1 %while.33 = (s32[]{:T(128)}, bf16[32,2048]{1,0:T(8,128)(2,1)S(1)}, bf16[8,32,2048]{2,1,0:T(8,128)(2,1)S(1)}, s32[23]{0:T(128)S(1)}, s32[]{:T(128)}, /*index=5*/p...) while((s32[]{:T(128)}, bf16[32,2048]{1,0:T(8,128)(2,1)S(1)}, ...), condition=%wide.region_12.13_spmd, body=%wide.region_7.12_spmd.sunk | while | flops 269353088 | bytes 10618172 | solution.py:100
  436.6 8.3 collective-permute-done.1
  448.2 7.6 collective-permute-done.1
  459.0 7.6 collective-permute-done.1
  469.9 7.6 collective-permute-done.1
  480.7 7.6 collective-permute-done.1
  491.6 7.6 collective-permute-done.1
  502.4 7.6 collective-permute-done.1
  513.3 7.6 collective-permute-done.1
  524.1 7.6 collective-permute-done.1
  534.9 7.6 collective-permute-done.1
  545.8 7.6 collective-permute-done.1
  556.6 83.7 %collective-permute-done.1 = bf16[32,2048]{1,0:T(8,128)(2,1)S(1)} collective-permute-done((bf16[32,2048]{1,0:T(8,128)(2,1)S(1)}, bf16[32,2048]{1,0:T(8,128)(2,1)S(1)}, u32[]{:S(2)}, u32[]{:S(2)}) %collective-permute-start.1) | collective-permute-done | bytes 131104 | tf_op jit(solution)/shard_map/while/body/eval_jaxpr/ppermute | solution.py:12
  641.6 7.2 conditional.5
  650.8 7.6 collective-permute-done.1
  659.6 7.2 conditional.5
  668.8 7.6 collective-permute-done.1
  677.6 7.2 conditional.5
  686.8 8.4 collective-permute-done.1
  696.4 7.2 conditional.5
  705.5 8.9 collective-permute-done.1
  715.7 7.2 conditional.5
  724.8 8.4 collective-permute-done.1
  734.4 7.2 conditional.5
  743.6 7.6 collective-permute-done.1
  752.4 7.2 conditional.5
  761.6 8.4 collective-permute-done.1
  771.3 7.2 conditional.5
  780.4 7.6 collective-permute-done.1
  826.3 141.2 %reduce-scatter.2.cloned.1.call-done = bf16[128,2048]{1,0:T(8,128)(2,1)} async-done(((bf16[2048,2048]{1,0:T(8,128)(2,1)}), bf16[128,2048]{1,0:T(8,128)(2,1)}) %reduce-scatter.2.cloned.1.call-update) | async-done | bytes 524304 | tf_op jit(solution)/shard_map/reduce_scatter | solution.py:103
  (272 shorter events, 378.3 us)
Async XLA Ops:
  7.2 108.6 %all-gather.3.cloned.1.call-start = ((), (), s32[]{:S(2)}) async-start(), calls=%async_computation.2 | async-start | bytes 8912896 | tf_op jit(solution)/shard_map/all_gather | solution.py:30
  7.9 959.6 %reduce-scatter.2.cloned.1.call-start = ((), (), s32[]{:S(2)}) async-start(), calls=%async_computation.1 | async-start | bytes 8912896 | tf_op jit(solution)/shard_map/reduce_scatter | solution.py:103
  117.3 11.4 %collective-permute-start = (bf16[32,2048]{1,0:T(8,128)(2,1)S(1)}, bf16[32,2048]{1,0:T(8,128)(2,1)S(1)}, u32[]{:S(2)}, u32[]{:S(2)}) collective-permute-start(bf16[32,2048]{1,0:T(8,128)(2,1)S(1)} %get-tuple-element.538), channel_id=1, source_target_pairs={{0,16},{16,32},{32,48},{48,64},{64,80},{80,96},{96,112},{112,128},... | collective-permute-start | bytes 393224 | tf_op jit(solution)/shard_map/while/body/eval_jaxpr/ppermute | solution.py:12
  130.1 9.6 collective-permute-start
  141.0 19.9 %collective-permute-start = (bf16[32,2048]{1,0:T(8,128)(2,1)S(1)}, bf16[32,2048]{1,0:T(8,128)(2,1)S(1)}, u32[]{:S(2)}, u32[]{:S(2)}) collective-permute-start(bf16[32,2048]{1,0:T(8,128)(2,1)S(1)} %get-tuple-element.538), channel_id=1, source_target_pairs={{0,16},{16,32},{32,48},{48,64},{64,80},{80,96},{96,112},{112,128},... | collective-permute-start | bytes 393224 | tf_op jit(solution)/shard_map/while/body/eval_jaxpr/ppermute | solution.py:12
  168.5 6.9 collective-permute-start
  183.0 7.1 collective-permute-start
  197.8 9.6 collective-permute-start
  215.0 9.6 collective-permute-start
  232.2 9.6 collective-permute-start
  249.4 9.6 collective-permute-start
  266.6 9.6 collective-permute-start
  283.8 9.6 collective-permute-start
  294.7 15.9 %collective-permute-start = (bf16[32,2048]{1,0:T(8,128)(2,1)S(1)}, bf16[32,2048]{1,0:T(8,128)(2,1)S(1)}, u32[]{:S(2)}, u32[]{:S(2)}) collective-permute-start(bf16[32,2048]{1,0:T(8,128)(2,1)S(1)} %get-tuple-element.538), channel_id=1, source_target_pairs={{0,16},{16,32},{32,48},{48,64},{64,80},{80,96},{96,112},{112,128},... | collective-permute-start | bytes 393224 | tf_op jit(solution)/shard_map/while/body/eval_jaxpr/ppermute | solution.py:12
  311.9 9.6 collective-permute-start
  322.8 9.6 collective-permute-start
  333.6 9.6 collective-permute-start
  344.5 9.6 collective-permute-start
  355.4 9.6 collective-permute-start
  366.3 9.9 %collective-permute-start = (bf16[32,2048]{1,0:T(8,128)(2,1)S(1)}, bf16[32,2048]{1,0:T(8,128)(2,1)S(1)}, u32[]{:S(2)}, u32[]{:S(2)}) collective-permute-start(bf16[32,2048]{1,0:T(8,128)(2,1)S(1)} %get-tuple-element.538), channel_id=1, source_target_pairs={{0,16},{16,32},{32,48},{48,64},{64,80},{80,96},{96,112},{112,128},... | collective-permute-start | bytes 393224 | tf_op jit(solution)/shard_map/while/body/eval_jaxpr/ppermute | solution.py:12
  377.5 10.8 %collective-permute-start = (bf16[32,2048]{1,0:T(8,128)(2,1)S(1)}, bf16[32,2048]{1,0:T(8,128)(2,1)S(1)}, u32[]{:S(2)}, u32[]{:S(2)}) collective-permute-start(bf16[32,2048]{1,0:T(8,128)(2,1)S(1)} %get-tuple-element.538), channel_id=1, source_target_pairs={{0,16},{16,32},{32,48},{48,64},{64,80},{80,96},{96,112},{112,128},... | collective-permute-start | bytes 393224 | tf_op jit(solution)/shard_map/while/body/eval_jaxpr/ppermute | solution.py:12
  389.6 9.9 %collective-permute-start = (bf16[32,2048]{1,0:T(8,128)(2,1)S(1)}, bf16[32,2048]{1,0:T(8,128)(2,1)S(1)}, u32[]{:S(2)}, u32[]{:S(2)}) collective-permute-start(bf16[32,2048]{1,0:T(8,128)(2,1)S(1)} %get-tuple-element.538), channel_id=1, source_target_pairs={{0,16},{16,32},{32,48},{48,64},{64,80},{80,96},{96,112},{112,128},... | collective-permute-start | bytes 393224 | tf_op jit(solution)/shard_map/while/body/eval_jaxpr/ppermute | solution.py:12
  400.9 9.6 collective-permute-start
  411.8 9.7 collective-permute-start
  422.8 9.7 collective-permute-start
  434.7 10.3 %collective-permute-start.1 = (bf16[32,2048]{1,0:T(8,128)(2,1)S(1)}, bf16[32,2048]{1,0:T(8,128)(2,1)S(1)}, u32[]{:S(2)}, u32[]{:S(2)}) collective-permute-start(bf16[32,2048]{1,0:T(8,128)(2,1)S(1)} %get-tuple-element.550), channel_id=1, source_target_pairs={{16,0},{32,16},{48,32},{64,48},{80,64},{96,80},{112,96},{128,112},... | collective-permute-start | bytes 393224 | tf_op jit(solution)/shard_map/while/body/eval_jaxpr/ppermute | solution.py:12
  446.3 9.6 collective-permute-start.1
  457.1 9.6 collective-permute-start.1
  468.0 9.6 collective-permute-start.1
  478.8 9.6 collective-permute-start.1
  489.6 9.6 collective-permute-start.1
  500.5 9.6 collective-permute-start.1
  511.3 9.6 collective-permute-start.1
  522.2 9.6 collective-permute-start.1
  533.0 9.6 collective-permute-start.1
  543.9 9.6 collective-permute-start.1
  554.7 85.7 %collective-permute-start.1 = (bf16[32,2048]{1,0:T(8,128)(2,1)S(1)}, bf16[32,2048]{1,0:T(8,128)(2,1)S(1)}, u32[]{:S(2)}, u32[]{:S(2)}) collective-permute-start(bf16[32,2048]{1,0:T(8,128)(2,1)S(1)} %get-tuple-element.550), channel_id=1, source_target_pairs={{16,0},{32,16},{48,32},{64,48},{80,64},{96,80},{112,96},{128,112},... | collective-permute-start | bytes 393224 | tf_op jit(solution)/shard_map/while/body/eval_jaxpr/ppermute | solution.py:12
  648.8 9.6 collective-permute-start.1
  666.8 9.6 collective-permute-start.1
  684.9 10.3 %collective-permute-start.1 = (bf16[32,2048]{1,0:T(8,128)(2,1)S(1)}, bf16[32,2048]{1,0:T(8,128)(2,1)S(1)}, u32[]{:S(2)}, u32[]{:S(2)}) collective-permute-start(bf16[32,2048]{1,0:T(8,128)(2,1)S(1)} %get-tuple-element.550), channel_id=1, source_target_pairs={{16,0},{32,16},{48,32},{64,48},{80,64},{96,80},{112,96},{128,112},... | collective-permute-start | bytes 393224 | tf_op jit(solution)/shard_map/while/body/eval_jaxpr/ppermute | solution.py:12
  703.6 10.8 %collective-permute-start.1 = (bf16[32,2048]{1,0:T(8,128)(2,1)S(1)}, bf16[32,2048]{1,0:T(8,128)(2,1)S(1)}, u32[]{:S(2)}, u32[]{:S(2)}) collective-permute-start(bf16[32,2048]{1,0:T(8,128)(2,1)S(1)} %get-tuple-element.550), channel_id=1, source_target_pairs={{16,0},{32,16},{48,32},{64,48},{80,64},{96,80},{112,96},{128,112},... | collective-permute-start | bytes 393224 | tf_op jit(solution)/shard_map/while/body/eval_jaxpr/ppermute | solution.py:12
  722.9 10.3 %collective-permute-start.1 = (bf16[32,2048]{1,0:T(8,128)(2,1)S(1)}, bf16[32,2048]{1,0:T(8,128)(2,1)S(1)}, u32[]{:S(2)}, u32[]{:S(2)}) collective-permute-start(bf16[32,2048]{1,0:T(8,128)(2,1)S(1)} %get-tuple-element.550), channel_id=1, source_target_pairs={{16,0},{32,16},{48,32},{64,48},{80,64},{96,80},{112,96},{128,112},... | collective-permute-start | bytes 393224 | tf_op jit(solution)/shard_map/while/body/eval_jaxpr/ppermute | solution.py:12
  741.6 9.6 collective-permute-start.1
  759.7 10.4 %collective-permute-start.1 = (bf16[32,2048]{1,0:T(8,128)(2,1)S(1)}, bf16[32,2048]{1,0:T(8,128)(2,1)S(1)}, u32[]{:S(2)}, u32[]{:S(2)}) collective-permute-start(bf16[32,2048]{1,0:T(8,128)(2,1)S(1)} %get-tuple-element.550), channel_id=1, source_target_pairs={{16,0},{32,16},{48,32},{64,48},{80,64},{96,80},{112,96},{128,112},... | collective-permute-start | bytes 393224 | tf_op jit(solution)/shard_map/while/body/eval_jaxpr/ppermute | solution.py:12
  778.5 9.6 collective-permute-start.1
  789.3 9.6 collective-permute-start.1
  800.2 9.6 collective-permute-start.1
  811.0 9.6 collective-permute-start.1
  (1 other events, 1.0 us)
Sparse Core Ops, SparseCore 0:
  10.7 104.9 all-gather.2
  826.4 141.0 reduce-scatter.1
where the time goes:
time: 984 us; the launch traced here: 977 us
  waiting for transfers between devices  564 us (57%)
  starting transfers between devices  217 us (22%)
  matrix products  95 us (10%)
  local copies, waits for them, and re-layouts  32.1 us (3%)
  loops' own time  32.1 us (3%)
  other arithmetic  22.5 us (2%)
  between operations  14.1 us (1%)
    ppermute x46, waiting for transfers between devices, from_behind(): lax.ppermute(value, axis, [(source, source + steps) for source in range(l...  319 us
    ppermute x46, starting transfers between devices, from_behind(): lax.ppermute(value, axis, [(source, source + steps) for source in range(l...  217 us
    reduce_scatter x1, waiting for transfers between devices, local(): lax.psum_scatter(lax.dot_general(normed_all, cot_all, (((0,), (0,)), ((),...  141 us
    all_gather x1, waiting for transfers between devices, local(): weight = lax.all_gather(layer_weight[0], 'dp', axis=0, tiled=True)  103 us
    dot_general x8, matrix products, run_back(): lax.dot_general(incoming, weight, (((1,), (1,)), ((), ())), preferred_ele...  48.5 us
    dot_general x8, matrix products, run_layer(): jnp.dot(normed, weight, preferred_element_type=jnp.float32)  40.8 us
    dynamic_slice x46, local copies, waits for them, and re-layouts, local(): lax.scan(forward_step, (blank, storage, storage), steps_total)  28 us
  transfers between devices with their start and end apart: 48, of which 48 were waited for; matrix products, arithmetic and copies ran while one was open for 0% of the time, Pallas kernels for 0%

commit v1 on v0

v1 whole, which is shorter than its diff:
```python
import functools

import jax
import jax.numpy as jnp
from jax import lax
from jax.experimental import pallas as pl
from jax.experimental.pallas import tpu as pltpu
from jax.sharding import Mesh
from jax.sharding import PartitionSpec as P

epsilon = 1e-05
STAGES = 4
DEPTH = 4
TILE = 512
PLANE = ("zl", "zh", "y", "c")


def forward_kernel(x_ref, base_ref, w_ref, out_ref, x_now, normed, y):
    layer, tile = pl.program_id(0), pl.program_id(1)
    tiles = pl.num_programs(1)

    @pl.when((layer == 0) & (tile == 0))
    def _():
        x_now[...] = x_ref[...].astype(jnp.float32)

    @pl.when(tile == 0)
    def _():
        values = x_now[...]
        scale = lax.rsqrt(jnp.mean(values * values, axis=-1, keepdims=True) + epsilon)
        normed[...] = (values * scale).astype(jnp.bfloat16)

    columns = pl.ds(pl.multiple_of(tile * TILE, TILE), TILE)
    y[:, columns] = x_now[:, columns] + jnp.dot(
        normed[...], w_ref[0], preferred_element_type=jnp.float32
    )

    @pl.when(tile == tiles - 1)
    def _():
        rows = y[...]
        base = base_ref[0].astype(jnp.float32)
        bound = 2.0 * jnp.sqrt(jnp.mean(rows * rows, axis=-1, keepdims=True) + epsilon)
        delta = jnp.clip(rows - base, -bound, bound).astype(jnp.bfloat16)
        coded = (base + delta.astype(jnp.float32)).astype(jnp.bfloat16)
        out_ref[0] = coded
        x_now[...] = coded.astype(jnp.float32)


def forward_stage(x, base, weight):
    depth, rows, width = base.shape
    return pl.pallas_call(
        forward_kernel,
        grid=(depth, width // TILE),
        in_specs=[
            pl.BlockSpec((rows, width), lambda i, j: (0, 0)),
            pl.BlockSpec((1, rows, width), lambda i, j: (i, 0, 0)),
            pl.BlockSpec((1, width, TILE), lambda i, j: (i, 0, j)),
        ],
        out_specs=pl.BlockSpec((1, rows, width), lambda i, j: (i, 0, 0)),
        out_shape=jax.ShapeDtypeStruct((depth, rows, width), jnp.bfloat16),
        scratch_shapes=[
            pltpu.VMEM((rows, width), jnp.float32),
            pltpu.VMEM((rows, width), jnp.bfloat16),
            pltpu.VMEM((rows, width), jnp.float32),
        ],
        compiler_params=pltpu.CompilerParams(vmem_limit_bytes=32 * 1024 * 1024),
        cost_estimate=pl.CostEstimate(
            flops=2 * depth * rows * width * width,
            bytes_accessed=2 * depth * width * width,
            transcendentals=0,
        ),
    )(x, base, weight)


def backward_kernel(g_ref, x_ref, w_ref, seen_ref, out_ref, g_now, back):
    step, tile = pl.program_id(0), pl.program_id(1)
    tiles = pl.num_programs(1)

    @pl.when((step == 0) & (tile == 0))
    def _():
        g_now[...] = g_ref[...]

    columns = pl.ds(pl.multiple_of(tile * TILE, TILE), TILE)
    back[:, columns] = lax.dot_general(
        g_now[...], w_ref[0], (((1,), (1,)), ((), ())), preferred_element_type=jnp.float32
    )

    @pl.when(tile == tiles - 1)
    def _():
        values = x_ref[0].astype(jnp.float32)
        scale = lax.rsqrt(jnp.mean(values * values, axis=-1, keepdims=True) + epsilon)
        through = back[...]
        along = jnp.mean(values * scale * through, axis=-1, keepdims=True)
        seen_ref[0] = g_now[...]
        sent = g_now[...].astype(jnp.float32) + scale * (through - values * scale * along)
        sent = sent.astype(jnp.bfloat16)
        g_now[...] = sent
        out_ref[...] = sent


def backward_stage(g, x, weight):
    depth, rows, width = x.shape
    last = depth - 1
    return pl.pallas_call(
        backward_kernel,
        grid=(depth, width // TILE),
        in_specs=[
            pl.BlockSpec((rows, width), lambda i, j: (0, 0)),
            pl.BlockSpec((1, rows, width), lambda i, j: (last - i, 0, 0)),
            pl.BlockSpec((1, TILE, width), lambda i, j: (last - i, j, 0)),
        ],
        out_specs=[
            pl.BlockSpec((1, rows, width), lambda i, j: (last - i, 0, 0)),
            pl.BlockSpec((rows, width), lambda i, j: (0, 0)),
        ],
        out_shape=[
            jax.ShapeDtypeStruct((depth, rows, width), jnp.bfloat16),
            jax.ShapeDtypeStruct((rows, width), jnp.bfloat16),
        ],
        scratch_shapes=[
            pltpu.VMEM((rows, width), jnp.bfloat16),
            pltpu.VMEM((rows, width), jnp.float32),
        ],
        compiler_params=pltpu.CompilerParams(vmem_limit_bytes=32 * 1024 * 1024),
        cost_estimate=pl.CostEstimate(
            flops=2 * depth * rows * width * width,
            bytes_accessed=2 * depth * width * width,
            transcendentals=0,
        ),
    )(g, x, weight)


def shift(value, axis, steps):
    count = lax.axis_size(axis)
    return lax.ppermute(value, axis, [(i, (i + steps) % count) for i in range(count)])


def exchange(value):
    return lax.all_to_all(value, "zl", 0, 0)


def gradient_sum(normed, g):
    rows, width = normed.shape
    core, y, zh = lax.axis_index("c"), lax.axis_index("y"), lax.axis_index("zh")
    chips = lax.axis_size("zh") * lax.axis_size("y")
    piece = width // (2 * chips)
    by_core = normed.reshape(rows, chips, 2, piece)
    mine = lax.dynamic_index_in_dim(by_core, core, 2, keepdims=False).reshape(rows, -1)
    theirs = lax.dynamic_index_in_dim(by_core, 1 - core, 2, keepdims=False).reshape(rows, -1)
    left = jnp.concatenate([mine, shift(theirs, "c", 1)], axis=0)
    right = jnp.concatenate([g, shift(g, "c", 1)], axis=0)

    left = left.reshape(2 * rows, 2, 4, piece)

    def block(steps):
        picked = lax.dynamic_index_in_dim(left, lax.rem(y + steps + 4, 4), 2, keepdims=False)
        return lax.dot_general(
            picked.reshape(2 * rows, 2 * piece), right, (((0,), (0,)), ((), ())),
            preferred_element_type=jnp.float32,
        )

    half = width // 2
    far = block(2).astype(jnp.bfloat16)
    up1 = shift(far[:, :half], "y", 1)
    down1 = shift(far[:, half:], "y", -1)
    up, down, own = block(1), block(-1), block(0)
    up = jnp.concatenate([up[:, :half] + up1.astype(jnp.float32), up[:, half:]], axis=1)
    down = jnp.concatenate([down[:, :half], down[:, half:] + down1.astype(jnp.float32)], axis=1)
    up2 = shift(up.astype(jnp.bfloat16), "y", 1)
    down2 = shift(down.astype(jnp.bfloat16), "y", -1)
    total = own + up2.astype(jnp.float32) + down2.astype(jnp.float32)
    total = total.reshape(2, piece, width)
    kept = lax.dynamic_index_in_dim(total, zh, 0, keepdims=False)
    given = lax.dynamic_index_in_dim(total, 1 - zh, 0, keepdims=False).astype(jnp.bfloat16)
    return kept + shift(given, "zh", 1).astype(jnp.float32)


def local(stream_in, sample_ids, epoch_buffer, layer_weight, top_cotangent):
    stage, lane = lax.axis_index("x"), lax.axis_index("zl")
    width = stream_in.shape[1]
    rows = stream_in.shape[0] // DEPTH
    weight = lax.all_gather(layer_weight[0], PLANE, axis=0, tiled=True)
    weight = weight.reshape(DEPTH, width, width)
    picked = jnp.take(epoch_buffer[0], sample_ids[0], axis=0)
    base = exchange(picked.reshape(DEPTH, rows, width))
    x = lax.dynamic_slice_in_dim(stream_in, lane * rows, rows, 0)
    g = lax.dynamic_slice_in_dim(top_cotangent, lane * rows, rows, 0)

    decoded = forward_stage(x, base, weight)
    for t in range(1, STAGES):
        arrived = lax.ppermute(decoded[DEPTH - 1], "x", [(t - 1, t)])
        x = jnp.where(stage == t, arrived, x)
        decoded = lax.cond(
            stage == t, lambda a, d: forward_stage(a, base, weight), lambda a, d: d, x, decoded
        )
    inputs = jnp.concatenate([x[None], decoded[: DEPTH - 1]], axis=0)

    seen, sent = backward_stage(g, inputs, weight)
    for t in range(STAGES - 2, -1, -1):
        arrived = lax.ppermute(sent, "x", [(t + 1, t)])
        g = jnp.where(stage == t, arrived, g)
        seen, sent = lax.cond(
            stage == t,
            lambda a, s, o: tuple(backward_stage(a, inputs, weight)),
            lambda a, s, o: (s, o),
            g, seen, sent,
        )

    decoded_rows = exchange(decoded).reshape(1, DEPTH * rows, width)
    input_rows = exchange(inputs).reshape(DEPTH * rows, width).astype(jnp.float32)
    scale = lax.rsqrt(jnp.mean(input_rows * input_rows, axis=-1, keepdims=True) + epsilon)
    normed = (input_rows * scale).astype(jnp.bfloat16)
    cotangents = exchange(seen).reshape(DEPTH * rows, width)
    return decoded_rows, gradient_sum(normed, cotangents)[None]


def solution(mesh):
    fine = Mesh(mesh.devices.reshape(4, 4, 2, 4, 2), ("x", "zl", "zh", "y", "c"))
    section, dp = ("x", "zl"), ("zh", "y", "c")
    in_specs = (
        P(dp, None),
        P(dp, None),
        P(section, dp, None, None),
        P(section, dp, None),
        P(dp, None),
    )
    out_specs = (P(section, dp, None), P(section, dp, None))
    return jax.shard_map(local, mesh=fine, in_specs=in_specs, out_specs=out_specs, check_vma=False)
```

time: 984 us -> 565 us (0.57)
  starting transfers between devices: 217 us -> 41 us
  waiting for transfers between devices: 564 us -> 407 us
  matrix products: 95 us -> 9.75 us
  Pallas kernels: 0 us -> 65.7 us
  loops' own time: 32.1 us -> 0.05 us
  local copies, waits for them, and re-layouts: 32.1 us -> 13.9 us
  other arithmetic: 22.5 us -> 8.09 us
    ppermute x46 -> x13, starting transfers between devices: 217 us -> 20 us  [the longest x7 12.6 us: shift(): lax.ppermute(value, axis, [(i, (i + steps) % count) for i in range(count)])]
    reduce_scatter x1 -> x0, waiting for transfers between devices: 141 us -> none  [local(): lax.psum_scatter(lax.dot_general(normed_all, cot_all, (((0,), (0,)), ((),...]
    ppermute x46 -> x13, waiting for transfers between devices: 319 us -> 190 us  [the longest x3 135 us: local(): arrived = lax.ppermute(sent, 'x', [(t + 1, t)])]
    dot_general x17 -> x4, matrix products: 95 us -> 9.75 us  [block(): lax.dot_general(picked.reshape(2 * rows, 2 * piece), right, (((0,), (0,))...]
    pallas_call x0 -> x3, Pallas kernels: none -> 65.7 us  [the longest x2 45.2 us: backward_stage(): pl.pallas_call(backward_kernel, grid=(depth, width // TILE), in_specs=[pl...]
    all_gather x1, waiting for transfers between devices: 103 us -> 166 us  [local(): weight = lax.all_gather(layer_weight[0], PLANE, axis=0, tiled=True)]
    all_to_all x0 -> x4, waiting for transfers between devices: none -> 50.6 us  [exchange(): return lax.all_to_all(value, 'zl', 0, 0)]
    another operation x48 -> x6, loops' own time: 32.1 us -> 0.05 us  [the longest x3 0.03 us: local(): lax.cond(stage == t, lambda a, d: forward_stage(a, base, weight), lambda...]
  transfers between devices with their start and end apart: 48 -> 18, of which waited for: 48 -> 11; matrix products, arithmetic and copies ran while one was open for 0% -> 4% of each run, Pallas kernels for 0% -> 4%
where the time goes in v1:
time: 565 us; the launch traced here: 560 us
  waiting for transfers between devices  407 us (72%)
  Pallas kernels  65.7 us (12%)
  starting transfers between devices  41 us (7%)
  between operations  14.4 us (3%)
  local copies, waits for them, and re-layouts  13.9 us (2%)
  matrix products  9.75 us (2%)
  other arithmetic  8.09 us (1%)
    all_gather x1, waiting for transfers between devices, local(): weight = lax.all_gather(layer_weight[0], PLANE, axis=0, tiled=True)  166 us
    ppermute x3, waiting for transfers between devices, local(): arrived = lax.ppermute(sent, 'x', [(t + 1, t)])  135 us
    all_to_all x4, waiting for transfers between devices, exchange(): return lax.all_to_all(value, 'zl', 0, 0)  50.6 us
    ppermute x7, waiting for transfers between devices, shift(): lax.ppermute(value, axis, [(i, (i + steps) % count) for i in range(count)])  49.4 us
    pallas_call x2, Pallas kernels, backward_stage(): pl.pallas_call(backward_kernel, grid=(depth, width // TILE), in_specs=[pl...  45.2 us
    all_to_all x4, starting transfers between devices, exchange(): return lax.all_to_all(value, 'zl', 0, 0)  21 us
    pallas_call x1, Pallas kernels, forward_stage(): pl.pallas_call(forward_kernel, grid=(depth, width // TILE), in_specs=[pl....  20.5 us
    ppermute x7, starting transfers between devices, shift(): lax.ppermute(value, axis, [(i, (i + steps) % count) for i in range(count)])  12.6 us
  transfers between devices with their start and end apart: 18, of which 11 were waited for; matrix products, arithmetic and copies ran while one was open for 4% of the time, Pallas kernels for 4%

profile of v1, /device:TPU:96, one launch (start us, length us, event | category | flops | bytes accessed | tf_op | source)
XLA Modules:
  0.0 560.2 jit_solution(4953361049103427882)
XLA Ops:
  7.2 0.7 all-gather.3.cloned.1.call-update
  8.4 1.3 reduce.4
  10.7 2.8 gather_fusion
  13.5 1.1 bitcast_select_fusion
  14.6 5.1 all-to-all-start
  19.7 32.2 %all-to-all-done.base_ref = bf16[4,64,2048]{2,1,0:T(8,128)(2,1)S(1)} async-done(((bf16[4,64,2048]{2,1,0:T(8,128)(2,1)}), bf16[4,64,2048]{2,1,0:T(8,128)(2,1)S(1)}, u32[]{:S(2)}, u32[]{:S(2)}) %all-to-all-start) | async-done | bytes 1048608 | tf_op jit(solution)/shard_map/all_to_all | solution.py:138
  51.9 166.1 %all-gather.3.cloned.1.call-done = bf16[1,8192,2048]{2,1,0:T(8,128)(2,1)} async-done(((bf16[1,128,2048]{2,1,0:T(8,128)(2,1)}), bf16[1,8192,2048]{2,1,0:T(8,128)(2,1)}) %all-gather.3.cloned.1.call-update) | async-done | bytes 33554448 | tf_op jit(solution)/shard_map/all_gather | solution.py:181
  218.0 20.5 %shard_map.68 = bf16[4,64,2048]{2,1,0:T(8,128)(2,1)} custom-call(bf16[64,2048]{1,0:T(8,128)(2,1)S(1)} %constant_dynamic-slice_fusion.3.x_ref, bf16[4,64,2048]{2,1,0:T(8,128)(2,1)S(1)} %all-to-all-done.base_ref, bf16[4,2048,2048]{2,1,0:T(8,128)(2,1)} %bitcast.38), custom_call_target="tpu_custom_call" | custom-call | flops 2147483648 | bytes 33554432 | tf_op jit(solution)/shard_map/pallas_call | solution.py:50
  238.5 1.0 slice_bitcast_fusion.2
  239.5 3.4 collective-permute-start
  242.9 5.9 %collective-permute-done = bf16[64,2048]{1,0:T(8,128)(2,1)S(1)} collective-permute-done((bf16[64,2048]{1,0:T(8,128)(2,1)S(1)}, bf16[64,2048]{1,0:T(8,128)(2,1)S(1)}, u32[]{:S(2)}, u32[]{:S(2)}) %collective-permute-start) | collective-permute-done | bytes 262176 | tf_op jit(solution)/shard_map/ppermute | solution.py:190
  248.9 1.0 slice_bitcast_fusion.1
  249.9 0.7 collective-permute-start.1
  250.7 1.1 slice_bitcast_fusion
  251.7 0.7 collective-permute-start.2
  252.5 1.2 slice.53
  253.8 1.1 pad_maximum_fusion.1.x_ref
  254.8 22.5 %shard_map.69 = (bf16[4,64,2048]{2,1,0:T(8,128)(2,1)}, bf16[64,2048]{1,0:T(8,128)(2,1)S(1)}) custom-call(bf16[64,2048]{1,0:T(8,128)(2,1)S(1)} %constant_dynamic-slice_fusion.g_ref, bf16[4,64,2048]{2,1,0:T(8,128)(2,1)} %pad_maximum_fusion.1.x_ref, bf16[4,2048,2048]{2,1,0:T(8,128)(2,1)} %bitcast.42), custom_call_target="tpu_custom_call" | custom-call | flops 2147483648 | bytes 33554432 | tf_op jit(solution)/shard_map/pallas_call | solution.py:103
  278.0 5.4 all-to-all-start.2
  283.5 0.7 collective-permute-start.5
  284.2 1.3 collective-permute-start.6
  285.5 134.6 %collective-permute-done.6 = bf16[64,2048]{1,0:T(8,128)(2,1)S(1)} collective-permute-done((bf16[64,2048]{1,0:T(8,128)(2,1)S(1)}, bf16[64,2048]{1,0:T(8,128)(2,1)S(1)}, u32[]{:S(2)}, u32[]{:S(2)}) %collective-permute-start.6) | collective-permute-done | bytes 262176 | tf_op jit(solution)/shard_map/ppermute | solution.py:199
  420.1 22.7 %conditional.11 = (bf16[4,64,2048]{2,1,0:T(8,128)(2,1)}) conditional(s32[]{:T(128)} %convert_element_type.61, bf16[4,64,2048]{2,1,0:T(8,128)(2,1)} %get-tuple-element.110, (pred[]{:T(512)}, bf16[64,2048]{1,0:T(8,128)(2,1)S(1)}, bf16[64,2048]{1,0:T(8,128)(2,1)S(1)}, bf16[4,64,2048]{2,1,0:T(8,128)(2,1)}, bf16[4,2048,2048]{2,1,0:T(8,128)(2,1)}) %tuple.96), branch_computations={%region_11.12_spmd, %region_12.13_spmd} | conditional | flops 2147614720 | bytes 34340872 | solution.py:201
  420.1 22.6 %branch_1_fun.11 = (bf16[4,64,2048]{2,1,0:T(8,128)(2,1)}, bf16[64,2048]{1,0:T(8,128)(2,1)}) custom-call(bf16[64,2048]{1,0:T(8,128)(2,1)S(1)} %broadcast_select_fusion.g_ref, bf16[4,64,2048]{2,1,0:T(8,128)(2,1)} %get-tuple-element.97.x_ref, bf16[4,2048,2048]{2,1,0:T(8,128)(2,1)} %get-tuple-element.98.w_ref), custom_call_target="tpu_custom_call" | custom-call | flops 2147483648 | bytes 33554432 | tf_op jit(solution)/shard_map/cond/branch_1_fun/pallas_call | solution.py:103
  442.8 5.4 all-to-all-start.3
  448.6 2.1 reshape.119
  450.7 18.4 %all-to-all-done.3 = bf16[4,64,2048]{2,1,0:T(8,128)(2,1)} async-done(((bf16[4,64,2048]{2,1,0:T(8,128)(2,1)}), bf16[4,64,2048]{2,1,0:T(8,128)(2,1)}, u32[]{:S(2)}, u32[]{:S(2)}) %all-to-all-start.3) | async-done | bytes 1048608 | tf_op jit(solution)/shard_map/all_to_all | solution.py:138
  469.1 0.7 fusion.1
  470.1 0.8 collective-permute-start.3
  470.9 1.6 collective-permute-done.3
  473.3 2.3 convolution_convert_fusion
  475.7 1.4 collective-permute-start.8
  477.1 2.2 fusion.12
  479.4 2.0 collective-permute-start.10
  481.4 2.2 fusion.11
  483.7 7.4 %collective-permute-done.8 = bf16[256,1024]{1,0:T(8,128)(2,1)S(1)} collective-permute-done((bf16[256,1024]{1,0:T(8,128)(2,1)S(1)}, bf16[256,1024]{1,0:T(8,128)(2,1)S(1)}, u32[]{:S(2)}, u32[]{:S(2)}) %collective-permute-start.8) | collective-permute-done | bytes 524320 | tf_op jit(solution)/shard_map/ppermute | solution.py:134
  491.5 1.8 collective-permute-done.10
  493.6 3.2 collective-permute-start.11
  496.8 5.1 all-to-all-start.1
  501.9 0.8 copy.16
  502.7 14.6 %collective-permute-done.9 = bf16[256,2048]{1,0:T(8,128)(2,1)} collective-permute-done((bf16[256,2048]{1,0:T(8,128)(2,1)S(1)}, bf16[256,2048]{1,0:T(8,128)(2,1)}, u32[]{:S(2)}, u32[]{:S(2)}) %collective-permute-start.9) | collective-permute-done | bytes 1048608 | tf_op jit(solution)/shard_map/ppermute | solution.py:134
  517.3 1.2 collective-permute-done.11
  518.5 3.0 fusion
  521.5 0.9 fusion.5
  522.4 5.0 collective-permute-start.12
  527.4 22.8 %collective-permute-done.12 = bf16[128,2048]{1,0:T(8,128)(2,1)} collective-permute-done((bf16[128,2048]{1,0:T(8,128)(2,1)}, bf16[128,2048]{1,0:T(8,128)(2,1)}, u32[]{:S(2)}, u32[]{:S(2)}) %collective-permute-start.12) | collective-permute-done | bytes 524320 | tf_op jit(solution)/shard_map/ppermute | solution.py:134
  550.3 2.1 fusion.4
  552.4 1.0 copy.40
  (52 shorter events, 4.9 us)
Async XLA Ops:
  7.2 210.9 %all-gather.3.cloned.1.call-start = ((), (), s32[]{:S(2)}) async-start(), calls=%async_computation.4 | async-start | bytes 34078720 | tf_op jit(solution)/shard_map/all_gather | solution.py:181
  13.5 6.2 %copy-start = (bf16[256,2048]{1,0:T(8,128)(2,1)S(1)}, bf16[256,2048]{1,0:T(8,128)(2,1)}, u32[]{:S(2)}) copy-start(bf16[256,2048]{1,0:T(8,128)(2,1)} %param.17) | copy-start | bytes 3145732
  14.6 37.3 %all-to-all-start = ((bf16[4,64,2048]{2,1,0:T(8,128)(2,1)}), bf16[4,64,2048]{2,1,0:T(8,128)(2,1)S(1)}, u32[]{:S(2)}, u32[]{:S(2)}) async-start(bf16[4,64,2048]{2,1,0:T(8,128)(2,1)} %bitcast_select_fusion), calls=%async_computation | async-start | bytes 2097152 | tf_op jit(solution)/shard_map/all_to_all | solution.py:138
  239.5 9.4 %collective-permute-start = (bf16[64,2048]{1,0:T(8,128)(2,1)S(1)}, bf16[64,2048]{1,0:T(8,128)(2,1)S(1)}, u32[]{:S(2)}, u32[]{:S(2)}) collective-permute-start(bf16[64,2048]{1,0:T(8,128)(2,1)S(1)} %slice_bitcast_fusion.2), channel_id=1, source_target_pairs={{0,64},{1,65},{2,66},{3,67},{4,68},{5,69},{6,70},{7,71},{8,72},{9,... | collective-permute-start | bytes 786440 | tf_op jit(solution)/shard_map/ppermute | solution.py:190
  249.9 0.7 collective-permute-start.1
  250.7 1.8 copy-start.1
  251.7 0.7 collective-permute-start.2
  277.3 6.0 %collective-permute-start.4 = (bf16[64,2048]{1,0:T(8,128)(2,1)S(1)}, bf16[64,2048]{1,0:T(8,128)(2,1)S(1)}, u32[]{:S(2)}, u32[]{:S(2)}) collective-permute-start(bf16[64,2048]{1,0:T(8,128)(2,1)S(1)} %get-tuple-element.107), channel_id=1, source_target_pairs={{192,128},{193,129},{194,130},{195,131},{196,132},{197,133},{198,1... | collective-permute-start | bytes 786440 | tf_op jit(solution)/shard_map/ppermute | solution.py:199
  278.0 164.8 %all-to-all-start.2 = ((bf16[4,64,2048]{2,1,0:T(8,128)(2,1)}), bf16[4,64,2048]{2,1,0:T(8,128)(2,1)S(1)}, u32[]{:S(2)}, u32[]{:S(2)}) async-start(bf16[4,64,2048]{2,1,0:T(8,128)(2,1)} %pad_maximum_fusion.1.x_ref), calls=%async_computation.2 | async-start | bytes 2097152 | tf_op jit(solution)/shard_map/all_to_all | solution.py:138
  283.5 0.7 collective-permute-start.5
  284.2 135.9 %collective-permute-start.6 = (bf16[64,2048]{1,0:T(8,128)(2,1)S(1)}, bf16[64,2048]{1,0:T(8,128)(2,1)S(1)}, u32[]{:S(2)}, u32[]{:S(2)}) collective-permute-start(bf16[64,2048]{1,0:T(8,128)(2,1)S(1)} %get-tuple-element.111), channel_id=1, source_target_pairs={{64,0},{65,1},{66,2},{67,3},{68,4},{69,5},{70,6},{71,7},{72,8},{73... | collective-permute-start | bytes 786440 | tf_op jit(solution)/shard_map/ppermute | solution.py:199
  442.8 26.3 %all-to-all-start.3 = ((bf16[4,64,2048]{2,1,0:T(8,128)(2,1)}), bf16[4,64,2048]{2,1,0:T(8,128)(2,1)}, u32[]{:S(2)}, u32[]{:S(2)}) async-start(bf16[4,64,2048]{2,1,0:T(8,128)(2,1)} %get-tuple-element.137), calls=%async_computation.3 | async-start | bytes 2097152 | tf_op jit(solution)/shard_map/all_to_all | solution.py:138
  469.1 4.2 collective-permute-start.7
  470.1 2.4 collective-permute-start.3
  475.7 15.4 %collective-permute-start.8 = (bf16[256,1024]{1,0:T(8,128)(2,1)S(1)}, bf16[256,1024]{1,0:T(8,128)(2,1)S(1)}, u32[]{:S(2)}, u32[]{:S(2)}) collective-permute-start(bf16[256,1024]{1,0:T(8,128)(2,1)S(1)} %get-tuple-element.112), channel_id=1, source_target_pairs={{0,2},{2,4},{4,6},{6,0},{1,3},{3,5},{5,7},{7,1},{8,10},{10,12},{12... | collective-permute-start | bytes 1572872 | tf_op jit(solution)/shard_map/ppermute | solution.py:134
  479.4 13.9 %collective-permute-start.10 = (bf16[256,1024]{1,0:T(8,128)(2,1)S(1)}, bf16[256,1024]{1,0:T(8,128)(2,1)S(1)}, u32[]{:S(2)}, u32[]{:S(2)}) collective-permute-start(bf16[256,1024]{1,0:T(8,128)(2,1)S(1)} %get-tuple-element.113), channel_id=1, source_target_pairs={{0,6},{2,0},{4,2},{6,4},{1,7},{3,1},{5,3},{7,5},{8,14},{10,8},{12,... | collective-permute-start | bytes 1572872 | tf_op jit(solution)/shard_map/ppermute | solution.py:134
  491.3 26.0 %collective-permute-start.9 = (bf16[256,2048]{1,0:T(8,128)(2,1)S(1)}, bf16[256,2048]{1,0:T(8,128)(2,1)}, u32[]{:S(2)}, u32[]{:S(2)}) collective-permute-start(bf16[256,2048]{1,0:T(8,128)(2,1)S(1)} %pad_maximum_fusion.2), channel_id=1, source_target_pairs={{0,2},{2,4},{4,6},{6,0},{1,3},{3,5},{5,7},{7,1},{8,10},{10,12},{12... | collective-permute-start | bytes 3145736 | tf_op jit(solution)/shard_map/ppermute | solution.py:134
  493.6 24.9 %collective-permute-start.11 = (bf16[256,2048]{1,0:T(8,128)(2,1)S(1)}, bf16[256,2048]{1,0:T(8,128)(2,1)}, u32[]{:S(2)}, u32[]{:S(2)}) collective-permute-start(bf16[256,2048]{1,0:T(8,128)(2,1)S(1)} %pad_maximum_fusion.3), channel_id=1, source_target_pairs={{0,6},{2,0},{4,2},{6,4},{1,7},{3,1},{5,3},{7,5},{8,14},{10,8},{12,... | collective-permute-start | bytes 3145736 | tf_op jit(solution)/shard_map/ppermute | solution.py:134
  496.8 30.7 %all-to-all-start.1 = ((bf16[4,64,2048]{2,1,0:T(8,128)(2,1)}), bf16[4,64,2048]{2,1,0:T(8,128)(2,1)S(1)}, u32[]{:S(2)}, u32[]{:S(2)}) async-start(bf16[4,64,2048]{2,1,0:T(8,128)(2,1)} %get-tuple-element.134), calls=%async_computation.1 | async-start | bytes 2097152 | tf_op jit(solution)/shard_map/all_to_all | solution.py:138
  522.4 27.9 %collective-permute-start.12 = (bf16[128,2048]{1,0:T(8,128)(2,1)}, bf16[128,2048]{1,0:T(8,128)(2,1)}, u32[]{:S(2)}, u32[]{:S(2)}) collective-permute-start(bf16[128,2048]{1,0:T(8,128)(2,1)} %fusion.5), channel_id=1, source_target_pairs={{0,8},{8,0},{1,9},{9,1},{2,10},{10,2},{3,11},{11,3},{4,12},{12,4},... | collective-permute-start | bytes 1572872 | tf_op jit(solution)/shard_map/ppermute | solution.py:134
Sparse Core Ops, SparseCore 0:
  9.9 208.1 all-gather.2

commit v2 on v1

--- a/solution.py
+++ b/solution.py
@@ -12,55 +12,101 @@
 STAGES = 4
 DEPTH = 4
 TILE = 512
+SLOTS = 8
 PLANE = ("zl", "zh", "y", "c")
 
 
-def forward_kernel(x_ref, base_ref, w_ref, out_ref, x_now, normed, y):
-    layer, tile = pl.program_id(0), pl.program_id(1)
-    tiles = pl.num_programs(1)
-
-    @pl.when((layer == 0) & (tile == 0))
-    def _():
-        x_now[...] = x_ref[...].astype(jnp.float32)
-
-    @pl.when(tile == 0)
-    def _():
+def tile_copies(w_ref, held, arrived, depth, tiles, order, by_rows):
+    slots = held.shape[0]
+
+    def copy(number):
+        slot = lax.rem(number, slots)
+        layer = order(number // tiles)
+        span = pl.ds(pl.multiple_of(lax.rem(number, tiles) * TILE, TILE), TILE)
+        source = w_ref.at[layer, span] if by_rows else w_ref.at[layer, :, span]
+        return pltpu.make_async_copy(source, held.at[slot], arrived.at[slot])
+
+    def refill(number):
+        @pl.when(number + slots < depth * tiles)
+        def _():
+            copy(number + slots).start()
+
+    for number in range(slots):
+        copy(jnp.int32(number)).start()
+    return copy, refill
+
+
+def forward_kernel(x_ref, base_ref, w_ref, out_ref, x_now, normed, y, held, arrived):
+    depth, rows, width = base_ref.shape
+    tiles, slots = width // TILE, held.shape[0]
+    copy, refill = tile_copies(w_ref, held, arrived, depth, tiles, lambda i: i, False)
+    x_now[...] = x_ref[...].astype(jnp.float32)
+
+    def run_layer(layer, carry):
         values = x_now[...]
         scale = lax.rsqrt(jnp.mean(values * values, axis=-1, keepdims=True) + epsilon)
         normed[...] = (values * scale).astype(jnp.bfloat16)
-
-    columns = pl.ds(pl.multiple_of(tile * TILE, TILE), TILE)
-    y[:, columns] = x_now[:, columns] + jnp.dot(
-        normed[...], w_ref[0], preferred_element_type=jnp.float32
-    )
-
-    @pl.when(tile == tiles - 1)
-    def _():
-        rows = y[...]
-        base = base_ref[0].astype(jnp.float32)
-        bound = 2.0 * jnp.sqrt(jnp.mean(rows * rows, axis=-1, keepdims=True) + epsilon)
-        delta = jnp.clip(rows - base, -bound, bound).astype(jnp.bfloat16)
+        for tile in range(tiles):
+            number = layer * tiles + tile
+            copy(number).wait()
+            columns = pl.ds(tile * TILE, TILE)
+            y[:, columns] = x_now[:, columns] + jnp.dot(
+                normed[...], held[lax.rem(number, slots)], preferred_element_type=jnp.float32
+            )
+            refill(number)
+        values = y[...]
+        base = base_ref[layer].astype(jnp.float32)
+        bound = 2.0 * jnp.sqrt(jnp.mean(values * values, axis=-1, keepdims=True) + epsilon)
+        delta = jnp.clip(values - base, -bound, bound).astype(jnp.bfloat16)
         coded = (base + delta.astype(jnp.float32)).astype(jnp.bfloat16)
-        out_ref[0] = coded
+        out_ref[layer] = coded
         x_now[...] = coded.astype(jnp.float32)
-
-
-def forward_stage(x, base, weight):
-    depth, rows, width = base.shape
+        return carry
+
+    lax.fori_loop(0, depth, run_layer, 0)
+
+
+def backward_kernel(g_ref, x_ref, w_ref, seen_ref, out_ref, g_now, back, held, arrived):
+    depth, rows, width = x_ref.shape
+    tiles, slots = width // TILE, held.shape[0]
+    copy, refill = tile_copies(w_ref, held, arrived, depth, tiles, lambda i: depth - 1 - i, True)
+    g_now[...] = g_ref[...]
+
+    def run_layer(step, carry):
+        layer = depth - 1 - step
+        seen_ref[layer] = g_now[...]
+        for tile in range(tiles):
+            number = step * tiles + tile
+            copy(number).wait()
+            back[:, pl.ds(tile * TILE, TILE)] = lax.dot_general(
+                g_now[...], held[lax.rem(number, slots)], (((1,), (1,)), ((), ())),
+                preferred_element_type=jnp.float32,
+            )
+            refill(number)
+        values = x_ref[layer].astype(jnp.float32)
+        scale = lax.rsqrt(jnp.mean(values * values, axis=-1, keepdims=True) + epsilon)
+        normed = values * scale
+        through = back[...]
+        along = jnp.mean(normed * through, axis=-1, keepdims=True)
+        sent = g_now[...].astype(jnp.float32) + scale * (through - normed * along)
+        g_now[...] = sent.astype(jnp.bfloat16)
+        return carry
+
+    lax.fori_loop(0, depth, run_layer, 0)
+    out_ref[...] = g_now[...]
+
+
+def stage_call(kernel, tile_shape, scratch, outs, depth, rows, width):
+    vmem = pl.BlockSpec(memory_space=pltpu.VMEM)
     return pl.pallas_call(
-        forward_kernel,
-        grid=(depth, width // TILE),
-        in_specs=[
-            pl.BlockSpec((rows, width), lambda i, j: (0, 0)),
-            pl.BlockSpec((1, rows, width), lambda i, j: (i, 0, 0)),
-            pl.BlockSpec((1, width, TILE), lambda i, j: (i, 0, j)),
-        ],
-        out_specs=pl.BlockSpec((1, rows, width), lambda i, j: (i, 0, 0)),
-        out_shape=jax.ShapeDtypeStruct((depth, rows, width), jnp.bfloat16),
+        kernel,
+        in_specs=[vmem, vmem, pl.BlockSpec(memory_space=pl.ANY)],
+        out_specs=[vmem] * len(outs),
+        out_shape=[jax.ShapeDtypeStruct(shape, jnp.bfloat16) for shape in outs],
         scratch_shapes=[
-            pltpu.VMEM((rows, width), jnp.float32),
-            pltpu.VMEM((rows, width), jnp.bfloat16),
-            pltpu.VMEM((rows, width), jnp.float32),
+            *scratch,
+            pltpu.VMEM((SLOTS, *tile_shape), jnp.bfloat16),
+            pltpu.SemaphoreType.DMA((SLOTS,)),
         ],
         compiler_params=pltpu.CompilerParams(vmem_limit_bytes=32 * 1024 * 1024),
         cost_estimate=pl.CostEstimate(
@@ -68,65 +114,28 @@
             bytes_accessed=2 * depth * width * width,
             transcendentals=0,
         ),
-    )(x, base, weight)
-
-
-def backward_kernel(g_ref, x_ref, w_ref, seen_ref, out_ref, g_now, back):
-    step, tile = pl.program_id(0), pl.program_id(1)
-    tiles = pl.num_programs(1)
-
-    @pl.when((step == 0) & (tile == 0))
-    def _():
-        g_now[...] = g_ref[...]
-
-    columns = pl.ds(pl.multiple_of(tile * TILE, TILE), TILE)
-    back[:, columns] = lax.dot_general(
-        g_now[...], w_ref[0], (((1,), (1,)), ((), ())), preferred_element_type=jnp.float32
     )
 
-    @pl.when(tile == tiles - 1)
-    def _():
-        values = x_ref[0].astype(jnp.float32)
-        scale = lax.rsqrt(jnp.mean(values * values, axis=-1, keepdims=True) + epsilon)
-        through = back[...]
-        along = jnp.mean(values * scale * through, axis=-1, keepdims=True)
-        seen_ref[0] = g_now[...]
-        sent = g_now[...].astype(jnp.float32) + scale * (through - values * scale * along)
-        sent = sent.astype(jnp.bfloat16)
-        g_now[...] = sent
-        out_ref[...] = sent
+
+def forward_stage(x, base, weight):
+    depth, rows, width = base.shape
+    scratch = [
+        pltpu.VMEM((rows, width), jnp.float32),
+        pltpu.VMEM((rows, width), jnp.bfloat16),
+        pltpu.VMEM((rows, width), jnp.float32),
+    ]
+    call = stage_call(
+        forward_kernel, (width, TILE), scratch, [(depth, rows, width)], depth, rows, width
+    )
+    return call(x, base, weight)[0]
 
 
 def backward_stage(g, x, weight):
     depth, rows, width = x.shape
-    last = depth - 1
-    return pl.pallas_call(
-        backward_kernel,
-        grid=(depth, width // TILE),
-        in_specs=[
-            pl.BlockSpec((rows, width), lambda i, j: (0, 0)),
-            pl.BlockSpec((1, rows, width), lambda i, j: (last - i, 0, 0)),
-            pl.BlockSpec((1, TILE, width), lambda i, j: (last - i, j, 0)),
-        ],
-        out_specs=[
-            pl.BlockSpec((1, rows, width), lambda i, j: (last - i, 0, 0)),
-            pl.BlockSpec((rows, width), lambda i, j: (0, 0)),
-        ],
-        out_shape=[
-            jax.ShapeDtypeStruct((depth, rows, width), jnp.bfloat16),
-            jax.ShapeDtypeStruct((rows, width), jnp.bfloat16),
-        ],
-        scratch_shapes=[
-            pltpu.VMEM((rows, width), jnp.bfloat16),
-            pltpu.VMEM((rows, width), jnp.float32),
-        ],
-        compiler_params=pltpu.CompilerParams(vmem_limit_bytes=32 * 1024 * 1024),
-        cost_estimate=pl.CostEstimate(
-            flops=2 * depth * rows * width * width,
-            bytes_accessed=2 * depth * width * width,
-            transcendentals=0,
-        ),
-    )(g, x, weight)
+    scratch = [pltpu.VMEM((rows, width), jnp.bfloat16), pltpu.VMEM((rows, width), jnp.float32)]
+    outs = [(depth, rows, width), (rows, width)]
+    call = stage_call(backward_kernel, (TILE, width), scratch, outs, depth, rows, width)
+    return call(g, x, weight)
 
 
 def shift(value, axis, steps):

time: 565 us -> 506 us (0.90)
  waiting for transfers between devices: 407 us -> 370 us
  Pallas kernels: 65.7 us -> 45 us
    ppermute x3, waiting for transfers between devices: 135 us -> 98.1 us  [local(): arrived = lax.ppermute(sent, 'x', [(t + 1, t)])]
    pallas_call x3, Pallas kernels: 65.7 us -> 45 us  [the longest x2 32.1 us: backward_stage(): return call(g, x, weight)]
  transfers between devices with their start and end apart: 18 -> 18, of which waited for: 11 -> 11; matrix products, arithmetic and copies ran while one was open for 4% -> 4% of each run, Pallas kernels for 4% -> 3%
where the time goes in v2:
time: 506 us; the launch traced here: 503 us
  waiting for transfers between devices  370 us (73%)
  Pallas kernels  45 us (9%)
  starting transfers between devices  41.1 us (8%)
  between operations  14.5 us (3%)
  local copies, waits for them, and re-layouts  13.9 us (3%)
  matrix products  9.75 us (2%)
  other arithmetic  8.09 us (2%)
    all_gather x1, waiting for transfers between devices, local(): weight = lax.all_gather(layer_weight[0], PLANE, axis=0, tiled=True)  166 us
    ppermute x3, waiting for transfers between devices, local(): arrived = lax.ppermute(sent, 'x', [(t + 1, t)])  98.1 us
    all_to_all x4, waiting for transfers between devices, exchange(): return lax.all_to_all(value, 'zl', 0, 0)  50.5 us
    ppermute x7, waiting for transfers between devices, shift(): lax.ppermute(value, axis, [(i, (i + steps) % count) for i in range(count)])  48.8 us
    pallas_call x2, Pallas kernels, backward_stage(): return call(g, x, weight)  32.1 us
    all_to_all x4, starting transfers between devices, exchange(): return lax.all_to_all(value, 'zl', 0, 0)  21 us
    pallas_call x1, Pallas kernels, forward_stage(): return call(x, base, weight)[0]  12.8 us
    ppermute x7, starting transfers between devices, shift(): lax.ppermute(value, axis, [(i, (i + steps) % count) for i in range(count)])  12.7 us
  transfers between devices with their start and end apart: 18, of which 11 were waited for; matrix products, arithmetic and copies ran while one was open for 4% of the time, Pallas kernels for 3%

profile of v2, /device:TPU:96, one launch (start us, length us, event | category | flops | bytes accessed | tf_op | source)
XLA Modules:
  0.0 502.7 jit_solution(8907863810144967754)
XLA Ops:
  7.2 0.7 all-gather.3.cloned.1.call-update
  8.4 1.3 reduce.4
  10.7 2.8 gather_fusion
  13.5 1.1 bitcast_select_fusion
  14.6 5.1 %all-to-all-start = ((bf16[4,64,2048]{2,1,0:T(8,128)(2,1)}), bf16[4,64,2048]{2,1,0:T(8,128)(2,1)S(1)}, u32[]{:S(2)}, u32[]{:S(2)}) async-start(bf16[4,64,2048]{2,1,0:T(8,128)(2,1)} %bitcast_select_fusion), calls=%async_computation | async-start | bytes 2097152 | tf_op jit(solution)/shard_map/all_to_all | solution.py:147
  19.7 32.2 %all-to-all-done.base_ref = bf16[4,64,2048]{2,1,0:T(8,128)(2,1)S(1)} async-done(((bf16[4,64,2048]{2,1,0:T(8,128)(2,1)}), bf16[4,64,2048]{2,1,0:T(8,128)(2,1)S(1)}, u32[]{:S(2)}, u32[]{:S(2)}) %all-to-all-start) | async-done | bytes 1048608 | tf_op jit(solution)/shard_map/all_to_all | solution.py:147
  51.9 166.1 %all-gather.3.cloned.1.call-done = bf16[1,8192,2048]{2,1,0:T(8,128)(2,1)} async-done(((bf16[1,128,2048]{2,1,0:T(8,128)(2,1)}), bf16[1,8192,2048]{2,1,0:T(8,128)(2,1)}) %all-gather.3.cloned.1.call-update) | async-done | bytes 33554448 | tf_op jit(solution)/shard_map/all_gather | solution.py:190
  218.0 12.8 %shard_map.68 = bf16[4,64,2048]{2,1,0:T(8,128)(2,1)} custom-call(bf16[64,2048]{1,0:T(8,128)(2,1)S(1)} %constant_dynamic-slice_fusion.3.x_ref, bf16[4,64,2048]{2,1,0:T(8,128)(2,1)S(1)} %all-to-all-done.base_ref, bf16[4,2048,2048]{2,1,0:T(8,128)(2,1)} %bitcast.38), custom_call_target="tpu_custom_call" | custom-call | flops 2147483648 | bytes 33554432 | tf_op jit(solution)/shard_map/pallas_call | solution.py:130
  230.9 1.0 slice_bitcast_fusion.2
  231.8 3.4 collective-permute-start
  235.3 5.9 %collective-permute-done = bf16[64,2048]{1,0:T(8,128)(2,1)S(1)} collective-permute-done((bf16[64,2048]{1,0:T(8,128)(2,1)S(1)}, bf16[64,2048]{1,0:T(8,128)(2,1)S(1)}, u32[]{:S(2)}, u32[]{:S(2)}) %collective-permute-start) | collective-permute-done | bytes 262176 | tf_op jit(solution)/shard_map/ppermute | solution.py:199
  241.3 1.0 slice_bitcast_fusion.1
  242.3 0.7 collective-permute-start.1
  243.0 1.1 slice_bitcast_fusion
  244.1 0.7 collective-permute-start.2
  244.9 1.2 slice.53
  246.1 1.1 pad_maximum_fusion.1.x_ref
  247.2 15.8 %shard_map.69 = (bf16[4,64,2048]{2,1,0:T(8,128)(2,1)}, bf16[64,2048]{1,0:T(8,128)(2,1)S(1)}) custom-call(bf16[64,2048]{1,0:T(8,128)(2,1)S(1)} %constant_dynamic-slice_fusion.g_ref, bf16[4,64,2048]{2,1,0:T(8,128)(2,1)} %pad_maximum_fusion.1.x_ref, bf16[4,2048,2048]{2,1,0:T(8,128)(2,1)} %bitcast.42), custom_call_target="tpu_custom_call" | custom-call | flops 2147483648 | bytes 33554432 | tf_op jit(solution)/shard_map/pallas_call | solution.py:138
  263.0 0.7 collective-permute-start.4
  263.6 5.4 %all-to-all-start.2 = ((bf16[4,64,2048]{2,1,0:T(8,128)(2,1)}), bf16[4,64,2048]{2,1,0:T(8,128)(2,1)S(1)}, u32[]{:S(2)}, u32[]{:S(2)}) async-start(bf16[4,64,2048]{2,1,0:T(8,128)(2,1)} %pad_maximum_fusion.1.x_ref), calls=%async_computation.2 | async-start | bytes 2097152 | tf_op jit(solution)/shard_map/all_to_all | solution.py:147
  269.1 0.7 collective-permute-start.5
  270.0 1.3 collective-permute-start.6
  271.3 98.1 %collective-permute-done.6 = bf16[64,2048]{1,0:T(8,128)(2,1)S(1)} collective-permute-done((bf16[64,2048]{1,0:T(8,128)(2,1)S(1)}, bf16[64,2048]{1,0:T(8,128)(2,1)S(1)}, u32[]{:S(2)}, u32[]{:S(2)}) %collective-permute-start.6) | collective-permute-done | bytes 262176 | tf_op jit(solution)/shard_map/ppermute | solution.py:208
  369.4 16.4 %conditional.11 = (bf16[4,64,2048]{2,1,0:T(8,128)(2,1)}) conditional(s32[]{:T(128)} %convert_element_type.61, bf16[4,64,2048]{2,1,0:T(8,128)(2,1)} %get-tuple-element.110, (pred[]{:T(512)}, bf16[64,2048]{1,0:T(8,128)(2,1)S(1)}, bf16[64,2048]{1,0:T(8,128)(2,1)S(1)}, bf16[4,64,2048]{2,1,0:T(8,128)(2,1)}, bf16[4,2048,2048]{2,1,0:T(8,128)(2,1)}) %tuple.96), branch_computations={%region_11.12_spmd, %region_12.13_spmd} | conditional | flops 2147614720 | bytes 34340872 | solution.py:210
  369.5 16.4 %branch_1_fun.11 = (bf16[4,64,2048]{2,1,0:T(8,128)(2,1)}, bf16[64,2048]{1,0:T(8,128)(2,1)}) custom-call(bf16[64,2048]{1,0:T(8,128)(2,1)S(1)} %broadcast_select_fusion.g_ref, bf16[4,64,2048]{2,1,0:T(8,128)(2,1)} %get-tuple-element.97.x_ref, bf16[4,2048,2048]{2,1,0:T(8,128)(2,1)} %get-tuple-element.98.w_ref), custom_call_target="tpu_custom_call" | custom-call | flops 2147483648 | bytes 33554432 | tf_op jit(solution)/shard_map/cond/branch_1_fun/pallas_call | solution.py:138
  385.9 5.5 %all-to-all-start.3 = ((bf16[4,64,2048]{2,1,0:T(8,128)(2,1)}), bf16[4,64,2048]{2,1,0:T(8,128)(2,1)}, u32[]{:S(2)}, u32[]{:S(2)}) async-start(bf16[4,64,2048]{2,1,0:T(8,128)(2,1)} %get-tuple-element.137), calls=%async_computation.3 | async-start | bytes 2097152 | tf_op jit(solution)/shard_map/all_to_all | solution.py:147
  391.7 2.1 reshape.119
  393.8 18.3 %all-to-all-done.3 = bf16[4,64,2048]{2,1,0:T(8,128)(2,1)} async-done(((bf16[4,64,2048]{2,1,0:T(8,128)(2,1)}), bf16[4,64,2048]{2,1,0:T(8,128)(2,1)}, u32[]{:S(2)}, u32[]{:S(2)}) %all-to-all-start.3) | async-done | bytes 1048608 | tf_op jit(solution)/shard_map/all_to_all | solution.py:147
  412.1 0.7 fusion.1
  413.8 1.8 collective-permute-done.3
  416.4 2.3 convolution_convert_fusion
  418.7 1.5 collective-permute-start.8
  420.2 2.2 fusion.12
  422.5 1.9 collective-permute-start.10
  424.4 2.2 fusion.11
  426.8 7.2 %collective-permute-done.8 = bf16[256,1024]{1,0:T(8,128)(2,1)S(1)} collective-permute-done((bf16[256,1024]{1,0:T(8,128)(2,1)S(1)}, bf16[256,1024]{1,0:T(8,128)(2,1)S(1)}, u32[]{:S(2)}, u32[]{:S(2)}) %collective-permute-start.8) | collective-permute-done | bytes 524320 | tf_op jit(solution)/shard_map/ppermute | solution.py:143
  434.7 1.6 collective-permute-done.10
  436.5 3.1 collective-permute-start.11
  439.7 5.1 %all-to-all-start.1 = ((bf16[4,64,2048]{2,1,0:T(8,128)(2,1)}), bf16[4,64,2048]{2,1,0:T(8,128)(2,1)S(1)}, u32[]{:S(2)}, u32[]{:S(2)}) async-start(bf16[4,64,2048]{2,1,0:T(8,128)(2,1)} %get-tuple-element.134), calls=%async_computation.1 | async-start | bytes 2097152 | tf_op jit(solution)/shard_map/all_to_all | solution.py:147
  444.8 0.8 copy.16
  445.6 14.6 %collective-permute-done.9 = bf16[256,2048]{1,0:T(8,128)(2,1)} collective-permute-done((bf16[256,2048]{1,0:T(8,128)(2,1)S(1)}, bf16[256,2048]{1,0:T(8,128)(2,1)}, u32[]{:S(2)}, u32[]{:S(2)}) %collective-permute-start.9) | collective-permute-done | bytes 1048608 | tf_op jit(solution)/shard_map/ppermute | solution.py:143
  460.2 1.0 collective-permute-done.11
  461.2 3.0 fusion
  464.2 0.9 fusion.5
  465.1 5.1 %collective-permute-start.12 = (bf16[128,2048]{1,0:T(8,128)(2,1)}, bf16[128,2048]{1,0:T(8,128)(2,1)}, u32[]{:S(2)}, u32[]{:S(2)}) collective-permute-start(bf16[128,2048]{1,0:T(8,128)(2,1)} %fusion.5), channel_id=1, source_target_pairs={{0,8},{8,0},{1,9},{9,1},{2,10},{10,2},{3,11},{11,3},{4,12},{12,4},... | collective-permute-start | bytes 1572872 | tf_op jit(solution)/shard_map/ppermute | solution.py:143
  470.2 22.6 %collective-permute-done.12 = bf16[128,2048]{1,0:T(8,128)(2,1)} collective-permute-done((bf16[128,2048]{1,0:T(8,128)(2,1)}, bf16[128,2048]{1,0:T(8,128)(2,1)}, u32[]{:S(2)}, u32[]{:S(2)}) %collective-permute-start.12) | collective-permute-done | bytes 524320 | tf_op jit(solution)/shard_map/ppermute | solution.py:143
  492.8 2.1 fusion.4
  494.9 1.0 copy.40
  (52 shorter events, 5.3 us)
Async XLA Ops:
  7.2 210.9 %all-gather.3.cloned.1.call-start = ((), (), s32[]{:S(2)}) async-start(), calls=%async_computation.4 | async-start | bytes 34078720 | tf_op jit(solution)/shard_map/all_gather | solution.py:190
  13.5 6.2 %copy-start = (bf16[256,2048]{1,0:T(8,128)(2,1)S(1)}, bf16[256,2048]{1,0:T(8,128)(2,1)}, u32[]{:S(2)}) copy-start(bf16[256,2048]{1,0:T(8,128)(2,1)} %param.17) | copy-start | bytes 3145732
  14.6 37.3 %all-to-all-start = ((bf16[4,64,2048]{2,1,0:T(8,128)(2,1)}), bf16[4,64,2048]{2,1,0:T(8,128)(2,1)S(1)}, u32[]{:S(2)}, u32[]{:S(2)}) async-start(bf16[4,64,2048]{2,1,0:T(8,128)(2,1)} %bitcast_select_fusion), calls=%async_computation | async-start | bytes 2097152 | tf_op jit(solution)/shard_map/all_to_all | solution.py:147
  231.8 9.4 %collective-permute-start = (bf16[64,2048]{1,0:T(8,128)(2,1)S(1)}, bf16[64,2048]{1,0:T(8,128)(2,1)S(1)}, u32[]{:S(2)}, u32[]{:S(2)}) collective-permute-start(bf16[64,2048]{1,0:T(8,128)(2,1)S(1)} %slice_bitcast_fusion.2), channel_id=1, source_target_pairs={{0,64},{1,65},{2,66},{3,67},{4,68},{5,69},{6,70},{7,71},{8,72},{9,... | collective-permute-start | bytes 786440 | tf_op jit(solution)/shard_map/ppermute | solution.py:199
  242.3 0.7 collective-permute-start.1
  243.0 1.8 copy-start.1
  244.1 0.7 collective-permute-start.2
  263.0 6.1 %collective-permute-start.4 = (bf16[64,2048]{1,0:T(8,128)(2,1)S(1)}, bf16[64,2048]{1,0:T(8,128)(2,1)S(1)}, u32[]{:S(2)}, u32[]{:S(2)}) collective-permute-start(bf16[64,2048]{1,0:T(8,128)(2,1)S(1)} %get-tuple-element.107), channel_id=1, source_target_pairs={{192,128},{193,129},{194,130},{195,131},{196,132},{197,133},{198,1... | collective-permute-start | bytes 786440 | tf_op jit(solution)/shard_map/ppermute | solution.py:208
  263.6 122.2 %all-to-all-start.2 = ((bf16[4,64,2048]{2,1,0:T(8,128)(2,1)}), bf16[4,64,2048]{2,1,0:T(8,128)(2,1)S(1)}, u32[]{:S(2)}, u32[]{:S(2)}) async-start(bf16[4,64,2048]{2,1,0:T(8,128)(2,1)} %pad_maximum_fusion.1.x_ref), calls=%async_computation.2 | async-start | bytes 2097152 | tf_op jit(solution)/shard_map/all_to_all | solution.py:147
  269.1 0.7 collective-permute-start.5
  270.0 99.4 %collective-permute-start.6 = (bf16[64,2048]{1,0:T(8,128)(2,1)S(1)}, bf16[64,2048]{1,0:T(8,128)(2,1)S(1)}, u32[]{:S(2)}, u32[]{:S(2)}) collective-permute-start(bf16[64,2048]{1,0:T(8,128)(2,1)S(1)} %get-tuple-element.111), channel_id=1, source_target_pairs={{64,0},{65,1},{66,2},{67,3},{68,4},{69,5},{70,6},{71,7},{72,8},{73... | collective-permute-start | bytes 786440 | tf_op jit(solution)/shard_map/ppermute | solution.py:208
  385.9 26.3 %all-to-all-start.3 = ((bf16[4,64,2048]{2,1,0:T(8,128)(2,1)}), bf16[4,64,2048]{2,1,0:T(8,128)(2,1)}, u32[]{:S(2)}, u32[]{:S(2)}) async-start(bf16[4,64,2048]{2,1,0:T(8,128)(2,1)} %get-tuple-element.137), calls=%async_computation.3 | async-start | bytes 2097152 | tf_op jit(solution)/shard_map/all_to_all | solution.py:147
  412.1 4.2 collective-permute-start.7
  413.2 2.4 collective-permute-start.3
  418.7 15.3 %collective-permute-start.8 = (bf16[256,1024]{1,0:T(8,128)(2,1)S(1)}, bf16[256,1024]{1,0:T(8,128)(2,1)S(1)}, u32[]{:S(2)}, u32[]{:S(2)}) collective-permute-start(bf16[256,1024]{1,0:T(8,128)(2,1)S(1)} %get-tuple-element.112), channel_id=1, source_target_pairs={{0,2},{2,4},{4,6},{6,0},{1,3},{3,5},{5,7},{7,1},{8,10},{10,12},{12... | collective-permute-start | bytes 1572872 | tf_op jit(solution)/shard_map/ppermute | solution.py:143
  422.5 13.8 %collective-permute-start.10 = (bf16[256,1024]{1,0:T(8,128)(2,1)S(1)}, bf16[256,1024]{1,0:T(8,128)(2,1)S(1)}, u32[]{:S(2)}, u32[]{:S(2)}) collective-permute-start(bf16[256,1024]{1,0:T(8,128)(2,1)S(1)} %get-tuple-element.113), channel_id=1, source_target_pairs={{0,6},{2,0},{4,2},{6,4},{1,7},{3,1},{5,3},{7,5},{8,14},{10,8},{12,... | collective-permute-start | bytes 1572872 | tf_op jit(solution)/shard_map/ppermute | solution.py:143
  434.2 26.0 %collective-permute-start.9 = (bf16[256,2048]{1,0:T(8,128)(2,1)S(1)}, bf16[256,2048]{1,0:T(8,128)(2,1)}, u32[]{:S(2)}, u32[]{:S(2)}) collective-permute-start(bf16[256,2048]{1,0:T(8,128)(2,1)S(1)} %pad_maximum_fusion.2), channel_id=1, source_target_pairs={{0,2},{2,4},{4,6},{6,0},{1,3},{3,5},{5,7},{7,1},{8,10},{10,12},{12... | collective-permute-start | bytes 3145736 | tf_op jit(solution)/shard_map/ppermute | solution.py:143
  436.5 24.7 %collective-permute-start.11 = (bf16[256,2048]{1,0:T(8,128)(2,1)S(1)}, bf16[256,2048]{1,0:T(8,128)(2,1)}, u32[]{:S(2)}, u32[]{:S(2)}) collective-permute-start(bf16[256,2048]{1,0:T(8,128)(2,1)S(1)} %pad_maximum_fusion.3), channel_id=1, source_target_pairs={{0,6},{2,0},{4,2},{6,4},{1,7},{3,1},{5,3},{7,5},{8,14},{10,8},{12,... | collective-permute-start | bytes 3145736 | tf_op jit(solution)/shard_map/ppermute | solution.py:143
  439.7 30.5 %all-to-all-start.1 = ((bf16[4,64,2048]{2,1,0:T(8,128)(2,1)}), bf16[4,64,2048]{2,1,0:T(8,128)(2,1)S(1)}, u32[]{:S(2)}, u32[]{:S(2)}) async-start(bf16[4,64,2048]{2,1,0:T(8,128)(2,1)} %get-tuple-element.134), calls=%async_computation.1 | async-start | bytes 2097152 | tf_op jit(solution)/shard_map/all_to_all | solution.py:147
  465.1 27.7 %collective-permute-start.12 = (bf16[128,2048]{1,0:T(8,128)(2,1)}, bf16[128,2048]{1,0:T(8,128)(2,1)}, u32[]{:S(2)}, u32[]{:S(2)}) collective-permute-start(bf16[128,2048]{1,0:T(8,128)(2,1)} %fusion.5), channel_id=1, source_target_pairs={{0,8},{8,0},{1,9},{9,1},{2,10},{10,2},{3,11},{11,3},{4,12},{12,4},... | collective-permute-start | bytes 1572872 | tf_op jit(solution)/shard_map/ppermute | solution.py:143
Sparse Core Ops, SparseCore 0:
  9.9 208.1 all-gather.2

commit v3 on v2

--- a/solution.py
+++ b/solution.py
@@ -11,49 +11,123 @@
 epsilon = 1e-05
 STAGES = 4
 DEPTH = 4
-TILE = 512
-SLOTS = 8
-PLANE = ("zl", "zh", "y", "c")
-
-
-def tile_copies(w_ref, held, arrived, depth, tiles, order, by_rows):
-    slots = held.shape[0]
-
-    def copy(number):
-        slot = lax.rem(number, slots)
-        layer = order(number // tiles)
-        span = pl.ds(pl.multiple_of(lax.rem(number, tiles) * TILE, TILE), TILE)
-        source = w_ref.at[layer, span] if by_rows else w_ref.at[layer, :, span]
-        return pltpu.make_async_copy(source, held.at[slot], arrived.at[slot])
-
-    def refill(number):
-        @pl.when(number + slots < depth * tiles)
+SLOTS = 2
+
+
+def shift(value, axis, steps):
+    count = lax.axis_size(axis)
+    return lax.ppermute(value, axis, [(i, (i + steps) % count) for i in range(count)])
+
+
+def shift_z(value, steps):
+    lows, highs = lax.axis_size("zl"), lax.axis_size("zh")
+    spot = [(z % lows) * highs + z // lows for z in range(lows * highs)]
+    count = len(spot)
+    return lax.ppermute(
+        value, ("zl", "zh"), [(spot[z], spot[(z + steps) % count]) for z in range(count)]
+    )
+
+
+def gather_pieces(shard):
+    split = shard.shape[1] * 5 // 8
+    half = shard.shape[0] // 2
+    one, two = shard[:, :split], shard[:, split:]
+    pieces = []
+
+    below, above = shift(two, "y", 1), shift(two, "y", -1)
+    column = jnp.stack([two, below, above, shift(below, "y", 1)])
+    offsets = (0, 3, 1, 2)
+
+    m1, p1 = shift_z(one, 1), shift_z(one, -1)
+    m2, p2 = shift_z(m1, 1), shift_z(p1, -1)
+    m3, p3 = shift_z(m2, 1), shift_z(p2, -1)
+    m4 = shift_z(m3, 1)
+    for units, zs in (((one, m1, p1), (0, 7, 1)), ((m2, p2, m3, p3, m4), (6, 2, 5, 3, 4))):
+        batch = jnp.stack(units)
+        below, above = shift(batch, "y", 1), shift(batch, "y", -1)
+        far_low = shift(below[:, :half], "y", 1)
+        far_high = shift(above[:, half:], "y", -1)
+        for array, first, y in (
+            (batch, 0, 0), (below, 0, 3), (above, 0, 1), (far_low, 0, 2), (far_high, half, 2)
+        ):
+            pieces.append((0, array, first, zs, (y,) * len(zs)))
+
+    pieces.append((1, column, 0, (0,) * 4, offsets))
+    low = high = column
+    for z in (1, 2, 3, 4):
+        high = shift_z(high, -1)
+        pieces.append((1, high, 0, (z,) * 4, offsets))
+        if z < 4:
+            low = shift_z(low, 1)
+            pieces.append((1, low, 0, (8 - z,) * 4, offsets))
+    arrays = [[array, shift(array, "c", 1)] for _, array, _, _, _ in pieces]
+    plan = [(part, first, zs, ys) for part, _, first, zs, ys in pieces]
+    return arrays, plan
+
+
+def layer_copies(plan, refs, held, arrived, order):
+    lane, zh = lax.axis_index("zl"), lax.axis_index("zh")
+    y, core = lax.axis_index("y"), lax.axis_index("c")
+    depth = DEPTH
+    piece = held[0].shape[1] // 16
+    slots = held[0].shape[0]
+
+    def start(step, part):
+        slot = lax.rem(step, slots)
+        nearest = lax.rem(order(step) - lane + depth, depth)
+        for offset in range(depth):
+
+            @pl.when(nearest == offset)
+            def _(offset=offset):
+                for index, (kind, first, zs, ys) in enumerate(plan):
+                    for unit, (dz, dy) in enumerate(zip(zs, ys)):
+                        if kind != part or dz % depth != offset:
+                            continue
+                        chip = lax.rem((zh * depth + lane + dz) // depth, 2) * 4 + lax.rem(y + dy, 4)
+                        for sibling in range(2):
+                            source = refs[2 * index + sibling].at[unit]
+                            owner = core if sibling == 0 else 1 - core
+                            row = (chip * 2 + owner) * piece + first
+                            row = pl.ds(pl.multiple_of(row, piece // 2), source.shape[0])
+                            pltpu.make_async_copy(
+                                source, held[part].at[slot, row], arrived[part].at[slot]
+                            ).start()
+
+    def wait(step, part):
+        slot = lax.rem(step, slots)
+        whole = held[part].at[slot]
+        pltpu.make_async_copy(whole, whole, arrived[part].at[slot]).wait()
+
+    def refill(step, part):
+        @pl.when(step + slots < depth)
         def _():
-            copy(number + slots).start()
-
-    for number in range(slots):
-        copy(jnp.int32(number)).start()
-    return copy, refill
-
-
-def forward_kernel(x_ref, base_ref, w_ref, out_ref, x_now, normed, y, held, arrived):
-    depth, rows, width = base_ref.shape
-    tiles, slots = width // TILE, held.shape[0]
-    copy, refill = tile_copies(w_ref, held, arrived, depth, tiles, lambda i: i, False)
+            start(step + slots, part)
+
+    for step in range(slots):
+        for part in range(2):
+            start(jnp.int32(step), part)
+    return wait, refill
+
+
+def forward_kernel(plan, x_ref, base_ref, *refs):
+    weights, (out_ref, x_now, normed, y, *rest) = refs[: 2 * len(plan)], refs[2 * len(plan) :]
+    held, arrived = rest[:2], rest[2:]
+    slots = held[0].shape[0]
+    split = held[0].shape[2]
+    spans = (pl.ds(0, split), pl.ds(split, held[1].shape[2]))
+    wait, refill = layer_copies(plan, weights, held, arrived, lambda i: i)
     x_now[...] = x_ref[...].astype(jnp.float32)
 
     def run_layer(layer, carry):
         values = x_now[...]
         scale = lax.rsqrt(jnp.mean(values * values, axis=-1, keepdims=True) + epsilon)
         normed[...] = (values * scale).astype(jnp.bfloat16)
-        for tile in range(tiles):
-            number = layer * tiles + tile
-            copy(number).wait()
-            columns = pl.ds(tile * TILE, TILE)
+        for part, columns in enumerate(spans):
+            wait(layer, part)
             y[:, columns] = x_now[:, columns] + jnp.dot(
-                normed[...], held[lax.rem(number, slots)], preferred_element_type=jnp.float32
+                normed[...], held[part][lax.rem(layer, slots)], preferred_element_type=jnp.float32
             )
-            refill(number)
+            refill(layer, part)
         values = y[...]
         base = base_ref[layer].astype(jnp.float32)
         bound = 2.0 * jnp.sqrt(jnp.mean(values * values, axis=-1, keepdims=True) + epsilon)
@@ -63,26 +137,32 @@
         x_now[...] = coded.astype(jnp.float32)
         return carry
 
-    lax.fori_loop(0, depth, run_layer, 0)
-
-
-def backward_kernel(g_ref, x_ref, w_ref, seen_ref, out_ref, g_now, back, held, arrived):
-    depth, rows, width = x_ref.shape
-    tiles, slots = width // TILE, held.shape[0]
-    copy, refill = tile_copies(w_ref, held, arrived, depth, tiles, lambda i: depth - 1 - i, True)
+    lax.fori_loop(0, DEPTH, run_layer, 0)
+
+
+def backward_kernel(plan, g_ref, x_ref, *refs):
+    weights, (seen_ref, out_ref, g_now, back, *rest) = refs[: 2 * len(plan)], refs[2 * len(plan) :]
+    held, arrived = rest[:2], rest[2:]
+    slots = held[0].shape[0]
+    split = held[0].shape[2]
+    spans = (pl.ds(0, split), pl.ds(split, held[1].shape[2]))
+    wait, refill = layer_copies(plan, weights, held, arrived, lambda i: DEPTH - 1 - i)
     g_now[...] = g_ref[...]
 
     def run_layer(step, carry):
-        layer = depth - 1 - step
+        layer = DEPTH - 1 - step
         seen_ref[layer] = g_now[...]
-        for tile in range(tiles):
-            number = step * tiles + tile
-            copy(number).wait()
-            back[:, pl.ds(tile * TILE, TILE)] = lax.dot_general(
-                g_now[...], held[lax.rem(number, slots)], (((1,), (1,)), ((), ())),
+        for part, columns in enumerate(spans):
+            wait(step, part)
+            product = lax.dot_general(
+                g_now[:, columns], held[part][lax.rem(step, slots)], (((1,), (1,)), ((), ())),
                 preferred_element_type=jnp.float32,
             )
-            refill(number)
+            if part == 0:
+                back[...] = product
+            else:
+                back[...] += product
+            refill(step, part)
         values = x_ref[layer].astype(jnp.float32)
         scale = lax.rsqrt(jnp.mean(values * values, axis=-1, keepdims=True) + epsilon)
         normed = values * scale
@@ -92,21 +172,25 @@
         g_now[...] = sent.astype(jnp.bfloat16)
         return carry
 
-    lax.fori_loop(0, depth, run_layer, 0)
+    lax.fori_loop(0, DEPTH, run_layer, 0)
     out_ref[...] = g_now[...]
 
 
-def stage_call(kernel, tile_shape, scratch, outs, depth, rows, width):
+def stage_call(kernel, scratch, outs, first, second, weights):
+    arrays, plan = weights
+    depth, rows, width = second.shape
     vmem = pl.BlockSpec(memory_space=pltpu.VMEM)
+    operands = [array for pair in arrays for array in pair]
+    widths = [next(pair[0].shape[2] for pair, p in zip(arrays, plan) if p[0] == part) for part in range(2)]
     return pl.pallas_call(
-        kernel,
-        in_specs=[vmem, vmem, pl.BlockSpec(memory_space=pl.ANY)],
+        functools.partial(kernel, plan),
+        in_specs=[vmem, vmem, *[pl.BlockSpec(memory_space=pl.ANY)] * len(operands)],
         out_specs=[vmem] * len(outs),
         out_shape=[jax.ShapeDtypeStruct(shape, jnp.bfloat16) for shape in outs],
         scratch_shapes=[
             *scratch,
-            pltpu.VMEM((SLOTS, *tile_shape), jnp.bfloat16),
-            pltpu.SemaphoreType.DMA((SLOTS,)),
+            *[pltpu.VMEM((SLOTS, width, columns), jnp.bfloat16) for columns in widths],
+            *[pltpu.SemaphoreType.DMA((SLOTS,)) for _ in widths],
         ],
         compiler_params=pltpu.CompilerParams(vmem_limit_bytes=32 * 1024 * 1024),
         cost_estimate=pl.CostEstimate(
@@ -114,33 +198,24 @@
             bytes_accessed=2 * depth * width * width,
             transcendentals=0,
         ),
-    )
-
-
-def forward_stage(x, base, weight):
+    )(first, second, *operands)
+
+
+def forward_stage(x, base, weights):
     depth, rows, width = base.shape
     scratch = [
         pltpu.VMEM((rows, width), jnp.float32),
         pltpu.VMEM((rows, width), jnp.bfloat16),
         pltpu.VMEM((rows, width), jnp.float32),
     ]
-    call = stage_call(
-        forward_kernel, (width, TILE), scratch, [(depth, rows, width)], depth, rows, width
-    )
-    return call(x, base, weight)[0]
-
-
-def backward_stage(g, x, weight):
+    return stage_call(forward_kernel, scratch, [(depth, rows, width)], x, base, weights)[0]
+
+
+def backward_stage(g, x, weights):
     depth, rows, width = x.shape
     scratch = [pltpu.VMEM((rows, width), jnp.bfloat16), pltpu.VMEM((rows, width), jnp.float32)]
     outs = [(depth, rows, width), (rows, width)]
-    call = stage_call(backward_kernel, (TILE, width), scratch, outs, depth, rows, width)
-    return call(g, x, weight)
-
-
-def shift(value, axis, steps):
-    count = lax.axis_size(axis)
-    return lax.ppermute(value, axis, [(i, (i + steps) % count) for i in range(count)])
+    return stage_call(backward_kernel, scratch, outs, g, x, weights)
 
 
 def exchange(value):
@@ -187,8 +262,7 @@
     stage, lane = lax.axis_index("x"), lax.axis_index("zl")
     width = stream_in.shape[1]
     rows = stream_in.shape[0] // DEPTH
-    weight = lax.all_gather(layer_weight[0], PLANE, axis=0, tiled=True)
-    weight = weight.reshape(DEPTH, width, width)
+    weight = gather_pieces(layer_weight[0])
     picked = jnp.take(epoch_buffer[0], sample_ids[0], axis=0)
     base = exchange(picked.reshape(DEPTH, rows, width))
     x = lax.dynamic_slice_in_dim(stream_in, lane * rows, rows, 0)

time: 506 us -> 507 us (level)
  the two profiles are of different devices: /device:TPU:96 before, /device:TPU:24 now
where the time goes in v3:
time: 507 us; the launch traced here: 498 us
  waiting for transfers between devices  304 us (60%)
  starting transfers between devices  74.1 us (15%)
  Pallas kernels  59.5 us (12%)
  local copies, waits for them, and re-layouts  27.2 us (5%)
  other arithmetic  13.2 us (3%)
  matrix products  8.8 us (2%)
  loops' own time  8.76 us (2%)
    ppermute x36, waiting for transfers between devices, shift(): lax.ppermute(value, axis, [(i, (i + steps) % count) for i in range(count)])  99.2 us
    ppermute x3, waiting for transfers between devices, local(): arrived = lax.ppermute(sent, 'x', [(t + 1, t)])  97.9 us
    ppermute x14, waiting for transfers between devices, shift_z(): lax.ppermute(value, ('zl', 'zh'), [(spot[z], spot[(z + steps) % count]) f...  66.8 us
    pallas_call x3, Pallas kernels, stage_call(): pl.pallas_call(functools.partial(kernel, plan), in_specs=[vmem, vmem, *[p...  59.5 us
    all_to_all x4, waiting for transfers between devices, exchange(): return lax.all_to_all(value, 'zl', 0, 0)  35.7 us
    ppermute x36, starting transfers between devices, shift(): lax.ppermute(value, axis, [(i, (i + steps) % count) for i in range(count)])  25.4 us
    ppermute x14, starting transfers between devices, shift_z(): lax.ppermute(value, ('zl', 'zh'), [(spot[z], spot[(z + steps) % count]) f...  22.8 us
    all_to_all x4, starting transfers between devices, exchange(): return lax.all_to_all(value, 'zl', 0, 0)  15.7 us
  transfers between devices with their start and end apart: 60, of which 28 were waited for; matrix products, arithmetic and copies ran while one was open for 7% of the time, Pallas kernels for 3%

profile of v3, /device:TPU:24, one launch (start us, length us, event | category | flops | bytes accessed | tf_op | source)
XLA Modules:
  0.0 497.6 jit_solution(436319585598581408)
XLA Ops:
  1.6 2.0 collective-permute-start
  3.6 4.0 collective-permute-start.1
  7.7 7.6 %collective-permute-done = bf16[128,1280]{1,0:T(8,128)(2,1)S(1)} collective-permute-done((bf16[128,1280]{1,0:T(8,128)(2,1)S(1)}, bf16[128,1280]{1,0:T(8,128)(2,1)S(1)}, u32[]{:S(2)}, u32[]{:S(2)}) %collective-permute-start) | collective-permute-done | bytes 327712 | tf_op jit(solution)/shard_map/ppermute | solution.py:26
  17.2 2.6 collective-permute-start.25
  19.8 3.2 collective-permute-start.12
  23.1 3.7 collective-permute-start.27
  26.8 17.1 %collective-permute-done.26 = bf16[128,768]{1,0:T(8,128)(2,1)S(1)} collective-permute-done((bf16[128,768]{1,0:T(8,128)(2,1)S(1)}, bf16[128,768]{1,0:T(8,128)(2,1)S(1)}, u32[]{:S(2)}, u32[]{:S(2)}) %collective-permute-start.26) | collective-permute-done | bytes 196640 | tf_op jit(solution)/shard_map/ppermute | solution.py:19
  43.9 3.2 collective-permute-start.14
  48.8 4.2 collective-permute-done.13
  53.1 2.2 collective-permute-done.14
  55.3 2.3 collective-permute-start.31
  58.4 10.7 %collective-permute-done.29.refs_22_ = bf16[4,128,768]{2,1,0:T(8,128)(2,1)S(1)} collective-permute-done((bf16[4,128,768]{2,1,0:T(8,128)(2,1)S(1)}, bf16[4,128,768]{2,1,0:T(8,128)(2,1)S(1)}, u32[]{:S(2)}, u32[]{:S(2)}) %collective-permute-start.29) | collective-permute-done | bytes 786464 | tf_op jit(solution)/shard_map/ppermute | solution.py:26
  69.2 2.2 collective-permute-start.15
  74.0 3.2 collective-permute-done.31.refs_24_
  77.2 2.0 collective-permute-start.35
  79.2 5.0 %collective-permute-done.15 = bf16[128,1280]{1,0:T(8,128)(2,1)S(1)} collective-permute-done((bf16[128,1280]{1,0:T(8,128)(2,1)S(1)}, bf16[128,1280]{1,0:T(8,128)(2,1)S(1)}, u32[]{:S(2)}, u32[]{:S(2)}) %collective-permute-start.15) | collective-permute-done | bytes 327712 | tf_op jit(solution)/shard_map/ppermute | solution.py:26
  86.8 6.2 %collective-permute-done.7.refs_6_ = bf16[3,64,1280]{2,1,0:T(8,128)(2,1)S(1)} collective-permute-done((bf16[3,64,1280]{2,1,0:T(8,128)(2,1)S(1)}, bf16[3,64,1280]{2,1,0:T(8,128)(2,1)S(1)}, u32[]{:S(2)}, u32[]{:S(2)}) %collective-permute-start.7) | collective-permute-done | bytes 491552 | tf_op jit(solution)/shard_map/ppermute | solution.py:19
  93.6 4.7 collective-permute-done.35.refs_28_
  102.0 2.1 collective-permute-start.39
  104.0 18.1 %collective-permute-done.37.refs_30_ = bf16[4,128,768]{2,1,0:T(8,128)(2,1)} collective-permute-done((bf16[4,128,768]{2,1,0:T(8,128)(2,1)}, bf16[4,128,768]{2,1,0:T(8,128)(2,1)}, u32[]{:S(2)}, u32[]{:S(2)}) %collective-permute-start.37) | collective-permute-done | bytes 786464 | tf_op jit(solution)/shard_map/ppermute | solution.py:26
  123.4 14.0 %collective-permute-done.17.refs_12_ = bf16[5,128,1280]{2,1,0:T(8,128)(2,1)S(1)} collective-permute-done((bf16[5,128,1280]{2,1,0:T(8,128)(2,1)}, bf16[5,128,1280]{2,1,0:T(8,128)(2,1)S(1)}, u32[]{:S(2)}, u32[]{:S(2)}) %collective-permute-start.17) | collective-permute-done | bytes 1638432 | tf_op jit(solution)/shard_map/ppermute | solution.py:19
  139.5 3.8 gather_fusion
  147.3 9.8 %collective-permute-done.41.refs_34_ = bf16[4,128,768]{2,1,0:T(8,128)(2,1)} collective-permute-done((bf16[4,128,768]{2,1,0:T(8,128)(2,1)}, bf16[4,128,768]{2,1,0:T(8,128)(2,1)}, u32[]{:S(2)}, u32[]{:S(2)}) %collective-permute-start.41) | collective-permute-done | bytes 786464 | tf_op jit(solution)/shard_map/ppermute | solution.py:26
  158.2 4.3 all-to-all-start
  163.1 3.0 collective-permute-done.21.refs_16_
  166.2 2.2 collective-permute-done.23.refs_18_
  169.8 19.4 %all-to-all-done.base_ref = bf16[4,64,2048]{2,1,0:T(8,128)(2,1)} async-done(((bf16[4,64,2048]{2,1,0:T(8,128)(2,1)}), bf16[4,64,2048]{2,1,0:T(8,128)(2,1)}, u32[]{:S(2)}, u32[]{:S(2)}) %all-to-all-start) | async-done | bytes 1048608 | tf_op jit(solution)/shard_map/all_to_all | solution.py:222
  189.3 14.9 %shard_map.68 = bf16[4,64,2048]{2,1,0:T(8,128)(2,1)} custom-call(bf16[64,2048]{1,0:T(8,128)(2,1)S(1)} %constant_dynamic-slice_fusion.3.x_ref, bf16[4,64,2048]{2,1,0:T(8,128)(2,1)} %all-to-all-done.base_ref, bf16[3,128,1280]{2,1,0:T(8,128)(2,1)} %copy-done, bf16[3,128,1280]{2,1,0:T(8,128)(2,1)} %copy-done.7, bf16[3,128,1280]{2,1,0:T(8,128)(2,1)} %copy-done.4, ...), custom_call_target="tpu_custom_call" | custom-call | flops 2147483648 | bytes 33554432 | tf_op jit(solution)/shard_map/pallas_call | solution.py:185
  205.2 4.1 collective-permute-start.43
  209.3 4.7 collective-permute-done.43
  215.1 8.5 %conditional.6 = (bf16[4,64,2048]{2,1,0:T(8,128)(2,1)}) conditional(s32[]{:T(128)} %convert_element_type.56, bf16[4,64,2048]{2,1,0:T(8,128)(2,1)} %shard_map.68, (bf16[64,2048]{1,0:T(8,128)(2,1)S(1)}, bf16[4,64,2048]{2,1,0:T(8,128)(2,1)}, bf16[3,128,1280]{2,1,0:T(8,128)(2,1)}, bf16[3,128,1280]{2,1,0:T(8,128)(2,1)}, bf16[3,128,1280]{2,1,0:T(8,128)(2,1)}, ...), branch_computations={%region_0.1_spmd, %region_1.2_spmd} | conditional | flops 2147483648 | bytes 33554440 | solution.py:275
  235.6 27.5 %shard_map.69 = (bf16[4,64,2048]{2,1,0:T(8,128)(2,1)}, bf16[64,2048]{1,0:T(8,128)(2,1)}) custom-call(bf16[64,2048]{1,0:T(8,128)(2,1)S(1)} %constant_dynamic-slice_fusion.g_ref, bf16[4,64,2048]{2,1,0:T(8,128)(2,1)S(1)} %pad_maximum_fusion.1.x_ref, bf16[3,128,1280]{2,1,0:T(8,128)(2,1)S(1)} %copy-done.1, bf16[3,128,1280]{2,1,0:T(8,128)(2,1)} %copy-done.7, ...), custom_call_target="tpu_custom_call" | custom-call | flops 2147483648 | bytes 33554432 | tf_op jit(solution)/shard_map/pallas_call | solution.py:185
  264.5 4.3 all-to-all-start.2
  272.6 97.9 %collective-permute-done.49 = bf16[64,2048]{1,0:T(8,128)(2,1)S(1)} collective-permute-done((bf16[64,2048]{1,0:T(8,128)(2,1)}, bf16[64,2048]{1,0:T(8,128)(2,1)S(1)}, u32[]{:S(2)}, u32[]{:S(2)}) %collective-permute-start.49) | collective-permute-done | bytes 262176 | tf_op jit(solution)/shard_map/ppermute | solution.py:282
  370.4 17.3 %conditional.11 = (bf16[4,64,2048]{2,1,0:T(8,128)(2,1)}) conditional(s32[]{:T(128)} %convert_element_type.61, bf16[4,64,2048]{2,1,0:T(8,128)(2,1)} %get-tuple-element.740, (pred[]{:T(512)}, bf16[64,2048]{1,0:T(8,128)(2,1)S(1)}, bf16[64,2048]{1,0:T(8,128)(2,1)}, bf16[4,64,2048]{2,1,0:T(8,128)(2,1)}, bf16[3,128,1280]{2,1,0:T(8,128)(2,1)}, ...), branch_computations={%region_11.12_spmd, %region_12.13_spmd} | conditional | flops 2147614720 | bytes 34340872 | solution.py:284
  370.5 17.0 %branch_1_fun.11 = (bf16[4,64,2048]{2,1,0:T(8,128)(2,1)}, bf16[64,2048]{1,0:T(8,128)(2,1)}) custom-call(bf16[64,2048]{1,0:T(8,128)(2,1)S(1)} %broadcast_select_fusion.g_ref, bf16[4,64,2048]{2,1,0:T(8,128)(2,1)} %get-tuple-element.692.x_ref, bf16[3,128,1280]{2,1,0:T(8,128)(2,1)} %get-tuple-element.693.refs_0_, ...), custom_call_target="tpu_custom_call" | custom-call | flops 2147483648 | bytes 33554432 | tf_op jit(solution)/shard_map/cond/branch_1_fun/pallas_call | solution.py:185
  387.7 3.5 all-to-all-start.3
  392.9 3.2 reshape.115
  396.1 16.3 %all-to-all-done.3 = bf16[4,64,2048]{2,1,0:T(8,128)(2,1)S(1)} async-done(((bf16[4,64,2048]{2,1,0:T(8,128)(2,1)}), bf16[4,64,2048]{2,1,0:T(8,128)(2,1)S(1)}, u32[]{:S(2)}, u32[]{:S(2)}) %all-to-all-start.3) | async-done | bytes 1048608 | tf_op jit(solution)/shard_map/all_to_all | solution.py:222
  424.8 7.9 %collective-permute-done.51 = bf16[256,1024]{1,0:T(8,128)(2,1)S(1)} collective-permute-done((bf16[256,1024]{1,0:T(8,128)(2,1)S(1)}, bf16[256,1024]{1,0:T(8,128)(2,1)S(1)}, u32[]{:S(2)}, u32[]{:S(2)}) %collective-permute-start.51) | collective-permute-done | bytes 524320 | tf_op jit(solution)/shard_map/ppermute | solution.py:19
  433.0 2.7 collective-permute-start.52
  437.5 3.5 all-to-all-start.1
  441.9 15.7 %collective-permute-done.52 = bf16[256,2048]{1,0:T(8,128)(2,1)} collective-permute-done((bf16[256,2048]{1,0:T(8,128)(2,1)S(1)}, bf16[256,2048]{1,0:T(8,128)(2,1)}, u32[]{:S(2)}, u32[]{:S(2)}) %collective-permute-start.52) | collective-permute-done | bytes 1048608 | tf_op jit(solution)/shard_map/ppermute | solution.py:19
  457.6 5.3 %collective-permute-done.54 = bf16[256,2048]{1,0:T(8,128)(2,1)} collective-permute-done((bf16[256,2048]{1,0:T(8,128)(2,1)S(1)}, bf16[256,2048]{1,0:T(8,128)(2,1)}, u32[]{:S(2)}, u32[]{:S(2)}) %collective-permute-start.54) | collective-permute-done | bytes 1048608 | tf_op jit(solution)/shard_map/ppermute | solution.py:19
  462.9 3.0 fusion
  466.8 3.7 collective-permute-start.55
  470.5 23.6 %collective-permute-done.55 = bf16[128,2048]{1,0:T(8,128)(2,1)} collective-permute-done((bf16[128,2048]{1,0:T(8,128)(2,1)}, bf16[128,2048]{1,0:T(8,128)(2,1)}, u32[]{:S(2)}, u32[]{:S(2)}) %collective-permute-start.55) | collective-permute-done | bytes 524320 | tf_op jit(solution)/shard_map/ppermute | solution.py:19
  494.1 2.1 fusion.4
  (194 shorter events, 63.1 us)
Async XLA Ops:
  1.6 13.6 %collective-permute-start = (bf16[128,1280]{1,0:T(8,128)(2,1)S(1)}, bf16[128,1280]{1,0:T(8,128)(2,1)S(1)}, u32[]{:S(2)}, u32[]{:S(2)}) collective-permute-start(bf16[128,1280]{1,0:T(8,128)(2,1)S(1)} %get-tuple-element.753), channel_id=1, source_target_pairs={{0,16},{16,32},{32,48},{48,8},{8,24},{24,40},{40,56},{56,0},{1,17}... | collective-permute-start | bytes 983048 | tf_op jit(solution)/shard_map/ppermute | solution.py:26
  3.6 11.7 %collective-permute-start.1 = (bf16[128,1280]{1,0:T(8,128)(2,1)S(1)}, bf16[128,1280]{1,0:T(8,128)(2,1)S(1)}, u32[]{:S(2)}, u32[]{:S(2)}) collective-permute-start(bf16[128,1280]{1,0:T(8,128)(2,1)S(1)} %get-tuple-element.753), channel_id=1, source_target_pairs={{0,56},{16,0},{32,16},{48,32},{8,48},{24,8},{40,24},{56,40},{1,57}... | collective-permute-start | bytes 983048 | tf_op jit(solution)/shard_map/ppermute | solution.py:26
  15.4 42.1 %collective-permute-start.5 = (bf16[3,128,1280]{2,1,0:T(8,128)(2,1)S(1)}, bf16[3,128,1280]{2,1,0:T(8,128)(2,1)S(1)}, u32[]{:S(2)}, u32[]{:S(2)}) collective-permute-start(bf16[3,128,1280]{2,1,0:T(8,128)(2,1)S(1)} %pad_maximum_fusion.4.refs_0_), channel_id=1, source_target_pairs={{0,6},{2,0},{4,2},{6,4},{1,7},{3,1},{5,3},{7,5},{8,14},{10,8},{12,... | collective-permute-start | bytes 2949128 | tf_op jit(solution)/shard_map/ppermute | solution.py:19
  19.8 24.1 %collective-permute-start.11 = (bf16[128,1280]{1,0:T(8,128)(2,1)S(1)}, bf16[128,1280]{1,0:T(8,128)(2,1)S(1)}, u32[]{:S(2)}, u32[]{:S(2)}) collective-permute-start(bf16[128,1280]{1,0:T(8,128)(2,1)S(1)} %collective-permute-done), channel_id=1, source_target_pairs={{0,16},{16,32},{32,48},{48,8},{8,24},{24,40},{40,56},{56,0},{1,17}... | collective-permute-start | bytes 983048 | tf_op jit(solution)/shard_map/ppermute | solution.py:26
  19.8 24.1 %collective-permute-start.12 = (bf16[128,1280]{1,0:T(8,128)(2,1)S(1)}, bf16[128,1280]{1,0:T(8,128)(2,1)S(1)}, u32[]{:S(2)}, u32[]{:S(2)}) collective-permute-start(bf16[128,1280]{1,0:T(8,128)(2,1)S(1)} %collective-permute-done.1), channel_id=1, source_target_pairs={{0,56},{16,0},{32,16},{48,32},{8,48},{24,8},{40,24},{56,40},{1,57}... | collective-permute-start | bytes 983048 | tf_op jit(solution)/shard_map/ppermute | solution.py:26
  23.0 20.9 %collective-permute-start.26 = (bf16[128,768]{1,0:T(8,128)(2,1)S(1)}, bf16[128,768]{1,0:T(8,128)(2,1)S(1)}, u32[]{:S(2)}, u32[]{:S(2)}) collective-permute-start(bf16[128,768]{1,0:T(8,128)(2,1)S(1)} %get-tuple-element.751), channel_id=1, source_target_pairs={{0,6},{2,0},{4,2},{6,4},{1,7},{3,1},{5,3},{7,5},{8,14},{10,8},{12,... | collective-permute-start | bytes 589832 | tf_op jit(solution)/shard_map/ppermute | solution.py:19
  23.1 24.0 %collective-permute-start.27 = (bf16[128,768]{1,0:T(8,128)(2,1)S(1)}, bf16[128,768]{1,0:T(8,128)(2,1)S(1)}, u32[]{:S(2)}, u32[]{:S(2)}) collective-permute-start(bf16[128,768]{1,0:T(8,128)(2,1)S(1)} %collective-permute-done.25), channel_id=1, source_target_pairs={{0,2},{2,4},{4,6},{6,0},{1,3},{3,5},{5,7},{7,1},{8,10},{10,12},{12... | collective-permute-start | bytes 589832 | tf_op jit(solution)/shard_map/ppermute | solution.py:19
  43.9 27.6 %collective-permute-start.3 = (bf16[3,128,1280]{2,1,0:T(8,128)(2,1)S(1)}, bf16[3,128,1280]{2,1,0:T(8,128)(2,1)S(1)}, u32[]{:S(2)}, u32[]{:S(2)}) collective-permute-start(bf16[3,128,1280]{2,1,0:T(8,128)(2,1)S(1)} %pad_maximum_fusion.4.refs_0_), channel_id=1, source_target_pairs={{0,2},{2,4},{4,6},{6,0},{1,3},{3,5},{5,7},{7,1},{8,10},{10,12},{12... | collective-permute-start | bytes 2949128 | tf_op jit(solution)/shard_map/ppermute | solution.py:19
  43.9 9.2 %collective-permute-start.13 = (bf16[128,1280]{1,0:T(8,128)(2,1)S(1)}, bf16[128,1280]{1,0:T(8,128)(2,1)S(1)}, u32[]{:S(2)}, u32[]{:S(2)}) collective-permute-start(bf16[128,1280]{1,0:T(8,128)(2,1)S(1)} %collective-permute-done.11), channel_id=1, source_target_pairs={{0,16},{16,32},{32,48},{48,8},{8,24},{24,40},{40,56},{56,0},{1,17}... | collective-permute-start | bytes 983048 | tf_op jit(solution)/shard_map/ppermute | solution.py:26
  43.9 11.4 %collective-permute-start.14 = (bf16[128,1280]{1,0:T(8,128)(2,1)S(1)}, bf16[128,1280]{1,0:T(8,128)(2,1)S(1)}, u32[]{:S(2)}, u32[]{:S(2)}) collective-permute-start(bf16[128,1280]{1,0:T(8,128)(2,1)S(1)} %collective-permute-done.12), channel_id=1, source_target_pairs={{0,56},{16,0},{32,16},{48,32},{8,48},{24,8},{40,24},{56,40},{1,57}... | collective-permute-start | bytes 983048 | tf_op jit(solution)/shard_map/ppermute | solution.py:26
  47.2 21.9 %collective-permute-start.29 = (bf16[4,128,768]{2,1,0:T(8,128)(2,1)S(1)}, bf16[4,128,768]{2,1,0:T(8,128)(2,1)S(1)}, u32[]{:S(2)}, u32[]{:S(2)}) collective-permute-start(bf16[4,128,768]{2,1,0:T(8,128)(2,1)S(1)} %pad_maximum_fusion.5.refs_20_), channel_id=1, source_target_pairs={{0,56},{16,0},{32,16},{48,32},{8,48},{24,8},{40,24},{56,40},{1,57}... | collective-permute-start | bytes 2359304 | tf_op jit(solution)/shard_map/ppermute | solution.py:26
  53.1 32.5 %collective-permute-start.2 = (bf16[3,128,1280]{2,1,0:T(8,128)(2,1)S(1)}, bf16[3,128,1280]{2,1,0:T(8,128)(2,1)S(1)}, u32[]{:S(2)}, u32[]{:S(2)}) collective-permute-start(bf16[3,128,1280]{2,1,0:T(8,128)(2,1)S(1)} %pad_maximum_fusion.4.refs_0_), channel_id=1, source_target_pairs={{0,1},{1,0},{2,3},{3,2},{4,5},{5,4},{6,7},{7,6},{8,9},{9,8},{10,11... | collective-permute-start | bytes 2949128 | tf_op jit(solution)/shard_map/ppermute | solution.py:19
  55.3 21.9 %collective-permute-start.31 = (bf16[4,128,768]{2,1,0:T(8,128)(2,1)S(1)}, bf16[4,128,768]{2,1,0:T(8,128)(2,1)S(1)}, u32[]{:S(2)}, u32[]{:S(2)}) collective-permute-start(bf16[4,128,768]{2,1,0:T(8,128)(2,1)S(1)} %pad_maximum_fusion.5.refs_20_), channel_id=1, source_target_pairs={{0,16},{16,32},{32,48},{48,8},{8,24},{24,40},{40,56},{56,0},{1,17}... | collective-permute-start | bytes 2359304 | tf_op jit(solution)/shard_map/ppermute | solution.py:26
  57.6 19.6 %collective-permute-start.28 = (bf16[4,128,768]{2,1,0:T(8,128)(2,1)S(1)}, bf16[4,128,768]{2,1,0:T(8,128)(2,1)S(1)}, u32[]{:S(2)}, u32[]{:S(2)}) collective-permute-start(bf16[4,128,768]{2,1,0:T(8,128)(2,1)S(1)} %pad_maximum_fusion.5.refs_20_), channel_id=1, source_target_pairs={{0,1},{1,0},{2,3},{3,2},{4,5},{5,4},{6,7},{7,6},{8,9},{9,8},{10,11... | collective-permute-start | bytes 2359304 | tf_op jit(solution)/shard_map/ppermute | solution.py:19
  69.2 15.0 %collective-permute-start.15 = (bf16[128,1280]{1,0:T(8,128)(2,1)S(1)}, bf16[128,1280]{1,0:T(8,128)(2,1)S(1)}, u32[]{:S(2)}, u32[]{:S(2)}) collective-permute-start(bf16[128,1280]{1,0:T(8,128)(2,1)S(1)} %collective-permute-done.13), channel_id=1, source_target_pairs={{0,16},{16,32},{32,48},{48,8},{8,24},{24,40},{40,56},{56,0},{1,17}... | collective-permute-start | bytes 983048 | tf_op jit(solution)/shard_map/ppermute | solution.py:26
  71.4 14.1 %collective-permute-start.9 = (bf16[3,64,1280]{2,1,0:T(8,128)(2,1)S(1)}, bf16[3,64,1280]{2,1,0:T(8,128)(2,1)S(1)}, u32[]{:S(2)}, u32[]{:S(2)}) collective-permute-start(bf16[3,64,1280]{2,1,0:T(8,128)(2,1)S(1)} %slice.76), channel_id=1, source_target_pairs={{0,6},{2,0},{4,2},{6,4},{1,7},{3,1},{5,3},{7,5},{8,14},{10,8},{12,... | collective-permute-start | bytes 1474568 | tf_op jit(solution)/shard_map/ppermute | solution.py:19
  77.2 15.9 %collective-permute-start.33 = (bf16[4,128,768]{2,1,0:T(8,128)(2,1)S(1)}, bf16[4,128,768]{2,1,0:T(8,128)(2,1)}, u32[]{:S(2)}, u32[]{:S(2)}) collective-permute-start(bf16[4,128,768]{2,1,0:T(8,128)(2,1)S(1)} %collective-permute-done.29.refs_22_), channel_id=1, source_target_pairs={{0,56},{16,0},{32,16},{48,32},{8,48},{24,8},{40,24},{56,40},{1,57}... | collective-permute-start | bytes 2359304 | tf_op jit(solution)/shard_map/ppermute | solution.py:26
  77.2 21.0 %collective-permute-start.35 = (bf16[4,128,768]{2,1,0:T(8,128)(2,1)S(1)}, bf16[4,128,768]{2,1,0:T(8,128)(2,1)}, u32[]{:S(2)}, u32[]{:S(2)}) collective-permute-start(bf16[4,128,768]{2,1,0:T(8,128)(2,1)S(1)} %collective-permute-done.31.refs_24_), channel_id=1, source_target_pairs={{0,16},{16,32},{32,48},{48,8},{8,24},{24,40},{40,56},{56,0},{1,17}... | collective-permute-start | bytes 2359304 | tf_op jit(solution)/shard_map/ppermute | solution.py:26
  85.5 13.4 %collective-permute-start.30 = (bf16[4,128,768]{2,1,0:T(8,128)(2,1)S(1)}, bf16[4,128,768]{2,1,0:T(8,128)(2,1)S(1)}, u32[]{:S(2)}, u32[]{:S(2)}) collective-permute-start(bf16[4,128,768]{2,1,0:T(8,128)(2,1)S(1)} %collective-permute-done.29.refs_22_), channel_id=1, source_target_pairs={{0,1},{1,0},{2,3},{3,2},{4,5},{5,4},{6,7},{7,6},{8,9},{9,8},{10,11... | collective-permute-start | bytes 2359304 | tf_op jit(solution)/shard_map/ppermute | solution.py:19
  85.6 13.7 %collective-permute-start.32 = (bf16[4,128,768]{2,1,0:T(8,128)(2,1)S(1)}, bf16[4,128,768]{2,1,0:T(8,128)(2,1)S(1)}, u32[]{:S(2)}, u32[]{:S(2)}) collective-permute-start(bf16[4,128,768]{2,1,0:T(8,128)(2,1)S(1)} %collective-permute-done.31.refs_24_), channel_id=1, source_target_pairs={{0,1},{1,0},{2,3},{3,2},{4,5},{5,4},{6,7},{7,6},{8,9},{9,8},{10,11... | collective-permute-start | bytes 2359304 | tf_op jit(solution)/shard_map/ppermute | solution.py:19
  93.1 8.9 %collective-permute-start.6 = (bf16[3,128,1280]{2,1,0:T(8,128)(2,1)S(1)}, bf16[3,128,1280]{2,1,0:T(8,128)(2,1)S(1)}, u32[]{:S(2)}, u32[]{:S(2)}) collective-permute-start(bf16[3,128,1280]{2,1,0:T(8,128)(2,1)S(1)} %collective-permute-done.5.refs_4_), channel_id=1, source_target_pairs={{0,1},{1,0},{2,3},{3,2},{4,5},{5,4},{6,7},{7,6},{8,9},{9,8},{10,11... | collective-permute-start | bytes 2949128 | tf_op jit(solution)/shard_map/ppermute | solution.py:19
  99.0 38.4 %collective-permute-start.17 = (bf16[5,128,1280]{2,1,0:T(8,128)(2,1)}, bf16[5,128,1280]{2,1,0:T(8,128)(2,1)S(1)}, u32[]{:S(2)}, u32[]{:S(2)}) collective-permute-start(bf16[5,128,1280]{2,1,0:T(8,128)(2,1)} %bitcast_dynamic-update-slice_fusion.refs_10_), channel_id=1, source_target_pairs={{0,2},{2,4},{4,6},{6,0},{1,3},{3,5},{5,7},{7,1},{8,10},{10,12},{12... | collective-permute-start | bytes 4915208 | tf_op jit(solution)/shard_map/ppermute | solution.py:19
  100.1 39.3 %collective-permute-start.19 = (bf16[5,128,1280]{2,1,0:T(8,128)(2,1)}, bf16[5,128,1280]{2,1,0:T(8,128)(2,1)S(1)}, u32[]{:S(2)}, u32[]{:S(2)}) collective-permute-start(bf16[5,128,1280]{2,1,0:T(8,128)(2,1)} %bitcast_dynamic-update-slice_fusion.refs_10_), channel_id=1, source_target_pairs={{0,6},{2,0},{4,2},{6,4},{1,7},{3,1},{5,3},{7,5},{8,14},{10,8},{12,... | collective-permute-start | bytes 4915208 | tf_op jit(solution)/shard_map/ppermute | solution.py:19
  101.8 45.4 %collective-permute-start.16 = (bf16[5,128,1280]{2,1,0:T(8,128)(2,1)}, bf16[5,128,1280]{2,1,0:T(8,128)(2,1)}, u32[]{:S(2)}, u32[]{:S(2)}) collective-permute-start(bf16[5,128,1280]{2,1,0:T(8,128)(2,1)} %bitcast_dynamic-update-slice_fusion.refs_10_), channel_id=1, source_target_pairs={{0,1},{1,0},{2,3},{3,2},{4,5},{5,4},{6,7},{7,6},{8,9},{9,8},{10,11... | collective-permute-start | bytes 4915208 | tf_op jit(solution)/shard_map/ppermute | solution.py:19
  101.8 20.3 %collective-permute-start.37 = (bf16[4,128,768]{2,1,0:T(8,128)(2,1)}, bf16[4,128,768]{2,1,0:T(8,128)(2,1)}, u32[]{:S(2)}, u32[]{:S(2)}) collective-permute-start(bf16[4,128,768]{2,1,0:T(8,128)(2,1)} %collective-permute-done.33.refs_26_), channel_id=1, source_target_pairs={{0,56},{16,0},{32,16},{48,32},{8,48},{24,8},{40,24},{56,40},{1,57}... | collective-permute-start | bytes 2359304 | tf_op jit(solution)/shard_map/ppermute | solution.py:26
  102.0 21.4 %collective-permute-start.39 = (bf16[4,128,768]{2,1,0:T(8,128)(2,1)}, bf16[4,128,768]{2,1,0:T(8,128)(2,1)S(1)}, u32[]{:S(2)}, u32[]{:S(2)}) collective-permute-start(bf16[4,128,768]{2,1,0:T(8,128)(2,1)} %collective-permute-done.35.refs_28_), channel_id=1, source_target_pairs={{0,16},{16,32},{32,48},{48,8},{8,24},{24,40},{40,56},{56,0},{1,17}... | collective-permute-start | bytes 2359304 | tf_op jit(solution)/shard_map/ppermute | solution.py:26
  122.1 23.1 %collective-permute-start.34 = (bf16[4,128,768]{2,1,0:T(8,128)(2,1)}, bf16[4,128,768]{2,1,0:T(8,128)(2,1)}, u32[]{:S(2)}, u32[]{:S(2)}) collective-permute-start(bf16[4,128,768]{2,1,0:T(8,128)(2,1)} %collective-permute-done.33.refs_26_), channel_id=1, source_target_pairs={{0,1},{1,0},{2,3},{3,2},{4,5},{5,4},{6,7},{7,6},{8,9},{9,8},{10,11... | collective-permute-start | bytes 2359304 | tf_op jit(solution)/shard_map/ppermute | solution.py:19
  123.3 23.1 %collective-permute-start.36 = (bf16[4,128,768]{2,1,0:T(8,128)(2,1)}, bf16[4,128,768]{2,1,0:T(8,128)(2,1)}, u32[]{:S(2)}, u32[]{:S(2)}) collective-permute-start(bf16[4,128,768]{2,1,0:T(8,128)(2,1)} %collective-permute-done.35.refs_28_), channel_id=1, source_target_pairs={{0,1},{1,0},{2,3},{3,2},{4,5},{5,4},{6,7},{7,6},{8,9},{9,8},{10,11... | collective-permute-start | bytes 2359304 | tf_op jit(solution)/shard_map/ppermute | solution.py:19
  137.5 19.6 %collective-permute-start.41 = (bf16[4,128,768]{2,1,0:T(8,128)(2,1)}, bf16[4,128,768]{2,1,0:T(8,128)(2,1)}, u32[]{:S(2)}, u32[]{:S(2)}) collective-permute-start(bf16[4,128,768]{2,1,0:T(8,128)(2,1)} %collective-permute-done.37.refs_30_), channel_id=1, source_target_pairs={{0,56},{16,0},{32,16},{48,32},{8,48},{24,8},{40,24},{56,40},{1,57}... | collective-permute-start | bytes 2359304 | tf_op jit(solution)/shard_map/ppermute | solution.py:26
  139.3 23.2 %collective-permute-start.38 = (bf16[4,128,768]{2,1,0:T(8,128)(2,1)}, bf16[4,128,768]{2,1,0:T(8,128)(2,1)}, u32[]{:S(2)}, u32[]{:S(2)}) collective-permute-start(bf16[4,128,768]{2,1,0:T(8,128)(2,1)} %collective-permute-done.37.refs_30_), channel_id=1, source_target_pairs={{0,1},{1,0},{2,3},{3,2},{4,5},{5,4},{6,7},{7,6},{8,9},{9,8},{10,11... | collective-permute-start | bytes 2359304 | tf_op jit(solution)/shard_map/ppermute | solution.py:19
  145.2 20.9 %collective-permute-start.21 = (bf16[5,64,1280]{2,1,0:T(8,128)(2,1)}, bf16[5,64,1280]{2,1,0:T(8,128)(2,1)}, u32[]{:S(2)}, u32[]{:S(2)}) collective-permute-start(bf16[5,64,1280]{2,1,0:T(8,128)(2,1)} %slice.77), channel_id=1, source_target_pairs={{0,2},{2,4},{4,6},{6,0},{1,3},{3,5},{5,7},{7,1},{8,10},{10,12},{12... | collective-permute-start | bytes 2457608 | tf_op jit(solution)/shard_map/ppermute | solution.py:19
  146.5 21.9 %collective-permute-start.23 = (bf16[5,64,1280]{2,1,0:T(8,128)(2,1)}, bf16[5,64,1280]{2,1,0:T(8,128)(2,1)}, u32[]{:S(2)}, u32[]{:S(2)}) collective-permute-start(bf16[5,64,1280]{2,1,0:T(8,128)(2,1)} %slice.78), channel_id=1, source_target_pairs={{0,6},{2,0},{4,2},{6,4},{1,7},{3,1},{5,3},{7,5},{8,14},{10,8},{12,... | collective-permute-start | bytes 2457608 | tf_op jit(solution)/shard_map/ppermute | solution.py:19
  147.3 42.0 %collective-permute-start.18 = (bf16[5,128,1280]{2,1,0:T(8,128)(2,1)S(1)}, bf16[5,128,1280]{2,1,0:T(8,128)(2,1)}, u32[]{:S(2)}, u32[]{:S(2)}) collective-permute-start(bf16[5,128,1280]{2,1,0:T(8,128)(2,1)S(1)} %collective-permute-done.17.refs_12_), channel_id=1, source_target_pairs={{0,1},{1,0},{2,3},{3,2},{4,5},{5,4},{6,7},{7,6},{8,9},{9,8},{10,11... | collective-permute-start | bytes 4915208 | tf_op jit(solution)/shard_map/ppermute | solution.py:19
  157.1 32.2 %collective-permute-start.20 = (bf16[5,128,1280]{2,1,0:T(8,128)(2,1)S(1)}, bf16[5,128,1280]{2,1,0:T(8,128)(2,1)}, u32[]{:S(2)}, u32[]{:S(2)}) collective-permute-start(bf16[5,128,1280]{2,1,0:T(8,128)(2,1)S(1)} %collective-permute-done.19.refs_14_), channel_id=1, source_target_pairs={{0,1},{1,0},{2,3},{3,2},{4,5},{5,4},{6,7},{7,6},{8,9},{9,8},{10,11... | collective-permute-start | bytes 4915208 | tf_op jit(solution)/shard_map/ppermute | solution.py:19
  158.2 31.1 %all-to-all-start = ((bf16[4,64,2048]{2,1,0:T(8,128)(2,1)}), bf16[4,64,2048]{2,1,0:T(8,128)(2,1)}, u32[]{:S(2)}, u32[]{:S(2)}) async-start(bf16[4,64,2048]{2,1,0:T(8,128)(2,1)} %bitcast_select_fusion), calls=%async_computation | async-start | bytes 2097152 | tf_op jit(solution)/shard_map/all_to_all | solution.py:222
  166.2 23.1 %collective-permute-start.22 = (bf16[5,64,1280]{2,1,0:T(8,128)(2,1)}, bf16[5,64,1280]{2,1,0:T(8,128)(2,1)}, u32[]{:S(2)}, u32[]{:S(2)}) collective-permute-start(bf16[5,64,1280]{2,1,0:T(8,128)(2,1)} %collective-permute-done.21.refs_16_), channel_id=1, source_target_pairs={{0,1},{1,0},{2,3},{3,2},{4,5},{5,4},{6,7},{7,6},{8,9},{9,8},{10,11... | collective-permute-start | bytes 2457608 | tf_op jit(solution)/shard_map/ppermute | solution.py:19
  168.4 20.9 %collective-permute-start.24 = (bf16[5,64,1280]{2,1,0:T(8,128)(2,1)}, bf16[5,64,1280]{2,1,0:T(8,128)(2,1)}, u32[]{:S(2)}, u32[]{:S(2)}) collective-permute-start(bf16[5,64,1280]{2,1,0:T(8,128)(2,1)} %collective-permute-done.23.refs_18_), channel_id=1, source_target_pairs={{0,1},{1,0},{2,3},{3,2},{4,5},{5,4},{6,7},{7,6},{8,9},{9,8},{10,11... | collective-permute-start | bytes 2457608 | tf_op jit(solution)/shard_map/ppermute | solution.py:19
  168.4 20.9 %collective-permute-start.42 = (bf16[4,128,768]{2,1,0:T(8,128)(2,1)}, bf16[4,128,768]{2,1,0:T(8,128)(2,1)}, u32[]{:S(2)}, u32[]{:S(2)}) collective-permute-start(bf16[4,128,768]{2,1,0:T(8,128)(2,1)} %collective-permute-done.41.refs_34_), channel_id=1, source_target_pairs={{0,1},{1,0},{2,3},{3,2},{4,5},{5,4},{6,7},{7,6},{8,9},{9,8},{10,11... | collective-permute-start | bytes 2359304 | tf_op jit(solution)/shard_map/ppermute | solution.py:19
  205.2 8.8 %collective-permute-start.43 = (bf16[64,2048]{1,0:T(8,128)(2,1)S(1)}, bf16[64,2048]{1,0:T(8,128)(2,1)}, u32[]{:S(2)}, u32[]{:S(2)}) collective-permute-start(bf16[64,2048]{1,0:T(8,128)(2,1)S(1)} %slice_bitcast_fusion.2), channel_id=1, source_target_pairs={{0,64},{1,65},{2,66},{3,67},{4,68},{5,69},{6,70},{7,71},{8,72},{9,... | collective-permute-start | bytes 786440 | tf_op jit(solution)/shard_map/ppermute | solution.py:273
  264.5 123.3 %all-to-all-start.2 = ((bf16[4,64,2048]{2,1,0:T(8,128)(2,1)}), bf16[4,64,2048]{2,1,0:T(8,128)(2,1)}, u32[]{:S(2)}, u32[]{:S(2)}) async-start(bf16[4,64,2048]{2,1,0:T(8,128)(2,1)} %copy-done.16), calls=%async_computation.2 | async-start | bytes 2097152 | tf_op jit(solution)/shard_map/all_to_all | solution.py:222
  271.3 99.2 %collective-permute-start.49 = (bf16[64,2048]{1,0:T(8,128)(2,1)}, bf16[64,2048]{1,0:T(8,128)(2,1)S(1)}, u32[]{:S(2)}, u32[]{:S(2)}) collective-permute-start(bf16[64,2048]{1,0:T(8,128)(2,1)} %get-tuple-element.741), channel_id=1, source_target_pairs={{64,0},{65,1},{66,2},{67,3},{68,4},{69,5},{70,6},{71,7},{72,8},{73... | collective-permute-start | bytes 786440 | tf_op jit(solution)/shard_map/ppermute | solution.py:282
  387.7 24.6 %all-to-all-start.3 = ((bf16[4,64,2048]{2,1,0:T(8,128)(2,1)}), bf16[4,64,2048]{2,1,0:T(8,128)(2,1)S(1)}, u32[]{:S(2)}, u32[]{:S(2)}) async-start(bf16[4,64,2048]{2,1,0:T(8,128)(2,1)} %get-tuple-element.771), calls=%async_computation.3 | async-start | bytes 2097152 | tf_op jit(solution)/shard_map/all_to_all | solution.py:222
  418.6 14.1 %collective-permute-start.51 = (bf16[256,1024]{1,0:T(8,128)(2,1)S(1)}, bf16[256,1024]{1,0:T(8,128)(2,1)S(1)}, u32[]{:S(2)}, u32[]{:S(2)}) collective-permute-start(bf16[256,1024]{1,0:T(8,128)(2,1)S(1)} %get-tuple-element.742), channel_id=1, source_target_pairs={{0,2},{2,4},{4,6},{6,0},{1,3},{3,5},{5,7},{7,1},{8,10},{10,12},{12... | collective-permute-start | bytes 1572872 | tf_op jit(solution)/shard_map/ppermute | solution.py:19
  422.2 15.0 %collective-permute-start.53 = (bf16[256,1024]{1,0:T(8,128)(2,1)S(1)}, bf16[256,1024]{1,0:T(8,128)(2,1)S(1)}, u32[]{:S(2)}, u32[]{:S(2)}) collective-permute-start(bf16[256,1024]{1,0:T(8,128)(2,1)S(1)} %get-tuple-element.743), channel_id=1, source_target_pairs={{0,6},{2,0},{4,2},{6,4},{1,7},{3,1},{5,3},{7,5},{8,14},{10,8},{12,... | collective-permute-start | bytes 1572872 | tf_op jit(solution)/shard_map/ppermute | solution.py:19
  433.0 24.6 %collective-permute-start.52 = (bf16[256,2048]{1,0:T(8,128)(2,1)S(1)}, bf16[256,2048]{1,0:T(8,128)(2,1)}, u32[]{:S(2)}, u32[]{:S(2)}) collective-permute-start(bf16[256,2048]{1,0:T(8,128)(2,1)S(1)} %pad_maximum_fusion.2), channel_id=1, source_target_pairs={{0,2},{2,4},{4,6},{6,0},{1,3},{3,5},{5,7},{7,1},{8,10},{10,12},{12... | collective-permute-start | bytes 3145736 | tf_op jit(solution)/shard_map/ppermute | solution.py:19
  437.4 25.4 %collective-permute-start.54 = (bf16[256,2048]{1,0:T(8,128)(2,1)S(1)}, bf16[256,2048]{1,0:T(8,128)(2,1)}, u32[]{:S(2)}, u32[]{:S(2)}) collective-permute-start(bf16[256,2048]{1,0:T(8,128)(2,1)S(1)} %pad_maximum_fusion.3), channel_id=1, source_target_pairs={{0,6},{2,0},{4,2},{6,4},{1,7},{3,1},{5,3},{7,5},{8,14},{10,8},{12,... | collective-permute-start | bytes 3145736 | tf_op jit(solution)/shard_map/ppermute | solution.py:19
  437.5 32.9 %all-to-all-start.1 = ((bf16[4,64,2048]{2,1,0:T(8,128)(2,1)}), bf16[4,64,2048]{2,1,0:T(8,128)(2,1)S(1)}, u32[]{:S(2)}, u32[]{:S(2)}) async-start(bf16[4,64,2048]{2,1,0:T(8,128)(2,1)} %get-tuple-element.768), calls=%async_computation.1 | async-start | bytes 2097152 | tf_op jit(solution)/shard_map/all_to_all | solution.py:222
  466.8 27.3 %collective-permute-start.55 = (bf16[128,2048]{1,0:T(8,128)(2,1)}, bf16[128,2048]{1,0:T(8,128)(2,1)}, u32[]{:S(2)}, u32[]{:S(2)}) collective-permute-start(bf16[128,2048]{1,0:T(8,128)(2,1)} %fusion.5), channel_id=1, source_target_pairs={{0,8},{8,0},{1,9},{9,1},{2,10},{10,2},{3,11},{11,3},{4,12},{12,4},... | collective-permute-start | bytes 1572872 | tf_op jit(solution)/shard_map/ppermute | solution.py:19
  (37 other events, 927.5 us)

commit v4 on v3

v4 whole, which is shorter than its diff:
```python
import functools

import jax
import jax.numpy as jnp
from jax import lax
from jax.experimental import pallas as pl
from jax.experimental.pallas import tpu as pltpu
from jax.sharding import Mesh
from jax.sharding import PartitionSpec as P

epsilon = 1e-05
STAGES = 4
DEPTH = 4
SLOTS = 2


def shift(value, axis, steps):
    count = lax.axis_size(axis)
    return lax.ppermute(value, axis, [(i, (i + steps) % count) for i in range(count)])


def shift_z(value, steps):
    lows, highs = lax.axis_size("zl"), lax.axis_size("zh")
    spot = [(z % lows) * highs + z // lows for z in range(lows * highs)]
    count = len(spot)
    return lax.ppermute(
        value, ("zl", "zh"), [(spot[z], spot[(z + steps) % count]) for z in range(count)]
    )


def base_round(picked, steps):
    lane = lax.axis_index("zl")
    target = lax.rem(lane + steps, DEPTH)
    return shift(lax.dynamic_index_in_dim(picked, target, 0, keepdims=False), "zl", steps)


def gather_pieces(shard, picked):
    split = shard.shape[1] * 11 // 16
    half = shard.shape[0] // 2
    one, two = shard[:, :split], shard[:, split:]
    pieces, waiting = [], []

    def keep(part, array, first, zs, ys):
        if array.ndim == 2:
            array = array[None]
        waiting.append([part, array, first, zs, ys])

    def swap():
        taken, waiting[:] = list(waiting), []
        swapped = [shift(entry[1], "c", 1) for entry in taken]
        return taken, swapped

    def close(taken, swapped, *arrived):
        arrived, swapped = lax.optimization_barrier((arrived, swapped))
        for entry, other in zip(taken, swapped):
            pieces.append((entry, other))
        return arrived

    def both(array, move):
        return move(array, 1), move(array, -1)

    def along_y(array, steps):
        return shift(array, "y", steps)

    def far(low, high, move):
        return move(low[..., :half, :], 1), move(high[..., half:, :], -1)

    def keep_y(part, pair, zs):
        keep(part, pair[0], 0, zs, (3,) * len(zs))
        keep(part, pair[1], 0, zs, (1,) * len(zs))

    def keep_far(part, pair, zs, ys):
        keep(part, pair[0], 0, zs, ys)
        keep(part, pair[1], half, zs, ys)

    keep(0, one, 0, (0,), (0,))
    taken, swapped = swap()
    m1, p1, low, high = close(taken, swapped, *both(one, shift_z), *both(two, along_y))
    pair1 = jnp.stack([m1, p1])
    keep(0, pair1, 0, (7, 1), (0, 0))
    taken, swapped = swap()
    m2, p2, far_low, far_high, y0_low, y0_high, base1, base3 = close(
        taken, swapped, shift_z(m1, 1), shift_z(p1, -1), *far(low, high, along_y),
        *both(one, along_y), base_round(picked, 1), base_round(picked, 3),
    )
    column = jnp.stack([two, low, high, jnp.concatenate([far_low, far_high], axis=0)])
    ys = (0, 3, 1, 2)
    pair2 = jnp.stack([m2, p2])
    keep(1, column, 0, (0,) * 4, ys)
    keep_y(0, (y0_low, y0_high), (0,))
    keep(0, pair2, 0, (6, 2), (0, 0))
    taken, swapped = swap()
    m3, p3, y1_low, y1_high, base2 = close(
        taken, swapped, shift_z(m2, 1), shift_z(p2, -1), *both(pair1, along_y), base_round(picked, 2)
    )
    pair3 = jnp.stack([m3, p3])
    keep(0, pair3, 0, (5, 3), (0, 0))
    keep_y(0, (y1_low, y1_high), (7, 1))
    taken, swapped = swap()
    c_m1, c_p1, f_low, f_high, y2_low, y2_high, y0f_low, y0f_high = close(
        taken, swapped, *both(column, shift_z), *far(m3, p3, shift_z), *both(pair2, along_y),
        *far(y0_low, y0_high, along_y),
    )
    m4 = jnp.concatenate([f_low, f_high], axis=0)
    keep(1, c_m1, 0, (7,) * 4, ys)
    keep(1, c_p1, 0, (1,) * 4, ys)
    keep(0, m4, 0, (4,), (0,))
    keep_y(0, (y2_low, y2_high), (6, 2))
    keep_far(0, (y0f_low, y0f_high), (0,), (2,))
    taken, swapped = swap()
    c_m2, c_p2, y3_low, y3_high, y1f_low, y1f_high = close(
        taken, swapped, shift_z(c_m1, 1), shift_z(c_p1, -1), *both(pair3, along_y),
        *far(y1_low, y1_high, along_y),
    )
    keep(1, c_m2, 0, (6,) * 4, ys)
    keep(1, c_p2, 0, (2,) * 4, ys)
    keep_y(0, (y3_low, y3_high), (5, 3))
    keep_far(0, (y1f_low, y1f_high), (7, 1), (2, 2))
    taken, swapped = swap()
    c_m3, c_p3, y4_low, y4_high, y2f_low, y2f_high = close(
        taken, swapped, shift_z(c_m2, 1), shift_z(c_p2, -1), *both(m4, along_y),
        *far(y2_low, y2_high, along_y),
    )
    keep(1, c_m3, 0, (5,) * 4, ys)
    keep(1, c_p3, 0, (3,) * 4, ys)
    keep_y(0, (y4_low, y4_high), (4,))
    keep_far(0, (y2f_low, y2f_high), (6, 2), (2, 2))
    taken, swapped = swap()
    c4_low, c4_high, y3f_low, y3f_high, y4f_low, y4f_high = close(
        taken, swapped, *far(c_m3, c_p3, shift_z), *far(y3_low, y3_high, along_y),
        *far(y4_low, y4_high, along_y),
    )
    keep_far(1, (c4_low, c4_high), (4,) * 4, ys)
    keep_far(0, (y3f_low, y3f_high), (5, 3), (2, 2))
    keep_far(0, (y4f_low, y4f_high), (4,), (2,))
    taken, swapped = swap()
    pieces.extend(zip(taken, swapped))

    own = lax.dynamic_index_in_dim(picked, lax.axis_index("zl"), 0, keepdims=False)
    base = jnp.stack([own, base1, base2, base3])
    arrays = [[entry[1], other] for entry, other in pieces]
    plan = [(part, first, zs, ys) for (part, _, first, zs, ys), _ in pieces]
    return (arrays, plan), base


def layer_copies(plan, refs, held, arrived, order):
    lane, zh = lax.axis_index("zl"), lax.axis_index("zh")
    y, core = lax.axis_index("y"), lax.axis_index("c")
    depth = DEPTH
    piece = held[0].shape[1] // 16
    slots = held[0].shape[0]

    def start(step, part):
        slot = lax.rem(step, slots)
        nearest = lax.rem(order(step) - lane + depth, depth)
        for offset in range(depth):

            @pl.when(nearest == offset)
            def _(offset=offset):
                for index, (kind, first, zs, ys) in enumerate(plan):
                    for unit, (dz, dy) in enumerate(zip(zs, ys)):
                        if kind != part or dz % depth != offset:
                            continue
                        chip = lax.rem((zh * depth + lane + dz) // depth, 2) * 4 + lax.rem(y + dy, 4)
                        for sibling in range(2):
                            source = refs[2 * index + sibling].at[unit]
                            owner = core if sibling == 0 else 1 - core
                            row = (chip * 2 + owner) * piece + first
                            row = pl.ds(pl.multiple_of(row, piece // 2), source.shape[0])
                            pltpu.make_async_copy(
                                source, held[part].at[slot, row], arrived[part].at[slot]
                            ).start()

    def wait(step, part):
        slot = lax.rem(step, slots)
        whole = held[part].at[slot]
        pltpu.make_async_copy(whole, whole, arrived[part].at[slot]).wait()

    return start, wait


def run_layers(copies, held, layer_start, part_product, layer_end):
    start, wait = copies
    slots = held[0].shape[0]
    split = held[0].shape[2]
    spans = (pl.ds(0, split), pl.ds(split, held[1].shape[2]))

    def iteration(count, carry):
        step = count - slots
        ready, more = step >= 0, count < DEPTH
        now = jnp.maximum(step, 0)

        @pl.when(ready)
        def _():
            layer_start(now)

        for part, columns in enumerate(spans):

            @pl.when(ready)
            def _(part=part, columns=columns):
                wait(now, part)
                part_product(part, columns, held[part].at[lax.rem(now, slots)])

            @pl.when(more)
            def _(part=part):
                start(count, part)

        @pl.when(ready)
        def _():
            layer_end(now)

        return carry

    lax.fori_loop(0, DEPTH + slots, iteration, 0)


def forward_kernel(plan, x_ref, base_ref, *refs):
    weights, rest = refs[: 2 * len(plan)], refs[2 * len(plan) :]
    in_ref, out_ref, last_ref, x_now, normed, y, *rest = rest
    held, arrived = rest[:2], rest[2:]
    lane = lax.axis_index("zl")
    copies = layer_copies(plan, weights, held, arrived, lambda i: i)
    x_now[...] = x_ref[...].astype(jnp.float32)
    in_ref[0] = x_ref[...]

    def layer_start(layer):
        values = x_now[...]
        scale = lax.rsqrt(jnp.mean(values * values, axis=-1, keepdims=True) + epsilon)
        normed[...] = (values * scale).astype(jnp.bfloat16)

    def part_product(part, columns, weight):
        y[:, columns] = x_now[:, columns] + jnp.dot(
            normed[...], weight[...], preferred_element_type=jnp.float32
        )

    def layer_end(layer):
        values = y[...]
        base = base_ref[lax.rem(lane - layer + DEPTH, DEPTH)].astype(jnp.float32)
        bound = 2.0 * jnp.sqrt(jnp.mean(values * values, axis=-1, keepdims=True) + epsilon)
        delta = jnp.clip(values - base, -bound, bound).astype(jnp.bfloat16)
        coded = (base + delta.astype(jnp.float32)).astype(jnp.bfloat16)
        out_ref[layer] = coded
        x_now[...] = coded.astype(jnp.float32)

        @pl.when(layer < DEPTH - 1)
        def _():
            in_ref[layer + 1] = coded

        @pl.when(layer == DEPTH - 1)
        def _():
            last_ref[...] = coded

    run_layers(copies, held, layer_start, part_product, layer_end)


def backward_kernel(plan, g_ref, x_ref, *refs):
    weights, (seen_ref, out_ref, g_now, back, *rest) = refs[: 2 * len(plan)], refs[2 * len(plan) :]
    held, arrived = rest[:2], rest[2:]
    copies = layer_copies(plan, weights, held, arrived, lambda i: DEPTH - 1 - i)
    g_now[...] = g_ref[...]

    def layer_start(step):
        seen_ref[DEPTH - 1 - step] = g_now[...]

    def part_product(part, columns, weight):
        product = lax.dot_general(
            g_now[:, columns], weight[...], (((1,), (1,)), ((), ())),
            preferred_element_type=jnp.float32,
        )
        if part == 0:
            back[...] = product
        else:
            back[...] += product

    def layer_end(step):
        values = x_ref[DEPTH - 1 - step].astype(jnp.float32)
        scale = lax.rsqrt(jnp.mean(values * values, axis=-1, keepdims=True) + epsilon)
        normed = values * scale
        through = back[...]
        along = jnp.mean(normed * through, axis=-1, keepdims=True)
        sent = g_now[...].astype(jnp.float32) + scale * (through - normed * along)
        g_now[...] = sent.astype(jnp.bfloat16)

    run_layers(copies, held, layer_start, part_product, layer_end)
    out_ref[...] = g_now[...]


def stage_call(kernel, scratch, outs, first, second, weights):
    arrays, plan = weights
    depth, rows, width = second.shape
    vmem = pl.BlockSpec(memory_space=pltpu.VMEM)
    operands = [array for pair in arrays for array in pair]
    widths = [next(pair[0].shape[2] for pair, p in zip(arrays, plan) if p[0] == part) for part in range(2)]
    return pl.pallas_call(
        functools.partial(kernel, plan),
        in_specs=[vmem, vmem, *[pl.BlockSpec(memory_space=pl.ANY)] * len(operands)],
        out_specs=[vmem] * len(outs),
        out_shape=[jax.ShapeDtypeStruct(shape, jnp.bfloat16) for shape in outs],
        scratch_shapes=[
            *scratch,
            *[pltpu.VMEM((SLOTS, width, columns), jnp.bfloat16) for columns in widths],
            *[pltpu.SemaphoreType.DMA((SLOTS,)) for _ in widths],
        ],
        compiler_params=pltpu.CompilerParams(vmem_limit_bytes=56 * 1024 * 1024),
        cost_estimate=pl.CostEstimate(
            flops=2 * depth * rows * width * width,
            bytes_accessed=2 * depth * width * width,
            transcendentals=0,
        ),
    )(first, second, *operands)


def forward_stage(x, base, weights):
    depth, rows, width = base.shape
    scratch = [
        pltpu.VMEM((rows, width), jnp.float32),
        pltpu.VMEM((rows, width), jnp.bfloat16),
        pltpu.VMEM((rows, width), jnp.float32),
    ]
    outs = [(depth, rows, width), (depth, rows, width), (rows, width)]
    return tuple(stage_call(forward_kernel, scratch, outs, x, base, weights))


def backward_stage(g, x, weights):
    depth, rows, width = x.shape
    scratch = [pltpu.VMEM((rows, width), jnp.bfloat16), pltpu.VMEM((rows, width), jnp.float32)]
    outs = [(depth, rows, width), (rows, width)]
    return tuple(stage_call(backward_kernel, scratch, outs, g, x, weights))


def exchange(value):
    return lax.all_to_all(value, "zl", 0, 0)


def gradient_sum(normed, g):
    rows, width = normed.shape
    core, y, zh = lax.axis_index("c"), lax.axis_index("y"), lax.axis_index("zh")
    chips = lax.axis_size("zh") * lax.axis_size("y")
    piece = width // (2 * chips)
    by_core = normed.reshape(rows, chips, 2, piece)
    mine = lax.dynamic_index_in_dim(by_core, core, 2, keepdims=False).reshape(rows, -1)
    theirs = lax.dynamic_index_in_dim(by_core, 1 - core, 2, keepdims=False).reshape(rows, -1)
    left = jnp.concatenate([mine, shift(theirs, "c", 1)], axis=0)
    right = jnp.concatenate([g, shift(g, "c", 1)], axis=0)

    left = left.reshape(2 * rows, 2, 4, piece)

    def block(steps, columns):
        picked = lax.dynamic_index_in_dim(left, lax.rem(y + steps + 4, 4), 2, keepdims=False)
        return lax.dot_general(
            picked.reshape(2 * rows, 2 * piece), columns, (((0,), (0,)), ((), ())),
            preferred_element_type=jnp.float32,
        )

    half = width // 4
    results = []
    for chunk in range(2):
        columns = right[:, chunk * 2 * half : (chunk + 1) * 2 * half]
        far = block(2, columns).astype(jnp.bfloat16)
        up1 = shift(far[:, :half], "y", 1)
        down1 = shift(far[:, half:], "y", -1)
        up, down, own = block(1, columns), block(-1, columns), block(0, columns)
        up = jnp.concatenate([up[:, :half] + up1.astype(jnp.float32), up[:, half:]], axis=1)
        down = jnp.concatenate([down[:, :half], down[:, half:] + down1.astype(jnp.float32)], axis=1)
        up2 = shift(up.astype(jnp.bfloat16), "y", 1)
        down2 = shift(down.astype(jnp.bfloat16), "y", -1)
        total = own + up2.astype(jnp.float32) + down2.astype(jnp.float32)
        total = total.reshape(2, piece, 2 * half)
        kept = lax.dynamic_index_in_dim(total, zh, 0, keepdims=False)
        given = lax.dynamic_index_in_dim(total, 1 - zh, 0, keepdims=False).astype(jnp.bfloat16)
        results.append(kept + shift(given, "zh", 1).astype(jnp.float32))
    return jnp.concatenate(results, axis=1)


def local(stream_in, sample_ids, epoch_buffer, layer_weight, top_cotangent):
    stage, lane = lax.axis_index("x"), lax.axis_index("zl")
    width = stream_in.shape[1]
    rows = stream_in.shape[0] // DEPTH
    picked = jnp.take(epoch_buffer[0], sample_ids[0], axis=0).reshape(DEPTH, rows, width)
    weight, base = gather_pieces(layer_weight[0], picked)
    x = lax.dynamic_slice_in_dim(stream_in, lane * rows, rows, 0)
    g = lax.dynamic_slice_in_dim(top_cotangent, lane * rows, rows, 0)

    state = forward_stage(x, base, weight)
    for t in range(1, STAGES):
        arrived = lax.ppermute(state[2], "x", [(t - 1, t)])
        state = lax.cond(
            stage == t, lambda a, s: forward_stage(a, base, weight), lambda a, s: s, arrived, state
        )
    inputs, decoded, _ = state

    state = backward_stage(g, inputs, weight)
    for t in range(STAGES - 2, -1, -1):
        arrived = lax.ppermute(state[1], "x", [(t + 1, t)])
        state = lax.cond(
            stage == t, lambda a, s: backward_stage(a, inputs, weight), lambda a, s: s, arrived, state
        )
    seen = state[0]

    decoded_rows = exchange(decoded).reshape(1, DEPTH * rows, width)
    input_rows = exchange(inputs).reshape(DEPTH * rows, width).astype(jnp.float32)
    scale = lax.rsqrt(jnp.mean(input_rows * input_rows, axis=-1, keepdims=True) + epsilon)
    normed = (input_rows * scale).astype(jnp.bfloat16)
    cotangents = exchange(seen).reshape(DEPTH * rows, width)
    return decoded_rows, gradient_sum(normed, cotangents)[None]


def solution(mesh):
    fine = Mesh(mesh.devices.reshape(4, 4, 2, 4, 2), ("x", "zl", "zh", "y", "c"))
    section, dp = ("x", "zl"), ("zh", "y", "c")
    in_specs = (
        P(dp, None),
        P(dp, None),
        P(section, dp, None, None),
        P(section, dp, None),
        P(dp, None),
    )
    out_specs = (P(section, dp, None), P(section, dp, None))
    return jax.shard_map(local, mesh=fine, in_specs=in_specs, out_specs=out_specs, check_vma=False)
```

time: 507 us -> 529 us (1.043)
  the two profiles are of different devices: /device:TPU:24 before, /device:TPU:1 now
where the time goes in v4:
time: 529 us; the launch traced here: 519 us
  waiting for transfers between devices  264 us (50%)
  starting transfers between devices  142 us (27%)
  Pallas kernels  56.1 us (11%)
  local copies, waits for them, and re-layouts  32.9 us (6%)
  other arithmetic  15.8 us (3%)
  matrix products  5.89 us (1%)
    ppermute x3, waiting for transfers between devices, local(): arrived = lax.ppermute(state[1], 'x', [(t + 1, t)])  115 us
    ppermute x73, waiting for transfers between devices, shift(): lax.ppermute(value, axis, [(i, (i + steps) % count) for i in range(count)])  97.8 us
    ppermute x73, starting transfers between devices, shift(): lax.ppermute(value, axis, [(i, (i + steps) % count) for i in range(count)])  87.5 us
    pallas_call x3, Pallas kernels, stage_call(): pl.pallas_call(functools.partial(kernel, plan), in_specs=[vmem, vmem, *[p...  56.1 us
    ppermute x16, starting transfers between devices, shift_z(): lax.ppermute(value, ('zl', 'zh'), [(spot[z], spot[(z + steps) % count]) f...  31.1 us
    ppermute x16, waiting for transfers between devices, shift_z(): lax.ppermute(value, ('zl', 'zh'), [(spot[z], spot[(z + steps) % count]) f...  27.7 us
    all_to_all x3, waiting for transfers between devices, exchange(): return lax.all_to_all(value, 'zl', 0, 0)  18.2 us
    all_to_all x3, starting transfers between devices, exchange(): return lax.all_to_all(value, 'zl', 0, 0)  12.9 us
  transfers between devices with their start and end apart: 98, of which 24 were waited for; matrix products, arithmetic and copies ran while one was open for 9% of the time, Pallas kernels for 8%

profile of v4, /device:TPU:1, one launch (start us, length us, event | category | flops | bytes accessed | tf_op | source)
XLA Modules:
  0.0 519.3 jit_solution(8368190477122493454)
XLA Ops:
  4.9 3.9 collective-permute-start.1
  16.8 2.8 gather_fusion
  24.7 3.3 collective-permute-start.12
  28.0 6.5 %collective-permute-done.11 = bf16[64,2048]{1,0:T(8,128)(2,1)S(1)} collective-permute-done((bf16[64,2048]{1,0:T(8,128)(2,1)S(1)}, bf16[64,2048]{1,0:T(8,128)(2,1)S(1)}, u32[]{:S(2)}, u32[]{:S(2)}) %collective-permute-start.11) | collective-permute-done | bytes 262176 | tf_op jit(solution)/shard_map/ppermute | solution.py:19
  34.5 3.7 collective-permute-done.12
  39.0 2.7 collective-permute-start.6
  41.8 2.7 collective-permute-start.8
  46.0 3.6 collective-permute-start.17
  52.9 10.2 %collective-permute-done.18 = bf16[64,2048]{1,0:T(8,128)(2,1)S(1)} collective-permute-done((bf16[64,2048]{1,0:T(8,128)(2,1)S(1)}, bf16[64,2048]{1,0:T(8,128)(2,1)S(1)}, u32[]{:S(2)}, u32[]{:S(2)}) %collective-permute-start.18) | collective-permute-done | bytes 262176 | tf_op jit(solution)/shard_map/ppermute | solution.py:19
  66.1 5.0 collective-permute-start.23
  75.1 2.9 collective-permute-done.29
  79.5 14.6 %collective-permute-done.30 = bf16[64,1408]{1,0:T(8,128)(2,1)S(1)} collective-permute-done((bf16[64,1408]{1,0:T(8,128)(2,1)S(1)}, bf16[64,1408]{1,0:T(8,128)(2,1)S(1)}, u32[]{:S(2)}, u32[]{:S(2)}) %collective-permute-start.30) | collective-permute-done | bytes 180256 | tf_op jit(solution)/shard_map/ppermute | solution.py:19
  100.4 4.5 collective-permute-done.25
  111.4 19.5 %collective-permute-done.38.refs_40_ = bf16[2,64,1408]{2,1,0:T(8,128)(2,1)S(1)} collective-permute-done((bf16[2,64,1408]{2,1,0:T(8,128)(2,1)S(1)}, bf16[2,64,1408]{2,1,0:T(8,128)(2,1)S(1)}, u32[]{:S(2)}, u32[]{:S(2)}) %collective-permute-start.38) | collective-permute-done | bytes 360480 | tf_op jit(solution)/shard_map/ppermute | solution.py:19
  136.6 12.4 %collective-permute-done.35.refs_34_ = bf16[4,128,640]{2,1,0:T(8,128)(2,1)S(1)} collective-permute-done((bf16[4,128,640]{2,1,0:T(8,128)(2,1)S(1)}, bf16[4,128,640]{2,1,0:T(8,128)(2,1)S(1)}, u32[]{:S(2)}, u32[]{:S(2)}) %collective-permute-start.35) | collective-permute-done | bytes 655392 | tf_op jit(solution)/shard_map/ppermute | solution.py:26
  154.1 2.9 collective-permute-start.52
  159.0 3.7 collective-permute-start.57
  162.8 4.0 collective-permute-done.51.refs_52_
  166.8 3.5 collective-permute-start.48
  173.8 8.7 %collective-permute-done.48.refs_46_ = bf16[4,128,640]{2,1,0:T(8,128)(2,1)} collective-permute-done((bf16[4,128,640]{2,1,0:T(8,128)(2,1)S(1)}, bf16[4,128,640]{2,1,0:T(8,128)(2,1)}, u32[]{:S(2)}, u32[]{:S(2)}) %collective-permute-start.48) | collective-permute-done | bytes 655392 | tf_op jit(solution)/shard_map/ppermute | solution.py:26
  182.5 2.8 collective-permute-start.62
  186.7 2.5 collective-permute-start.64
  189.2 3.9 collective-permute-start.67
  195.3 3.6 collective-permute-start.60
  198.9 2.7 collective-permute-start.65
  203.5 2.9 collective-permute-start.68
  216.9 17.1 %shard_map.68 = (bf16[4,64,2048]{2,1,0:T(8,128)(2,1)}, bf16[4,64,2048]{2,1,0:T(8,128)(2,1)}, bf16[64,2048]{1,0:T(8,128)(2,1)}) custom-call(bf16[64,2048]{1,0:T(8,128)(2,1)} %get-tuple-element.1487.x_ref, bf16[4,64,2048]{2,1,0:T(8,128)(2,1)S(1)} %pad_maximum_fusion.1.base_ref, bf16[1,128,1408]{2,1,0:T(8,128)(2,1)} %copy-done.26, ...), custom_call_target="tpu_custom_call" | custom-call | flops 2147483648 | bytes 33554432 | tf_op jit(solution)/shard_map/pallas_call | solution.py:294
  234.0 3.8 collective-permute-start.77
  237.9 4.9 collective-permute-done.77
  245.6 4.9 all-to-all-start.1
  250.5 19.5 %shard_map.69 = (bf16[4,64,2048]{2,1,0:T(8,128)(2,1)}, bf16[64,2048]{1,0:T(8,128)(2,1)}) custom-call(bf16[64,2048]{1,0:T(8,128)(2,1)} %get-tuple-element.1486.g_ref, bf16[4,64,2048]{2,1,0:T(8,128)(2,1)} %get-tuple-element.1460.x_ref, bf16[1,128,1408]{2,1,0:T(8,128)(2,1)} %copy-done.26, bf16[1,128,1408]{2,1,0:T(8,128)(2,1)} %copy-done.32, ...), custom_call_target="tpu_custom_call" | custom-call | flops 2147483648 | bytes 33554432 | tf_op jit(solution)/shard_map/pallas_call | solution.py:294
  274.3 115.3 %collective-permute-done.83 = bf16[64,2048]{1,0:T(8,128)(2,1)} collective-permute-done((bf16[64,2048]{1,0:T(8,128)(2,1)}, bf16[64,2048]{1,0:T(8,128)(2,1)}, u32[]{:S(2)}, u32[]{:S(2)}) %collective-permute-start.83) | collective-permute-done | bytes 262176 | tf_op jit(solution)/shard_map/ppermute | solution.py:394
  389.6 19.5 %conditional.11 = (bf16[4,64,2048]{2,1,0:T(8,128)(2,1)}) conditional(s32[]{:T(128)} %convert_element_type.87, bf16[4,64,2048]{2,1,0:T(8,128)(2,1)} %get-tuple-element.1464, (bf16[64,2048]{1,0:T(8,128)(2,1)}, bf16[4,64,2048]{2,1,0:T(8,128)(2,1)}, bf16[1,128,1408]{2,1,0:T(8,128)(2,1)}, bf16[1,128,1408]{2,1,0:T(8,128)(2,1)}, ...), branch_computations={%region_11.12_spmd, %region_12.13_spmd} | conditional | flops 2147483648 | bytes 33554440 | solution.py:395
  389.6 19.5 %branch_1_fun.11 = (bf16[4,64,2048]{2,1,0:T(8,128)(2,1)}, bf16[64,2048]{1,0:T(8,128)(2,1)}) custom-call(bf16[64,2048]{1,0:T(8,128)(2,1)} %get-tuple-element.1227.g_ref, bf16[4,64,2048]{2,1,0:T(8,128)(2,1)} %get-tuple-element.1228.x_ref, bf16[1,128,1408]{2,1,0:T(8,128)(2,1)} %get-tuple-element.1229.refs_0_, ...), custom_call_target="tpu_custom_call" | custom-call | flops 2147483648 | bytes 33554432 | tf_op jit(solution)/shard_map/cond/branch_1_fun/pallas_call | solution.py:294
  409.1 4.2 all-to-all-start.2
  414.9 3.2 reshape.124
  418.1 18.2 %all-to-all-done.2 = bf16[4,64,2048]{2,1,0:T(8,128)(2,1)} async-done(((bf16[4,64,2048]{2,1,0:T(8,128)(2,1)}), bf16[4,64,2048]{2,1,0:T(8,128)(2,1)}, u32[]{:S(2)}, u32[]{:S(2)}) %all-to-all-start.2) | async-done | bytes 1048608 | tf_op jit(solution)/shard_map/all_to_all | solution.py:332
  436.3 3.8 collective-permute-start.84
  445.0 3.8 all-to-all-start
  458.0 2.7 collective-permute-start.87
  461.4 2.7 collective-permute-start.92
  468.4 2.7 collective-permute-start.88
  474.0 2.7 collective-permute-start.93
  477.8 5.3 %collective-permute-done.86 = bf16[256,1024]{1,0:T(8,128)(2,1)} collective-permute-done((bf16[256,1024]{1,0:T(8,128)(2,1)}, bf16[256,1024]{1,0:T(8,128)(2,1)}, u32[]{:S(2)}, u32[]{:S(2)}) %collective-permute-start.86) | collective-permute-done | bytes 524320 | tf_op jit(solution)/shard_map/ppermute | solution.py:19
  485.6 2.8 collective-permute-start.89
  488.4 6.0 %collective-permute-done.91 = bf16[256,1024]{1,0:T(8,128)(2,1)} collective-permute-done((bf16[256,1024]{1,0:T(8,128)(2,1)}, bf16[256,1024]{1,0:T(8,128)(2,1)}, u32[]{:S(2)}, u32[]{:S(2)}) %collective-permute-start.91) | collective-permute-done | bytes 524320 | tf_op jit(solution)/shard_map/ppermute | solution.py:19
  496.1 2.9 collective-permute-start.94
  500.1 16.7 %collective-permute-done.94 = bf16[128,1024]{1,0:T(8,128)(2,1)S(1)} collective-permute-done((bf16[128,1024]{1,0:T(8,128)(2,1)S(1)}, bf16[128,1024]{1,0:T(8,128)(2,1)S(1)}, u32[]{:S(2)}, u32[]{:S(2)}) %collective-permute-start.94) | collective-permute-done | bytes 262176 | tf_op jit(solution)/shard_map/ppermute | solution.py:19
  (362 shorter events, 114.9 us)
Async XLA Ops:
  2.4 19.0 %collective-permute-start = (bf16[128,1408]{1,0:T(8,128)(2,1)}, bf16[128,1408]{1,0:T(8,128)(2,1)}, u32[]{:S(2)}, u32[]{:S(2)}) collective-permute-start(bf16[128,1408]{1,0:T(8,128)(2,1)} %get-tuple-element.1485), channel_id=1, source_target_pairs={{0,16},{16,32},{32,48},{48,8},{8,24},{24,40},{40,56},{56,0},{1,17}... | collective-permute-start | bytes 1081352 | tf_op jit(solution)/shard_map/ppermute | solution.py:26
  4.9 16.6 %collective-permute-start.1 = (bf16[128,1408]{1,0:T(8,128)(2,1)}, bf16[128,1408]{1,0:T(8,128)(2,1)}, u32[]{:S(2)}, u32[]{:S(2)}) collective-permute-start(bf16[128,1408]{1,0:T(8,128)(2,1)} %get-tuple-element.1485), channel_id=1, source_target_pairs={{0,56},{16,0},{32,16},{48,32},{8,48},{24,8},{40,24},{56,40},{1,57}... | collective-permute-start | bytes 1081352 | tf_op jit(solution)/shard_map/ppermute | solution.py:26
  19.8 19.2 %collective-permute-start.10 = (bf16[128,1408]{1,0:T(8,128)(2,1)}, bf16[128,1408]{1,0:T(8,128)(2,1)S(1)}, u32[]{:S(2)}, u32[]{:S(2)}) collective-permute-start(bf16[128,1408]{1,0:T(8,128)(2,1)} %get-tuple-element.1485), channel_id=1, source_target_pairs={{0,6},{2,0},{4,2},{6,4},{1,7},{3,1},{5,3},{7,5},{8,14},{10,8},{12,... | collective-permute-start | bytes 1081352 | tf_op jit(solution)/shard_map/ppermute | solution.py:19
  21.4 20.2 %collective-permute-start.9 = (bf16[128,1408]{1,0:T(8,128)(2,1)}, bf16[128,1408]{1,0:T(8,128)(2,1)S(1)}, u32[]{:S(2)}, u32[]{:S(2)}) collective-permute-start(bf16[128,1408]{1,0:T(8,128)(2,1)} %get-tuple-element.1485), channel_id=1, source_target_pairs={{0,2},{2,4},{4,6},{6,0},{1,3},{3,5},{5,7},{7,1},{8,10},{10,12},{12... | collective-permute-start | bytes 1081352 | tf_op jit(solution)/shard_map/ppermute | solution.py:19
  23.3 26.7 %collective-permute-start.13 = (bf16[2,128,1408]{2,1,0:T(8,128)(2,1)S(1)}, bf16[2,128,1408]{2,1,0:T(8,128)(2,1)S(1)}, u32[]{:S(2)}, u32[]{:S(2)}) collective-permute-start(bf16[2,128,1408]{2,1,0:T(8,128)(2,1)S(1)} %pad_maximum_fusion.2.refs_2_), channel_id=1, source_target_pairs={{0,1},{1,0},{2,3},{3,2},{4,5},{5,4},{6,7},{7,6},{8,9},{9,8},{10,11... | collective-permute-start | bytes 2162696 | tf_op jit(solution)/shard_map/ppermute | solution.py:19
  24.7 13.5 %collective-permute-start.12 = (bf16[64,2048]{1,0:T(8,128)(2,1)S(1)}, bf16[64,2048]{1,0:T(8,128)(2,1)S(1)}, u32[]{:S(2)}, u32[]{:S(2)}) collective-permute-start(bf16[64,2048]{1,0:T(8,128)(2,1)S(1)} %get-tuple-element.1476), channel_id=1, source_target_pairs={{0,48},{16,0},{32,16},{48,32},{1,49},{17,1},{33,17},{49,33},{2,50}... | collective-permute-start | bytes 786440 | tf_op jit(solution)/shard_map/ppermute | solution.py:19
  41.6 22.2 %collective-permute-start.16 = (bf16[2,128,1408]{2,1,0:T(8,128)(2,1)S(1)}, bf16[2,128,1408]{2,1,0:T(8,128)(2,1)S(1)}, u32[]{:S(2)}, u32[]{:S(2)}) collective-permute-start(bf16[2,128,1408]{2,1,0:T(8,128)(2,1)S(1)} %pad_maximum_fusion.2.refs_2_), channel_id=1, source_target_pairs={{0,2},{2,4},{4,6},{6,0},{1,3},{3,5},{5,7},{7,1},{8,10},{10,12},{12... | collective-permute-start | bytes 2162696 | tf_op jit(solution)/shard_map/ppermute | solution.py:19
  46.0 18.1 %collective-permute-start.17 = (bf16[2,128,1408]{2,1,0:T(8,128)(2,1)S(1)}, bf16[2,128,1408]{2,1,0:T(8,128)(2,1)S(1)}, u32[]{:S(2)}, u32[]{:S(2)}) collective-permute-start(bf16[2,128,1408]{2,1,0:T(8,128)(2,1)S(1)} %pad_maximum_fusion.2.refs_2_), channel_id=1, source_target_pairs={{0,6},{2,0},{4,2},{6,4},{1,7},{3,1},{5,3},{7,5},{8,14},{10,8},{12,... | collective-permute-start | bytes 2162696 | tf_op jit(solution)/shard_map/ppermute | solution.py:19
  50.0 13.0 %collective-permute-start.18 = (bf16[64,2048]{1,0:T(8,128)(2,1)S(1)}, bf16[64,2048]{1,0:T(8,128)(2,1)S(1)}, u32[]{:S(2)}, u32[]{:S(2)}) collective-permute-start(bf16[64,2048]{1,0:T(8,128)(2,1)S(1)} %get-tuple-element.1475), channel_id=1, source_target_pairs={{0,32},{16,48},{32,0},{48,16},{1,33},{17,49},{33,1},{49,17},{2,34}... | collective-permute-start | bytes 786440 | tf_op jit(solution)/shard_map/ppermute | solution.py:19
  50.0 16.0 %collective-permute-start.14 = (bf16[128,1408]{1,0:T(8,128)(2,1)S(1)}, bf16[128,1408]{1,0:T(8,128)(2,1)S(1)}, u32[]{:S(2)}, u32[]{:S(2)}) collective-permute-start(bf16[128,1408]{1,0:T(8,128)(2,1)S(1)} %collective-permute-done.5), channel_id=1, source_target_pairs={{0,16},{16,32},{32,48},{48,8},{8,24},{24,40},{40,56},{56,0},{1,17}... | collective-permute-start | bytes 1081352 | tf_op jit(solution)/shard_map/ppermute | solution.py:26
  51.0 15.1 %collective-permute-start.15 = (bf16[128,1408]{1,0:T(8,128)(2,1)S(1)}, bf16[128,1408]{1,0:T(8,128)(2,1)S(1)}, u32[]{:S(2)}, u32[]{:S(2)}) collective-permute-start(bf16[128,1408]{1,0:T(8,128)(2,1)S(1)} %collective-permute-done.6), channel_id=1, source_target_pairs={{0,56},{16,0},{32,16},{48,32},{8,48},{24,8},{40,24},{56,40},{1,57}... | collective-permute-start | bytes 1081352 | tf_op jit(solution)/shard_map/ppermute | solution.py:26
  66.1 30.0 %collective-permute-start.23 = (bf16[4,128,640]{2,1,0:T(8,128)(2,1)S(1)}, bf16[4,128,640]{2,1,0:T(8,128)(2,1)S(1)}, u32[]{:S(2)}, u32[]{:S(2)}) collective-permute-start(bf16[4,128,640]{2,1,0:T(8,128)(2,1)S(1)} %pad_maximum_fusion.5.refs_4_), channel_id=1, source_target_pairs={{0,16},{16,32},{32,48},{48,8},{8,24},{24,40},{40,56},{56,0},{1,17}... | collective-permute-start | bytes 1966088 | tf_op jit(solution)/shard_map/ppermute | solution.py:26
  71.0 25.2 %collective-permute-start.24 = (bf16[4,128,640]{2,1,0:T(8,128)(2,1)S(1)}, bf16[4,128,640]{2,1,0:T(8,128)(2,1)S(1)}, u32[]{:S(2)}, u32[]{:S(2)}) collective-permute-start(bf16[4,128,640]{2,1,0:T(8,128)(2,1)S(1)} %pad_maximum_fusion.5.refs_4_), channel_id=1, source_target_pairs={{0,56},{16,0},{32,16},{48,32},{8,48},{24,8},{40,24},{56,40},{1,57}... | collective-permute-start | bytes 1966088 | tf_op jit(solution)/shard_map/ppermute | solution.py:26
  71.4 25.3 %collective-permute-start.27 = (bf16[2,128,1408]{2,1,0:T(8,128)(2,1)S(1)}, bf16[2,128,1408]{2,1,0:T(8,128)(2,1)S(1)}, u32[]{:S(2)}, u32[]{:S(2)}) collective-permute-start(bf16[2,128,1408]{2,1,0:T(8,128)(2,1)S(1)} %pad_maximum_fusion.3.refs_10_), channel_id=1, source_target_pairs={{0,2},{2,4},{4,6},{6,0},{1,3},{3,5},{5,7},{7,1},{8,10},{10,12},{12... | collective-permute-start | bytes 2162696 | tf_op jit(solution)/shard_map/ppermute | solution.py:19
  72.8 25.5 %collective-permute-start.28 = (bf16[2,128,1408]{2,1,0:T(8,128)(2,1)S(1)}, bf16[2,128,1408]{2,1,0:T(8,128)(2,1)S(1)}, u32[]{:S(2)}, u32[]{:S(2)}) collective-permute-start(bf16[2,128,1408]{2,1,0:T(8,128)(2,1)S(1)} %pad_maximum_fusion.3.refs_10_), channel_id=1, source_target_pairs={{0,6},{2,0},{4,2},{6,4},{1,7},{3,1},{5,3},{7,5},{8,14},{10,8},{12,... | collective-permute-start | bytes 2162696 | tf_op jit(solution)/shard_map/ppermute | solution.py:19
  78.0 16.1 %collective-permute-start.30 = (bf16[64,1408]{1,0:T(8,128)(2,1)S(1)}, bf16[64,1408]{1,0:T(8,128)(2,1)S(1)}, u32[]{:S(2)}, u32[]{:S(2)}) collective-permute-start(bf16[64,1408]{1,0:T(8,128)(2,1)S(1)} %slice.107), channel_id=1, source_target_pairs={{0,6},{2,0},{4,2},{6,4},{1,7},{3,1},{5,3},{7,5},{8,14},{10,8},{12,... | collective-permute-start | bytes 540680 | tf_op jit(solution)/shard_map/ppermute | solution.py:19
  94.1 13.7 %collective-permute-start.31 = (bf16[2,128,1408]{2,1,0:T(8,128)(2,1)S(1)}, bf16[2,128,1408]{2,1,0:T(8,128)(2,1)S(1)}, u32[]{:S(2)}, u32[]{:S(2)}) collective-permute-start(bf16[2,128,1408]{2,1,0:T(8,128)(2,1)S(1)} %pad_maximum_fusion.4.refs_12_), channel_id=1, source_target_pairs={{0,1},{1,0},{2,3},{3,2},{4,5},{5,4},{6,7},{7,6},{8,9},{9,8},{10,11... | collective-permute-start | bytes 2162696 | tf_op jit(solution)/shard_map/ppermute | solution.py:19
  96.2 14.2 %collective-permute-start.33 = (bf16[2,128,1408]{2,1,0:T(8,128)(2,1)S(1)}, bf16[2,128,1408]{2,1,0:T(8,128)(2,1)S(1)}, u32[]{:S(2)}, u32[]{:S(2)}) collective-permute-start(bf16[2,128,1408]{2,1,0:T(8,128)(2,1)S(1)} %collective-permute-done.17.refs_16_), channel_id=1, source_target_pairs={{0,1},{1,0},{2,3},{3,2},{4,5},{5,4},{6,7},{7,6},{8,9},{9,8},{10,11... | collective-permute-start | bytes 2162696 | tf_op jit(solution)/shard_map/ppermute | solution.py:19
  104.9 27.9 %collective-permute-start.36 = (bf16[2,128,1408]{2,1,0:T(8,128)(2,1)S(1)}, bf16[2,128,1408]{2,1,0:T(8,128)(2,1)S(1)}, u32[]{:S(2)}, u32[]{:S(2)}) collective-permute-start(bf16[2,128,1408]{2,1,0:T(8,128)(2,1)S(1)} %pad_maximum_fusion.4.refs_12_), channel_id=1, source_target_pairs={{0,2},{2,4},{4,6},{6,0},{1,3},{3,5},{5,7},{7,1},{8,10},{10,12},{12... | collective-permute-start | bytes 2162696 | tf_op jit(solution)/shard_map/ppermute | solution.py:19
  106.5 26.6 %collective-permute-start.37 = (bf16[2,128,1408]{2,1,0:T(8,128)(2,1)S(1)}, bf16[2,128,1408]{2,1,0:T(8,128)(2,1)S(1)}, u32[]{:S(2)}, u32[]{:S(2)}) collective-permute-start(bf16[2,128,1408]{2,1,0:T(8,128)(2,1)S(1)} %pad_maximum_fusion.4.refs_12_), channel_id=1, source_target_pairs={{0,6},{2,0},{4,2},{6,4},{1,7},{3,1},{5,3},{7,5},{8,14},{10,8},{12,... | collective-permute-start | bytes 2162696 | tf_op jit(solution)/shard_map/ppermute | solution.py:19
  107.8 23.1 %collective-permute-start.38 = (bf16[2,64,1408]{2,1,0:T(8,128)(2,1)S(1)}, bf16[2,64,1408]{2,1,0:T(8,128)(2,1)S(1)}, u32[]{:S(2)}, u32[]{:S(2)}) collective-permute-start(bf16[2,64,1408]{2,1,0:T(8,128)(2,1)S(1)} %slice.108), channel_id=1, source_target_pairs={{0,2},{2,4},{4,6},{6,0},{1,3},{3,5},{5,7},{7,1},{8,10},{10,12},{12... | collective-permute-start | bytes 1081352 | tf_op jit(solution)/shard_map/ppermute | solution.py:19
  108.0 24.4 %collective-permute-start.39 = (bf16[2,64,1408]{2,1,0:T(8,128)(2,1)S(1)}, bf16[2,64,1408]{2,1,0:T(8,128)(2,1)S(1)}, u32[]{:S(2)}, u32[]{:S(2)}) collective-permute-start(bf16[2,64,1408]{2,1,0:T(8,128)(2,1)S(1)} %slice.109), channel_id=1, source_target_pairs={{0,6},{2,0},{4,2},{6,4},{1,7},{3,1},{5,3},{7,5},{8,14},{10,8},{12,... | collective-permute-start | bytes 1081352 | tf_op jit(solution)/shard_map/ppermute | solution.py:19
  110.5 25.5 %collective-permute-start.34 = (bf16[4,128,640]{2,1,0:T(8,128)(2,1)S(1)}, bf16[4,128,640]{2,1,0:T(8,128)(2,1)S(1)}, u32[]{:S(2)}, u32[]{:S(2)}) collective-permute-start(bf16[4,128,640]{2,1,0:T(8,128)(2,1)S(1)} %collective-permute-done.23.refs_18_), channel_id=1, source_target_pairs={{0,16},{16,32},{32,48},{48,8},{8,24},{24,40},{40,56},{56,0},{1,17}... | collective-permute-start | bytes 1966088 | tf_op jit(solution)/shard_map/ppermute | solution.py:26
  133.0 16.0 %collective-permute-start.35 = (bf16[4,128,640]{2,1,0:T(8,128)(2,1)S(1)}, bf16[4,128,640]{2,1,0:T(8,128)(2,1)S(1)}, u32[]{:S(2)}, u32[]{:S(2)}) collective-permute-start(bf16[4,128,640]{2,1,0:T(8,128)(2,1)S(1)} %collective-permute-done.24.refs_20_), channel_id=1, source_target_pairs={{0,56},{16,0},{32,16},{48,32},{8,48},{24,8},{40,24},{56,40},{1,57}... | collective-permute-start | bytes 1966088 | tf_op jit(solution)/shard_map/ppermute | solution.py:26
  134.5 15.1 %collective-permute-start.40 = (bf16[4,128,640]{2,1,0:T(8,128)(2,1)S(1)}, bf16[4,128,640]{2,1,0:T(8,128)(2,1)S(1)}, u32[]{:S(2)}, u32[]{:S(2)}) collective-permute-start(bf16[4,128,640]{2,1,0:T(8,128)(2,1)S(1)} %collective-permute-done.23.refs_18_), channel_id=1, source_target_pairs={{0,1},{1,0},{2,3},{3,2},{4,5},{5,4},{6,7},{7,6},{8,9},{9,8},{10,11... | collective-permute-start | bytes 1966088 | tf_op jit(solution)/shard_map/ppermute | solution.py:19
  135.2 16.5 %collective-permute-start.43 = (bf16[2,128,1408]{2,1,0:T(8,128)(2,1)S(1)}, bf16[2,128,1408]{2,1,0:T(8,128)(2,1)S(1)}, u32[]{:S(2)}, u32[]{:S(2)}) collective-permute-start(bf16[2,128,1408]{2,1,0:T(8,128)(2,1)S(1)} %collective-permute-done.27.refs_24_), channel_id=1, source_target_pairs={{0,1},{1,0},{2,3},{3,2},{4,5},{5,4},{6,7},{7,6},{8,9},{9,8},{10,11... | collective-permute-start | bytes 2162696 | tf_op jit(solution)/shard_map/ppermute | solution.py:19
  135.8 15.9 %collective-permute-start.44 = (bf16[2,128,1408]{2,1,0:T(8,128)(2,1)S(1)}, bf16[2,128,1408]{2,1,0:T(8,128)(2,1)S(1)}, u32[]{:S(2)}, u32[]{:S(2)}) collective-permute-start(bf16[2,128,1408]{2,1,0:T(8,128)(2,1)S(1)} %collective-permute-done.28.refs_26_), channel_id=1, source_target_pairs={{0,1},{1,0},{2,3},{3,2},{4,5},{5,4},{6,7},{7,6},{8,9},{9,8},{10,11... | collective-permute-start | bytes 2162696 | tf_op jit(solution)/shard_map/ppermute | solution.py:19
  136.0 15.8 %collective-permute-start.41 = (bf16[4,128,640]{2,1,0:T(8,128)(2,1)S(1)}, bf16[4,128,640]{2,1,0:T(8,128)(2,1)S(1)}, u32[]{:S(2)}, u32[]{:S(2)}) collective-permute-start(bf16[4,128,640]{2,1,0:T(8,128)(2,1)S(1)} %collective-permute-done.24.refs_20_), channel_id=1, source_target_pairs={{0,1},{1,0},{2,3},{3,2},{4,5},{5,4},{6,7},{7,6},{8,9},{9,8},{10,11... | collective-permute-start | bytes 1966088 | tf_op jit(solution)/shard_map/ppermute | solution.py:19
  149.5 13.2 %collective-permute-start.50 = (bf16[128,1408]{1,0:T(8,128)(2,1)S(1)}, bf16[128,1408]{1,0:T(8,128)(2,1)}, u32[]{:S(2)}, u32[]{:S(2)}) collective-permute-start(bf16[128,1408]{1,0:T(8,128)(2,1)S(1)} %constant_dynamic-update-slice_fusion), channel_id=1, source_target_pairs={{0,6},{2,0},{4,2},{6,4},{1,7},{3,1},{5,3},{7,5},{8,14},{10,8},{12,... | collective-permute-start | bytes 1081352 | tf_op jit(solution)/shard_map/ppermute | solution.py:19
  153.5 19.6 %collective-permute-start.47 = (bf16[4,128,640]{2,1,0:T(8,128)(2,1)S(1)}, bf16[4,128,640]{2,1,0:T(8,128)(2,1)}, u32[]{:S(2)}, u32[]{:S(2)}) collective-permute-start(bf16[4,128,640]{2,1,0:T(8,128)(2,1)S(1)} %collective-permute-done.34.refs_32_), channel_id=1, source_target_pairs={{0,16},{16,32},{32,48},{48,8},{8,24},{24,40},{40,56},{56,0},{1,17}... | collective-permute-start | bytes 1966088 | tf_op jit(solution)/shard_map/ppermute | solution.py:26
  153.9 12.9 %collective-permute-start.51 = (bf16[2,64,1408]{2,1,0:T(8,128)(2,1)S(1)}, bf16[2,64,1408]{2,1,0:T(8,128)(2,1)}, u32[]{:S(2)}, u32[]{:S(2)}) collective-permute-start(bf16[2,64,1408]{2,1,0:T(8,128)(2,1)S(1)} %slice.110), channel_id=1, source_target_pairs={{0,2},{2,4},{4,6},{6,0},{1,3},{3,5},{5,7},{7,1},{8,10},{10,12},{12... | collective-permute-start | bytes 1081352 | tf_op jit(solution)/shard_map/ppermute | solution.py:19
  154.1 16.3 %collective-permute-start.52 = (bf16[2,64,1408]{2,1,0:T(8,128)(2,1)S(1)}, bf16[2,64,1408]{2,1,0:T(8,128)(2,1)}, u32[]{:S(2)}, u32[]{:S(2)}) collective-permute-start(bf16[2,64,1408]{2,1,0:T(8,128)(2,1)S(1)} %slice.111), channel_id=1, source_target_pairs={{0,6},{2,0},{4,2},{6,4},{1,7},{3,1},{5,3},{7,5},{8,14},{10,8},{12,... | collective-permute-start | bytes 1081352 | tf_op jit(solution)/shard_map/ppermute | solution.py:19
  159.0 13.5 %collective-permute-start.57 = (bf16[2,64,1408]{2,1,0:T(8,128)(2,1)S(1)}, bf16[2,64,1408]{2,1,0:T(8,128)(2,1)}, u32[]{:S(2)}, u32[]{:S(2)}) collective-permute-start(bf16[2,64,1408]{2,1,0:T(8,128)(2,1)S(1)} %collective-permute-done.38.refs_40_), channel_id=1, source_target_pairs={{0,1},{1,0},{2,3},{3,2},{4,5},{5,4},{6,7},{7,6},{8,9},{9,8},{10,11... | collective-permute-start | bytes 1081352 | tf_op jit(solution)/shard_map/ppermute | solution.py:19
  166.8 15.7 %collective-permute-start.48 = (bf16[4,128,640]{2,1,0:T(8,128)(2,1)S(1)}, bf16[4,128,640]{2,1,0:T(8,128)(2,1)}, u32[]{:S(2)}, u32[]{:S(2)}) collective-permute-start(bf16[4,128,640]{2,1,0:T(8,128)(2,1)S(1)} %collective-permute-done.35.refs_34_), channel_id=1, source_target_pairs={{0,56},{16,0},{32,16},{48,32},{8,48},{24,8},{40,24},{56,40},{1,57}... | collective-permute-start | bytes 1966088 | tf_op jit(solution)/shard_map/ppermute | solution.py:26
  185.4 13.6 %collective-permute-start.63 = (bf16[64,1408]{1,0:T(8,128)(2,1)S(1)}, bf16[64,1408]{1,0:T(8,128)(2,1)S(1)}, u32[]{:S(2)}, u32[]{:S(2)}) collective-permute-start(bf16[64,1408]{1,0:T(8,128)(2,1)S(1)} %slice.116), channel_id=1, source_target_pairs={{0,2},{2,4},{4,6},{6,0},{1,3},{3,5},{5,7},{7,1},{8,10},{10,12},{12... | collective-permute-start | bytes 540680 | tf_op jit(solution)/shard_map/ppermute | solution.py:19
  186.7 15.0 %collective-permute-start.64 = (bf16[64,1408]{1,0:T(8,128)(2,1)S(1)}, bf16[64,1408]{1,0:T(8,128)(2,1)S(1)}, u32[]{:S(2)}, u32[]{:S(2)}) collective-permute-start(bf16[64,1408]{1,0:T(8,128)(2,1)S(1)} %slice.117), channel_id=1, source_target_pairs={{0,6},{2,0},{4,2},{6,4},{1,7},{3,1},{5,3},{7,5},{8,14},{10,8},{12,... | collective-permute-start | bytes 540680 | tf_op jit(solution)/shard_map/ppermute | solution.py:19
  189.2 17.7 %collective-permute-start.67 = (bf16[1,128,1408]{2,1,0:T(8,128)(2,1)S(1)}, bf16[1,128,1408]{2,1,0:T(8,128)(2,1)S(1)}, u32[]{:S(2)}, u32[]{:S(2)}) collective-permute-start(bf16[1,128,1408]{2,1,0:T(8,128)(2,1)S(1)} %bitcast.96), channel_id=1, source_target_pairs={{0,1},{1,0},{2,3},{3,2},{4,5},{5,4},{6,7},{7,6},{8,9},{9,8},{10,11... | collective-permute-start | bytes 1081352 | tf_op jit(solution)/shard_map/ppermute | solution.py:19
  245.6 163.4 %all-to-all-start.1 = ((bf16[4,64,2048]{2,1,0:T(8,128)(2,1)}), bf16[4,64,2048]{2,1,0:T(8,128)(2,1)}, u32[]{:S(2)}, u32[]{:S(2)}) async-start(bf16[4,64,2048]{2,1,0:T(8,128)(2,1)} %get-tuple-element.1460.x_ref), calls=%async_computation.1 | async-start | bytes 2097152 | tf_op jit(solution)/shard_map/all_to_all | solution.py:332
  273.0 116.6 %collective-permute-start.83 = (bf16[64,2048]{1,0:T(8,128)(2,1)}, bf16[64,2048]{1,0:T(8,128)(2,1)}, u32[]{:S(2)}, u32[]{:S(2)}) collective-permute-start(bf16[64,2048]{1,0:T(8,128)(2,1)} %get-tuple-element.1465), channel_id=1, source_target_pairs={{64,0},{65,1},{66,2},{67,3},{68,4},{69,5},{70,6},{71,7},{72,8},{73... | collective-permute-start | bytes 786440 | tf_op jit(solution)/shard_map/ppermute | solution.py:394
  409.1 27.2 %all-to-all-start.2 = ((bf16[4,64,2048]{2,1,0:T(8,128)(2,1)}), bf16[4,64,2048]{2,1,0:T(8,128)(2,1)}, u32[]{:S(2)}, u32[]{:S(2)}) async-start(bf16[4,64,2048]{2,1,0:T(8,128)(2,1)} %get-tuple-element.1521), calls=%async_computation.2 | async-start | bytes 2097152 | tf_op jit(solution)/shard_map/all_to_all | solution.py:332
  436.3 17.5 %collective-permute-start.84 = (bf16[256,2048]{1,0:T(8,128)(2,1)}, bf16[256,2048]{1,0:T(8,128)(2,1)}, u32[]{:S(2)}, u32[]{:S(2)}) collective-permute-start(bf16[256,2048]{1,0:T(8,128)(2,1)} %bitcast.36), channel_id=1, source_target_pairs={{0,1},{1,0},{2,3},{3,2},{4,5},{5,4},{6,7},{7,6},{8,9},{9,8},{10,11... | collective-permute-start | bytes 3145736 | tf_op jit(solution)/shard_map/ppermute | solution.py:19
  445.0 53.9 %all-to-all-start = ((bf16[4,64,2048]{2,1,0:T(8,128)(2,1)}), bf16[4,64,2048]{2,1,0:T(8,128)(2,1)S(1)}, u32[]{:S(2)}, u32[]{:S(2)}) async-start(bf16[4,64,2048]{2,1,0:T(8,128)(2,1)} %get-tuple-element.1459), calls=%async_computation | async-start | bytes 2097152 | tf_op jit(solution)/shard_map/all_to_all | solution.py:332
  467.5 15.6 %collective-permute-start.86 = (bf16[256,1024]{1,0:T(8,128)(2,1)}, bf16[256,1024]{1,0:T(8,128)(2,1)}, u32[]{:S(2)}, u32[]{:S(2)}) collective-permute-start(bf16[256,1024]{1,0:T(8,128)(2,1)} %pad_maximum_fusion.6), channel_id=1, source_target_pairs={{0,2},{2,4},{4,6},{6,0},{1,3},{3,5},{5,7},{7,1},{8,10},{10,12},{12... | collective-permute-start | bytes 1572872 | tf_op jit(solution)/shard_map/ppermute | solution.py:19
  468.4 14.7 %collective-permute-start.88 = (bf16[256,1024]{1,0:T(8,128)(2,1)}, bf16[256,1024]{1,0:T(8,128)(2,1)}, u32[]{:S(2)}, u32[]{:S(2)}) collective-permute-start(bf16[256,1024]{1,0:T(8,128)(2,1)} %pad_maximum_fusion.7), channel_id=1, source_target_pairs={{0,6},{2,0},{4,2},{6,4},{1,7},{3,1},{5,3},{7,5},{8,14},{10,8},{12,... | collective-permute-start | bytes 1572872 | tf_op jit(solution)/shard_map/ppermute | solution.py:19
  473.1 21.3 %collective-permute-start.91 = (bf16[256,1024]{1,0:T(8,128)(2,1)}, bf16[256,1024]{1,0:T(8,128)(2,1)}, u32[]{:S(2)}, u32[]{:S(2)}) collective-permute-start(bf16[256,1024]{1,0:T(8,128)(2,1)} %pad_maximum_fusion.8), channel_id=1, source_target_pairs={{0,2},{2,4},{4,6},{6,0},{1,3},{3,5},{5,7},{7,1},{8,10},{10,12},{12... | collective-permute-start | bytes 1572872 | tf_op jit(solution)/shard_map/ppermute | solution.py:19
  474.0 20.3 %collective-permute-start.93 = (bf16[256,1024]{1,0:T(8,128)(2,1)}, bf16[256,1024]{1,0:T(8,128)(2,1)}, u32[]{:S(2)}, u32[]{:S(2)}) collective-permute-start(bf16[256,1024]{1,0:T(8,128)(2,1)} %pad_maximum_fusion.9), channel_id=1, source_target_pairs={{0,6},{2,0},{4,2},{6,4},{1,7},{3,1},{5,3},{7,5},{8,14},{10,8},{12,... | collective-permute-start | bytes 1572872 | tf_op jit(solution)/shard_map/ppermute | solution.py:19
  485.6 13.3 %collective-permute-start.89 = (bf16[128,1024]{1,0:T(8,128)(2,1)}, bf16[128,1024]{1,0:T(8,128)(2,1)}, u32[]{:S(2)}, u32[]{:S(2)}) collective-permute-start(bf16[128,1024]{1,0:T(8,128)(2,1)} %fusion.7), channel_id=1, source_target_pairs={{0,8},{8,0},{1,9},{9,1},{2,10},{10,2},{3,11},{11,3},{4,12},{12,4},... | collective-permute-start | bytes 786440 | tf_op jit(solution)/shard_map/ppermute | solution.py:19
  496.1 20.7 %collective-permute-start.94 = (bf16[128,1024]{1,0:T(8,128)(2,1)S(1)}, bf16[128,1024]{1,0:T(8,128)(2,1)S(1)}, u32[]{:S(2)}, u32[]{:S(2)}) collective-permute-start(bf16[128,1024]{1,0:T(8,128)(2,1)S(1)} %fusion.8), channel_id=1, source_target_pairs={{0,8},{8,0},{1,9},{9,1},{2,10},{10,2},{3,11},{11,3},{4,12},{12,4},... | collective-permute-start | bytes 786440 | tf_op jit(solution)/shard_map/ppermute | solution.py:19
  (112 other events, 1949.3 us)

commit v5 on v2

--- a/solution.py
+++ b/solution.py
@@ -13,34 +13,52 @@
 DEPTH = 4
 TILE = 512
 SLOTS = 8
-PLANE = ("zl", "zh", "y", "c")
-
-
-def tile_copies(w_ref, held, arrived, depth, tiles, order, by_rows):
-    slots = held.shape[0]
-
-    def copy(number):
+PLANE = ("zh", "zl", "y", "c")
+
+
+def tile_copies(w_ref, held, arrived, order, by_rows):
+    halves, depth, rows, width = w_ref.shape
+    tiles, slots = width // TILE, held.shape[0]
+
+    def start(number):
         slot = lax.rem(number, slots)
         layer = order(number // tiles)
-        span = pl.ds(pl.multiple_of(lax.rem(number, tiles) * TILE, TILE), TILE)
-        source = w_ref.at[layer, span] if by_rows else w_ref.at[layer, :, span]
-        return pltpu.make_async_copy(source, held.at[slot], arrived.at[slot])
+        tile = lax.rem(number, tiles)
+        if by_rows:
+            inner = rows // TILE
+            span = pl.ds(pl.multiple_of(lax.rem(tile, inner) * TILE, TILE), TILE)
+            parts = [(w_ref.at[tile // inner, layer, span], held.at[slot])]
+        else:
+            span = pl.ds(pl.multiple_of(tile * TILE, TILE), TILE)
+            parts = [
+                (w_ref.at[half, layer, :, span], held.at[slot, pl.ds(half * rows, rows)])
+                for half in range(halves)
+            ]
+        for source, target in parts:
+            pltpu.make_async_copy(source, target, arrived.at[slot]).start()
+
+    def wait(number):
+        whole = held.at[lax.rem(number, slots)]
+        pltpu.make_async_copy(whole, whole, arrived.at[lax.rem(number, slots)]).wait()
 
     def refill(number):
         @pl.when(number + slots < depth * tiles)
         def _():
-            copy(number + slots).start()
+            start(number + slots)
 
     for number in range(slots):
-        copy(jnp.int32(number)).start()
-    return copy, refill
-
-
-def forward_kernel(x_ref, base_ref, w_ref, out_ref, x_now, normed, y, held, arrived):
+        start(jnp.int32(number))
+    return wait, refill
+
+
+def forward_kernel(
+    x_ref, base_ref, w_ref, in_ref, out_ref, last_ref, x_now, normed, y, held, arrived
+):
     depth, rows, width = base_ref.shape
     tiles, slots = width // TILE, held.shape[0]
-    copy, refill = tile_copies(w_ref, held, arrived, depth, tiles, lambda i: i, False)
+    wait, refill = tile_copies(w_ref, held, arrived, lambda i: i, False)
     x_now[...] = x_ref[...].astype(jnp.float32)
+    in_ref[0] = x_ref[...]
 
     def run_layer(layer, carry):
         values = x_now[...]
@@ -48,7 +66,7 @@
         normed[...] = (values * scale).astype(jnp.bfloat16)
         for tile in range(tiles):
             number = layer * tiles + tile
-            copy(number).wait()
+            wait(number)
             columns = pl.ds(tile * TILE, TILE)
             y[:, columns] = x_now[:, columns] + jnp.dot(
                 normed[...], held[lax.rem(number, slots)], preferred_element_type=jnp.float32
@@ -61,6 +79,15 @@
         coded = (base + delta.astype(jnp.float32)).astype(jnp.bfloat16)
         out_ref[layer] = coded
         x_now[...] = coded.astype(jnp.float32)
+
+        @pl.when(layer < depth - 1)
+        def _():
+            in_ref[layer + 1] = coded
+
+        @pl.when(layer == depth - 1)
+        def _():
+            last_ref[...] = coded
+
         return carry
 
     lax.fori_loop(0, depth, run_layer, 0)
@@ -69,7 +96,7 @@
 def backward_kernel(g_ref, x_ref, w_ref, seen_ref, out_ref, g_now, back, held, arrived):
     depth, rows, width = x_ref.shape
     tiles, slots = width // TILE, held.shape[0]
-    copy, refill = tile_copies(w_ref, held, arrived, depth, tiles, lambda i: depth - 1 - i, True)
+    wait, refill = tile_copies(w_ref, held, arrived, lambda i: depth - 1 - i, True)
     g_now[...] = g_ref[...]
 
     def run_layer(step, carry):
@@ -77,7 +104,7 @@
         seen_ref[layer] = g_now[...]
         for tile in range(tiles):
             number = step * tiles + tile
-            copy(number).wait()
+            wait(number)
             back[:, pl.ds(tile * TILE, TILE)] = lax.dot_general(
                 g_now[...], held[lax.rem(number, slots)], (((1,), (1,)), ((), ())),
                 preferred_element_type=jnp.float32,
@@ -124,10 +151,9 @@
         pltpu.VMEM((rows, width), jnp.bfloat16),
         pltpu.VMEM((rows, width), jnp.float32),
     ]
-    call = stage_call(
-        forward_kernel, (width, TILE), scratch, [(depth, rows, width)], depth, rows, width
-    )
-    return call(x, base, weight)[0]
+    outs = [(depth, rows, width), (depth, rows, width), (rows, width)]
+    call = stage_call(forward_kernel, (width, TILE), scratch, outs, depth, rows, width)
+    return tuple(call(x, base, weight))
 
 
 def backward_stage(g, x, weight):
@@ -135,7 +161,7 @@
     scratch = [pltpu.VMEM((rows, width), jnp.bfloat16), pltpu.VMEM((rows, width), jnp.float32)]
     outs = [(depth, rows, width), (rows, width)]
     call = stage_call(backward_kernel, (TILE, width), scratch, outs, depth, rows, width)
-    return call(g, x, weight)
+    return tuple(call(g, x, weight))
 
 
 def shift(value, axis, steps):
@@ -188,34 +214,36 @@
     width = stream_in.shape[1]
     rows = stream_in.shape[0] // DEPTH
     weight = lax.all_gather(layer_weight[0], PLANE, axis=0, tiled=True)
-    weight = weight.reshape(DEPTH, width, width)
+    weight = weight.reshape(2, DEPTH, width // 2, width)
     picked = jnp.take(epoch_buffer[0], sample_ids[0], axis=0)
     base = exchange(picked.reshape(DEPTH, rows, width))
     x = lax.dynamic_slice_in_dim(stream_in, lane * rows, rows, 0)
     g = lax.dynamic_slice_in_dim(top_cotangent, lane * rows, rows, 0)
 
-    decoded = forward_stage(x, base, weight)
+    state = forward_stage(x, base, weight)
     for t in range(1, STAGES):
-        arrived = lax.ppermute(decoded[DEPTH - 1], "x", [(t - 1, t)])
-        x = jnp.where(stage == t, arrived, x)
-        decoded = lax.cond(
-            stage == t, lambda a, d: forward_stage(a, base, weight), lambda a, d: d, x, decoded
+        arrived = lax.ppermute(state[2], "x", [(t - 1, t)])
+        state = lax.cond(
+            stage == t, lambda a, s: forward_stage(a, base, weight), lambda a, s: s, arrived, state
         )
-    inputs = jnp.concatenate([x[None], decoded[: DEPTH - 1]], axis=0)
-
-    seen, sent = backward_stage(g, inputs, weight)
+    inputs, decoded, _ = state
+
+    state = backward_stage(g, inputs, weight)
     for t in range(STAGES - 2, -1, -1):
-        arrived = lax.ppermute(sent, "x", [(t + 1, t)])
-        g = jnp.where(stage == t, arrived, g)
-        seen, sent = lax.cond(
-            stage == t,
-            lambda a, s, o: tuple(backward_stage(a, inputs, weight)),
-            lambda a, s, o: (s, o),
-            g, seen, sent,
+        arrived = lax.ppermute(state[1], "x", [(t + 1, t)])
+        if t == STAGES - 2:
+            held, passed, _ = lax.optimization_barrier((decoded, inputs, state[1]))
+            decoded_rows, input_rows = exchange(held), exchange(passed)
+            arrived, decoded_rows, input_rows = lax.optimization_barrier(
+                (arrived, decoded_rows, input_rows)
+            )
+        state = lax.cond(
+            stage == t, lambda a, s: backward_stage(a, inputs, weight), lambda a, s: s, arrived, state
         )
-
-    decoded_rows = exchange(decoded).reshape(1, DEPTH * rows, width)
-    input_rows = exchange(inputs).reshape(DEPTH * rows, width).astype(jnp.float32)
+    seen = state[0]
+
+    decoded_rows = decoded_rows.reshape(1, DEPTH * rows, width)
+    input_rows = input_rows.reshape(DEPTH * rows, width).astype(jnp.float32)
     scale = lax.rsqrt(jnp.mean(input_rows * input_rows, axis=-1, keepdims=True) + epsilon)
     normed = (input_rows * scale).astype(jnp.bfloat16)
     cotangents = exchange(seen).reshape(DEPTH * rows, width)

time: 506 us -> 492 us (0.972)
  waiting for transfers between devices: 370 us -> 331 us
  blocking collectives: 0 us -> 28 us
    all_gather x1, waiting for transfers between devices: 166 us -> 117 us  [local(): weight = lax.all_gather(layer_weight[0], PLANE, axis=0, tiled=True)]
    all_to_all x0 -> x1, blocking collectives: none -> 28 us  [exchange(): return lax.all_to_all(value, 'zl', 0, 0)]
    all_to_all x4 -> x3, waiting for transfers between devices: 50.5 us -> 71.4 us  [exchange(): return lax.all_to_all(value, 'zl', 0, 0)]
    ppermute x6, waiting for transfers between devices: 104 us -> 86.2 us  [the longest x3 80.2 us: local(): arrived = lax.ppermute(state[1], 'x', [(t + 1, t)])]
    ppermute x7, waiting for transfers between devices: 48.8 us -> 56 us  [shift(): lax.ppermute(value, axis, [(i, (i + steps) % count) for i in range(count)])]
    all_to_all x4 -> x3, starting transfers between devices: 21 us -> 19.2 us  [exchange(): return lax.all_to_all(value, 'zl', 0, 0)]
  transfers between devices with their start and end apart: 18 -> 17, of which waited for: 11 -> 12; matrix products, arithmetic and copies ran while one was open for 4% -> 4% of each run, Pallas kernels for 3% -> 0%
where the time goes in v5:
time: 492 us; the launch traced here: 487 us
  waiting for transfers between devices  331 us (67%)
  Pallas kernels  45 us (9%)
  starting transfers between devices  37 us (8%)
  blocking collectives  28 us (6%)
  between operations  14.4 us (3%)
  local copies, waits for them, and re-layouts  13.5 us (3%)
  matrix products  9.35 us (2%)
  other arithmetic  8.06 us (2%)
    all_gather x1, waiting for transfers between devices, local(): weight = lax.all_gather(layer_weight[0], PLANE, axis=0, tiled=True)  117 us
    ppermute x3, waiting for transfers between devices, local(): arrived = lax.ppermute(state[1], 'x', [(t + 1, t)])  80.2 us
    all_to_all x3, waiting for transfers between devices, exchange(): return lax.all_to_all(value, 'zl', 0, 0)  71.4 us
    ppermute x7, waiting for transfers between devices, shift(): lax.ppermute(value, axis, [(i, (i + steps) % count) for i in range(count)])  56 us
    pallas_call x2, Pallas kernels, backward_stage(): return tuple(call(g, x, weight))  32.1 us
    all_to_all x1, blocking collectives, exchange(): return lax.all_to_all(value, 'zl', 0, 0)  28 us
    all_to_all x3, starting transfers between devices, exchange(): return lax.all_to_all(value, 'zl', 0, 0)  19.2 us
    pallas_call x1, Pallas kernels, forward_stage(): return tuple(call(x, base, weight))  12.8 us
  transfers between devices with their start and end apart: 17, of which 12 were waited for; matrix products, arithmetic and copies ran while one was open for 4% of the time, Pallas kernels for 0%

profile of v5, /device:TPU:96, one launch (start us, length us, event | category | flops | bytes accessed | tf_op | source)
XLA Modules:
  0.0 486.9 jit_solution(6555997357583106610)
XLA Ops:
  7.2 0.7 all-gather.3.cloned.1.call-update
  8.4 1.3 reduce.4
  10.0 0.7 fusion.9
  10.7 2.8 gather_fusion
  13.5 1.1 bitcast_select_fusion
  14.6 5.1 %all-to-all-start = ((bf16[4,64,2048]{2,1,0:T(8,128)(2,1)}), bf16[4,64,2048]{2,1,0:T(8,128)(2,1)S(1)}, u32[]{:S(2)}, u32[]{:S(2)}) async-start(bf16[4,64,2048]{2,1,0:T(8,128)(2,1)} %bitcast_select_fusion), calls=%async_computation | async-start | bytes 2097152 | tf_op jit(solution)/shard_map/all_to_all | solution.py:173
  19.7 30.5 %all-to-all-done.base_ref = bf16[4,64,2048]{2,1,0:T(8,128)(2,1)S(1)} async-done(((bf16[4,64,2048]{2,1,0:T(8,128)(2,1)}), bf16[4,64,2048]{2,1,0:T(8,128)(2,1)S(1)}, u32[]{:S(2)}, u32[]{:S(2)}) %all-to-all-start) | async-done | bytes 1048608 | tf_op jit(solution)/shard_map/all_to_all | solution.py:173
  50.2 117.2 %all-gather.3.cloned.1.call-done = bf16[1,8192,2048]{2,1,0:T(8,128)(2,1)} async-done(((bf16[1,128,2048]{2,1,0:T(8,128)(2,1)}), bf16[1,8192,2048]{2,1,0:T(8,128)(2,1)}) %all-gather.3.cloned.1.call-update) | async-done | bytes 33554448 | tf_op jit(solution)/shard_map/all_gather | solution.py:216
  167.4 12.8 %shard_map.68 = (bf16[4,64,2048]{2,1,0:T(8,128)(2,1)}, bf16[4,64,2048]{2,1,0:T(8,128)(2,1)S(1)}, bf16[64,2048]{1,0:T(8,128)(2,1)S(1)}) custom-call(bf16[64,2048]{1,0:T(8,128)(2,1)S(1)} %constant_dynamic-slice_fusion.2.x_ref, bf16[4,64,2048]{2,1,0:T(8,128)(2,1)S(1)} %all-to-all-done.base_ref, bf16[2,4,1024,2048]{3,2,1,0:T(8,128)(2,1)} %bitcast.31), custom_call_target="tpu_custom_call" | custom-call | flops 2147483648 | bytes 33554432 | tf_op jit(solution)/shard_map/pallas_call | solution.py:156
  180.3 3.4 collective-permute-start
  183.7 5.9 %collective-permute-done = bf16[64,2048]{1,0:T(8,128)(2,1)S(1)} collective-permute-done((bf16[64,2048]{1,0:T(8,128)(2,1)S(1)}, bf16[64,2048]{1,0:T(8,128)(2,1)S(1)}, u32[]{:S(2)}, u32[]{:S(2)}) %collective-permute-start) | collective-permute-done | bytes 262176 | tf_op jit(solution)/shard_map/ppermute | solution.py:225
  189.6 0.7 collective-permute-start.1
  190.3 0.7 collective-permute-start.2
  191.0 1.0 constant_dynamic-slice_fusion.3.g_ref
  192.0 15.8 %shard_map.69 = (bf16[4,64,2048]{2,1,0:T(8,128)(2,1)}, bf16[64,2048]{1,0:T(8,128)(2,1)S(1)}) custom-call(bf16[64,2048]{1,0:T(8,128)(2,1)S(1)} %constant_dynamic-slice_fusion.3.g_ref, bf16[4,64,2048]{2,1,0:T(8,128)(2,1)} %get-tuple-element.120.x_ref, bf16[2,4,1024,2048]{3,2,1,0:T(8,128)(2,1)} %bitcast.35), custom_call_target="tpu_custom_call" | custom-call | flops 2147483648 | bytes 33554432 | tf_op jit(solution)/shard_map/pallas_call | solution.py:164
  207.8 28.0 %all_to_all.20 = bf16[4,64,2048]{2,1,0:T(8,128)(2,1)} all-to-all(bf16[4,64,2048]{2,1,0:T(8,128)(2,1)S(1)} %get-tuple-element.119), channel_id=1, replica_groups=mesh['x'=4,'zl'=4,'zh'=2,'y'=4,'c'=2] {'zl'}, dimensions={0} | all-to-all | bytes 2097152 | tf_op jit(solution)/shard_map/all_to_all | solution.py:173
  235.8 5.9 %all-to-all-start.2 = ((bf16[4,64,2048]{2,1,0:T(8,128)(2,1)}), bf16[4,64,2048]{2,1,0:T(8,128)(2,1)S(1)}, u32[]{:S(2)}, u32[]{:S(2)}) async-start(bf16[4,64,2048]{2,1,0:T(8,128)(2,1)} %get-tuple-element.120.x_ref), calls=%async_computation.2 | async-start | bytes 2097152 | tf_op jit(solution)/shard_map/all_to_all | solution.py:173
  241.6 0.7 collective-permute-start.3
  242.3 21.7 %all-to-all-done.2 = bf16[4,64,2048]{2,1,0:T(8,128)(2,1)S(1)} async-done(((bf16[4,64,2048]{2,1,0:T(8,128)(2,1)}), bf16[4,64,2048]{2,1,0:T(8,128)(2,1)S(1)}, u32[]{:S(2)}, u32[]{:S(2)}) %all-to-all-start.2) | async-done | bytes 1048608 | tf_op jit(solution)/shard_map/all_to_all | solution.py:173
  264.0 0.7 collective-permute-start.5
  264.9 1.3 collective-permute-start.6
  266.2 80.2 %collective-permute-done.6 = bf16[64,2048]{1,0:T(8,128)(2,1)S(1)} collective-permute-done((bf16[64,2048]{1,0:T(8,128)(2,1)S(1)}, bf16[64,2048]{1,0:T(8,128)(2,1)S(1)}, u32[]{:S(2)}, u32[]{:S(2)}) %collective-permute-start.6) | collective-permute-done | bytes 262176 | tf_op jit(solution)/shard_map/ppermute | solution.py:233
  346.4 16.4 %conditional.11 = (bf16[4,64,2048]{2,1,0:T(8,128)(2,1)}) conditional(s32[]{:T(128)} %convert_element_type.61, bf16[4,64,2048]{2,1,0:T(8,128)(2,1)} %get-tuple-element.126, (bf16[64,2048]{1,0:T(8,128)(2,1)S(1)}, bf16[4,64,2048]{2,1,0:T(8,128)(2,1)}, bf16[2,4,1024,2048]{3,2,1,0:T(8,128)(2,1)}) %tuple.96), branch_computations={%region_11.12_spmd, %region_12.13_spmd} | conditional | flops 2147483648 | bytes 33554440 | solution.py:240
  346.4 16.4 %branch_1_fun.11 = (bf16[4,64,2048]{2,1,0:T(8,128)(2,1)}, bf16[64,2048]{1,0:T(8,128)(2,1)}) custom-call(bf16[64,2048]{1,0:T(8,128)(2,1)S(1)} %get-tuple-element.88.g_ref, bf16[4,64,2048]{2,1,0:T(8,128)(2,1)} %get-tuple-element.89.x_ref, bf16[2,4,1024,2048]{3,2,1,0:T(8,128)(2,1)} %get-tuple-element.90.w_ref), custom_call_target="tpu_custom_call" | custom-call | flops 2147483648 | bytes 33554432 | tf_op jit(solution)/shard_map/cond/branch_1_fun/pallas_call | solution.py:164
  362.8 8.3 %all-to-all-start.3 = ((bf16[4,64,2048]{2,1,0:T(8,128)(2,1)}), bf16[4,64,2048]{2,1,0:T(8,128)(2,1)}, u32[]{:S(2)}, u32[]{:S(2)}) async-start(bf16[4,64,2048]{2,1,0:T(8,128)(2,1)} %get-tuple-element.169), calls=%async_computation.3 | async-start | bytes 2097152 | tf_op jit(solution)/shard_map/all_to_all | solution.py:173
  371.1 2.1 reshape.119
  373.6 19.2 %all-to-all-done.3 = bf16[4,64,2048]{2,1,0:T(8,128)(2,1)} async-done(((bf16[4,64,2048]{2,1,0:T(8,128)(2,1)}), bf16[4,64,2048]{2,1,0:T(8,128)(2,1)}, u32[]{:S(2)}, u32[]{:S(2)}) %all-to-all-start.3) | async-done | bytes 1048608 | tf_op jit(solution)/shard_map/all_to_all | solution.py:173
  392.8 0.8 multiply_convert_fusion
  393.6 2.2 constant_dynamic-slice_fusion
  395.8 0.9 copy.13
  396.7 0.6 collective-permute-start.4
  397.5 1.3 collective-permute-done.4
  399.6 2.3 convolution_convert_fusion
  402.5 2.2 fusion.11
  404.8 3.1 collective-permute-start.10
  407.9 2.2 fusion.10
  410.3 7.4 %collective-permute-done.8 = bf16[256,1024]{1,0:T(8,128)(2,1)S(1)} collective-permute-done((bf16[256,1024]{1,0:T(8,128)(2,1)S(1)}, bf16[256,1024]{1,0:T(8,128)(2,1)S(1)}, u32[]{:S(2)}, u32[]{:S(2)}) %collective-permute-start.8) | collective-permute-done | bytes 524320 | tf_op jit(solution)/shard_map/ppermute | solution.py:169
  418.0 1.3 collective-permute-done.10
  419.5 1.1 pad_maximum_fusion.2
  420.6 3.7 collective-permute-start.11
  424.4 19.4 %collective-permute-done.9 = bf16[256,2048]{1,0:T(8,128)(2,1)S(1)} collective-permute-done((bf16[256,2048]{1,0:T(8,128)(2,1)S(1)}, bf16[256,2048]{1,0:T(8,128)(2,1)S(1)}, u32[]{:S(2)}, u32[]{:S(2)}) %collective-permute-start.9) | collective-permute-done | bytes 1048608 | tf_op jit(solution)/shard_map/ppermute | solution.py:169
  443.8 2.6 collective-permute-done.11
  446.4 2.6 fusion
  449.0 1.3 copy-done.3
  450.5 2.4 collective-permute-start.12
  452.9 23.9 %collective-permute-done.12 = bf16[128,2048]{1,0:T(8,128)(2,1)S(1)} collective-permute-done((bf16[128,2048]{1,0:T(8,128)(2,1)S(1)}, bf16[128,2048]{1,0:T(8,128)(2,1)S(1)}, u32[]{:S(2)}, u32[]{:S(2)}) %collective-permute-start.12) | collective-permute-done | bytes 524320 | tf_op jit(solution)/shard_map/ppermute | solution.py:169
  476.8 2.3 fusion.3
  479.1 1.0 copy.46
  (45 shorter events, 3.9 us)
Async XLA Ops:
  7.2 12.6 %copy-start = (bf16[256,2048]{1,0:T(8,128)(2,1)S(1)}, bf16[256,2048]{1,0:T(8,128)(2,1)}, u32[]{:S(2)}) copy-start(bf16[256,2048]{1,0:T(8,128)(2,1)} %param.17) | copy-start | bytes 3145732
  7.2 160.3 %all-gather.3.cloned.1.call-start = ((), (), s32[]{:S(2)}) async-start(), calls=%async_computation.4 | async-start | bytes 34078720 | tf_op jit(solution)/shard_map/all_gather | solution.py:216
  14.6 35.6 %all-to-all-start = ((bf16[4,64,2048]{2,1,0:T(8,128)(2,1)}), bf16[4,64,2048]{2,1,0:T(8,128)(2,1)S(1)}, u32[]{:S(2)}, u32[]{:S(2)}) async-start(bf16[4,64,2048]{2,1,0:T(8,128)(2,1)} %bitcast_select_fusion), calls=%async_computation | async-start | bytes 2097152 | tf_op jit(solution)/shard_map/all_to_all | solution.py:173
  180.3 9.4 %collective-permute-start = (bf16[64,2048]{1,0:T(8,128)(2,1)S(1)}, bf16[64,2048]{1,0:T(8,128)(2,1)S(1)}, u32[]{:S(2)}, u32[]{:S(2)}) collective-permute-start(bf16[64,2048]{1,0:T(8,128)(2,1)S(1)} %get-tuple-element.111), channel_id=1, source_target_pairs={{0,64},{1,65},{2,66},{3,67},{4,68},{5,69},{6,70},{7,71},{8,72},{9,... | collective-permute-start | bytes 786440 | tf_op jit(solution)/shard_map/ppermute | solution.py:225
  189.6 0.7 collective-permute-start.1
  190.3 1.7 collective-permute-start.2
  235.8 28.3 %all-to-all-start.2 = ((bf16[4,64,2048]{2,1,0:T(8,128)(2,1)}), bf16[4,64,2048]{2,1,0:T(8,128)(2,1)S(1)}, u32[]{:S(2)}, u32[]{:S(2)}) async-start(bf16[4,64,2048]{2,1,0:T(8,128)(2,1)} %get-tuple-element.120.x_ref), calls=%async_computation.2 | async-start | bytes 2097152 | tf_op jit(solution)/shard_map/all_to_all | solution.py:173
  241.6 0.7 collective-permute-start.3
  264.0 0.7 collective-permute-start.5
  264.9 81.5 %collective-permute-start.6 = (bf16[64,2048]{1,0:T(8,128)(2,1)S(1)}, bf16[64,2048]{1,0:T(8,128)(2,1)S(1)}, u32[]{:S(2)}, u32[]{:S(2)}) collective-permute-start(bf16[64,2048]{1,0:T(8,128)(2,1)S(1)} %get-tuple-element.127), channel_id=1, source_target_pairs={{64,0},{65,1},{66,2},{67,3},{68,4},{69,5},{70,6},{71,7},{72,8},{73... | collective-permute-start | bytes 786440 | tf_op jit(solution)/shard_map/ppermute | solution.py:233
  362.8 29.9 %all-to-all-start.3 = ((bf16[4,64,2048]{2,1,0:T(8,128)(2,1)}), bf16[4,64,2048]{2,1,0:T(8,128)(2,1)}, u32[]{:S(2)}, u32[]{:S(2)}) async-start(bf16[4,64,2048]{2,1,0:T(8,128)(2,1)} %get-tuple-element.169), calls=%async_computation.3 | async-start | bytes 2097152 | tf_op jit(solution)/shard_map/all_to_all | solution.py:173
  392.8 6.9 %collective-permute-start.7 = (bf16[256,2048]{1,0:T(8,128)(2,1)}, bf16[256,2048]{1,0:T(8,128)(2,1)}, u32[]{:S(2)}, u32[]{:S(2)}) collective-permute-start(bf16[256,2048]{1,0:T(8,128)(2,1)} %bitcast.10), channel_id=1, source_target_pairs={{0,1},{1,0},{2,3},{3,2},{4,5},{5,4},{6,7},{7,6},{8,9},{9,8},{10,11... | collective-permute-start | bytes 3145736 | tf_op jit(solution)/shard_map/ppermute | solution.py:169
  396.7 2.1 collective-permute-start.4
  402.0 15.7 %collective-permute-start.8 = (bf16[256,1024]{1,0:T(8,128)(2,1)S(1)}, bf16[256,1024]{1,0:T(8,128)(2,1)S(1)}, u32[]{:S(2)}, u32[]{:S(2)}) collective-permute-start(bf16[256,1024]{1,0:T(8,128)(2,1)S(1)} %get-tuple-element.128), channel_id=1, source_target_pairs={{0,2},{2,4},{4,6},{6,0},{1,3},{3,5},{5,7},{7,1},{8,10},{10,12},{12... | collective-permute-start | bytes 1572872 | tf_op jit(solution)/shard_map/ppermute | solution.py:169
  404.8 14.5 %collective-permute-start.10 = (bf16[256,1024]{1,0:T(8,128)(2,1)S(1)}, bf16[256,1024]{1,0:T(8,128)(2,1)S(1)}, u32[]{:S(2)}, u32[]{:S(2)}) collective-permute-start(bf16[256,1024]{1,0:T(8,128)(2,1)S(1)} %get-tuple-element.129), channel_id=1, source_target_pairs={{0,6},{2,0},{4,2},{6,4},{1,7},{3,1},{5,3},{7,5},{8,14},{10,8},{12,... | collective-permute-start | bytes 1572872 | tf_op jit(solution)/shard_map/ppermute | solution.py:169
  417.9 25.9 %collective-permute-start.9 = (bf16[256,2048]{1,0:T(8,128)(2,1)S(1)}, bf16[256,2048]{1,0:T(8,128)(2,1)S(1)}, u32[]{:S(2)}, u32[]{:S(2)}) collective-permute-start(bf16[256,2048]{1,0:T(8,128)(2,1)S(1)} %pad_maximum_fusion.1), channel_id=1, source_target_pairs={{0,2},{2,4},{4,6},{6,0},{1,3},{3,5},{5,7},{7,1},{8,10},{10,12},{12... | collective-permute-start | bytes 3145736 | tf_op jit(solution)/shard_map/ppermute | solution.py:169
  420.6 25.8 %collective-permute-start.11 = (bf16[256,2048]{1,0:T(8,128)(2,1)}, bf16[256,2048]{1,0:T(8,128)(2,1)}, u32[]{:S(2)}, u32[]{:S(2)}) collective-permute-start(bf16[256,2048]{1,0:T(8,128)(2,1)} %pad_maximum_fusion.2), channel_id=1, source_target_pairs={{0,6},{2,0},{4,2},{6,4},{1,7},{3,1},{5,3},{7,5},{8,14},{10,8},{12,... | collective-permute-start | bytes 3145736 | tf_op jit(solution)/shard_map/ppermute | solution.py:169
  449.0 1.4 copy-start.3
  449.0 30.1 %copy-start.2 = (bf16[4,64,2048]{2,1,0:T(8,128)(2,1)S(1)}, bf16[4,64,2048]{2,1,0:T(8,128)(2,1)}, u32[]{:S(2)}) copy-start(bf16[4,64,2048]{2,1,0:T(8,128)(2,1)} %all_to_all.20) | copy-start | bytes 3145732
  450.5 26.4 %collective-permute-start.12 = (bf16[128,2048]{1,0:T(8,128)(2,1)S(1)}, bf16[128,2048]{1,0:T(8,128)(2,1)S(1)}, u32[]{:S(2)}, u32[]{:S(2)}) collective-permute-start(bf16[128,2048]{1,0:T(8,128)(2,1)S(1)} %fusion.4), channel_id=1, source_target_pairs={{0,8},{8,0},{1,9},{9,1},{2,10},{10,2},{3,11},{11,3},{4,12},{12,4},... | collective-permute-start | bytes 1572872 | tf_op jit(solution)/shard_map/ppermute | solution.py:169
  452.9 27.2 %copy-start.1 = (bf16[256,2048]{1,0:T(8,128)(2,1)S(1)}, bf16[256,2048]{1,0:T(8,128)(2,1)}, u32[]{:S(2)}) copy-start(bf16[256,2048]{1,0:T(8,128)(2,1)} %param.17) | copy-start | bytes 3145732
Sparse Core Ops, SparseCore 0:
  10.8 156.6 all-gather.2

commit v6 on v5

--- a/solution.py
+++ b/solution.py
@@ -16,26 +16,20 @@
 PLANE = ("zh", "zl", "y", "c")
 
 
-def tile_copies(w_ref, held, arrived, order, by_rows):
+def tile_copies(w_ref, held, arrived, order):
     halves, depth, rows, width = w_ref.shape
     tiles, slots = width // TILE, held.shape[0]
 
     def start(number):
         slot = lax.rem(number, slots)
         layer = order(number // tiles)
-        tile = lax.rem(number, tiles)
-        if by_rows:
-            inner = rows // TILE
-            span = pl.ds(pl.multiple_of(lax.rem(tile, inner) * TILE, TILE), TILE)
-            parts = [(w_ref.at[tile // inner, layer, span], held.at[slot])]
-        else:
-            span = pl.ds(pl.multiple_of(tile * TILE, TILE), TILE)
-            parts = [
-                (w_ref.at[half, layer, :, span], held.at[slot, pl.ds(half * rows, rows)])
-                for half in range(halves)
-            ]
-        for source, target in parts:
-            pltpu.make_async_copy(source, target, arrived.at[slot]).start()
+        span = pl.ds(pl.multiple_of(lax.rem(number, tiles) * TILE, TILE), TILE)
+        for half in range(halves):
+            pltpu.make_async_copy(
+                w_ref.at[half, layer, :, span],
+                held.at[slot, pl.ds(half * rows, rows)],
+                arrived.at[slot],
+            ).start()
 
     def wait(number):
         whole = held.at[lax.rem(number, slots)]
@@ -56,7 +50,7 @@
 ):
     depth, rows, width = base_ref.shape
     tiles, slots = width // TILE, held.shape[0]
-    wait, refill = tile_copies(w_ref, held, arrived, lambda i: i, False)
+    wait, refill = tile_copies(w_ref, held, arrived, lambda i: i)
     x_now[...] = x_ref[...].astype(jnp.float32)
     in_ref[0] = x_ref[...]
 
@@ -96,7 +90,7 @@
 def backward_kernel(g_ref, x_ref, w_ref, seen_ref, out_ref, g_now, back, held, arrived):
     depth, rows, width = x_ref.shape
     tiles, slots = width // TILE, held.shape[0]
-    wait, refill = tile_copies(w_ref, held, arrived, lambda i: depth - 1 - i, True)
+    wait, refill = tile_copies(w_ref, held, arrived, lambda i: depth - 1 - i)
     g_now[...] = g_ref[...]
 
     def run_layer(step, carry):
@@ -105,10 +99,14 @@
         for tile in range(tiles):
             number = step * tiles + tile
             wait(number)
-            back[:, pl.ds(tile * TILE, TILE)] = lax.dot_general(
-                g_now[...], held[lax.rem(number, slots)], (((1,), (1,)), ((), ())),
-                preferred_element_type=jnp.float32,
+            product = lax.dot_general(
+                g_now[:, pl.ds(tile * TILE, TILE)], held[lax.rem(number, slots)],
+                (((1,), (1,)), ((), ())), preferred_element_type=jnp.float32,
             )
+            if tile == 0:
+                back[...] = product
+            else:
+                back[...] += product
             refill(number)
         values = x_ref[layer].astype(jnp.float32)
         scale = lax.rsqrt(jnp.mean(values * values, axis=-1, keepdims=True) + epsilon)
@@ -123,7 +121,7 @@
     out_ref[...] = g_now[...]
 
 
-def stage_call(kernel, tile_shape, scratch, outs, depth, rows, width):
+def stage_call(kernel, scratch, outs, depth, rows, width):
     vmem = pl.BlockSpec(memory_space=pltpu.VMEM)
     return pl.pallas_call(
         kernel,
@@ -132,7 +130,7 @@
         out_shape=[jax.ShapeDtypeStruct(shape, jnp.bfloat16) for shape in outs],
         scratch_shapes=[
             *scratch,
-            pltpu.VMEM((SLOTS, *tile_shape), jnp.bfloat16),
+            pltpu.VMEM((SLOTS, width, TILE), jnp.bfloat16),
             pltpu.SemaphoreType.DMA((SLOTS,)),
         ],
         compiler_params=pltpu.CompilerParams(vmem_limit_bytes=32 * 1024 * 1024),
@@ -152,7 +150,7 @@
         pltpu.VMEM((rows, width), jnp.float32),
     ]
     outs = [(depth, rows, width), (depth, rows, width), (rows, width)]
-    call = stage_call(forward_kernel, (width, TILE), scratch, outs, depth, rows, width)
+    call = stage_call(forward_kernel, scratch, outs, depth, rows, width)
     return tuple(call(x, base, weight))
 
 
@@ -160,7 +158,7 @@
     depth, rows, width = x.shape
     scratch = [pltpu.VMEM((rows, width), jnp.bfloat16), pltpu.VMEM((rows, width), jnp.float32)]
     outs = [(depth, rows, width), (rows, width)]
-    call = stage_call(backward_kernel, (TILE, width), scratch, outs, depth, rows, width)
+    call = stage_call(backward_kernel, scratch, outs, depth, rows, width)
     return tuple(call(g, x, weight))
 
 
@@ -170,18 +168,35 @@
 
 
 def exchange(value):
-    return lax.all_to_all(value, "zl", 0, 0)
-
-
-def gradient_sum(normed, g):
+    lane = lax.axis_index("zl")
+    blocks = []
+    for steps in range(DEPTH):
+        block = lax.dynamic_index_in_dim(value, lax.rem(lane + steps, DEPTH), 0, keepdims=False)
+        blocks.append(shift(block, "zl", steps) if steps else block)
+    return jnp.stack(blocks)
+
+
+def by_sender(blocks):
+    lane = lax.axis_index("zl")
+    order = [lax.rem(lane - sender + DEPTH, DEPTH) for sender in range(DEPTH)]
+    return jnp.stack([lax.dynamic_index_in_dim(blocks, i, 0, keepdims=False) for i in order])
+
+
+def pair_rows(normed):
     rows, width = normed.shape
-    core, y, zh = lax.axis_index("c"), lax.axis_index("y"), lax.axis_index("zh")
+    core = lax.axis_index("c")
+    chips = lax.axis_size("zh") * lax.axis_size("y")
+    by_core = normed.reshape(rows, chips, 2, width // (2 * chips))
+    mine = lax.dynamic_index_in_dim(by_core, core, 2, keepdims=False).reshape(rows, -1)
+    theirs = lax.dynamic_index_in_dim(by_core, 1 - core, 2, keepdims=False).reshape(rows, -1)
+    return jnp.concatenate([mine, shift(theirs, "c", 1)], axis=0)
+
+
+def gradient_sum(left, g):
+    rows, width = g.shape
+    y, zh = lax.axis_index("y"), lax.axis_index("zh")
     chips = lax.axis_size("zh") * lax.axis_size("y")
     piece = width // (2 * chips)
-    by_core = normed.reshape(rows, chips, 2, piece)
-    mine = lax.dynamic_index_in_dim(by_core, core, 2, keepdims=False).reshape(rows, -1)
-    theirs = lax.dynamic_index_in_dim(by_core, 1 - core, 2, keepdims=False).reshape(rows, -1)
-    left = jnp.concatenate([mine, shift(theirs, "c", 1)], axis=0)
     right = jnp.concatenate([g, shift(g, "c", 1)], axis=0)
 
     left = left.reshape(2 * rows, 2, 4, piece)
@@ -216,7 +231,7 @@
     weight = lax.all_gather(layer_weight[0], PLANE, axis=0, tiled=True)
     weight = weight.reshape(2, DEPTH, width // 2, width)
     picked = jnp.take(epoch_buffer[0], sample_ids[0], axis=0)
-    base = exchange(picked.reshape(DEPTH, rows, width))
+    base = lax.all_to_all(picked.reshape(DEPTH, rows, width), "zl", 0, 0)
     x = lax.dynamic_slice_in_dim(stream_in, lane * rows, rows, 0)
     g = lax.dynamic_slice_in_dim(top_cotangent, lane * rows, rows, 0)
 
@@ -234,20 +249,17 @@
         if t == STAGES - 2:
             held, passed, _ = lax.optimization_barrier((decoded, inputs, state[1]))
             decoded_rows, input_rows = exchange(held), exchange(passed)
-            arrived, decoded_rows, input_rows = lax.optimization_barrier(
-                (arrived, decoded_rows, input_rows)
-            )
+        if t == 0:
+            decoded_rows = by_sender(decoded_rows).reshape(1, DEPTH * rows, width)
+            values = input_rows.reshape(DEPTH * rows, width).astype(jnp.float32)
+            scale = lax.rsqrt(jnp.mean(values * values, axis=-1, keepdims=True) + epsilon)
+            left = pair_rows((values * scale).astype(jnp.bfloat16))
+            arrived, left, decoded_rows = lax.optimization_barrier((arrived, left, decoded_rows))
         state = lax.cond(
             stage == t, lambda a, s: backward_stage(a, inputs, weight), lambda a, s: s, arrived, state
         )
-    seen = state[0]
-
-    decoded_rows = decoded_rows.reshape(1, DEPTH * rows, width)
-    input_rows = input_rows.reshape(DEPTH * rows, width).astype(jnp.float32)
-    scale = lax.rsqrt(jnp.mean(input_rows * input_rows, axis=-1, keepdims=True) + epsilon)
-    normed = (input_rows * scale).astype(jnp.bfloat16)
-    cotangents = exchange(seen).reshape(DEPTH * rows, width)
-    return decoded_rows, gradient_sum(normed, cotangents)[None]
+    cotangents = exchange(state[0]).reshape(DEPTH * rows, width)
+    return decoded_rows, gradient_sum(left, cotangents)[None]
 
 
 def solution(mesh):

time: 492 us -> 470 us (0.955)
  blocking collectives: 28 us -> 0 us
  local copies, waits for them, and re-layouts: 13.5 us -> 20.4 us
  other arithmetic: 8.06 us -> 13.3 us
    ppermute x7 -> x16, waiting for transfers between devices: 56 us -> 99.4 us  [shift(): lax.ppermute(value, axis, [(i, (i + steps) % count) for i in range(count)])]
    all_to_all x3 -> x1, waiting for transfers between devices: 71.4 us -> 30.5 us  [local(): base = lax.all_to_all(picked.reshape(DEPTH, rows, width), 'zl', 0, 0)]
    all_to_all x1 -> x0, blocking collectives: 28 us -> none  [exchange(): return lax.all_to_all(value, 'zl', 0, 0)]
    all_to_all x3 -> x1, starting transfers between devices: 19.2 us -> 5.09 us  [local(): base = lax.all_to_all(picked.reshape(DEPTH, rows, width), 'zl', 0, 0)]
    ppermute x7 -> x16, starting transfers between devices: 10.4 us -> 21.7 us  [shift(): lax.ppermute(value, axis, [(i, (i + steps) % count) for i in range(count)])]
    dynamic_slice x3 -> x7, local copies, waits for them, and re-layouts: 3.29 us -> 8.34 us  [the longest x3 3.18 us: exchange(): lax.dynamic_index_in_dim(value, lax.rem(lane + steps, DEPTH), 0, keepdims...]
  transfers between devices with their start and end apart: 17 -> 24, of which waited for: 12 -> 15; matrix products, arithmetic and copies ran while one was open for 4% -> 6% of each run, Pallas kernels for 0% -> 0%
where the time goes in v6:
time: 470 us; the launch traced here: 465 us
  waiting for transfers between devices  335 us (71%)
  Pallas kernels  40.1 us (9%)
  starting transfers between devices  35.7 us (8%)
  local copies, waits for them, and re-layouts  20.4 us (4%)
  between operations  14.5 us (3%)
  other arithmetic  13.3 us (3%)
  matrix products  6.41 us (1%)
    all_gather x1, waiting for transfers between devices, local(): weight = lax.all_gather(layer_weight[0], PLANE, axis=0, tiled=True)  117 us
    ppermute x16, waiting for transfers between devices, shift(): lax.ppermute(value, axis, [(i, (i + steps) % count) for i in range(count)])  99.4 us
    ppermute x3, waiting for transfers between devices, local(): arrived = lax.ppermute(state[1], 'x', [(t + 1, t)])  80.8 us
    all_to_all x1, waiting for transfers between devices, local(): base = lax.all_to_all(picked.reshape(DEPTH, rows, width), 'zl', 0, 0)  30.5 us
    pallas_call x2, Pallas kernels, backward_stage(): return tuple(call(g, x, weight))  27.5 us
    ppermute x16, starting transfers between devices, shift(): lax.ppermute(value, axis, [(i, (i + steps) % count) for i in range(count)])  21.7 us
    pallas_call x1, Pallas kernels, forward_stage(): return tuple(call(x, base, weight))  12.5 us
  transfers between devices with their start and end apart: 24, of which 15 were waited for; matrix products, arithmetic and copies ran while one was open for 6% of the time, Pallas kernels for 0%

profile of v6, /device:TPU:96, one launch (start us, length us, event | category | flops | bytes accessed | tf_op | source)
XLA Modules:
  0.0 465.2 jit_solution(1173368250744062037)
XLA Ops:
  8.4 1.3 reduce.4
  10.7 2.8 gather_fusion
  13.5 1.1 bitcast_select_fusion
  14.6 5.1 %all-to-all-start = ((bf16[4,64,2048]{2,1,0:T(8,128)(2,1)}), bf16[4,64,2048]{2,1,0:T(8,128)(2,1)S(1)}, u32[]{:S(2)}, u32[]{:S(2)}) async-start(bf16[4,64,2048]{2,1,0:T(8,128)(2,1)} %bitcast_select_fusion), calls=%async_computation | async-start | bytes 2097152 | tf_op jit(solution)/shard_map/all_to_all | solution.py:234
  19.7 30.5 %all-to-all-done.base_ref = bf16[4,64,2048]{2,1,0:T(8,128)(2,1)S(1)} async-done(((bf16[4,64,2048]{2,1,0:T(8,128)(2,1)}), bf16[4,64,2048]{2,1,0:T(8,128)(2,1)S(1)}, u32[]{:S(2)}, u32[]{:S(2)}) %all-to-all-start) | async-done | bytes 1048608 | tf_op jit(solution)/shard_map/all_to_all | solution.py:234
  50.2 117.2 %all-gather.3.cloned.1.call-done = bf16[1,8192,2048]{2,1,0:T(8,128)(2,1)} async-done(((bf16[1,128,2048]{2,1,0:T(8,128)(2,1)}), bf16[1,8192,2048]{2,1,0:T(8,128)(2,1)}) %all-gather.3.cloned.1.call-update) | async-done | bytes 33554448 | tf_op jit(solution)/shard_map/all_gather | solution.py:231
  167.4 12.5 %shard_map.68 = (bf16[4,64,2048]{2,1,0:T(8,128)(2,1)S(1)}, bf16[4,64,2048]{2,1,0:T(8,128)(2,1)S(1)}, bf16[64,2048]{1,0:T(8,128)(2,1)}) custom-call(bf16[64,2048]{1,0:T(8,128)(2,1)S(1)} %constant_dynamic-slice_fusion.13.x_ref, bf16[4,64,2048]{2,1,0:T(8,128)(2,1)S(1)} %all-to-all-done.base_ref, bf16[2,4,1024,2048]{3,2,1,0:T(8,128)(2,1)} %bitcast.66), custom_call_target="tpu_custom_call" | custom-call | flops 2147483648 | bytes 33554432 | tf_op jit(solution)/shard_map/pallas_call | solution.py:154
  180.0 3.4 collective-permute-start
  183.4 6.3 %collective-permute-done = bf16[64,2048]{1,0:T(8,128)(2,1)S(1)} collective-permute-done((bf16[64,2048]{1,0:T(8,128)(2,1)}, bf16[64,2048]{1,0:T(8,128)(2,1)S(1)}, u32[]{:S(2)}, u32[]{:S(2)}) %collective-permute-start) | collective-permute-done | bytes 262176 | tf_op jit(solution)/shard_map/ppermute | solution.py:240
  190.4 1.4 collective-permute-start.2
  191.7 1.0 constant_dynamic-slice_fusion.14.g_ref
  192.7 13.8 %shard_map.69 = (bf16[4,64,2048]{2,1,0:T(8,128)(2,1)}, bf16[64,2048]{1,0:T(8,128)(2,1)}) custom-call(bf16[64,2048]{1,0:T(8,128)(2,1)S(1)} %constant_dynamic-slice_fusion.14.g_ref, bf16[4,64,2048]{2,1,0:T(8,128)(2,1)S(1)} %get-tuple-element.122.x_ref, bf16[2,4,1024,2048]{3,2,1,0:T(8,128)(2,1)} %bitcast.70), custom_call_target="tpu_custom_call" | custom-call | flops 2147483648 | bytes 33554432 | tf_op jit(solution)/shard_map/pallas_call | solution.py:162
  207.4 3.8 collective-permute-start.6
  211.2 1.4 collective-permute-start.3
  212.6 1.0 constant_dynamic-slice_fusion.9
  214.1 4.5 collective-permute-done.8
  218.7 3.0 collective-permute-start.11
  221.7 3.2 collective-permute-done.6
  224.9 9.1 %collective-permute-done.7 = bf16[64,2048]{1,0:T(8,128)(2,1)S(1)} collective-permute-done((bf16[64,2048]{1,0:T(8,128)(2,1)S(1)}, bf16[64,2048]{1,0:T(8,128)(2,1)S(1)}, u32[]{:S(2)}, u32[]{:S(2)}) %collective-permute-start.7) | collective-permute-done | bytes 262176 | tf_op jit(solution)/shard_map/ppermute | solution.py:167
  235.0 1.3 maximum_convert_fusion
  236.4 2.8 reshape.122
  239.2 2.4 multiply_convert_fusion
  241.6 2.2 constant_dynamic-slice_fusion.11
  243.7 2.0 copy.12
  246.6 7.7 %collective-permute-done.11 = bf16[64,2048]{1,0:T(8,128)(2,1)} collective-permute-done((bf16[64,2048]{1,0:T(8,128)(2,1)}, bf16[64,2048]{1,0:T(8,128)(2,1)}, u32[]{:S(2)}, u32[]{:S(2)}) %collective-permute-start.11) | collective-permute-done | bytes 262176 | tf_op jit(solution)/shard_map/ppermute | solution.py:167
  254.3 1.2 pad_maximum_fusion.2
  255.6 1.3 collective-permute-start.5
  256.9 1.1 pad_maximum_fusion.3
  259.0 1.1 pad_maximum_fusion.1
  260.1 80.8 %collective-permute-done.5 = bf16[64,2048]{1,0:T(8,128)(2,1)S(1)} collective-permute-done((bf16[64,2048]{1,0:T(8,128)(2,1)}, bf16[64,2048]{1,0:T(8,128)(2,1)S(1)}, u32[]{:S(2)}, u32[]{:S(2)}) %collective-permute-start.5) | collective-permute-done | bytes 262176 | tf_op jit(solution)/shard_map/ppermute | solution.py:248
  340.9 13.7 %conditional.11 = (bf16[4,64,2048]{2,1,0:T(8,128)(2,1)}) conditional(s32[]{:T(128)} %convert_element_type.61, bf16[4,64,2048]{2,1,0:T(8,128)(2,1)} %get-tuple-element.126, (bf16[64,2048]{1,0:T(8,128)(2,1)S(1)}, bf16[4,64,2048]{2,1,0:T(8,128)(2,1)S(1)}, bf16[2,4,1024,2048]{3,2,1,0:T(8,128)(2,1)}) %tuple.106), branch_computations={%region_11.12_spmd, %region_12.13_spmd} | conditional | flops 2147483648 | bytes 33554440 | solution.py:258
  340.9 13.7 %branch_1_fun.11 = (bf16[4,64,2048]{2,1,0:T(8,128)(2,1)}, bf16[64,2048]{1,0:T(8,128)(2,1)}) custom-call(bf16[64,2048]{1,0:T(8,128)(2,1)S(1)} %get-tuple-element.88.g_ref, bf16[4,64,2048]{2,1,0:T(8,128)(2,1)S(1)} %get-tuple-element.89.x_ref, bf16[2,4,1024,2048]{3,2,1,0:T(8,128)(2,1)} %get-tuple-element.90.w_ref), custom_call_target="tpu_custom_call" | custom-call | flops 2147483648 | bytes 33554432 | tf_op jit(solution)/shard_map/cond/branch_1_fun/pallas_call | solution.py:162
  354.7 1.3 constant_dynamic-slice_fusion.3
  356.2 1.9 collective-permute-start.15
  358.1 7.3 %collective-permute-done.13 = bf16[64,2048]{1,0:T(8,128)(2,1)S(1)} collective-permute-done((bf16[64,2048]{1,0:T(8,128)(2,1)S(1)}, bf16[64,2048]{1,0:T(8,128)(2,1)S(1)}, u32[]{:S(2)}, u32[]{:S(2)}) %collective-permute-start.13) | collective-permute-done | bytes 262176 | tf_op jit(solution)/shard_map/ppermute | solution.py:167
  365.4 11.2 %collective-permute-done.14 = bf16[64,2048]{1,0:T(8,128)(2,1)S(1)} collective-permute-done((bf16[64,2048]{1,0:T(8,128)(2,1)S(1)}, bf16[64,2048]{1,0:T(8,128)(2,1)S(1)}, u32[]{:S(2)}, u32[]{:S(2)}) %collective-permute-start.14) | collective-permute-done | bytes 262176 | tf_op jit(solution)/shard_map/ppermute | solution.py:167
  377.0 2.5 collective-permute-done.16
  379.5 1.0 copy-done.7
  380.5 2.0 convolution_convert_fusion
  384.5 2.3 collective-permute-start.19
  387.5 10.3 %collective-permute-done.17 = bf16[256,1024]{1,0:T(8,128)(2,1)S(1)} collective-permute-done((bf16[256,1024]{1,0:T(8,128)(2,1)S(1)}, bf16[256,1024]{1,0:T(8,128)(2,1)S(1)}, u32[]{:S(2)}, u32[]{:S(2)}) %collective-permute-start.17) | collective-permute-done | bytes 524320 | tf_op jit(solution)/shard_map/ppermute | solution.py:167
  398.8 3.2 collective-permute-start.20
  402.0 21.8 %collective-permute-done.18 = bf16[256,2048]{1,0:T(8,128)(2,1)} collective-permute-done((bf16[256,2048]{1,0:T(8,128)(2,1)S(1)}, bf16[256,2048]{1,0:T(8,128)(2,1)}, u32[]{:S(2)}, u32[]{:S(2)}) %collective-permute-start.18) | collective-permute-done | bytes 1048608 | tf_op jit(solution)/shard_map/ppermute | solution.py:167
  423.8 1.0 copy-done.9
  424.8 3.0 fusion
  428.7 6.3 %collective-permute-start.21 = (bf16[128,2048]{1,0:T(8,128)(2,1)}, bf16[128,2048]{1,0:T(8,128)(2,1)}, u32[]{:S(2)}, u32[]{:S(2)}) collective-permute-start(bf16[128,2048]{1,0:T(8,128)(2,1)} %fusion.4), channel_id=1, source_target_pairs={{0,8},{8,0},{1,9},{9,1},{2,10},{10,2},{3,11},{11,3},{4,12},{12,4},... | collective-permute-start | bytes 1572872 | tf_op jit(solution)/shard_map/ppermute | solution.py:167
  435.0 21.3 %collective-permute-done.21 = bf16[128,2048]{1,0:T(8,128)(2,1)} collective-permute-done((bf16[128,2048]{1,0:T(8,128)(2,1)}, bf16[128,2048]{1,0:T(8,128)(2,1)}, u32[]{:S(2)}, u32[]{:S(2)}) %collective-permute-start.21) | collective-permute-done | bytes 524320 | tf_op jit(solution)/shard_map/ppermute | solution.py:167
  456.3 2.1 fusion.3
  (73 shorter events, 12.4 us)
Async XLA Ops:
  7.2 12.6 %copy-start = (bf16[256,2048]{1,0:T(8,128)(2,1)S(1)}, bf16[256,2048]{1,0:T(8,128)(2,1)}, u32[]{:S(2)}) copy-start(bf16[256,2048]{1,0:T(8,128)(2,1)} %param.17) | copy-start | bytes 3145732
  7.2 160.3 %all-gather.3.cloned.1.call-start = ((), (), s32[]{:S(2)}) async-start(), calls=%async_computation.1 | async-start | bytes 34078720 | tf_op jit(solution)/shard_map/all_gather | solution.py:231
  14.6 35.6 %all-to-all-start = ((bf16[4,64,2048]{2,1,0:T(8,128)(2,1)}), bf16[4,64,2048]{2,1,0:T(8,128)(2,1)S(1)}, u32[]{:S(2)}, u32[]{:S(2)}) async-start(bf16[4,64,2048]{2,1,0:T(8,128)(2,1)} %bitcast_select_fusion), calls=%async_computation | async-start | bytes 2097152 | tf_op jit(solution)/shard_map/all_to_all | solution.py:234
  180.0 9.7 %collective-permute-start = (bf16[64,2048]{1,0:T(8,128)(2,1)}, bf16[64,2048]{1,0:T(8,128)(2,1)S(1)}, u32[]{:S(2)}, u32[]{:S(2)}) collective-permute-start(bf16[64,2048]{1,0:T(8,128)(2,1)} %get-tuple-element.111), channel_id=1, source_target_pairs={{0,64},{1,65},{2,66},{3,67},{4,68},{5,69},{6,70},{7,71},{8,72},{9,... | collective-permute-start | bytes 786440 | tf_op jit(solution)/shard_map/ppermute | solution.py:240
  189.7 0.7 collective-permute-start.1
  190.4 2.3 collective-permute-start.2
  207.4 11.3 %collective-permute-start.8 = (bf16[64,2048]{1,0:T(8,128)(2,1)}, bf16[64,2048]{1,0:T(8,128)(2,1)S(1)}, u32[]{:S(2)}, u32[]{:S(2)}) collective-permute-start(bf16[64,2048]{1,0:T(8,128)(2,1)} %get-tuple-element.149), channel_id=1, source_target_pairs={{0,48},{16,0},{32,16},{48,32},{1,49},{17,1},{33,17},{49,33},{2,50}... | collective-permute-start | bytes 786440 | tf_op jit(solution)/shard_map/ppermute | solution.py:167
  207.4 17.5 %collective-permute-start.6 = (bf16[64,2048]{1,0:T(8,128)(2,1)}, bf16[64,2048]{1,0:T(8,128)(2,1)S(1)}, u32[]{:S(2)}, u32[]{:S(2)}) collective-permute-start(bf16[64,2048]{1,0:T(8,128)(2,1)} %get-tuple-element.151), channel_id=1, source_target_pairs={{0,16},{16,32},{32,48},{48,0},{1,17},{17,33},{33,49},{49,1},{2,18}... | collective-permute-start | bytes 786440 | tf_op jit(solution)/shard_map/ppermute | solution.py:167
  211.2 22.8 %collective-permute-start.7 = (bf16[64,2048]{1,0:T(8,128)(2,1)S(1)}, bf16[64,2048]{1,0:T(8,128)(2,1)S(1)}, u32[]{:S(2)}, u32[]{:S(2)}) collective-permute-start(bf16[64,2048]{1,0:T(8,128)(2,1)S(1)} %get-tuple-element.150), channel_id=1, source_target_pairs={{0,32},{16,48},{32,0},{48,16},{1,33},{17,49},{33,1},{49,17},{2,34}... | collective-permute-start | bytes 786440 | tf_op jit(solution)/shard_map/ppermute | solution.py:167
  211.2 34.5 %collective-permute-start.3 = (bf16[64,2048]{1,0:T(8,128)(2,1)}, bf16[64,2048]{1,0:T(8,128)(2,1)}, u32[]{:S(2)}, u32[]{:S(2)}) collective-permute-start(bf16[64,2048]{1,0:T(8,128)(2,1)} %get-tuple-element.117), channel_id=1, source_target_pairs={{192,128},{193,129},{194,130},{195,131},{196,132},{197,133},{198,1... | collective-permute-start | bytes 786440 | tf_op jit(solution)/shard_map/ppermute | solution.py:248
  213.6 33.0 %collective-permute-start.10 = (bf16[64,2048]{1,0:T(8,128)(2,1)}, bf16[64,2048]{1,0:T(8,128)(2,1)}, u32[]{:S(2)}, u32[]{:S(2)}) collective-permute-start(bf16[64,2048]{1,0:T(8,128)(2,1)} %get-tuple-element.145), channel_id=1, source_target_pairs={{0,16},{16,32},{32,48},{48,0},{1,17},{17,33},{33,49},{49,1},{2,18}... | collective-permute-start | bytes 786440 | tf_op jit(solution)/shard_map/ppermute | solution.py:167
  218.7 15.4 %copy-start.3 = (bf16[64,2048]{1,0:T(8,128)(2,1)}, bf16[64,2048]{1,0:T(8,128)(2,1)S(1)}, u32[]{:S(2)}) copy-start(bf16[64,2048]{1,0:T(8,128)(2,1)S(1)} %collective-permute-done.8) | copy-start | bytes 786436
  218.7 35.6 %collective-permute-start.11 = (bf16[64,2048]{1,0:T(8,128)(2,1)}, bf16[64,2048]{1,0:T(8,128)(2,1)}, u32[]{:S(2)}, u32[]{:S(2)}) collective-permute-start(bf16[64,2048]{1,0:T(8,128)(2,1)} %get-tuple-element.144), channel_id=1, source_target_pairs={{0,32},{16,48},{32,0},{48,16},{1,33},{17,49},{33,1},{49,17},{2,34}... | collective-permute-start | bytes 786440 | tf_op jit(solution)/shard_map/ppermute | solution.py:167
  224.9 9.2 %copy-start.4 = (bf16[64,2048]{1,0:T(8,128)(2,1)}, bf16[64,2048]{1,0:T(8,128)(2,1)S(1)}, u32[]{:S(2)}) copy-start(bf16[64,2048]{1,0:T(8,128)(2,1)S(1)} %collective-permute-done.6) | copy-start | bytes 786436
  224.9 29.4 %collective-permute-start.12 = (bf16[64,2048]{1,0:T(8,128)(2,1)}, bf16[64,2048]{1,0:T(8,128)(2,1)}, u32[]{:S(2)}, u32[]{:S(2)}) collective-permute-start(bf16[64,2048]{1,0:T(8,128)(2,1)} %get-tuple-element.143), channel_id=1, source_target_pairs={{0,48},{16,0},{32,16},{48,32},{1,49},{17,1},{33,17},{49,33},{2,50}... | collective-permute-start | bytes 786440 | tf_op jit(solution)/shard_map/ppermute | solution.py:167
  234.0 0.7 copy-start.5
  245.7 13.2 %collective-permute-start.9 = (bf16[256,1024]{0,1:T(8,128)(2,1)}, bf16[256,1024]{0,1:T(8,128)(2,1)}, u32[]{:S(2)}, u32[]{:S(2)}) collective-permute-start(bf16[256,1024]{0,1:T(8,128)(2,1)} %bitcast.91), channel_id=1, source_target_pairs={{0,1},{1,0},{2,3},{3,2},{4,5},{5,4},{6,7},{7,6},{8,9},{9,8},{10,11... | collective-permute-start | bytes 1572872 | tf_op jit(solution)/shard_map/ppermute | solution.py:167
  245.7 8.5 %copy-start.6 = (bf16[1,64,2048]{2,1,0:T(8,128)(2,1)S(1)}, bf16[1,64,2048]{2,1,0:T(8,128)(2,1)}, u32[]{:S(2)}) copy-start(bf16[1,64,2048]{2,1,0:T(8,128)(2,1)} %get-tuple-element.142) | copy-start | bytes 786436
  245.7 9.9 %collective-permute-start.4 = (bf16[64,2048]{1,0:T(8,128)(2,1)}, bf16[64,2048]{1,0:T(8,128)(2,1)S(1)}, u32[]{:S(2)}, u32[]{:S(2)}) collective-permute-start(bf16[64,2048]{1,0:T(8,128)(2,1)} %get-tuple-element.118), channel_id=1, source_target_pairs={{128,64},{129,65},{130,66},{131,67},{132,68},{133,69},{134,70},{13... | collective-permute-start | bytes 786440 | tf_op jit(solution)/shard_map/ppermute | solution.py:248
  255.6 85.3 %collective-permute-start.5 = (bf16[64,2048]{1,0:T(8,128)(2,1)}, bf16[64,2048]{1,0:T(8,128)(2,1)S(1)}, u32[]{:S(2)}, u32[]{:S(2)}) collective-permute-start(bf16[64,2048]{1,0:T(8,128)(2,1)} %get-tuple-element.120), channel_id=1, source_target_pairs={{64,0},{65,1},{66,2},{67,3},{68,4},{69,5},{70,6},{71,7},{72,8},{73... | collective-permute-start | bytes 786440 | tf_op jit(solution)/shard_map/ppermute | solution.py:248
  356.0 9.4 %collective-permute-start.13 = (bf16[64,2048]{1,0:T(8,128)(2,1)S(1)}, bf16[64,2048]{1,0:T(8,128)(2,1)S(1)}, u32[]{:S(2)}, u32[]{:S(2)}) collective-permute-start(bf16[64,2048]{1,0:T(8,128)(2,1)S(1)} %get-tuple-element.137), channel_id=1, source_target_pairs={{0,16},{16,32},{32,48},{48,0},{1,17},{17,33},{33,49},{49,1},{2,18}... | collective-permute-start | bytes 786440 | tf_op jit(solution)/shard_map/ppermute | solution.py:167
  356.1 20.5 %collective-permute-start.14 = (bf16[64,2048]{1,0:T(8,128)(2,1)S(1)}, bf16[64,2048]{1,0:T(8,128)(2,1)S(1)}, u32[]{:S(2)}, u32[]{:S(2)}) collective-permute-start(bf16[64,2048]{1,0:T(8,128)(2,1)S(1)} %get-tuple-element.136), channel_id=1, source_target_pairs={{0,32},{16,48},{32,0},{48,16},{1,33},{17,49},{33,1},{49,17},{2,34}... | collective-permute-start | bytes 786440 | tf_op jit(solution)/shard_map/ppermute | solution.py:167
  356.2 20.4 %collective-permute-start.15 = (bf16[64,2048]{1,0:T(8,128)(2,1)S(1)}, bf16[64,2048]{1,0:T(8,128)(2,1)S(1)}, u32[]{:S(2)}, u32[]{:S(2)}) collective-permute-start(bf16[64,2048]{1,0:T(8,128)(2,1)S(1)} %get-tuple-element.135), channel_id=1, source_target_pairs={{0,48},{16,0},{32,16},{48,32},{1,49},{17,1},{33,17},{49,33},{2,50}... | collective-permute-start | bytes 786440 | tf_op jit(solution)/shard_map/ppermute | solution.py:167
  376.8 10.0 %copy-start.2 = (bf16[4,64,2048]{2,1,0:T(8,128)(2,1)}, bf16[4,64,2048]{2,1,0:T(8,128)(2,1)S(1)}, u32[]{:S(2)}) copy-start(bf16[4,64,2048]{2,1,0:T(8,128)(2,1)S(1)} %pad_maximum_fusion.4) | copy-start | bytes 3145732
  376.8 2.7 collective-permute-start.16
  379.5 1.0 copy-start.7
  382.5 1.2 copy-start.8
  382.6 15.3 %collective-permute-start.17 = (bf16[256,1024]{1,0:T(8,128)(2,1)S(1)}, bf16[256,1024]{1,0:T(8,128)(2,1)S(1)}, u32[]{:S(2)}, u32[]{:S(2)}) collective-permute-start(bf16[256,1024]{1,0:T(8,128)(2,1)S(1)} %get-tuple-element.128), channel_id=1, source_target_pairs={{0,2},{2,4},{4,6},{6,0},{1,3},{3,5},{5,7},{7,1},{8,10},{10,12},{12... | collective-permute-start | bytes 1572872 | tf_op jit(solution)/shard_map/ppermute | solution.py:167
  384.5 14.0 %collective-permute-start.19 = (bf16[256,1024]{1,0:T(8,128)(2,1)S(1)}, bf16[256,1024]{1,0:T(8,128)(2,1)S(1)}, u32[]{:S(2)}, u32[]{:S(2)}) collective-permute-start(bf16[256,1024]{1,0:T(8,128)(2,1)S(1)} %get-tuple-element.129), channel_id=1, source_target_pairs={{0,6},{2,0},{4,2},{6,4},{1,7},{3,1},{5,3},{7,5},{8,14},{10,8},{12,... | collective-permute-start | bytes 1572872 | tf_op jit(solution)/shard_map/ppermute | solution.py:167
  398.1 25.8 %collective-permute-start.18 = (bf16[256,2048]{1,0:T(8,128)(2,1)S(1)}, bf16[256,2048]{1,0:T(8,128)(2,1)}, u32[]{:S(2)}, u32[]{:S(2)}) collective-permute-start(bf16[256,2048]{1,0:T(8,128)(2,1)S(1)} %pad_maximum_fusion.5), channel_id=1, source_target_pairs={{0,2},{2,4},{4,6},{6,0},{1,3},{3,5},{5,7},{7,1},{8,10},{10,12},{12... | collective-permute-start | bytes 3145736 | tf_op jit(solution)/shard_map/ppermute | solution.py:167
  398.8 25.0 %collective-permute-start.20 = (bf16[256,2048]{1,0:T(8,128)(2,1)S(1)}, bf16[256,2048]{1,0:T(8,128)(2,1)S(1)}, u32[]{:S(2)}, u32[]{:S(2)}) collective-permute-start(bf16[256,2048]{1,0:T(8,128)(2,1)S(1)} %pad_maximum_fusion.6), channel_id=1, source_target_pairs={{0,6},{2,0},{4,2},{6,4},{1,7},{3,1},{5,3},{7,5},{8,14},{10,8},{12,... | collective-permute-start | bytes 3145736 | tf_op jit(solution)/shard_map/ppermute | solution.py:167
  423.8 1.0 copy-start.9
  424.8 33.6 %copy-start.1 = (bf16[256,2048]{1,0:T(8,128)(2,1)S(1)}, bf16[256,2048]{1,0:T(8,128)(2,1)}, u32[]{:S(2)}) copy-start(bf16[256,2048]{1,0:T(8,128)(2,1)} %param.17) | copy-start | bytes 3145732
  428.7 27.6 %collective-permute-start.21 = (bf16[128,2048]{1,0:T(8,128)(2,1)}, bf16[128,2048]{1,0:T(8,128)(2,1)}, u32[]{:S(2)}, u32[]{:S(2)}) collective-permute-start(bf16[128,2048]{1,0:T(8,128)(2,1)} %fusion.4), channel_id=1, source_target_pairs={{0,8},{8,0},{1,9},{9,1},{2,10},{10,2},{3,11},{11,3},{4,12},{12,4},... | collective-permute-start | bytes 1572872 | tf_op jit(solution)/shard_map/ppermute | solution.py:167
Sparse Core Ops, SparseCore 0:
  10.8 156.6 all-gather.2

commit v7 on v6

--- a/solution.py
+++ b/solution.py
@@ -243,12 +243,20 @@
         )
     inputs, decoded, _ = state
 
-    state = backward_stage(g, inputs, weight)
+    state = lax.cond(
+        stage == STAGES - 1,
+        lambda a, s: backward_stage(a, inputs, weight),
+        lambda a, s: s,
+        g, (decoded, g),
+    )
     for t in range(STAGES - 2, -1, -1):
         arrived = lax.ppermute(state[1], "x", [(t + 1, t)])
         if t == STAGES - 2:
-            held, passed, _ = lax.optimization_barrier((decoded, inputs, state[1]))
-            decoded_rows, input_rows = exchange(held), exchange(passed)
+            passed, _ = lax.optimization_barrier((inputs, state[1]))
+            input_rows = exchange(passed)
+        if t == STAGES - 3:
+            held, _ = lax.optimization_barrier((decoded, state[1]))
+            decoded_rows = exchange(held)
         if t == 0:
             decoded_rows = by_sender(decoded_rows).reshape(1, DEPTH * rows, width)
             values = input_rows.reshape(DEPTH * rows, width).astype(jnp.float32)

time: 470 us -> 441 us (0.938)
  waiting for transfers between devices: 335 us -> 321 us
  Pallas kernels: 40.1 us -> 27.5 us
    ppermute x3, waiting for transfers between devices: 80.8 us -> 63.9 us  [local(): arrived = lax.ppermute(state[1], 'x', [(t + 1, t)])]
    pallas_call x2 -> x1, Pallas kernels: 27.5 us -> 14.7 us  [backward_stage(): return tuple(call(g, x, weight))]
  transfers between devices with their start and end apart: 24 -> 24, of which waited for: 15 -> 15; matrix products, arithmetic and copies ran while one was open for 6% -> 7% of each run, Pallas kernels for 0% -> 0%
where the time goes in v7:
time: 441 us; the launch traced here: 440 us
  waiting for transfers between devices  321 us (73%)
  starting transfers between devices  32.6 us (7%)
  Pallas kernels  27.5 us (6%)
  local copies, waits for them, and re-layouts  24.3 us (6%)
  between operations  14.4 us (3%)
  other arithmetic  13.3 us (3%)
  matrix products  6.4 us (1%)
    all_gather x1, waiting for transfers between devices, local(): weight = lax.all_gather(layer_weight[0], PLANE, axis=0, tiled=True)  117 us
    ppermute x16, waiting for transfers between devices, shift(): lax.ppermute(value, axis, [(i, (i + steps) % count) for i in range(count)])  103 us
    ppermute x3, waiting for transfers between devices, local(): arrived = lax.ppermute(state[1], 'x', [(t + 1, t)])  63.9 us
    all_to_all x1, waiting for transfers between devices, local(): base = lax.all_to_all(picked.reshape(DEPTH, rows, width), 'zl', 0, 0)  30.5 us
    ppermute x16, starting transfers between devices, shift(): lax.ppermute(value, axis, [(i, (i + steps) % count) for i in range(count)])  18.7 us
    pallas_call x1, Pallas kernels, backward_stage(): return tuple(call(g, x, weight))  14.7 us
    pallas_call x1, Pallas kernels, forward_stage(): return tuple(call(x, base, weight))  12.8 us
  transfers between devices with their start and end apart: 24, of which 15 were waited for; matrix products, arithmetic and copies ran while one was open for 7% of the time, Pallas kernels for 0%

profile of v7, /device:TPU:96, one launch (start us, length us, event | category | flops | bytes accessed | tf_op | source)
XLA Modules:
  0.0 440.0 jit_solution(1086873378878381740)
XLA Ops:
  8.4 1.3 reduce.4
  10.7 2.8 gather_fusion
  13.5 1.1 bitcast_select_fusion
  14.6 5.1 %all-to-all-start = ((bf16[4,64,2048]{2,1,0:T(8,128)(2,1)}), bf16[4,64,2048]{2,1,0:T(8,128)(2,1)S(1)}, u32[]{:S(2)}, u32[]{:S(2)}) async-start(bf16[4,64,2048]{2,1,0:T(8,128)(2,1)} %bitcast_select_fusion), calls=%async_computation | async-start | bytes 2097152 | tf_op jit(solution)/shard_map/all_to_all | solution.py:234
  19.7 30.5 %all-to-all-done.base_ref = bf16[4,64,2048]{2,1,0:T(8,128)(2,1)S(1)} async-done(((bf16[4,64,2048]{2,1,0:T(8,128)(2,1)}), bf16[4,64,2048]{2,1,0:T(8,128)(2,1)S(1)}, u32[]{:S(2)}, u32[]{:S(2)}) %all-to-all-start) | async-done | bytes 1048608 | tf_op jit(solution)/shard_map/all_to_all | solution.py:234
  50.2 117.2 %all-gather.3.cloned.1.call-done = bf16[1,8192,2048]{2,1,0:T(8,128)(2,1)} async-done(((bf16[1,128,2048]{2,1,0:T(8,128)(2,1)}), bf16[1,8192,2048]{2,1,0:T(8,128)(2,1)}) %all-gather.3.cloned.1.call-update) | async-done | bytes 33554448 | tf_op jit(solution)/shard_map/all_gather | solution.py:231
  167.4 12.8 %shard_map.68 = (bf16[4,64,2048]{2,1,0:T(8,128)(2,1)S(1)}, bf16[4,64,2048]{2,1,0:T(8,128)(2,1)}, bf16[64,2048]{1,0:T(8,128)(2,1)S(1)}) custom-call(bf16[64,2048]{1,0:T(8,128)(2,1)S(1)} %constant_dynamic-slice_fusion.14.x_ref, bf16[4,64,2048]{2,1,0:T(8,128)(2,1)S(1)} %all-to-all-done.base_ref, bf16[2,4,1024,2048]{3,2,1,0:T(8,128)(2,1)} %bitcast.66), custom_call_target="tpu_custom_call" | custom-call | flops 2147483648 | bytes 33554432 | tf_op jit(solution)/shard_map/pallas_call | solution.py:154
  180.3 3.4 collective-permute-start
  183.7 5.9 %collective-permute-done = bf16[64,2048]{1,0:T(8,128)(2,1)S(1)} collective-permute-done((bf16[64,2048]{1,0:T(8,128)(2,1)S(1)}, bf16[64,2048]{1,0:T(8,128)(2,1)S(1)}, u32[]{:S(2)}, u32[]{:S(2)}) %collective-permute-start) | collective-permute-done | bytes 262176 | tf_op jit(solution)/shard_map/ppermute | solution.py:240
  191.0 1.7 constant_dynamic-slice_fusion.13
  192.7 2.3 conditional.10
  192.7 2.3 copy.37
  195.2 3.8 collective-permute-start.6
  199.0 1.4 collective-permute-start.3
  200.4 5.9 %collective-permute-done.8 = bf16[64,2048]{1,0:T(8,128)(2,1)S(1)} collective-permute-done((bf16[64,2048]{1,0:T(8,128)(2,1)S(1)}, bf16[64,2048]{1,0:T(8,128)(2,1)S(1)}, u32[]{:S(2)}, u32[]{:S(2)}) %collective-permute-start.8) | collective-permute-done | bytes 262176 | tf_op jit(solution)/shard_map/ppermute | solution.py:167
  206.2 3.8 collective-permute-done.6
  210.1 9.2 %collective-permute-done.7 = bf16[64,2048]{1,0:T(8,128)(2,1)S(1)} collective-permute-done((bf16[64,2048]{1,0:T(8,128)(2,1)S(1)}, bf16[64,2048]{1,0:T(8,128)(2,1)S(1)}, u32[]{:S(2)}, u32[]{:S(2)}) %collective-permute-start.7) | collective-permute-done | bytes 262176 | tf_op jit(solution)/shard_map/ppermute | solution.py:167
  220.2 1.3 maximum_convert_fusion
  221.7 1.4 collective-permute-start.4
  223.1 2.1 constant_dynamic-slice_fusion.9
  225.7 1.5 collective-permute-start.12
  227.3 2.8 reshape.122
  230.1 2.4 multiply_convert_fusion
  232.5 2.2 constant_dynamic-slice_fusion.11
  234.6 2.0 copy.12
  236.6 2.0 copy.11
  238.6 1.3 collective-permute-start.5
  239.9 7.0 %collective-permute-done.11 = bf16[64,2048]{1,0:T(8,128)(2,1)} collective-permute-done((bf16[64,2048]{1,0:T(8,128)(2,1)}, bf16[64,2048]{1,0:T(8,128)(2,1)}, u32[]{:S(2)}, u32[]{:S(2)}) %collective-permute-start.11) | collective-permute-done | bytes 262176 | tf_op jit(solution)/shard_map/ppermute | solution.py:167
  246.9 1.2 pad_maximum_fusion.2
  248.3 1.1 pad_maximum_fusion.3
  249.4 1.1 pad_maximum_fusion.1
  250.5 63.9 %collective-permute-done.5 = bf16[64,2048]{1,0:T(8,128)(2,1)S(1)} collective-permute-done((bf16[64,2048]{1,0:T(8,128)(2,1)}, bf16[64,2048]{1,0:T(8,128)(2,1)S(1)}, u32[]{:S(2)}, u32[]{:S(2)}) %collective-permute-start.5) | collective-permute-done | bytes 262176 | tf_op jit(solution)/shard_map/ppermute | solution.py:253
  314.3 15.6 %conditional.13 = (bf16[4,64,2048]{2,1,0:T(8,128)(2,1)S(1)}) conditional(s32[]{:T(128)} %convert_element_type.62, bf16[4,64,2048]{2,1,0:T(8,128)(2,1)S(1)} %copy-done.2, (bf16[64,2048]{1,0:T(8,128)(2,1)S(1)}, bf16[4,64,2048]{2,1,0:T(8,128)(2,1)S(1)}, bf16[2,4,1024,2048]{3,2,1,0:T(8,128)(2,1)}) %tuple.121), branch_computations={%region_13.14_spmd, %region_14.15_spmd} | conditional | flops 2147483648 | bytes 34603044 | solution.py:266
  315.1 14.7 %branch_1_fun.13 = (bf16[4,64,2048]{2,1,0:T(8,128)(2,1)S(1)}, bf16[64,2048]{1,0:T(8,128)(2,1)}) custom-call(bf16[64,2048]{1,0:T(8,128)(2,1)} %copy-done.8, bf16[4,64,2048]{2,1,0:T(8,128)(2,1)S(1)} %get-tuple-element.102.x_ref, bf16[2,4,1024,2048]{3,2,1,0:T(8,128)(2,1)} %get-tuple-element.103.w_ref), custom_call_target="tpu_custom_call" | custom-call | flops 2147483648 | bytes 33554432 | tf_op jit(solution)/shard_map/cond/branch_1_fun/pallas_call | solution.py:162
  330.8 2.4 collective-permute-start.14
  333.1 1.9 collective-permute-start.15
  335.1 5.1 %collective-permute-done.13 = bf16[64,2048]{1,0:T(8,128)(2,1)S(1)} collective-permute-done((bf16[64,2048]{1,0:T(8,128)(2,1)S(1)}, bf16[64,2048]{1,0:T(8,128)(2,1)S(1)}, u32[]{:S(2)}, u32[]{:S(2)}) %collective-permute-start.13) | collective-permute-done | bytes 262176 | tf_op jit(solution)/shard_map/ppermute | solution.py:167
  340.1 11.0 %collective-permute-done.14 = bf16[64,2048]{1,0:T(8,128)(2,1)S(1)} collective-permute-done((bf16[64,2048]{1,0:T(8,128)(2,1)S(1)}, bf16[64,2048]{1,0:T(8,128)(2,1)S(1)}, u32[]{:S(2)}, u32[]{:S(2)}) %collective-permute-start.14) | collective-permute-done | bytes 262176 | tf_op jit(solution)/shard_map/ppermute | solution.py:167
  351.5 2.5 collective-permute-done.16
  355.0 2.0 convolution_convert_fusion
  359.0 2.3 collective-permute-start.19
  362.0 10.3 %collective-permute-done.17 = bf16[256,1024]{1,0:T(8,128)(2,1)S(1)} collective-permute-done((bf16[256,1024]{1,0:T(8,128)(2,1)S(1)}, bf16[256,1024]{1,0:T(8,128)(2,1)S(1)}, u32[]{:S(2)}, u32[]{:S(2)}) %collective-permute-start.17) | collective-permute-done | bytes 524320 | tf_op jit(solution)/shard_map/ppermute | solution.py:167
  373.3 3.2 collective-permute-start.20
  376.4 21.8 %collective-permute-done.18 = bf16[256,2048]{1,0:T(8,128)(2,1)} collective-permute-done((bf16[256,2048]{1,0:T(8,128)(2,1)S(1)}, bf16[256,2048]{1,0:T(8,128)(2,1)}, u32[]{:S(2)}, u32[]{:S(2)}) %collective-permute-start.18) | collective-permute-done | bytes 1048608 | tf_op jit(solution)/shard_map/ppermute | solution.py:167
  399.3 3.0 fusion
  403.2 1.8 collective-permute-start.21
  405.0 26.0 %collective-permute-done.21 = bf16[128,2048]{1,0:T(8,128)(2,1)} collective-permute-done((bf16[128,2048]{1,0:T(8,128)(2,1)}, bf16[128,2048]{1,0:T(8,128)(2,1)}, u32[]{:S(2)}, u32[]{:S(2)}) %collective-permute-start.21) | collective-permute-done | bytes 524320 | tf_op jit(solution)/shard_map/ppermute | solution.py:167
  431.1 2.1 fusion.3
  (78 shorter events, 14.0 us)
Async XLA Ops:
  7.2 12.6 %copy-start = (bf16[256,2048]{1,0:T(8,128)(2,1)S(1)}, bf16[256,2048]{1,0:T(8,128)(2,1)}, u32[]{:S(2)}) copy-start(bf16[256,2048]{1,0:T(8,128)(2,1)} %param.19) | copy-start | bytes 3145732
  7.2 160.3 %all-gather.3.cloned.1.call-start = ((), (), s32[]{:S(2)}) async-start(), calls=%async_computation.1 | async-start | bytes 34078720 | tf_op jit(solution)/shard_map/all_gather | solution.py:231
  14.6 35.6 %all-to-all-start = ((bf16[4,64,2048]{2,1,0:T(8,128)(2,1)}), bf16[4,64,2048]{2,1,0:T(8,128)(2,1)S(1)}, u32[]{:S(2)}, u32[]{:S(2)}) async-start(bf16[4,64,2048]{2,1,0:T(8,128)(2,1)} %bitcast_select_fusion), calls=%async_computation | async-start | bytes 2097152 | tf_op jit(solution)/shard_map/all_to_all | solution.py:234
  180.3 9.4 %collective-permute-start = (bf16[64,2048]{1,0:T(8,128)(2,1)S(1)}, bf16[64,2048]{1,0:T(8,128)(2,1)S(1)}, u32[]{:S(2)}, u32[]{:S(2)}) collective-permute-start(bf16[64,2048]{1,0:T(8,128)(2,1)S(1)} %get-tuple-element.124), channel_id=1, source_target_pairs={{0,64},{1,65},{2,66},{3,67},{4,68},{5,69},{6,70},{7,71},{8,72},{9,... | collective-permute-start | bytes 786440 | tf_op jit(solution)/shard_map/ppermute | solution.py:240
  189.6 0.7 collective-permute-start.1
  190.3 2.4 collective-permute-start.2
  195.1 11.1 %collective-permute-start.8 = (bf16[64,2048]{1,0:T(8,128)(2,1)S(1)}, bf16[64,2048]{1,0:T(8,128)(2,1)S(1)}, u32[]{:S(2)}, u32[]{:S(2)}) collective-permute-start(bf16[64,2048]{1,0:T(8,128)(2,1)S(1)} %get-tuple-element.162), channel_id=1, source_target_pairs={{0,48},{16,0},{32,16},{48,32},{1,49},{17,1},{33,17},{49,33},{2,50}... | collective-permute-start | bytes 786440 | tf_op jit(solution)/shard_map/ppermute | solution.py:167
  195.2 14.8 %collective-permute-start.6 = (bf16[64,2048]{1,0:T(8,128)(2,1)S(1)}, bf16[64,2048]{1,0:T(8,128)(2,1)S(1)}, u32[]{:S(2)}, u32[]{:S(2)}) collective-permute-start(bf16[64,2048]{1,0:T(8,128)(2,1)S(1)} %get-tuple-element.164), channel_id=1, source_target_pairs={{0,16},{16,32},{32,48},{48,0},{1,17},{17,33},{33,49},{49,1},{2,18}... | collective-permute-start | bytes 786440 | tf_op jit(solution)/shard_map/ppermute | solution.py:167
  199.0 20.2 %collective-permute-start.7 = (bf16[64,2048]{1,0:T(8,128)(2,1)S(1)}, bf16[64,2048]{1,0:T(8,128)(2,1)S(1)}, u32[]{:S(2)}, u32[]{:S(2)}) collective-permute-start(bf16[64,2048]{1,0:T(8,128)(2,1)S(1)} %get-tuple-element.163), channel_id=1, source_target_pairs={{0,32},{16,48},{32,0},{48,16},{1,33},{17,49},{33,1},{49,17},{2,34}... | collective-permute-start | bytes 786440 | tf_op jit(solution)/shard_map/ppermute | solution.py:167
  199.0 22.5 %collective-permute-start.3 = (bf16[64,2048]{1,0:T(8,128)(2,1)}, bf16[64,2048]{1,0:T(8,128)(2,1)}, u32[]{:S(2)}, u32[]{:S(2)}) collective-permute-start(bf16[64,2048]{1,0:T(8,128)(2,1)} %get-tuple-element.131), channel_id=1, source_target_pairs={{192,128},{193,129},{194,130},{195,131},{196,132},{197,133},{198,1... | collective-permute-start | bytes 786440 | tf_op jit(solution)/shard_map/ppermute | solution.py:253
  206.2 13.0 %copy-start.5 = (bf16[64,2048]{1,0:T(8,128)(2,1)}, bf16[64,2048]{1,0:T(8,128)(2,1)S(1)}, u32[]{:S(2)}) copy-start(bf16[64,2048]{1,0:T(8,128)(2,1)S(1)} %collective-permute-done.8) | copy-start | bytes 786436
  210.0 9.2 %copy-start.6 = (bf16[64,2048]{1,0:T(8,128)(2,1)}, bf16[64,2048]{1,0:T(8,128)(2,1)S(1)}, u32[]{:S(2)}) copy-start(bf16[64,2048]{1,0:T(8,128)(2,1)S(1)} %collective-permute-done.6) | copy-start | bytes 786436
  219.2 0.7 copy-start.7
  221.7 16.9 %collective-permute-start.4 = (bf16[64,2048]{1,0:T(8,128)(2,1)}, bf16[64,2048]{1,0:T(8,128)(2,1)}, u32[]{:S(2)}, u32[]{:S(2)}) collective-permute-start(bf16[64,2048]{1,0:T(8,128)(2,1)} %get-tuple-element.132), channel_id=1, source_target_pairs={{128,64},{129,65},{130,66},{131,67},{132,68},{133,69},{134,70},{13... | collective-permute-start | bytes 786440 | tf_op jit(solution)/shard_map/ppermute | solution.py:253
  225.2 14.7 %collective-permute-start.10 = (bf16[64,2048]{1,0:T(8,128)(2,1)}, bf16[64,2048]{1,0:T(8,128)(2,1)}, u32[]{:S(2)}, u32[]{:S(2)}) collective-permute-start(bf16[64,2048]{1,0:T(8,128)(2,1)} %get-tuple-element.158), channel_id=1, source_target_pairs={{0,16},{16,32},{32,48},{48,0},{1,17},{17,33},{33,49},{49,1},{2,18}... | collective-permute-start | bytes 786440 | tf_op jit(solution)/shard_map/ppermute | solution.py:167
  225.7 21.2 %collective-permute-start.11 = (bf16[64,2048]{1,0:T(8,128)(2,1)}, bf16[64,2048]{1,0:T(8,128)(2,1)}, u32[]{:S(2)}, u32[]{:S(2)}) collective-permute-start(bf16[64,2048]{1,0:T(8,128)(2,1)} %get-tuple-element.157), channel_id=1, source_target_pairs={{0,32},{16,48},{32,0},{48,16},{1,33},{17,49},{33,1},{49,17},{2,34}... | collective-permute-start | bytes 786440 | tf_op jit(solution)/shard_map/ppermute | solution.py:167
  225.7 21.2 %collective-permute-start.12 = (bf16[64,2048]{1,0:T(8,128)(2,1)}, bf16[64,2048]{1,0:T(8,128)(2,1)}, u32[]{:S(2)}, u32[]{:S(2)}) collective-permute-start(bf16[64,2048]{1,0:T(8,128)(2,1)} %get-tuple-element.156), channel_id=1, source_target_pairs={{0,48},{16,0},{32,16},{48,32},{1,49},{17,1},{33,17},{49,33},{2,50}... | collective-permute-start | bytes 786440 | tf_op jit(solution)/shard_map/ppermute | solution.py:167
  236.6 12.7 %collective-permute-start.9 = (bf16[256,1024]{0,1:T(8,128)(2,1)}, bf16[256,1024]{0,1:T(8,128)(2,1)}, u32[]{:S(2)}, u32[]{:S(2)}) collective-permute-start(bf16[256,1024]{0,1:T(8,128)(2,1)} %bitcast.91), channel_id=1, source_target_pairs={{0,1},{1,0},{2,3},{3,2},{4,5},{5,4},{6,7},{7,6},{8,9},{9,8},{10,11... | collective-permute-start | bytes 1572872 | tf_op jit(solution)/shard_map/ppermute | solution.py:167
  238.6 75.7 %collective-permute-start.5 = (bf16[64,2048]{1,0:T(8,128)(2,1)}, bf16[64,2048]{1,0:T(8,128)(2,1)S(1)}, u32[]{:S(2)}, u32[]{:S(2)}) collective-permute-start(bf16[64,2048]{1,0:T(8,128)(2,1)} %get-tuple-element.134), channel_id=1, source_target_pairs={{64,0},{65,1},{66,2},{67,3},{68,4},{69,5},{70,6},{71,7},{72,8},{73... | collective-permute-start | bytes 786440 | tf_op jit(solution)/shard_map/ppermute | solution.py:253
  248.1 1.2 copy-start.3
  248.2 66.1 %copy-start.2 = (bf16[4,64,2048]{2,1,0:T(8,128)(2,1)S(1)}, bf16[4,64,2048]{2,1,0:T(8,128)(2,1)}, u32[]{:S(2)}) copy-start(bf16[4,64,2048]{2,1,0:T(8,128)(2,1)} %get-tuple-element.139) | copy-start | bytes 3145732
  314.3 0.7 copy-start.8
  330.0 10.1 %collective-permute-start.13 = (bf16[64,2048]{1,0:T(8,128)(2,1)S(1)}, bf16[64,2048]{1,0:T(8,128)(2,1)S(1)}, u32[]{:S(2)}, u32[]{:S(2)}) collective-permute-start(bf16[64,2048]{1,0:T(8,128)(2,1)S(1)} %get-tuple-element.150), channel_id=1, source_target_pairs={{0,16},{16,32},{32,48},{48,0},{1,17},{17,33},{33,49},{49,1},{2,18}... | collective-permute-start | bytes 786440 | tf_op jit(solution)/shard_map/ppermute | solution.py:167
  330.8 20.3 %collective-permute-start.14 = (bf16[64,2048]{1,0:T(8,128)(2,1)S(1)}, bf16[64,2048]{1,0:T(8,128)(2,1)S(1)}, u32[]{:S(2)}, u32[]{:S(2)}) collective-permute-start(bf16[64,2048]{1,0:T(8,128)(2,1)S(1)} %get-tuple-element.149), channel_id=1, source_target_pairs={{0,32},{16,48},{32,0},{48,16},{1,33},{17,49},{33,1},{49,17},{2,34}... | collective-permute-start | bytes 786440 | tf_op jit(solution)/shard_map/ppermute | solution.py:167
  333.1 18.0 %collective-permute-start.15 = (bf16[64,2048]{1,0:T(8,128)(2,1)S(1)}, bf16[64,2048]{1,0:T(8,128)(2,1)S(1)}, u32[]{:S(2)}, u32[]{:S(2)}) collective-permute-start(bf16[64,2048]{1,0:T(8,128)(2,1)S(1)} %get-tuple-element.148), channel_id=1, source_target_pairs={{0,48},{16,0},{32,16},{48,32},{1,49},{17,1},{33,17},{49,33},{2,50}... | collective-permute-start | bytes 786440 | tf_op jit(solution)/shard_map/ppermute | solution.py:167
  351.2 10.0 %copy-start.4 = (bf16[4,64,2048]{2,1,0:T(8,128)(2,1)}, bf16[4,64,2048]{2,1,0:T(8,128)(2,1)S(1)}, u32[]{:S(2)}) copy-start(bf16[4,64,2048]{2,1,0:T(8,128)(2,1)S(1)} %pad_maximum_fusion.4) | copy-start | bytes 3145732
  351.2 2.7 collective-permute-start.16
  354.0 1.0 copy-start.9
  356.9 1.2 copy-start.10
  357.0 15.3 %collective-permute-start.17 = (bf16[256,1024]{1,0:T(8,128)(2,1)S(1)}, bf16[256,1024]{1,0:T(8,128)(2,1)S(1)}, u32[]{:S(2)}, u32[]{:S(2)}) collective-permute-start(bf16[256,1024]{1,0:T(8,128)(2,1)S(1)} %get-tuple-element.141), channel_id=1, source_target_pairs={{0,2},{2,4},{4,6},{6,0},{1,3},{3,5},{5,7},{7,1},{8,10},{10,12},{12... | collective-permute-start | bytes 1572872 | tf_op jit(solution)/shard_map/ppermute | solution.py:167
  359.0 14.0 %collective-permute-start.19 = (bf16[256,1024]{1,0:T(8,128)(2,1)S(1)}, bf16[256,1024]{1,0:T(8,128)(2,1)S(1)}, u32[]{:S(2)}, u32[]{:S(2)}) collective-permute-start(bf16[256,1024]{1,0:T(8,128)(2,1)S(1)} %get-tuple-element.142), channel_id=1, source_target_pairs={{0,6},{2,0},{4,2},{6,4},{1,7},{3,1},{5,3},{7,5},{8,14},{10,8},{12,... | collective-permute-start | bytes 1572872 | tf_op jit(solution)/shard_map/ppermute | solution.py:167
  372.5 25.8 %collective-permute-start.18 = (bf16[256,2048]{1,0:T(8,128)(2,1)S(1)}, bf16[256,2048]{1,0:T(8,128)(2,1)}, u32[]{:S(2)}, u32[]{:S(2)}) collective-permute-start(bf16[256,2048]{1,0:T(8,128)(2,1)S(1)} %pad_maximum_fusion.5), channel_id=1, source_target_pairs={{0,2},{2,4},{4,6},{6,0},{1,3},{3,5},{5,7},{7,1},{8,10},{10,12},{12... | collective-permute-start | bytes 3145736 | tf_op jit(solution)/shard_map/ppermute | solution.py:167
  373.3 25.0 %collective-permute-start.20 = (bf16[256,2048]{1,0:T(8,128)(2,1)S(1)}, bf16[256,2048]{1,0:T(8,128)(2,1)S(1)}, u32[]{:S(2)}, u32[]{:S(2)}) collective-permute-start(bf16[256,2048]{1,0:T(8,128)(2,1)S(1)} %pad_maximum_fusion.6), channel_id=1, source_target_pairs={{0,6},{2,0},{4,2},{6,4},{1,7},{3,1},{5,3},{7,5},{8,14},{10,8},{12,... | collective-permute-start | bytes 3145736 | tf_op jit(solution)/shard_map/ppermute | solution.py:167
  398.3 1.0 copy-start.11
  399.3 33.8 %copy-start.1 = (bf16[256,2048]{1,0:T(8,128)(2,1)S(1)}, bf16[256,2048]{1,0:T(8,128)(2,1)}, u32[]{:S(2)}) copy-start(bf16[256,2048]{1,0:T(8,128)(2,1)} %param.19) | copy-start | bytes 3145732
  403.2 27.8 %collective-permute-start.21 = (bf16[128,2048]{1,0:T(8,128)(2,1)}, bf16[128,2048]{1,0:T(8,128)(2,1)}, u32[]{:S(2)}, u32[]{:S(2)}) collective-permute-start(bf16[128,2048]{1,0:T(8,128)(2,1)} %fusion.4), channel_id=1, source_target_pairs={{0,8},{8,0},{1,9},{9,1},{2,10},{10,2},{3,11},{11,3},{4,12},{12,4},... | collective-permute-start | bytes 1572872 | tf_op jit(solution)/shard_map/ppermute | solution.py:167
Sparse Core Ops, SparseCore 0:
  10.8 156.6 all-gather.2

commit v8 on v7

--- a/solution.py
+++ b/solution.py
@@ -41,12 +41,12 @@
             start(number + slots)
 
     for number in range(slots):
-        start(jnp.int32(number))
+        start(jnp.int32(tiles + number))
     return wait, refill
 
 
 def forward_kernel(
-    x_ref, base_ref, w_ref, in_ref, out_ref, last_ref, x_now, normed, y, held, arrived
+    x_ref, base_ref, first_ref, w_ref, in_ref, out_ref, last_ref, x_now, normed, y, held, arrived
 ):
     depth, rows, width = base_ref.shape
     tiles, slots = width // TILE, held.shape[0]
@@ -54,18 +54,21 @@
     x_now[...] = x_ref[...].astype(jnp.float32)
     in_ref[0] = x_ref[...]
 
-    def run_layer(layer, carry):
+    def run_layer(layer, carry, first=False):
         values = x_now[...]
         scale = lax.rsqrt(jnp.mean(values * values, axis=-1, keepdims=True) + epsilon)
         normed[...] = (values * scale).astype(jnp.bfloat16)
         for tile in range(tiles):
             number = layer * tiles + tile
-            wait(number)
             columns = pl.ds(tile * TILE, TILE)
+            if not first:
+                wait(number)
+            weight = first_ref[:, columns] if first else held[lax.rem(number, slots)]
             y[:, columns] = x_now[:, columns] + jnp.dot(
-                normed[...], held[lax.rem(number, slots)], preferred_element_type=jnp.float32
+                normed[...], weight, preferred_element_type=jnp.float32
             )
-            refill(number)
+            if not first:
+                refill(number)
         values = y[...]
         base = base_ref[layer].astype(jnp.float32)
         bound = 2.0 * jnp.sqrt(jnp.mean(values * values, axis=-1, keepdims=True) + epsilon)
@@ -84,30 +87,37 @@
 
         return carry
 
-    lax.fori_loop(0, depth, run_layer, 0)
-
-
-def backward_kernel(g_ref, x_ref, w_ref, seen_ref, out_ref, g_now, back, held, arrived):
+    run_layer(jnp.int32(0), 0, first=True)
+    lax.fori_loop(1, depth, run_layer, 0)
+
+
+def backward_kernel(
+    g_ref, x_ref, first_ref, w_ref, seen_ref, out_ref, g_now, back, held, arrived
+):
     depth, rows, width = x_ref.shape
     tiles, slots = width // TILE, held.shape[0]
     wait, refill = tile_copies(w_ref, held, arrived, lambda i: depth - 1 - i)
     g_now[...] = g_ref[...]
 
-    def run_layer(step, carry):
+    def run_layer(step, carry, first=False):
         layer = depth - 1 - step
         seen_ref[layer] = g_now[...]
         for tile in range(tiles):
             number = step * tiles + tile
-            wait(number)
+            columns = pl.ds(tile * TILE, TILE)
+            if not first:
+                wait(number)
+            weight = first_ref[:, columns] if first else held[lax.rem(number, slots)]
             product = lax.dot_general(
-                g_now[:, pl.ds(tile * TILE, TILE)], held[lax.rem(number, slots)],
-                (((1,), (1,)), ((), ())), preferred_element_type=jnp.float32,
+                g_now[:, columns], weight, (((1,), (1,)), ((), ())),
+                preferred_element_type=jnp.float32,
             )
             if tile == 0:
                 back[...] = product
             else:
                 back[...] += product
-            refill(number)
+            if not first:
+                refill(number)
         values = x_ref[layer].astype(jnp.float32)
         scale = lax.rsqrt(jnp.mean(values * values, axis=-1, keepdims=True) + epsilon)
         normed = values * scale
@@ -117,7 +127,8 @@
         g_now[...] = sent.astype(jnp.bfloat16)
         return carry
 
-    lax.fori_loop(0, depth, run_layer, 0)
+    run_layer(jnp.int32(0), 0, first=True)
+    lax.fori_loop(1, depth, run_layer, 0)
     out_ref[...] = g_now[...]
 
 
@@ -125,7 +136,7 @@
     vmem = pl.BlockSpec(memory_space=pltpu.VMEM)
     return pl.pallas_call(
         kernel,
-        in_specs=[vmem, vmem, pl.BlockSpec(memory_space=pl.ANY)],
+        in_specs=[vmem, vmem, vmem, pl.BlockSpec(memory_space=pl.ANY)],
         out_specs=[vmem] * len(outs),
         out_shape=[jax.ShapeDtypeStruct(shape, jnp.bfloat16) for shape in outs],
         scratch_shapes=[
@@ -142,7 +153,7 @@
     )
 
 
-def forward_stage(x, base, weight):
+def forward_stage(x, base, first, weight):
     depth, rows, width = base.shape
     scratch = [
         pltpu.VMEM((rows, width), jnp.float32),
@@ -151,15 +162,15 @@
     ]
     outs = [(depth, rows, width), (depth, rows, width), (rows, width)]
     call = stage_call(forward_kernel, scratch, outs, depth, rows, width)
-    return tuple(call(x, base, weight))
-
-
-def backward_stage(g, x, weight):
+    return tuple(call(x, base, first, weight))
+
+
+def backward_stage(g, x, first, weight):
     depth, rows, width = x.shape
     scratch = [pltpu.VMEM((rows, width), jnp.bfloat16), pltpu.VMEM((rows, width), jnp.float32)]
     outs = [(depth, rows, width), (rows, width)]
     call = stage_call(backward_kernel, scratch, outs, depth, rows, width)
-    return tuple(call(g, x, weight))
+    return tuple(call(g, x, first, weight))
 
 
 def shift(value, axis, steps):
@@ -235,17 +246,20 @@
     x = lax.dynamic_slice_in_dim(stream_in, lane * rows, rows, 0)
     g = lax.dynamic_slice_in_dim(top_cotangent, lane * rows, rows, 0)
 
-    state = forward_stage(x, base, weight)
+    first = weight[:, 0].reshape(width, width)
+    state = forward_stage(x, base, first, weight)
+    index, _ = lax.optimization_barrier((jnp.int32(DEPTH - 1), state[2]))
+    final = lax.dynamic_index_in_dim(weight, index, 1, keepdims=False).reshape(width, width)
     for t in range(1, STAGES):
         arrived = lax.ppermute(state[2], "x", [(t - 1, t)])
         state = lax.cond(
-            stage == t, lambda a, s: forward_stage(a, base, weight), lambda a, s: s, arrived, state
+            stage == t, lambda a, s: forward_stage(a, base, first, weight), lambda a, s: s, arrived, state
         )
     inputs, decoded, _ = state
 
     state = lax.cond(
         stage == STAGES - 1,
-        lambda a, s: backward_stage(a, inputs, weight),
+        lambda a, s: backward_stage(a, inputs, final, weight),
         lambda a, s: s,
         g, (decoded, g),
     )
@@ -264,7 +278,7 @@
             left = pair_rows((values * scale).astype(jnp.bfloat16))
             arrived, left, decoded_rows = lax.optimization_barrier((arrived, left, decoded_rows))
         state = lax.cond(
-            stage == t, lambda a, s: backward_stage(a, inputs, weight), lambda a, s: s, arrived, state
+            stage == t, lambda a, s: backward_stage(a, inputs, final, weight), lambda a, s: s, arrived, state
         )
     cotangents = exchange(state[0]).reshape(DEPTH * rows, width)
     return decoded_rows, gradient_sum(left, cotangents)[None]

time: 441 us -> 467 us (1.059)
  the two profiles are of different devices: /device:TPU:96 before, /device:TPU:57 now
where the time goes in v8:
time: 467 us; the launch traced here: 458 us
  waiting for transfers between devices  318 us (68%)
  local copies, waits for them, and re-layouts  40.2 us (9%)
  starting transfers between devices  36 us (8%)
  Pallas kernels  29.4 us (6%)
  between operations  14.6 us (3%)
  other arithmetic  13.3 us (3%)
  matrix products  6.4 us (1%)
    all_gather x1, waiting for transfers between devices, local(): weight = lax.all_gather(layer_weight[0], PLANE, axis=0, tiled=True)  145 us
    ppermute x16, waiting for transfers between devices, shift(): lax.ppermute(value, axis, [(i, (i + steps) % count) for i in range(count)])  111 us
    ppermute x3, waiting for transfers between devices, local(): arrived = lax.ppermute(state[1], 'x', [(t + 1, t)])  55.3 us
    ppermute x16, starting transfers between devices, shift(): lax.ppermute(value, axis, [(i, (i + steps) % count) for i in range(count)])  22 us
    pallas_call x1, Pallas kernels, backward_stage(): return tuple(call(g, x, first, weight))  15.6 us
    pallas_call x1, Pallas kernels, forward_stage(): return tuple(call(x, base, first, weight))  13.8 us
  transfers between devices with their start and end apart: 24, of which 15 were waited for; matrix products, arithmetic and copies ran while one was open for 10% of the time, Pallas kernels for 0%

profile of v8, /device:TPU:57, one launch (start us, length us, event | category | flops | bytes accessed | tf_op | source)
XLA Modules:
  0.0 458.1 jit_solution(15439590585185126111)
XLA Ops:
  8.4 1.3 reduce.4
  10.7 2.8 gather_fusion
  14.6 5.4 %all-to-all-start = ((bf16[4,64,2048]{2,1,0:T(8,128)(2,1)}), bf16[4,64,2048]{2,1,0:T(8,128)(2,1)S(1)}, u32[]{:S(2)}, u32[]{:S(2)}) async-start(bf16[4,64,2048]{2,1,0:T(8,128)(2,1)} %bitcast_select_fusion), calls=%async_computation | async-start | bytes 2097152 | tf_op jit(solution)/shard_map/all_to_all | solution.py:245
  20.1 145.1 %all-gather.3.cloned.1.call-done = bf16[1,8192,2048]{2,1,0:T(8,128)(2,1)} async-done(((bf16[1,128,2048]{2,1,0:T(8,128)(2,1)}), bf16[1,8192,2048]{2,1,0:T(8,128)(2,1)}) %all-gather.3.cloned.1.call-update) | async-done | bytes 33554448 | tf_op jit(solution)/shard_map/all_gather | solution.py:242
  165.2 8.4 %slice.32 = bf16[2,1,1024,2048]{3,2,1,0:T(8,128)(2,1)} slice(bf16[2,4,1024,2048]{3,2,1,0:T(8,128)(2,1)} %bitcast.68), slice={[0:2], [0:1], [0:1024], [0:2048]} | slice | bytes 16777216 | tf_op jit(solution)/shard_map/slice | solution.py:249
  173.6 13.8 %shard_map.68 = (bf16[4,64,2048]{2,1,0:T(8,128)(2,1)S(1)}, bf16[4,64,2048]{2,1,0:T(8,128)(2,1)}, bf16[64,2048]{1,0:T(8,128)(2,1)S(1)}) custom-call(bf16[64,2048]{1,0:T(8,128)(2,1)S(1)} %constant_dynamic-slice_fusion.15.x_ref, bf16[4,64,2048]{2,1,0:T(8,128)(2,1)S(1)} %all-to-all-done.base_ref, bf16[2048,2048]{1,0:T(8,128)(2,1)} %bitcast.82, ...), custom_call_target="tpu_custom_call" | custom-call | flops 2147483648 | bytes 33554432 | tf_op jit(solution)/shard_map/pallas_call | solution.py:165
  187.3 3.1 collective-permute-start
  190.4 5.4 %collective-permute-done = bf16[64,2048]{1,0:T(8,128)(2,1)S(1)} collective-permute-done((bf16[64,2048]{1,0:T(8,128)(2,1)S(1)}, bf16[64,2048]{1,0:T(8,128)(2,1)S(1)}, u32[]{:S(2)}, u32[]{:S(2)}) %collective-permute-start) | collective-permute-done | bytes 262176 | tf_op jit(solution)/shard_map/ppermute | solution.py:254
  196.6 1.7 constant_dynamic-slice_fusion.14
  199.0 8.3 %constant_dynamic-slice_fusion.13 = bf16[2,1,1024,2048]{3,2,1,0:T(8,128)(2,1)} fusion(bf16[2,4,1024,2048]{3,2,1,0:T(8,128)(2,1)} %bitcast.72, s32[]{:T(128)S(6)} %select_n.88), kind=kLoop, calls=%fused_computation.47 | loop fusion | bytes 16777220 | tf_op jit(solution)/shard_map/jit(dynamic_index_in_dim)/dynamic_slice | solution.py:252
  207.5 2.3 conditional.10
  207.5 2.3 copy.37
  209.9 3.6 collective-permute-start.7
  213.4 1.5 collective-permute-start.6
  214.9 1.3 collective-permute-start.3
  216.2 13.2 %collective-permute-done.7 = bf16[64,2048]{1,0:T(8,128)(2,1)S(1)} collective-permute-done((bf16[64,2048]{1,0:T(8,128)(2,1)S(1)}, bf16[64,2048]{1,0:T(8,128)(2,1)S(1)}, u32[]{:S(2)}, u32[]{:S(2)}) %collective-permute-start.7) | collective-permute-done | bytes 262176 | tf_op jit(solution)/shard_map/ppermute | solution.py:178
  229.4 7.3 %collective-permute-done.8 = bf16[64,2048]{1,0:T(8,128)(2,1)S(1)} collective-permute-done((bf16[64,2048]{1,0:T(8,128)(2,1)S(1)}, bf16[64,2048]{1,0:T(8,128)(2,1)S(1)}, u32[]{:S(2)}, u32[]{:S(2)}) %collective-permute-start.8) | collective-permute-done | bytes 262176 | tf_op jit(solution)/shard_map/ppermute | solution.py:178
  237.8 1.3 maximum_convert_fusion
  239.1 1.4 collective-permute-start.4
  240.5 2.1 constant_dynamic-slice_fusion.9
  243.4 1.3 collective-permute-start.12
  244.8 2.8 reshape.127
  247.6 2.4 multiply_convert_fusion
  250.0 2.2 constant_dynamic-slice_fusion.11
  252.1 2.0 copy.12
  255.2 2.0 copy.11
  257.2 1.3 collective-permute-start.5
  258.5 7.3 %collective-permute-done.11 = bf16[64,2048]{1,0:T(8,128)(2,1)} collective-permute-done((bf16[64,2048]{1,0:T(8,128)(2,1)}, bf16[64,2048]{1,0:T(8,128)(2,1)}, u32[]{:S(2)}, u32[]{:S(2)}) %collective-permute-start.11) | collective-permute-done | bytes 262176 | tf_op jit(solution)/shard_map/ppermute | solution.py:178
  269.4 55.2 %collective-permute-done.5 = bf16[64,2048]{1,0:T(8,128)(2,1)S(1)} collective-permute-done((bf16[64,2048]{1,0:T(8,128)(2,1)}, bf16[64,2048]{1,0:T(8,128)(2,1)S(1)}, u32[]{:S(2)}, u32[]{:S(2)}) %collective-permute-start.5) | collective-permute-done | bytes 262176 | tf_op jit(solution)/shard_map/ppermute | solution.py:267
  324.6 16.5 %conditional.13 = (bf16[4,64,2048]{2,1,0:T(8,128)(2,1)S(1)}) conditional(s32[]{:T(128)} %convert_element_type.62, bf16[4,64,2048]{2,1,0:T(8,128)(2,1)S(1)} %copy-done.2, (bf16[64,2048]{1,0:T(8,128)(2,1)S(1)}, bf16[4,64,2048]{2,1,0:T(8,128)(2,1)S(1)}, bf16[2048,2048]{1,0:T(8,128)(2,1)}, bf16[2,4,1024,2048]{3,2,1,0:T(8,128)(2,1)}) %tuple.127), branch_computations={%region_13.14_spmd, %region_14.15_spmd} | conditional | flops 2147483648 | bytes 34603044 | solution.py:280
  325.5 15.6 %branch_1_fun.13 = (bf16[4,64,2048]{2,1,0:T(8,128)(2,1)S(1)}, bf16[64,2048]{1,0:T(8,128)(2,1)}) custom-call(bf16[64,2048]{1,0:T(8,128)(2,1)} %copy-done.8, bf16[4,64,2048]{2,1,0:T(8,128)(2,1)S(1)} %get-tuple-element.122.x_ref, bf16[2048,2048]{1,0:T(8,128)(2,1)} %get-tuple-element.123.first_ref, bf16[2,4,1024,2048]{3,2,1,0:T(8,128)(2,1)} %get-tuple-element.124.w_ref), custom_call_target="tpu_custom_call" | custom-call | flops 2147483648 | bytes 33554432 | tf_op jit(solution)/shard_map/cond/branch_1_fun/pallas_call | solution.py:173
  341.3 2.1 collective-permute-start.14
  343.3 1.3 collective-permute-start.15
  344.6 1.9 collective-permute-done.13
  346.5 8.0 %collective-permute-done.14 = bf16[64,2048]{1,0:T(8,128)(2,1)S(1)} collective-permute-done((bf16[64,2048]{1,0:T(8,128)(2,1)S(1)}, bf16[64,2048]{1,0:T(8,128)(2,1)S(1)}, u32[]{:S(2)}, u32[]{:S(2)}) %collective-permute-start.14) | collective-permute-done | bytes 262176 | tf_op jit(solution)/shard_map/ppermute | solution.py:178
  354.4 11.7 %collective-permute-done.15 = bf16[64,2048]{1,0:T(8,128)(2,1)S(1)} collective-permute-done((bf16[64,2048]{1,0:T(8,128)(2,1)S(1)}, bf16[64,2048]{1,0:T(8,128)(2,1)S(1)}, u32[]{:S(2)}, u32[]{:S(2)}) %collective-permute-start.15) | collective-permute-done | bytes 262176 | tf_op jit(solution)/shard_map/ppermute | solution.py:178
  366.2 1.5 collective-permute-start.16
  367.8 2.2 collective-permute-done.16
  371.0 2.0 convolution_convert_fusion
  373.0 2.2 collective-permute-start.17
  376.9 9.3 %collective-permute-done.17 = bf16[256,1024]{1,0:T(8,128)(2,1)S(1)} collective-permute-done((bf16[256,1024]{1,0:T(8,128)(2,1)S(1)}, bf16[256,1024]{1,0:T(8,128)(2,1)S(1)}, u32[]{:S(2)}, u32[]{:S(2)}) %collective-permute-start.17) | collective-permute-done | bytes 524320 | tf_op jit(solution)/shard_map/ppermute | solution.py:178
  386.5 3.4 collective-permute-start.18
  390.5 20.7 %collective-permute-done.18 = bf16[256,2048]{1,0:T(8,128)(2,1)} collective-permute-done((bf16[256,2048]{1,0:T(8,128)(2,1)S(1)}, bf16[256,2048]{1,0:T(8,128)(2,1)}, u32[]{:S(2)}, u32[]{:S(2)}) %collective-permute-start.18) | collective-permute-done | bytes 1048608 | tf_op jit(solution)/shard_map/ppermute | solution.py:178
  411.2 3.6 collective-permute-done.20
  415.8 3.0 fusion
  419.7 3.1 collective-permute-start.21
  422.9 26.1 %collective-permute-done.21 = bf16[128,2048]{1,0:T(8,128)(2,1)} collective-permute-done((bf16[128,2048]{1,0:T(8,128)(2,1)}, bf16[128,2048]{1,0:T(8,128)(2,1)}, u32[]{:S(2)}, u32[]{:S(2)}) %collective-permute-start.21) | collective-permute-done | bytes 524320 | tf_op jit(solution)/shard_map/ppermute | solution.py:178
  449.0 2.1 fusion.3
  (81 shorter events, 18.0 us)
Async XLA Ops:
  7.2 12.9 %copy-start = (bf16[256,2048]{1,0:T(8,128)(2,1)S(1)}, bf16[256,2048]{1,0:T(8,128)(2,1)}, u32[]{:S(2)}) copy-start(bf16[256,2048]{1,0:T(8,128)(2,1)} %param.19) | copy-start | bytes 3145732
  7.2 158.0 %all-gather.3.cloned.1.call-start = ((), (), s32[]{:S(2)}) async-start(), calls=%async_computation.1 | async-start | bytes 34078720 | tf_op jit(solution)/shard_map/all_gather | solution.py:242
  14.6 158.9 %all-to-all-start = ((bf16[4,64,2048]{2,1,0:T(8,128)(2,1)}), bf16[4,64,2048]{2,1,0:T(8,128)(2,1)S(1)}, u32[]{:S(2)}, u32[]{:S(2)}) async-start(bf16[4,64,2048]{2,1,0:T(8,128)(2,1)} %bitcast_select_fusion), calls=%async_computation | async-start | bytes 2097152 | tf_op jit(solution)/shard_map/all_to_all | solution.py:245
  187.3 8.5 %collective-permute-start = (bf16[64,2048]{1,0:T(8,128)(2,1)S(1)}, bf16[64,2048]{1,0:T(8,128)(2,1)S(1)}, u32[]{:S(2)}, u32[]{:S(2)}) collective-permute-start(bf16[64,2048]{1,0:T(8,128)(2,1)S(1)} %get-tuple-element.146), channel_id=1, source_target_pairs={{0,64},{1,65},{2,66},{3,67},{4,68},{5,69},{6,70},{7,71},{8,72},{9,... | collective-permute-start | bytes 786440 | tf_op jit(solution)/shard_map/ppermute | solution.py:254
  195.9 2.4 collective-permute-start.1
  198.3 9.0 %collective-permute-start.2 = (bf16[64,2048]{1,0:T(8,128)(2,1)S(1)}, bf16[64,2048]{1,0:T(8,128)(2,1)S(1)}, u32[]{:S(2)}, u32[]{:S(2)}) collective-permute-start(bf16[64,2048]{1,0:T(8,128)(2,1)S(1)} %get-tuple-element.150), channel_id=1, source_target_pairs={{128,192},{129,193},{130,194},{131,195},{132,196},{133,197},{134,1... | collective-permute-start | bytes 786440 | tf_op jit(solution)/shard_map/ppermute | solution.py:254
  209.9 19.6 %collective-permute-start.7 = (bf16[64,2048]{1,0:T(8,128)(2,1)S(1)}, bf16[64,2048]{1,0:T(8,128)(2,1)S(1)}, u32[]{:S(2)}, u32[]{:S(2)}) collective-permute-start(bf16[64,2048]{1,0:T(8,128)(2,1)S(1)} %get-tuple-element.186), channel_id=1, source_target_pairs={{0,32},{16,48},{32,0},{48,16},{1,33},{17,49},{33,1},{49,17},{2,34}... | collective-permute-start | bytes 786440 | tf_op jit(solution)/shard_map/ppermute | solution.py:178
  213.4 23.3 %collective-permute-start.8 = (bf16[64,2048]{1,0:T(8,128)(2,1)S(1)}, bf16[64,2048]{1,0:T(8,128)(2,1)S(1)}, u32[]{:S(2)}, u32[]{:S(2)}) collective-permute-start(bf16[64,2048]{1,0:T(8,128)(2,1)S(1)} %get-tuple-element.185), channel_id=1, source_target_pairs={{0,48},{16,0},{32,16},{48,32},{1,49},{17,1},{33,17},{49,33},{2,50}... | collective-permute-start | bytes 786440 | tf_op jit(solution)/shard_map/ppermute | solution.py:178
  213.4 23.3 %collective-permute-start.6 = (bf16[64,2048]{1,0:T(8,128)(2,1)S(1)}, bf16[64,2048]{1,0:T(8,128)(2,1)S(1)}, u32[]{:S(2)}, u32[]{:S(2)}) collective-permute-start(bf16[64,2048]{1,0:T(8,128)(2,1)S(1)} %get-tuple-element.187), channel_id=1, source_target_pairs={{0,16},{16,32},{32,48},{48,0},{1,17},{17,33},{33,49},{49,1},{2,18}... | collective-permute-start | bytes 786440 | tf_op jit(solution)/shard_map/ppermute | solution.py:178
  214.9 24.2 %collective-permute-start.3 = (bf16[64,2048]{1,0:T(8,128)(2,1)}, bf16[64,2048]{1,0:T(8,128)(2,1)}, u32[]{:S(2)}, u32[]{:S(2)}) collective-permute-start(bf16[64,2048]{1,0:T(8,128)(2,1)} %get-tuple-element.154), channel_id=1, source_target_pairs={{192,128},{193,129},{194,130},{195,131},{196,132},{197,133},{198,1... | collective-permute-start | bytes 786440 | tf_op jit(solution)/shard_map/ppermute | solution.py:267
  229.4 7.3 %copy-start.5 = (bf16[64,2048]{1,0:T(8,128)(2,1)}, bf16[64,2048]{1,0:T(8,128)(2,1)S(1)}, u32[]{:S(2)}) copy-start(bf16[64,2048]{1,0:T(8,128)(2,1)S(1)} %collective-permute-done.7) | copy-start | bytes 786436
  236.7 0.7 copy-start.6
  236.7 0.8 copy-start.7
  239.1 18.0 %collective-permute-start.4 = (bf16[64,2048]{1,0:T(8,128)(2,1)}, bf16[64,2048]{1,0:T(8,128)(2,1)}, u32[]{:S(2)}, u32[]{:S(2)}) collective-permute-start(bf16[64,2048]{1,0:T(8,128)(2,1)} %get-tuple-element.155), channel_id=1, source_target_pairs={{128,64},{129,65},{130,66},{131,67},{132,68},{133,69},{134,70},{13... | collective-permute-start | bytes 786440 | tf_op jit(solution)/shard_map/ppermute | solution.py:267
  242.6 15.9 %collective-permute-start.10 = (bf16[64,2048]{1,0:T(8,128)(2,1)}, bf16[64,2048]{1,0:T(8,128)(2,1)}, u32[]{:S(2)}, u32[]{:S(2)}) collective-permute-start(bf16[64,2048]{1,0:T(8,128)(2,1)} %get-tuple-element.181), channel_id=1, source_target_pairs={{0,16},{16,32},{32,48},{48,0},{1,17},{17,33},{33,49},{49,1},{2,18}... | collective-permute-start | bytes 786440 | tf_op jit(solution)/shard_map/ppermute | solution.py:178
  243.4 22.4 %collective-permute-start.11 = (bf16[64,2048]{1,0:T(8,128)(2,1)}, bf16[64,2048]{1,0:T(8,128)(2,1)}, u32[]{:S(2)}, u32[]{:S(2)}) collective-permute-start(bf16[64,2048]{1,0:T(8,128)(2,1)} %get-tuple-element.180), channel_id=1, source_target_pairs={{0,32},{16,48},{32,0},{48,16},{1,33},{17,49},{33,1},{49,17},{2,34}... | collective-permute-start | bytes 786440 | tf_op jit(solution)/shard_map/ppermute | solution.py:178
  243.4 22.4 %collective-permute-start.12 = (bf16[64,2048]{1,0:T(8,128)(2,1)}, bf16[64,2048]{1,0:T(8,128)(2,1)}, u32[]{:S(2)}, u32[]{:S(2)}) collective-permute-start(bf16[64,2048]{1,0:T(8,128)(2,1)} %get-tuple-element.179), channel_id=1, source_target_pairs={{0,48},{16,0},{32,16},{48,32},{1,49},{17,1},{33,17},{49,33},{2,50}... | collective-permute-start | bytes 786440 | tf_op jit(solution)/shard_map/ppermute | solution.py:178
  254.1 14.1 %collective-permute-start.9 = (bf16[256,1024]{0,1:T(8,128)(2,1)}, bf16[256,1024]{0,1:T(8,128)(2,1)}, u32[]{:S(2)}, u32[]{:S(2)}) collective-permute-start(bf16[256,1024]{0,1:T(8,128)(2,1)} %bitcast.103), channel_id=1, source_target_pairs={{0,1},{1,0},{2,3},{3,2},{4,5},{5,4},{6,7},{7,6},{8,9},{9,8},{10,11... | collective-permute-start | bytes 1572872 | tf_op jit(solution)/shard_map/ppermute | solution.py:178
  257.2 67.4 %collective-permute-start.5 = (bf16[64,2048]{1,0:T(8,128)(2,1)}, bf16[64,2048]{1,0:T(8,128)(2,1)S(1)}, u32[]{:S(2)}, u32[]{:S(2)}) collective-permute-start(bf16[64,2048]{1,0:T(8,128)(2,1)} %get-tuple-element.157), channel_id=1, source_target_pairs={{64,0},{65,1},{66,2},{67,3},{68,4},{69,5},{70,6},{71,7},{72,8},{73... | collective-permute-start | bytes 786440 | tf_op jit(solution)/shard_map/ppermute | solution.py:267
  267.0 1.2 copy-start.3
  267.1 57.5 %copy-start.2 = (bf16[4,64,2048]{2,1,0:T(8,128)(2,1)S(1)}, bf16[4,64,2048]{2,1,0:T(8,128)(2,1)}, u32[]{:S(2)}) copy-start(bf16[4,64,2048]{2,1,0:T(8,128)(2,1)} %get-tuple-element.162) | copy-start | bytes 3145732
  324.8 0.7 copy-start.8
  341.2 5.3 %collective-permute-start.13 = (bf16[64,2048]{1,0:T(8,128)(2,1)S(1)}, bf16[64,2048]{1,0:T(8,128)(2,1)S(1)}, u32[]{:S(2)}, u32[]{:S(2)}) collective-permute-start(bf16[64,2048]{1,0:T(8,128)(2,1)S(1)} %get-tuple-element.173), channel_id=1, source_target_pairs={{0,16},{16,32},{32,48},{48,0},{1,17},{17,33},{33,49},{49,1},{2,18}... | collective-permute-start | bytes 786440 | tf_op jit(solution)/shard_map/ppermute | solution.py:178
  341.3 13.2 %collective-permute-start.14 = (bf16[64,2048]{1,0:T(8,128)(2,1)S(1)}, bf16[64,2048]{1,0:T(8,128)(2,1)S(1)}, u32[]{:S(2)}, u32[]{:S(2)}) collective-permute-start(bf16[64,2048]{1,0:T(8,128)(2,1)S(1)} %get-tuple-element.172), channel_id=1, source_target_pairs={{0,32},{16,48},{32,0},{48,16},{1,33},{17,49},{33,1},{49,17},{2,34}... | collective-permute-start | bytes 786440 | tf_op jit(solution)/shard_map/ppermute | solution.py:178
  343.3 22.8 %collective-permute-start.15 = (bf16[64,2048]{1,0:T(8,128)(2,1)S(1)}, bf16[64,2048]{1,0:T(8,128)(2,1)S(1)}, u32[]{:S(2)}, u32[]{:S(2)}) collective-permute-start(bf16[64,2048]{1,0:T(8,128)(2,1)S(1)} %get-tuple-element.171), channel_id=1, source_target_pairs={{0,48},{16,0},{32,16},{48,32},{1,49},{17,1},{33,17},{49,33},{2,50}... | collective-permute-start | bytes 786440 | tf_op jit(solution)/shard_map/ppermute | solution.py:178
  366.2 9.9 %copy-start.4 = (bf16[4,64,2048]{2,1,0:T(8,128)(2,1)}, bf16[4,64,2048]{2,1,0:T(8,128)(2,1)S(1)}, u32[]{:S(2)}) copy-start(bf16[4,64,2048]{2,1,0:T(8,128)(2,1)S(1)} %pad_maximum_fusion.4) | copy-start | bytes 3145732
  366.2 3.8 collective-permute-start.16
  370.0 1.0 copy-start.9
  373.0 2.3 copy-start.10
  373.0 13.2 %collective-permute-start.17 = (bf16[256,1024]{1,0:T(8,128)(2,1)S(1)}, bf16[256,1024]{1,0:T(8,128)(2,1)S(1)}, u32[]{:S(2)}, u32[]{:S(2)}) collective-permute-start(bf16[256,1024]{1,0:T(8,128)(2,1)S(1)} %get-tuple-element.164), channel_id=1, source_target_pairs={{0,2},{2,4},{4,6},{6,0},{1,3},{3,5},{5,7},{7,1},{8,10},{10,12},{12... | collective-permute-start | bytes 1572872 | tf_op jit(solution)/shard_map/ppermute | solution.py:178
  376.0 14.1 %collective-permute-start.19 = (bf16[256,1024]{1,0:T(8,128)(2,1)S(1)}, bf16[256,1024]{1,0:T(8,128)(2,1)S(1)}, u32[]{:S(2)}, u32[]{:S(2)}) collective-permute-start(bf16[256,1024]{1,0:T(8,128)(2,1)S(1)} %get-tuple-element.165), channel_id=1, source_target_pairs={{0,6},{2,0},{4,2},{6,4},{1,7},{3,1},{5,3},{7,5},{8,14},{10,8},{12,... | collective-permute-start | bytes 1572872 | tf_op jit(solution)/shard_map/ppermute | solution.py:178
  386.5 24.7 %collective-permute-start.18 = (bf16[256,2048]{1,0:T(8,128)(2,1)S(1)}, bf16[256,2048]{1,0:T(8,128)(2,1)}, u32[]{:S(2)}, u32[]{:S(2)}) collective-permute-start(bf16[256,2048]{1,0:T(8,128)(2,1)S(1)} %pad_maximum_fusion.5), channel_id=1, source_target_pairs={{0,2},{2,4},{4,6},{6,0},{1,3},{3,5},{5,7},{7,1},{8,10},{10,12},{12... | collective-permute-start | bytes 3145736 | tf_op jit(solution)/shard_map/ppermute | solution.py:178
  390.4 24.4 %collective-permute-start.20 = (bf16[256,2048]{1,0:T(8,128)(2,1)S(1)}, bf16[256,2048]{1,0:T(8,128)(2,1)S(1)}, u32[]{:S(2)}, u32[]{:S(2)}) collective-permute-start(bf16[256,2048]{1,0:T(8,128)(2,1)S(1)} %pad_maximum_fusion.6), channel_id=1, source_target_pairs={{0,6},{2,0},{4,2},{6,4},{1,7},{3,1},{5,3},{7,5},{8,14},{10,8},{12,... | collective-permute-start | bytes 3145736 | tf_op jit(solution)/shard_map/ppermute | solution.py:178
  414.8 1.0 copy-start.11
  415.8 35.3 %copy-start.1 = (bf16[256,2048]{1,0:T(8,128)(2,1)S(1)}, bf16[256,2048]{1,0:T(8,128)(2,1)}, u32[]{:S(2)}) copy-start(bf16[256,2048]{1,0:T(8,128)(2,1)} %param.19) | copy-start | bytes 3145732
  419.7 29.3 %collective-permute-start.21 = (bf16[128,2048]{1,0:T(8,128)(2,1)}, bf16[128,2048]{1,0:T(8,128)(2,1)}, u32[]{:S(2)}, u32[]{:S(2)}) collective-permute-start(bf16[128,2048]{1,0:T(8,128)(2,1)} %fusion.4), channel_id=1, source_target_pairs={{0,8},{8,0},{1,9},{9,1},{2,10},{10,2},{3,11},{11,3},{4,12},{12,4},... | collective-permute-start | bytes 1572872 | tf_op jit(solution)/shard_map/ppermute | solution.py:178
Sparse Core Ops, SparseCore 0:
  10.8 154.3 all-gather.2

commit v9 on v7

--- a/solution.py
+++ b/solution.py
@@ -199,29 +199,47 @@
     piece = width // (2 * chips)
     right = jnp.concatenate([g, shift(g, "c", 1)], axis=0)
 
+    def product(columns, block):
+        return lax.dot_general(
+            columns, block, (((0,), (0,)), ((), ())), preferred_element_type=jnp.float32
+        )
+
+    def round_y(block):
+        far = block(2).astype(jnp.bfloat16)
+        half = far.shape[1] // 2
+        up1 = shift(far[:, :half], "y", 1)
+        down1 = shift(far[:, half:], "y", -1)
+        up, down, own = block(1), block(-1), block(0)
+        up = jnp.concatenate([up[:, :half] + up1.astype(jnp.float32), up[:, half:]], axis=1)
+        down = jnp.concatenate([down[:, :half], down[:, half:] + down1.astype(jnp.float32)], axis=1)
+        up2 = shift(up.astype(jnp.bfloat16), "y", 1)
+        down2 = shift(down.astype(jnp.bfloat16), "y", -1)
+        return own + up2.astype(jnp.float32) + down2.astype(jnp.float32)
+
+    def pick_y(array, steps, axis):
+        return lax.dynamic_index_in_dim(array, lax.rem(y + steps + 4, 4), axis, keepdims=False)
+
+    split = width * 3 // 4
     left = left.reshape(2 * rows, 2, 4, piece)
 
+    def plane(which):
+        picked = lax.dynamic_index_in_dim(left, which, 1, keepdims=False)
+        return product(picked.reshape(2 * rows, 4 * piece), right[:, split:])
+
+    passed = shift(plane(1 - zh).astype(jnp.bfloat16), "zh", 1)
+
     def block(steps):
-        picked = lax.dynamic_index_in_dim(left, lax.rem(y + steps + 4, 4), 2, keepdims=False)
-        return lax.dot_general(
-            picked.reshape(2 * rows, 2 * piece), right, (((0,), (0,)), ((), ())),
-            preferred_element_type=jnp.float32,
-        )
-
-    half = width // 2
-    far = block(2).astype(jnp.bfloat16)
-    up1 = shift(far[:, :half], "y", 1)
-    down1 = shift(far[:, half:], "y", -1)
-    up, down, own = block(1), block(-1), block(0)
-    up = jnp.concatenate([up[:, :half] + up1.astype(jnp.float32), up[:, half:]], axis=1)
-    down = jnp.concatenate([down[:, :half], down[:, half:] + down1.astype(jnp.float32)], axis=1)
-    up2 = shift(up.astype(jnp.bfloat16), "y", 1)
-    down2 = shift(down.astype(jnp.bfloat16), "y", -1)
-    total = own + up2.astype(jnp.float32) + down2.astype(jnp.float32)
-    total = total.reshape(2, piece, width)
+        picked = pick_y(left, steps, 2).reshape(2 * rows, 2 * piece)
+        return product(picked, right[:, :split])
+
+    total = round_y(block).reshape(2, piece, split)
     kept = lax.dynamic_index_in_dim(total, zh, 0, keepdims=False)
     given = lax.dynamic_index_in_dim(total, 1 - zh, 0, keepdims=False).astype(jnp.bfloat16)
-    return kept + shift(given, "zh", 1).astype(jnp.float32)
+    one = kept + shift(given, "zh", 1).astype(jnp.float32)
+
+    both = (plane(zh) + passed.astype(jnp.float32)).reshape(4, piece, width - split)
+    two = round_y(lambda steps: pick_y(both, steps, 0))
+    return jnp.concatenate([one, two], axis=1)
 
 
 def local(stream_in, sample_ids, epoch_buffer, layer_weight, top_cotangent):

time: 441 us -> 423 us (0.959)
  waiting for transfers between devices: 321 us -> 302 us
  starting transfers between devices: 32.6 us -> 41.6 us
    ppermute x16 -> x21, waiting for transfers between devices: 103 us -> 83.9 us  [shift(): lax.ppermute(value, axis, [(i, (i + steps) % count) for i in range(count)])]
    ppermute x16 -> x21, starting transfers between devices: 18.7 us -> 27.8 us  [shift(): lax.ppermute(value, axis, [(i, (i + steps) % count) for i in range(count)])]
  transfers between devices with their start and end apart: 24 -> 29, of which waited for: 15 -> 17; matrix products, arithmetic and copies ran while one was open for 7% -> 7% of each run, Pallas kernels for 0% -> 0%
where the time goes in v9:
time: 423 us
  waiting for transfers between devices  302 us (71%)
  starting transfers between devices  41.6 us (10%)
  Pallas kernels  27.5 us (7%)
  local copies, waits for them, and re-layouts  20.9 us (5%)
  between operations  14.6 us (3%)
  other arithmetic  12.4 us (3%)
    all_gather x1, waiting for transfers between devices, local(): weight = lax.all_gather(layer_weight[0], PLANE, axis=0, tiled=True)  117 us
    ppermute x21, waiting for transfers between devices, shift(): lax.ppermute(value, axis, [(i, (i + steps) % count) for i in range(count)])  83.9 us
    ppermute x3, waiting for transfers between devices, local(): arrived = lax.ppermute(state[1], 'x', [(t + 1, t)])  63.7 us
    all_to_all x1, waiting for transfers between devices, local(): base = lax.all_to_all(picked.reshape(DEPTH, rows, width), 'zl', 0, 0)  30.5 us
    ppermute x21, starting transfers between devices, shift(): lax.ppermute(value, axis, [(i, (i + steps) % count) for i in range(count)])  27.8 us
    pallas_call x1, Pallas kernels, backward_stage(): return tuple(call(g, x, weight))  14.7 us
    pallas_call x1, Pallas kernels, forward_stage(): return tuple(call(x, base, weight))  12.8 us
  transfers between devices with their start and end apart: 29, of which 17 were waited for; matrix products, arithmetic and copies ran while one was open for 7% of the time, Pallas kernels for 0%

profile of v9, /device:TPU:96, one launch (start us, length us, event | category | flops | bytes accessed | tf_op | source)
XLA Modules:
  0.0 422.6 jit_solution(2654892681579994424)
XLA Ops:
  8.4 1.3 reduce.4
  10.7 2.8 gather_fusion
  14.6 5.1 %all-to-all-start = ((bf16[4,64,2048]{2,1,0:T(8,128)(2,1)}), bf16[4,64,2048]{2,1,0:T(8,128)(2,1)S(1)}, u32[]{:S(2)}, u32[]{:S(2)}) async-start(bf16[4,64,2048]{2,1,0:T(8,128)(2,1)} %bitcast_select_fusion), calls=%async_computation | async-start | bytes 2097152 | tf_op jit(solution)/shard_map/all_to_all | solution.py:252
  19.7 30.5 %all-to-all-done.base_ref = bf16[4,64,2048]{2,1,0:T(8,128)(2,1)S(1)} async-done(((bf16[4,64,2048]{2,1,0:T(8,128)(2,1)}), bf16[4,64,2048]{2,1,0:T(8,128)(2,1)S(1)}, u32[]{:S(2)}, u32[]{:S(2)}) %all-to-all-start) | async-done | bytes 1048608 | tf_op jit(solution)/shard_map/all_to_all | solution.py:252
  50.2 117.2 %all-gather.3.cloned.1.call-done = bf16[1,8192,2048]{2,1,0:T(8,128)(2,1)} async-done(((bf16[1,128,2048]{2,1,0:T(8,128)(2,1)}), bf16[1,8192,2048]{2,1,0:T(8,128)(2,1)}) %all-gather.3.cloned.1.call-update) | async-done | bytes 33554448 | tf_op jit(solution)/shard_map/all_gather | solution.py:249
  167.4 12.8 %shard_map.68 = (bf16[4,64,2048]{2,1,0:T(8,128)(2,1)S(1)}, bf16[4,64,2048]{2,1,0:T(8,128)(2,1)}, bf16[64,2048]{1,0:T(8,128)(2,1)S(1)}) custom-call(bf16[64,2048]{1,0:T(8,128)(2,1)S(1)} %constant_dynamic-slice_fusion.16.x_ref, bf16[4,64,2048]{2,1,0:T(8,128)(2,1)S(1)} %all-to-all-done.base_ref, bf16[2,4,1024,2048]{3,2,1,0:T(8,128)(2,1)} %bitcast.85), custom_call_target="tpu_custom_call" | custom-call | flops 2147483648 | bytes 33554432 | tf_op jit(solution)/shard_map/pallas_call | solution.py:154
  180.3 3.4 collective-permute-start
  183.7 5.9 %collective-permute-done = bf16[64,2048]{1,0:T(8,128)(2,1)S(1)} collective-permute-done((bf16[64,2048]{1,0:T(8,128)(2,1)S(1)}, bf16[64,2048]{1,0:T(8,128)(2,1)S(1)}, u32[]{:S(2)}, u32[]{:S(2)}) %collective-permute-start) | collective-permute-done | bytes 262176 | tf_op jit(solution)/shard_map/ppermute | solution.py:258
  191.0 1.7 constant_dynamic-slice_fusion.15
  192.7 2.4 conditional.10
  192.7 2.4 copy.37
  195.2 3.8 collective-permute-start.6
  199.0 1.4 collective-permute-start.3
  200.4 5.8 %collective-permute-done.8 = bf16[64,2048]{1,0:T(8,128)(2,1)S(1)} collective-permute-done((bf16[64,2048]{1,0:T(8,128)(2,1)S(1)}, bf16[64,2048]{1,0:T(8,128)(2,1)S(1)}, u32[]{:S(2)}, u32[]{:S(2)}) %collective-permute-start.8) | collective-permute-done | bytes 262176 | tf_op jit(solution)/shard_map/ppermute | solution.py:167
  206.3 3.8 collective-permute-done.6
  210.1 9.2 %collective-permute-done.7 = bf16[64,2048]{1,0:T(8,128)(2,1)S(1)} collective-permute-done((bf16[64,2048]{1,0:T(8,128)(2,1)S(1)}, bf16[64,2048]{1,0:T(8,128)(2,1)S(1)}, u32[]{:S(2)}, u32[]{:S(2)}) %collective-permute-start.7) | collective-permute-done | bytes 262176 | tf_op jit(solution)/shard_map/ppermute | solution.py:167
  220.3 1.3 maximum_convert_fusion
  221.8 1.4 collective-permute-start.4
  223.1 2.1 constant_dynamic-slice_fusion.11
  225.7 1.5 collective-permute-start.12
  227.3 2.8 reshape.137
  230.1 2.4 multiply_convert_fusion
  232.5 2.2 constant_dynamic-slice_fusion.13
  234.7 2.0 copy.12
  236.7 2.0 copy.11
  238.7 1.3 collective-permute-start.5
  240.0 7.0 %collective-permute-done.11 = bf16[64,2048]{1,0:T(8,128)(2,1)} collective-permute-done((bf16[64,2048]{1,0:T(8,128)(2,1)}, bf16[64,2048]{1,0:T(8,128)(2,1)}, u32[]{:S(2)}, u32[]{:S(2)}) %collective-permute-start.11) | collective-permute-done | bytes 262176 | tf_op jit(solution)/shard_map/ppermute | solution.py:167
  246.9 1.2 pad_maximum_fusion.1
  249.4 1.2 pad_maximum_fusion
  250.6 63.7 %collective-permute-done.5 = bf16[64,2048]{1,0:T(8,128)(2,1)S(1)} collective-permute-done((bf16[64,2048]{1,0:T(8,128)(2,1)}, bf16[64,2048]{1,0:T(8,128)(2,1)S(1)}, u32[]{:S(2)}, u32[]{:S(2)}) %collective-permute-start.5) | collective-permute-done | bytes 262176 | tf_op jit(solution)/shard_map/ppermute | solution.py:271
  314.3 15.6 %conditional.13 = (bf16[4,64,2048]{2,1,0:T(8,128)(2,1)S(1)}) conditional(s32[]{:T(128)} %convert_element_type.88, bf16[4,64,2048]{2,1,0:T(8,128)(2,1)S(1)} %copy-done.2, (bf16[64,2048]{1,0:T(8,128)(2,1)S(1)}, bf16[4,64,2048]{2,1,0:T(8,128)(2,1)S(1)}, bf16[2,4,1024,2048]{3,2,1,0:T(8,128)(2,1)}) %tuple.124), branch_computations={%region_13.14_spmd, %region_14.15_spmd} | conditional | flops 2147483648 | bytes 34603044 | solution.py:284
  315.0 14.7 %branch_1_fun.13 = (bf16[4,64,2048]{2,1,0:T(8,128)(2,1)S(1)}, bf16[64,2048]{1,0:T(8,128)(2,1)}) custom-call(bf16[64,2048]{1,0:T(8,128)(2,1)} %copy-done.7, bf16[4,64,2048]{2,1,0:T(8,128)(2,1)S(1)} %get-tuple-element.102.x_ref, bf16[2,4,1024,2048]{3,2,1,0:T(8,128)(2,1)} %get-tuple-element.103.w_ref), custom_call_target="tpu_custom_call" | custom-call | flops 2147483648 | bytes 33554432 | tf_op jit(solution)/shard_map/cond/branch_1_fun/pallas_call | solution.py:162
  330.8 2.4 collective-permute-start.14
  333.1 1.9 collective-permute-start.15
  335.1 5.1 %collective-permute-done.13 = bf16[64,2048]{1,0:T(8,128)(2,1)S(1)} collective-permute-done((bf16[64,2048]{1,0:T(8,128)(2,1)S(1)}, bf16[64,2048]{1,0:T(8,128)(2,1)S(1)}, u32[]{:S(2)}, u32[]{:S(2)}) %collective-permute-start.13) | collective-permute-done | bytes 262176 | tf_op jit(solution)/shard_map/ppermute | solution.py:167
  340.1 11.0 %collective-permute-done.14 = bf16[64,2048]{1,0:T(8,128)(2,1)S(1)} collective-permute-done((bf16[64,2048]{1,0:T(8,128)(2,1)S(1)}, bf16[64,2048]{1,0:T(8,128)(2,1)S(1)}, u32[]{:S(2)}, u32[]{:S(2)}) %collective-permute-start.14) | collective-permute-done | bytes 262176 | tf_op jit(solution)/shard_map/ppermute | solution.py:167
  351.6 2.4 collective-permute-done.16
  355.7 3.1 collective-permute-start.19
  359.9 1.9 collective-permute-start.22
  361.8 6.0 %collective-permute-done.17 = bf16[256,768]{1,0:T(8,128)(2,1)S(1)} collective-permute-done((bf16[256,768]{1,0:T(8,128)(2,1)S(1)}, bf16[256,768]{1,0:T(8,128)(2,1)S(1)}, u32[]{:S(2)}, u32[]{:S(2)}) %collective-permute-start.17) | collective-permute-done | bytes 393248 | tf_op jit(solution)/shard_map/ppermute | solution.py:167
  368.2 3.3 collective-permute-start.20
  371.5 17.2 %collective-permute-done.22 = bf16[512,512]{1,0:T(8,128)(2,1)S(1)} collective-permute-done((bf16[512,512]{1,0:T(8,128)(2,1)S(1)}, bf16[512,512]{1,0:T(8,128)(2,1)S(1)}, u32[]{:S(2)}, u32[]{:S(2)}) %collective-permute-start.22) | collective-permute-done | bytes 524320 | tf_op jit(solution)/shard_map/ppermute | solution.py:167
  389.3 3.3 collective-permute-start.25
  392.6 2.7 collective-permute-done.23
  396.1 1.3 collective-permute-start.21
  397.5 3.3 collective-permute-start.26
  401.6 1.7 collective-permute-done.26
  403.3 11.3 %collective-permute-done.21 = bf16[128,1536]{1,0:T(8,128)(2,1)S(1)} collective-permute-done((bf16[128,1536]{1,0:T(8,128)(2,1)S(1)}, bf16[128,1536]{1,0:T(8,128)(2,1)S(1)}, u32[]{:S(2)}, u32[]{:S(2)}) %collective-permute-start.21) | collective-permute-done | bytes 393248 | tf_op jit(solution)/shard_map/ppermute | solution.py:167
  (96 shorter events, 16.4 us)
Async XLA Ops:
  7.2 12.6 %copy-start = (bf16[256,2048]{1,0:T(8,128)(2,1)S(1)}, bf16[256,2048]{1,0:T(8,128)(2,1)}, u32[]{:S(2)}) copy-start(bf16[256,2048]{1,0:T(8,128)(2,1)} %param.19) | copy-start | bytes 3145732
  7.2 160.3 %all-gather.3.cloned.1.call-start = ((), (), s32[]{:S(2)}) async-start(), calls=%async_computation.1 | async-start | bytes 34078720 | tf_op jit(solution)/shard_map/all_gather | solution.py:249
  14.6 35.6 %all-to-all-start = ((bf16[4,64,2048]{2,1,0:T(8,128)(2,1)}), bf16[4,64,2048]{2,1,0:T(8,128)(2,1)S(1)}, u32[]{:S(2)}, u32[]{:S(2)}) async-start(bf16[4,64,2048]{2,1,0:T(8,128)(2,1)} %bitcast_select_fusion), calls=%async_computation | async-start | bytes 2097152 | tf_op jit(solution)/shard_map/all_to_all | solution.py:252
  180.3 9.4 %collective-permute-start = (bf16[64,2048]{1,0:T(8,128)(2,1)S(1)}, bf16[64,2048]{1,0:T(8,128)(2,1)S(1)}, u32[]{:S(2)}, u32[]{:S(2)}) collective-permute-start(bf16[64,2048]{1,0:T(8,128)(2,1)S(1)} %get-tuple-element.124), channel_id=1, source_target_pairs={{0,64},{1,65},{2,66},{3,67},{4,68},{5,69},{6,70},{7,71},{8,72},{9,... | collective-permute-start | bytes 786440 | tf_op jit(solution)/shard_map/ppermute | solution.py:258
  189.6 0.7 collective-permute-start.1
  190.3 2.4 collective-permute-start.2
  195.1 11.1 %collective-permute-start.8 = (bf16[64,2048]{1,0:T(8,128)(2,1)S(1)}, bf16[64,2048]{1,0:T(8,128)(2,1)S(1)}, u32[]{:S(2)}, u32[]{:S(2)}) collective-permute-start(bf16[64,2048]{1,0:T(8,128)(2,1)S(1)} %get-tuple-element.164), channel_id=1, source_target_pairs={{0,48},{16,0},{32,16},{48,32},{1,49},{17,1},{33,17},{49,33},{2,50}... | collective-permute-start | bytes 786440 | tf_op jit(solution)/shard_map/ppermute | solution.py:167
  195.2 14.8 %collective-permute-start.6 = (bf16[64,2048]{1,0:T(8,128)(2,1)S(1)}, bf16[64,2048]{1,0:T(8,128)(2,1)S(1)}, u32[]{:S(2)}, u32[]{:S(2)}) collective-permute-start(bf16[64,2048]{1,0:T(8,128)(2,1)S(1)} %get-tuple-element.166), channel_id=1, source_target_pairs={{0,16},{16,32},{32,48},{48,0},{1,17},{17,33},{33,49},{49,1},{2,18}... | collective-permute-start | bytes 786440 | tf_op jit(solution)/shard_map/ppermute | solution.py:167
  199.0 20.2 %collective-permute-start.7 = (bf16[64,2048]{1,0:T(8,128)(2,1)S(1)}, bf16[64,2048]{1,0:T(8,128)(2,1)S(1)}, u32[]{:S(2)}, u32[]{:S(2)}) collective-permute-start(bf16[64,2048]{1,0:T(8,128)(2,1)S(1)} %get-tuple-element.165), channel_id=1, source_target_pairs={{0,32},{16,48},{32,0},{48,16},{1,33},{17,49},{33,1},{49,17},{2,34}... | collective-permute-start | bytes 786440 | tf_op jit(solution)/shard_map/ppermute | solution.py:167
  199.0 22.5 %collective-permute-start.3 = (bf16[64,2048]{1,0:T(8,128)(2,1)}, bf16[64,2048]{1,0:T(8,128)(2,1)}, u32[]{:S(2)}, u32[]{:S(2)}) collective-permute-start(bf16[64,2048]{1,0:T(8,128)(2,1)} %get-tuple-element.131), channel_id=1, source_target_pairs={{192,128},{193,129},{194,130},{195,131},{196,132},{197,133},{198,1... | collective-permute-start | bytes 786440 | tf_op jit(solution)/shard_map/ppermute | solution.py:271
  206.3 13.0 %copy-start.4 = (bf16[64,2048]{1,0:T(8,128)(2,1)}, bf16[64,2048]{1,0:T(8,128)(2,1)S(1)}, u32[]{:S(2)}) copy-start(bf16[64,2048]{1,0:T(8,128)(2,1)S(1)} %collective-permute-done.8) | copy-start | bytes 786436
  210.1 9.2 %copy-start.5 = (bf16[64,2048]{1,0:T(8,128)(2,1)}, bf16[64,2048]{1,0:T(8,128)(2,1)S(1)}, u32[]{:S(2)}) copy-start(bf16[64,2048]{1,0:T(8,128)(2,1)S(1)} %collective-permute-done.6) | copy-start | bytes 786436
  219.3 0.7 copy-start.6
  221.8 16.9 %collective-permute-start.4 = (bf16[64,2048]{1,0:T(8,128)(2,1)}, bf16[64,2048]{1,0:T(8,128)(2,1)}, u32[]{:S(2)}, u32[]{:S(2)}) collective-permute-start(bf16[64,2048]{1,0:T(8,128)(2,1)} %get-tuple-element.132), channel_id=1, source_target_pairs={{128,64},{129,65},{130,66},{131,67},{132,68},{133,69},{134,70},{13... | collective-permute-start | bytes 786440 | tf_op jit(solution)/shard_map/ppermute | solution.py:271
  225.2 14.7 %collective-permute-start.10 = (bf16[64,2048]{1,0:T(8,128)(2,1)}, bf16[64,2048]{1,0:T(8,128)(2,1)}, u32[]{:S(2)}, u32[]{:S(2)}) collective-permute-start(bf16[64,2048]{1,0:T(8,128)(2,1)} %get-tuple-element.160), channel_id=1, source_target_pairs={{0,16},{16,32},{32,48},{48,0},{1,17},{17,33},{33,49},{49,1},{2,18}... | collective-permute-start | bytes 786440 | tf_op jit(solution)/shard_map/ppermute | solution.py:167
  225.7 21.2 %collective-permute-start.11 = (bf16[64,2048]{1,0:T(8,128)(2,1)}, bf16[64,2048]{1,0:T(8,128)(2,1)}, u32[]{:S(2)}, u32[]{:S(2)}) collective-permute-start(bf16[64,2048]{1,0:T(8,128)(2,1)} %get-tuple-element.159), channel_id=1, source_target_pairs={{0,32},{16,48},{32,0},{48,16},{1,33},{17,49},{33,1},{49,17},{2,34}... | collective-permute-start | bytes 786440 | tf_op jit(solution)/shard_map/ppermute | solution.py:167
  225.7 21.2 %collective-permute-start.12 = (bf16[64,2048]{1,0:T(8,128)(2,1)}, bf16[64,2048]{1,0:T(8,128)(2,1)}, u32[]{:S(2)}, u32[]{:S(2)}) collective-permute-start(bf16[64,2048]{1,0:T(8,128)(2,1)} %get-tuple-element.158), channel_id=1, source_target_pairs={{0,48},{16,0},{32,16},{48,32},{1,49},{17,1},{33,17},{49,33},{2,50}... | collective-permute-start | bytes 786440 | tf_op jit(solution)/shard_map/ppermute | solution.py:167
  236.7 12.7 %collective-permute-start.9 = (bf16[256,1024]{0,1:T(8,128)(2,1)}, bf16[256,1024]{0,1:T(8,128)(2,1)}, u32[]{:S(2)}, u32[]{:S(2)}) collective-permute-start(bf16[256,1024]{0,1:T(8,128)(2,1)} %bitcast.118), channel_id=1, source_target_pairs={{0,1},{1,0},{2,3},{3,2},{4,5},{5,4},{6,7},{7,6},{8,9},{9,8},{10,11... | collective-permute-start | bytes 1572872 | tf_op jit(solution)/shard_map/ppermute | solution.py:167
  238.7 75.7 %collective-permute-start.5 = (bf16[64,2048]{1,0:T(8,128)(2,1)}, bf16[64,2048]{1,0:T(8,128)(2,1)S(1)}, u32[]{:S(2)}, u32[]{:S(2)}) collective-permute-start(bf16[64,2048]{1,0:T(8,128)(2,1)} %get-tuple-element.134), channel_id=1, source_target_pairs={{64,0},{65,1},{66,2},{67,3},{68,4},{69,5},{70,6},{71,7},{72,8},{73... | collective-permute-start | bytes 786440 | tf_op jit(solution)/shard_map/ppermute | solution.py:271
  248.3 1.1 copy-start.3
  249.4 64.9 %copy-start.2 = (bf16[4,64,2048]{2,1,0:T(8,128)(2,1)S(1)}, bf16[4,64,2048]{2,1,0:T(8,128)(2,1)}, u32[]{:S(2)}) copy-start(bf16[4,64,2048]{2,1,0:T(8,128)(2,1)} %get-tuple-element.139) | copy-start | bytes 3145732
  314.3 0.7 copy-start.7
  330.0 10.1 %collective-permute-start.13 = (bf16[64,2048]{1,0:T(8,128)(2,1)S(1)}, bf16[64,2048]{1,0:T(8,128)(2,1)S(1)}, u32[]{:S(2)}, u32[]{:S(2)}) collective-permute-start(bf16[64,2048]{1,0:T(8,128)(2,1)S(1)} %get-tuple-element.152), channel_id=1, source_target_pairs={{0,16},{16,32},{32,48},{48,0},{1,17},{17,33},{33,49},{49,1},{2,18}... | collective-permute-start | bytes 786440 | tf_op jit(solution)/shard_map/ppermute | solution.py:167
  330.8 20.3 %collective-permute-start.14 = (bf16[64,2048]{1,0:T(8,128)(2,1)S(1)}, bf16[64,2048]{1,0:T(8,128)(2,1)S(1)}, u32[]{:S(2)}, u32[]{:S(2)}) collective-permute-start(bf16[64,2048]{1,0:T(8,128)(2,1)S(1)} %get-tuple-element.151), channel_id=1, source_target_pairs={{0,32},{16,48},{32,0},{48,16},{1,33},{17,49},{33,1},{49,17},{2,34}... | collective-permute-start | bytes 786440 | tf_op jit(solution)/shard_map/ppermute | solution.py:167
  333.1 18.0 %collective-permute-start.15 = (bf16[64,2048]{1,0:T(8,128)(2,1)S(1)}, bf16[64,2048]{1,0:T(8,128)(2,1)S(1)}, u32[]{:S(2)}, u32[]{:S(2)}) collective-permute-start(bf16[64,2048]{1,0:T(8,128)(2,1)S(1)} %get-tuple-element.150), channel_id=1, source_target_pairs={{0,48},{16,0},{32,16},{48,32},{1,49},{17,1},{33,17},{49,33},{2,50}... | collective-permute-start | bytes 786440 | tf_op jit(solution)/shard_map/ppermute | solution.py:167
  351.2 2.7 collective-permute-start.16
  355.3 12.4 %collective-permute-start.17 = (bf16[256,768]{1,0:T(8,128)(2,1)S(1)}, bf16[256,768]{1,0:T(8,128)(2,1)S(1)}, u32[]{:S(2)}, u32[]{:S(2)}) collective-permute-start(bf16[256,768]{1,0:T(8,128)(2,1)S(1)} %get-tuple-element.167), channel_id=1, source_target_pairs={{0,2},{2,4},{4,6},{6,0},{1,3},{3,5},{5,7},{7,1},{8,10},{10,12},{12... | collective-permute-start | bytes 1179656 | tf_op jit(solution)/shard_map/ppermute | solution.py:167
  355.7 12.4 %collective-permute-start.19 = (bf16[256,768]{1,0:T(8,128)(2,1)S(1)}, bf16[256,768]{1,0:T(8,128)(2,1)S(1)}, u32[]{:S(2)}, u32[]{:S(2)}) collective-permute-start(bf16[256,768]{1,0:T(8,128)(2,1)S(1)} %get-tuple-element.168), channel_id=1, source_target_pairs={{0,6},{2,0},{4,2},{6,4},{1,7},{3,1},{5,3},{7,5},{8,14},{10,8},{12,... | collective-permute-start | bytes 1179656 | tf_op jit(solution)/shard_map/ppermute | solution.py:167
  359.9 28.8 %collective-permute-start.22 = (bf16[512,512]{1,0:T(8,128)(2,1)S(1)}, bf16[512,512]{1,0:T(8,128)(2,1)S(1)}, u32[]{:S(2)}, u32[]{:S(2)}) collective-permute-start(bf16[512,512]{1,0:T(8,128)(2,1)S(1)} %convolution_convert_fusion.1), channel_id=1, source_target_pairs={{0,8},{8,0},{1,9},{9,1},{2,10},{10,2},{3,11},{11,3},{4,12},{12,4},... | collective-permute-start | bytes 1572872 | tf_op jit(solution)/shard_map/ppermute | solution.py:167
  367.9 27.5 %collective-permute-start.18 = (bf16[256,1536]{1,0:T(8,128)(2,1)S(1)}, bf16[256,1536]{1,0:T(8,128)(2,1)S(1)}, u32[]{:S(2)}, u32[]{:S(2)}) collective-permute-start(bf16[256,1536]{1,0:T(8,128)(2,1)S(1)} %pad_maximum_fusion.4), channel_id=1, source_target_pairs={{0,2},{2,4},{4,6},{6,0},{1,3},{3,5},{5,7},{7,1},{8,10},{10,12},{12... | collective-permute-start | bytes 2359304 | tf_op jit(solution)/shard_map/ppermute | solution.py:167
  368.2 27.3 %collective-permute-start.20 = (bf16[256,1536]{1,0:T(8,128)(2,1)S(1)}, bf16[256,1536]{1,0:T(8,128)(2,1)S(1)}, u32[]{:S(2)}, u32[]{:S(2)}) collective-permute-start(bf16[256,1536]{1,0:T(8,128)(2,1)S(1)} %pad_maximum_fusion.5), channel_id=1, source_target_pairs={{0,6},{2,0},{4,2},{6,4},{1,7},{3,1},{5,3},{7,5},{8,14},{10,8},{12,... | collective-permute-start | bytes 2359304 | tf_op jit(solution)/shard_map/ppermute | solution.py:167
  389.2 6.1 %collective-permute-start.23 = (bf16[128,256]{1,0:T(8,128)(2,1)S(1)}, bf16[128,256]{1,0:T(8,128)(2,1)S(1)}, u32[]{:S(2)}, u32[]{:S(2)}) collective-permute-start(bf16[128,256]{1,0:T(8,128)(2,1)S(1)} %get-tuple-element.169), channel_id=1, source_target_pairs={{0,2},{2,4},{4,6},{6,0},{1,3},{3,5},{5,7},{7,1},{8,10},{10,12},{12... | collective-permute-start | bytes 196616 | tf_op jit(solution)/shard_map/ppermute | solution.py:167
  389.3 6.1 %collective-permute-start.25 = (bf16[128,256]{1,0:T(8,128)(2,1)S(1)}, bf16[128,256]{1,0:T(8,128)(2,1)S(1)}, u32[]{:S(2)}, u32[]{:S(2)}) collective-permute-start(bf16[128,256]{1,0:T(8,128)(2,1)S(1)} %get-tuple-element.170), channel_id=1, source_target_pairs={{0,6},{2,0},{4,2},{6,4},{1,7},{3,1},{5,3},{7,5},{8,14},{10,8},{12,... | collective-permute-start | bytes 196616 | tf_op jit(solution)/shard_map/ppermute | solution.py:167
  395.3 6.3 %collective-permute-start.24 = (bf16[128,512]{1,0:T(8,128)(2,1)S(1)}, bf16[128,512]{1,0:T(8,128)(2,1)S(1)}, u32[]{:S(2)}, u32[]{:S(2)}) collective-permute-start(bf16[128,512]{1,0:T(8,128)(2,1)S(1)} %pad_maximum_fusion.7), channel_id=1, source_target_pairs={{0,2},{2,4},{4,6},{6,0},{1,3},{3,5},{5,7},{7,1},{8,10},{10,12},{12... | collective-permute-start | bytes 393224 | tf_op jit(solution)/shard_map/ppermute | solution.py:167
  396.1 18.5 %collective-permute-start.21 = (bf16[128,1536]{1,0:T(8,128)(2,1)S(1)}, bf16[128,1536]{1,0:T(8,128)(2,1)S(1)}, u32[]{:S(2)}, u32[]{:S(2)}) collective-permute-start(bf16[128,1536]{1,0:T(8,128)(2,1)S(1)} %fusion.4), channel_id=1, source_target_pairs={{0,8},{8,0},{1,9},{9,1},{2,10},{10,2},{3,11},{11,3},{4,12},{12,4},... | collective-permute-start | bytes 1179656 | tf_op jit(solution)/shard_map/ppermute | solution.py:167
  397.5 5.8 %collective-permute-start.26 = (bf16[128,512]{1,0:T(8,128)(2,1)S(1)}, bf16[128,512]{1,0:T(8,128)(2,1)S(1)}, u32[]{:S(2)}, u32[]{:S(2)}) collective-permute-start(bf16[128,512]{1,0:T(8,128)(2,1)S(1)} %pad_maximum_fusion.8), channel_id=1, source_target_pairs={{0,6},{2,0},{4,2},{6,4},{1,7},{3,1},{5,3},{7,5},{8,14},{10,8},{12,... | collective-permute-start | bytes 393224 | tf_op jit(solution)/shard_map/ppermute | solution.py:167
  403.3 12.5 %copy-start.1 = (bf16[256,2048]{1,0:T(8,128)(2,1)S(1)}, bf16[256,2048]{1,0:T(8,128)(2,1)}, u32[]{:S(2)}) copy-start(bf16[256,2048]{1,0:T(8,128)(2,1)} %param.19) | copy-start | bytes 3145732
Sparse Core Ops, SparseCore 0:
  10.8 156.6 all-gather.2

commit v10 on v9

--- a/solution.py
+++ b/solution.py
@@ -16,12 +16,15 @@
 PLANE = ("zh", "zl", "y", "c")
 
 
-def tile_copies(w_ref, held, arrived, order):
+def tile_copies(w_ref, held, arrived, order, resident=0):
     halves, depth, rows, width = w_ref.shape
     tiles, slots = width // TILE, held.shape[0]
 
+    def slot_of(number):
+        return lax.rem(number + resident // 2, slots)
+
     def start(number):
-        slot = lax.rem(number, slots)
+        slot = slot_of(number)
         layer = order(number // tiles)
         span = pl.ds(pl.multiple_of(lax.rem(number, tiles) * TILE, TILE), TILE)
         for half in range(halves):
@@ -32,17 +35,19 @@
             ).start()
 
     def wait(number):
-        whole = held.at[lax.rem(number, slots)]
-        pltpu.make_async_copy(whole, whole, arrived.at[lax.rem(number, slots)]).wait()
+        @pl.when(number >= resident)
+        def _():
+            whole = held.at[slot_of(number)]
+            pltpu.make_async_copy(whole, whole, arrived.at[slot_of(number)]).wait()
 
     def refill(number):
         @pl.when(number + slots < depth * tiles)
         def _():
             start(number + slots)
 
-    for number in range(slots):
+    for number in range(resident, slots):
         start(jnp.int32(number))
-    return wait, refill
+    return wait, refill, slot_of
 
 
 def forward_kernel(
@@ -50,7 +55,7 @@
 ):
     depth, rows, width = base_ref.shape
     tiles, slots = width // TILE, held.shape[0]
-    wait, refill = tile_copies(w_ref, held, arrived, lambda i: i)
+    wait, refill, slot_of = tile_copies(w_ref, held, arrived, lambda i: i)
     x_now[...] = x_ref[...].astype(jnp.float32)
     in_ref[0] = x_ref[...]
 
@@ -63,7 +68,7 @@
             wait(number)
             columns = pl.ds(tile * TILE, TILE)
             y[:, columns] = x_now[:, columns] + jnp.dot(
-                normed[...], held[lax.rem(number, slots)], preferred_element_type=jnp.float32
+                normed[...], held[slot_of(number)], preferred_element_type=jnp.float32
             )
             refill(number)
         values = y[...]
@@ -87,10 +92,14 @@
     lax.fori_loop(0, depth, run_layer, 0)
 
 
-def backward_kernel(g_ref, x_ref, w_ref, seen_ref, out_ref, g_now, back, held, arrived):
+def backward_kernel(
+    g_ref, x_ref, w_ref, seen_ref, out_ref, g_now, back, held, arrived, resident=0
+):
     depth, rows, width = x_ref.shape
     tiles, slots = width // TILE, held.shape[0]
-    wait, refill = tile_copies(w_ref, held, arrived, lambda i: depth - 1 - i)
+    wait, refill, slot_of = tile_copies(
+        w_ref, held, arrived, lambda i: depth - 1 - i, resident
+    )
     g_now[...] = g_ref[...]
 
     def run_layer(step, carry):
@@ -100,7 +109,7 @@
             number = step * tiles + tile
             wait(number)
             product = lax.dot_general(
-                g_now[:, pl.ds(tile * TILE, TILE)], held[lax.rem(number, slots)],
+                g_now[:, pl.ds(tile * TILE, TILE)], held[slot_of(number)],
                 (((1,), (1,)), ((), ())), preferred_element_type=jnp.float32,
             )
             if tile == 0:
@@ -121,11 +130,23 @@
     out_ref[...] = g_now[...]
 
 
-def stage_call(kernel, scratch, outs, depth, rows, width):
+def turn_kernel(
+    x_ref, base_ref, w_ref, g_ref, in_ref, out_ref, seen_ref, sent_ref,
+    x_now, normed, y, g_now, back, held, arrived,
+):
+    forward_kernel(
+        x_ref, base_ref, w_ref, in_ref, out_ref, sent_ref, x_now, normed, y, held, arrived
+    )
+    backward_kernel(
+        g_ref, in_ref, w_ref, seen_ref, sent_ref, g_now, back, held, arrived, resident=SLOTS
+    )
+
+
+def stage_call(kernel, scratch, outs, depth, rows, width, more=()):
     vmem = pl.BlockSpec(memory_space=pltpu.VMEM)
     return pl.pallas_call(
         kernel,
-        in_specs=[vmem, vmem, pl.BlockSpec(memory_space=pl.ANY)],
+        in_specs=[vmem, vmem, pl.BlockSpec(memory_space=pl.ANY), *more],
         out_specs=[vmem] * len(outs),
         out_shape=[jax.ShapeDtypeStruct(shape, jnp.bfloat16) for shape in outs],
         scratch_shapes=[
@@ -162,6 +183,17 @@
     return tuple(call(g, x, weight))
 
 
+def turn_stage(x, base, weight, g):
+    depth, rows, width = base.shape
+    wide, narrow = pltpu.VMEM((rows, width), jnp.float32), pltpu.VMEM((rows, width), jnp.bfloat16)
+    stack = (depth, rows, width)
+    call = stage_call(
+        turn_kernel, [wide, narrow, wide, narrow, wide], [stack, stack, stack, (rows, width)],
+        depth, rows, width, more=[pl.BlockSpec(memory_space=pltpu.VMEM)],
+    )
+    return tuple(call(x, base, weight, g))
+
+
 def shift(value, axis, steps):
     count = lax.axis_size(axis)
     return lax.ppermute(value, axis, [(i, (i + steps) % count) for i in range(count)])
@@ -254,19 +286,20 @@
     g = lax.dynamic_slice_in_dim(top_cotangent, lane * rows, rows, 0)
 
     state = forward_stage(x, base, weight)
-    for t in range(1, STAGES):
+    for t in range(1, STAGES - 1):
         arrived = lax.ppermute(state[2], "x", [(t - 1, t)])
         state = lax.cond(
             stage == t, lambda a, s: forward_stage(a, base, weight), lambda a, s: s, arrived, state
         )
-    inputs, decoded, _ = state
-
-    state = lax.cond(
+    arrived = lax.ppermute(state[2], "x", [(STAGES - 2, STAGES - 1)])
+    inputs, decoded, *state = lax.cond(
         stage == STAGES - 1,
-        lambda a, s: backward_stage(a, inputs, weight),
-        lambda a, s: s,
-        g, (decoded, g),
-    )
+        lambda a, s: turn_stage(a, base, weight, g),
+        lambda a, s: (s[0], s[1], s[1], g),
+        arrived, state,
+    )
+    state = tuple(state)
+
     for t in range(STAGES - 2, -1, -1):
         arrived = lax.ppermute(state[1], "x", [(t + 1, t)])
         if t == STAGES - 2:

time: 423 us -> 421 us (level)
  no operation moved by 1% of the time
where the time goes in v10:
time: 421 us; the launch traced here: 420 us
  waiting for transfers between devices  300 us (71%)
  starting transfers between devices  41.6 us (10%)
  Pallas kernels  27.5 us (7%)
  local copies, waits for them, and re-layouts  20.8 us (5%)
  between operations  14.6 us (3%)
  other arithmetic  12.4 us (3%)
    all_gather x1, waiting for transfers between devices, local(): weight = lax.all_gather(layer_weight[0], PLANE, axis=0, tiled=True)  117 us
    ppermute x21, waiting for transfers between devices, shift(): lax.ppermute(value, axis, [(i, (i + steps) % count) for i in range(count)])  84 us
    ppermute x3, waiting for transfers between devices, local(): arrived = lax.ppermute(state[1], 'x', [(t + 1, t)])  61.5 us
    all_to_all x1, waiting for transfers between devices, local(): base = lax.all_to_all(picked.reshape(DEPTH, rows, width), 'zl', 0, 0)  30.5 us
    ppermute x21, starting transfers between devices, shift(): lax.ppermute(value, axis, [(i, (i + steps) % count) for i in range(count)])  27.7 us
    pallas_call x1, Pallas kernels, backward_stage(): return tuple(call(g, x, weight))  14.7 us
    pallas_call x1, Pallas kernels, forward_stage(): return tuple(call(x, base, weight))  12.8 us
  transfers between devices with their start and end apart: 29, of which 17 were waited for; matrix products, arithmetic and copies ran while one was open for 7% of the time, Pallas kernels for 0%

profile of v10, /device:TPU:96, one launch (start us, length us, event | category | flops | bytes accessed | tf_op | source)
XLA Modules:
  0.0 420.3 jit_solution(14505791424211788570)
XLA Ops:
  8.4 1.3 reduce.4
  10.7 2.8 gather_fusion
  14.6 5.1 %all-to-all-start = ((bf16[4,64,2048]{2,1,0:T(8,128)(2,1)}), bf16[4,64,2048]{2,1,0:T(8,128)(2,1)S(1)}, u32[]{:S(2)}, u32[]{:S(2)}) async-start(bf16[4,64,2048]{2,1,0:T(8,128)(2,1)} %bitcast_select_fusion), calls=%async_computation | async-start | bytes 2097152 | tf_op jit(solution)/shard_map/all_to_all | solution.py:284
  19.7 30.5 %all-to-all-done.base_ref = bf16[4,64,2048]{2,1,0:T(8,128)(2,1)S(1)} async-done(((bf16[4,64,2048]{2,1,0:T(8,128)(2,1)}), bf16[4,64,2048]{2,1,0:T(8,128)(2,1)S(1)}, u32[]{:S(2)}, u32[]{:S(2)}) %all-to-all-start) | async-done | bytes 1048608 | tf_op jit(solution)/shard_map/all_to_all | solution.py:284
  50.2 117.2 %all-gather.3.cloned.1.call-done = bf16[1,8192,2048]{2,1,0:T(8,128)(2,1)} async-done(((bf16[1,128,2048]{2,1,0:T(8,128)(2,1)}), bf16[1,8192,2048]{2,1,0:T(8,128)(2,1)}) %all-gather.3.cloned.1.call-update) | async-done | bytes 33554448 | tf_op jit(solution)/shard_map/all_gather | solution.py:281
  167.4 12.8 %shard_map.68 = (bf16[4,64,2048]{2,1,0:T(8,128)(2,1)S(1)}, bf16[4,64,2048]{2,1,0:T(8,128)(2,1)}, bf16[64,2048]{1,0:T(8,128)(2,1)S(1)}) custom-call(bf16[64,2048]{1,0:T(8,128)(2,1)S(1)} %constant_dynamic-slice_fusion.16.x_ref, bf16[4,64,2048]{2,1,0:T(8,128)(2,1)S(1)} %all-to-all-done.base_ref, bf16[2,4,1024,2048]{3,2,1,0:T(8,128)(2,1)} %bitcast.85), custom_call_target="tpu_custom_call" | custom-call | flops 2147483648 | bytes 33554432 | tf_op jit(solution)/shard_map/pallas_call | solution.py:175
  180.3 3.4 collective-permute-start
  183.7 5.9 %collective-permute-done = bf16[64,2048]{1,0:T(8,128)(2,1)S(1)} collective-permute-done((bf16[64,2048]{1,0:T(8,128)(2,1)S(1)}, bf16[64,2048]{1,0:T(8,128)(2,1)S(1)}, u32[]{:S(2)}, u32[]{:S(2)}) %collective-permute-start) | collective-permute-done | bytes 262176 | tf_op jit(solution)/shard_map/ppermute | solution.py:290
  191.0 1.7 constant_dynamic-slice_fusion.15
  192.7 2.4 conditional.8
  192.7 2.4 copy.35
  195.2 3.8 collective-permute-start.6
  199.0 1.4 collective-permute-start.3
  200.4 5.9 %collective-permute-done.8 = bf16[64,2048]{1,0:T(8,128)(2,1)S(1)} collective-permute-done((bf16[64,2048]{1,0:T(8,128)(2,1)S(1)}, bf16[64,2048]{1,0:T(8,128)(2,1)S(1)}, u32[]{:S(2)}, u32[]{:S(2)}) %collective-permute-start.8) | collective-permute-done | bytes 262176 | tf_op jit(solution)/shard_map/ppermute | solution.py:199
  206.2 3.8 collective-permute-done.6
  210.1 9.2 %collective-permute-done.7 = bf16[64,2048]{1,0:T(8,128)(2,1)S(1)} collective-permute-done((bf16[64,2048]{1,0:T(8,128)(2,1)S(1)}, bf16[64,2048]{1,0:T(8,128)(2,1)S(1)}, u32[]{:S(2)}, u32[]{:S(2)}) %collective-permute-start.7) | collective-permute-done | bytes 262176 | tf_op jit(solution)/shard_map/ppermute | solution.py:199
  220.2 1.3 maximum_convert_fusion
  221.7 1.4 collective-permute-start.4
  223.1 2.1 constant_dynamic-slice_fusion.11
  225.7 1.5 collective-permute-start.12
  227.3 2.8 reshape.137
  230.1 2.4 multiply_convert_fusion
  232.5 2.2 constant_dynamic-slice_fusion.13
  234.6 2.0 copy.12
  236.6 2.0 copy.11
  238.6 1.3 collective-permute-start.5
  239.9 7.0 %collective-permute-done.11 = bf16[64,2048]{1,0:T(8,128)(2,1)} collective-permute-done((bf16[64,2048]{1,0:T(8,128)(2,1)}, bf16[64,2048]{1,0:T(8,128)(2,1)}, u32[]{:S(2)}, u32[]{:S(2)}) %collective-permute-start.11) | collective-permute-done | bytes 262176 | tf_op jit(solution)/shard_map/ppermute | solution.py:199
  246.9 1.2 pad_maximum_fusion.1
  249.4 1.2 pad_maximum_fusion
  250.6 61.5 %collective-permute-done.5 = bf16[64,2048]{1,0:T(8,128)(2,1)S(1)} collective-permute-done((bf16[64,2048]{1,0:T(8,128)(2,1)}, bf16[64,2048]{1,0:T(8,128)(2,1)S(1)}, u32[]{:S(2)}, u32[]{:S(2)}) %collective-permute-start.5) | collective-permute-done | bytes 262176 | tf_op jit(solution)/shard_map/ppermute | solution.py:304
  312.1 15.6 %conditional.11 = (bf16[4,64,2048]{2,1,0:T(8,128)(2,1)S(1)}) conditional(s32[]{:T(128)} %convert_element_type.87, bf16[4,64,2048]{2,1,0:T(8,128)(2,1)S(1)} %copy-done.2, (bf16[64,2048]{1,0:T(8,128)(2,1)S(1)}, bf16[4,64,2048]{2,1,0:T(8,128)(2,1)S(1)}, bf16[2,4,1024,2048]{3,2,1,0:T(8,128)(2,1)}) %tuple.113), branch_computations={%region_11.12_spmd, %region_12.13_spmd} | conditional | flops 2147483648 | bytes 34603044 | solution.py:317
  312.8 14.7 %branch_1_fun.11 = (bf16[4,64,2048]{2,1,0:T(8,128)(2,1)S(1)}, bf16[64,2048]{1,0:T(8,128)(2,1)}) custom-call(bf16[64,2048]{1,0:T(8,128)(2,1)} %copy-done.7, bf16[4,64,2048]{2,1,0:T(8,128)(2,1)S(1)} %get-tuple-element.95.x_ref, bf16[2,4,1024,2048]{3,2,1,0:T(8,128)(2,1)} %get-tuple-element.96.w_ref), custom_call_target="tpu_custom_call" | custom-call | flops 2147483648 | bytes 33554432 | tf_op jit(solution)/shard_map/cond/branch_1_fun/pallas_call | solution.py:183
  328.5 2.4 collective-permute-start.14
  330.9 1.9 collective-permute-start.15
  332.8 5.0 %collective-permute-done.13 = bf16[64,2048]{1,0:T(8,128)(2,1)S(1)} collective-permute-done((bf16[64,2048]{1,0:T(8,128)(2,1)S(1)}, bf16[64,2048]{1,0:T(8,128)(2,1)S(1)}, u32[]{:S(2)}, u32[]{:S(2)}) %collective-permute-start.13) | collective-permute-done | bytes 262176 | tf_op jit(solution)/shard_map/ppermute | solution.py:199
  337.8 11.0 %collective-permute-done.14 = bf16[64,2048]{1,0:T(8,128)(2,1)S(1)} collective-permute-done((bf16[64,2048]{1,0:T(8,128)(2,1)S(1)}, bf16[64,2048]{1,0:T(8,128)(2,1)S(1)}, u32[]{:S(2)}, u32[]{:S(2)}) %collective-permute-start.14) | collective-permute-done | bytes 262176 | tf_op jit(solution)/shard_map/ppermute | solution.py:199
  349.3 2.4 collective-permute-done.16
  353.4 3.1 collective-permute-start.19
  357.6 1.9 collective-permute-start.22
  359.5 6.0 %collective-permute-done.17 = bf16[256,768]{1,0:T(8,128)(2,1)S(1)} collective-permute-done((bf16[256,768]{1,0:T(8,128)(2,1)S(1)}, bf16[256,768]{1,0:T(8,128)(2,1)S(1)}, u32[]{:S(2)}, u32[]{:S(2)}) %collective-permute-start.17) | collective-permute-done | bytes 393248 | tf_op jit(solution)/shard_map/ppermute | solution.py:199
  365.9 3.3 collective-permute-start.20
  369.2 17.2 %collective-permute-done.22 = bf16[512,512]{1,0:T(8,128)(2,1)S(1)} collective-permute-done((bf16[512,512]{1,0:T(8,128)(2,1)S(1)}, bf16[512,512]{1,0:T(8,128)(2,1)S(1)}, u32[]{:S(2)}, u32[]{:S(2)}) %collective-permute-start.22) | collective-permute-done | bytes 524320 | tf_op jit(solution)/shard_map/ppermute | solution.py:199
  387.1 3.3 collective-permute-start.25
  390.4 2.7 collective-permute-done.23
  393.9 1.3 collective-permute-start.21
  395.2 3.3 collective-permute-start.26
  399.3 1.6 collective-permute-done.26
  401.0 11.3 %collective-permute-done.21 = bf16[128,1536]{1,0:T(8,128)(2,1)S(1)} collective-permute-done((bf16[128,1536]{1,0:T(8,128)(2,1)S(1)}, bf16[128,1536]{1,0:T(8,128)(2,1)S(1)}, u32[]{:S(2)}, u32[]{:S(2)}) %collective-permute-start.21) | collective-permute-done | bytes 393248 | tf_op jit(solution)/shard_map/ppermute | solution.py:199
  (95 shorter events, 16.4 us)
Async XLA Ops:
  7.2 12.6 %copy-start = (bf16[256,2048]{1,0:T(8,128)(2,1)S(1)}, bf16[256,2048]{1,0:T(8,128)(2,1)}, u32[]{:S(2)}) copy-start(bf16[256,2048]{1,0:T(8,128)(2,1)} %param.17) | copy-start | bytes 3145732
  7.2 160.3 %all-gather.3.cloned.1.call-start = ((), (), s32[]{:S(2)}) async-start(), calls=%async_computation.1 | async-start | bytes 34078720 | tf_op jit(solution)/shard_map/all_gather | solution.py:281
  14.6 35.6 %all-to-all-start = ((bf16[4,64,2048]{2,1,0:T(8,128)(2,1)}), bf16[4,64,2048]{2,1,0:T(8,128)(2,1)S(1)}, u32[]{:S(2)}, u32[]{:S(2)}) async-start(bf16[4,64,2048]{2,1,0:T(8,128)(2,1)} %bitcast_select_fusion), calls=%async_computation | async-start | bytes 2097152 | tf_op jit(solution)/shard_map/all_to_all | solution.py:284
  180.3 9.4 %collective-permute-start = (bf16[64,2048]{1,0:T(8,128)(2,1)S(1)}, bf16[64,2048]{1,0:T(8,128)(2,1)S(1)}, u32[]{:S(2)}, u32[]{:S(2)}) collective-permute-start(bf16[64,2048]{1,0:T(8,128)(2,1)S(1)} %get-tuple-element.118), channel_id=1, source_target_pairs={{0,64},{1,65},{2,66},{3,67},{4,68},{5,69},{6,70},{7,71},{8,72},{9,... | collective-permute-start | bytes 786440 | tf_op jit(solution)/shard_map/ppermute | solution.py:290
  189.6 0.7 collective-permute-start.1
  190.3 2.4 collective-permute-start.2
  195.1 11.1 %collective-permute-start.8 = (bf16[64,2048]{1,0:T(8,128)(2,1)S(1)}, bf16[64,2048]{1,0:T(8,128)(2,1)S(1)}, u32[]{:S(2)}, u32[]{:S(2)}) collective-permute-start(bf16[64,2048]{1,0:T(8,128)(2,1)S(1)} %get-tuple-element.159), channel_id=1, source_target_pairs={{0,48},{16,0},{32,16},{48,32},{1,49},{17,1},{33,17},{49,33},{2,50}... | collective-permute-start | bytes 786440 | tf_op jit(solution)/shard_map/ppermute | solution.py:199
  195.2 14.8 %collective-permute-start.6 = (bf16[64,2048]{1,0:T(8,128)(2,1)S(1)}, bf16[64,2048]{1,0:T(8,128)(2,1)S(1)}, u32[]{:S(2)}, u32[]{:S(2)}) collective-permute-start(bf16[64,2048]{1,0:T(8,128)(2,1)S(1)} %get-tuple-element.161), channel_id=1, source_target_pairs={{0,16},{16,32},{32,48},{48,0},{1,17},{17,33},{33,49},{49,1},{2,18}... | collective-permute-start | bytes 786440 | tf_op jit(solution)/shard_map/ppermute | solution.py:199
  199.0 20.2 %collective-permute-start.7 = (bf16[64,2048]{1,0:T(8,128)(2,1)S(1)}, bf16[64,2048]{1,0:T(8,128)(2,1)S(1)}, u32[]{:S(2)}, u32[]{:S(2)}) collective-permute-start(bf16[64,2048]{1,0:T(8,128)(2,1)S(1)} %get-tuple-element.160), channel_id=1, source_target_pairs={{0,32},{16,48},{32,0},{48,16},{1,33},{17,49},{33,1},{49,17},{2,34}... | collective-permute-start | bytes 786440 | tf_op jit(solution)/shard_map/ppermute | solution.py:199
  199.0 22.5 %collective-permute-start.3 = (bf16[64,2048]{1,0:T(8,128)(2,1)}, bf16[64,2048]{1,0:T(8,128)(2,1)}, u32[]{:S(2)}, u32[]{:S(2)}) collective-permute-start(bf16[64,2048]{1,0:T(8,128)(2,1)} %get-tuple-element.124), channel_id=1, source_target_pairs={{192,128},{193,129},{194,130},{195,131},{196,132},{197,133},{198,1... | collective-permute-start | bytes 786440 | tf_op jit(solution)/shard_map/ppermute | solution.py:304
  206.2 13.0 %copy-start.4 = (bf16[64,2048]{1,0:T(8,128)(2,1)}, bf16[64,2048]{1,0:T(8,128)(2,1)S(1)}, u32[]{:S(2)}) copy-start(bf16[64,2048]{1,0:T(8,128)(2,1)S(1)} %collective-permute-done.8) | copy-start | bytes 786436
  210.1 9.2 %copy-start.5 = (bf16[64,2048]{1,0:T(8,128)(2,1)}, bf16[64,2048]{1,0:T(8,128)(2,1)S(1)}, u32[]{:S(2)}) copy-start(bf16[64,2048]{1,0:T(8,128)(2,1)S(1)} %collective-permute-done.6) | copy-start | bytes 786436
  219.3 0.7 copy-start.6
  221.7 16.9 %collective-permute-start.4 = (bf16[64,2048]{1,0:T(8,128)(2,1)}, bf16[64,2048]{1,0:T(8,128)(2,1)}, u32[]{:S(2)}, u32[]{:S(2)}) collective-permute-start(bf16[64,2048]{1,0:T(8,128)(2,1)} %get-tuple-element.126), channel_id=1, source_target_pairs={{128,64},{129,65},{130,66},{131,67},{132,68},{133,69},{134,70},{13... | collective-permute-start | bytes 786440 | tf_op jit(solution)/shard_map/ppermute | solution.py:304
  225.2 14.7 %collective-permute-start.10 = (bf16[64,2048]{1,0:T(8,128)(2,1)}, bf16[64,2048]{1,0:T(8,128)(2,1)}, u32[]{:S(2)}, u32[]{:S(2)}) collective-permute-start(bf16[64,2048]{1,0:T(8,128)(2,1)} %get-tuple-element.155), channel_id=1, source_target_pairs={{0,16},{16,32},{32,48},{48,0},{1,17},{17,33},{33,49},{49,1},{2,18}... | collective-permute-start | bytes 786440 | tf_op jit(solution)/shard_map/ppermute | solution.py:199
  225.7 21.2 %collective-permute-start.11 = (bf16[64,2048]{1,0:T(8,128)(2,1)}, bf16[64,2048]{1,0:T(8,128)(2,1)}, u32[]{:S(2)}, u32[]{:S(2)}) collective-permute-start(bf16[64,2048]{1,0:T(8,128)(2,1)} %get-tuple-element.154), channel_id=1, source_target_pairs={{0,32},{16,48},{32,0},{48,16},{1,33},{17,49},{33,1},{49,17},{2,34}... | collective-permute-start | bytes 786440 | tf_op jit(solution)/shard_map/ppermute | solution.py:199
  225.7 21.2 %collective-permute-start.12 = (bf16[64,2048]{1,0:T(8,128)(2,1)}, bf16[64,2048]{1,0:T(8,128)(2,1)}, u32[]{:S(2)}, u32[]{:S(2)}) collective-permute-start(bf16[64,2048]{1,0:T(8,128)(2,1)} %get-tuple-element.153), channel_id=1, source_target_pairs={{0,48},{16,0},{32,16},{48,32},{1,49},{17,1},{33,17},{49,33},{2,50}... | collective-permute-start | bytes 786440 | tf_op jit(solution)/shard_map/ppermute | solution.py:199
  236.6 12.7 %collective-permute-start.9 = (bf16[256,1024]{0,1:T(8,128)(2,1)}, bf16[256,1024]{0,1:T(8,128)(2,1)}, u32[]{:S(2)}, u32[]{:S(2)}) collective-permute-start(bf16[256,1024]{0,1:T(8,128)(2,1)} %bitcast.117), channel_id=1, source_target_pairs={{0,1},{1,0},{2,3},{3,2},{4,5},{5,4},{6,7},{7,6},{8,9},{9,8},{10,11... | collective-permute-start | bytes 1572872 | tf_op jit(solution)/shard_map/ppermute | solution.py:199
  238.6 73.4 %collective-permute-start.5 = (bf16[64,2048]{1,0:T(8,128)(2,1)}, bf16[64,2048]{1,0:T(8,128)(2,1)S(1)}, u32[]{:S(2)}, u32[]{:S(2)}) collective-permute-start(bf16[64,2048]{1,0:T(8,128)(2,1)} %get-tuple-element.128), channel_id=1, source_target_pairs={{64,0},{65,1},{66,2},{67,3},{68,4},{69,5},{70,6},{71,7},{72,8},{73... | collective-permute-start | bytes 786440 | tf_op jit(solution)/shard_map/ppermute | solution.py:304
  248.2 1.1 copy-start.3
  249.4 62.7 %copy-start.2 = (bf16[4,64,2048]{2,1,0:T(8,128)(2,1)S(1)}, bf16[4,64,2048]{2,1,0:T(8,128)(2,1)}, u32[]{:S(2)}) copy-start(bf16[4,64,2048]{2,1,0:T(8,128)(2,1)} %get-tuple-element.134) | copy-start | bytes 3145732
  312.1 0.7 copy-start.7
  327.8 10.1 %collective-permute-start.13 = (bf16[64,2048]{1,0:T(8,128)(2,1)S(1)}, bf16[64,2048]{1,0:T(8,128)(2,1)S(1)}, u32[]{:S(2)}, u32[]{:S(2)}) collective-permute-start(bf16[64,2048]{1,0:T(8,128)(2,1)S(1)} %get-tuple-element.147), channel_id=1, source_target_pairs={{0,16},{16,32},{32,48},{48,0},{1,17},{17,33},{33,49},{49,1},{2,18}... | collective-permute-start | bytes 786440 | tf_op jit(solution)/shard_map/ppermute | solution.py:199
  328.5 20.4 %collective-permute-start.14 = (bf16[64,2048]{1,0:T(8,128)(2,1)S(1)}, bf16[64,2048]{1,0:T(8,128)(2,1)S(1)}, u32[]{:S(2)}, u32[]{:S(2)}) collective-permute-start(bf16[64,2048]{1,0:T(8,128)(2,1)S(1)} %get-tuple-element.146), channel_id=1, source_target_pairs={{0,32},{16,48},{32,0},{48,16},{1,33},{17,49},{33,1},{49,17},{2,34}... | collective-permute-start | bytes 786440 | tf_op jit(solution)/shard_map/ppermute | solution.py:199
  330.9 18.0 %collective-permute-start.15 = (bf16[64,2048]{1,0:T(8,128)(2,1)S(1)}, bf16[64,2048]{1,0:T(8,128)(2,1)S(1)}, u32[]{:S(2)}, u32[]{:S(2)}) collective-permute-start(bf16[64,2048]{1,0:T(8,128)(2,1)S(1)} %get-tuple-element.145), channel_id=1, source_target_pairs={{0,48},{16,0},{32,16},{48,32},{1,49},{17,1},{33,17},{49,33},{2,50}... | collective-permute-start | bytes 786440 | tf_op jit(solution)/shard_map/ppermute | solution.py:199
  349.0 2.7 collective-permute-start.16
  353.1 12.4 %collective-permute-start.17 = (bf16[256,768]{1,0:T(8,128)(2,1)S(1)}, bf16[256,768]{1,0:T(8,128)(2,1)S(1)}, u32[]{:S(2)}, u32[]{:S(2)}) collective-permute-start(bf16[256,768]{1,0:T(8,128)(2,1)S(1)} %get-tuple-element.162), channel_id=1, source_target_pairs={{0,2},{2,4},{4,6},{6,0},{1,3},{3,5},{5,7},{7,1},{8,10},{10,12},{12... | collective-permute-start | bytes 1179656 | tf_op jit(solution)/shard_map/ppermute | solution.py:199
  353.4 12.4 %collective-permute-start.19 = (bf16[256,768]{1,0:T(8,128)(2,1)S(1)}, bf16[256,768]{1,0:T(8,128)(2,1)S(1)}, u32[]{:S(2)}, u32[]{:S(2)}) collective-permute-start(bf16[256,768]{1,0:T(8,128)(2,1)S(1)} %get-tuple-element.163), channel_id=1, source_target_pairs={{0,6},{2,0},{4,2},{6,4},{1,7},{3,1},{5,3},{7,5},{8,14},{10,8},{12,... | collective-permute-start | bytes 1179656 | tf_op jit(solution)/shard_map/ppermute | solution.py:199
  357.6 28.8 %collective-permute-start.22 = (bf16[512,512]{1,0:T(8,128)(2,1)S(1)}, bf16[512,512]{1,0:T(8,128)(2,1)S(1)}, u32[]{:S(2)}, u32[]{:S(2)}) collective-permute-start(bf16[512,512]{1,0:T(8,128)(2,1)S(1)} %convolution_convert_fusion.1), channel_id=1, source_target_pairs={{0,8},{8,0},{1,9},{9,1},{2,10},{10,2},{3,11},{11,3},{4,12},{12,4},... | collective-permute-start | bytes 1572872 | tf_op jit(solution)/shard_map/ppermute | solution.py:199
  365.7 27.5 %collective-permute-start.18 = (bf16[256,1536]{1,0:T(8,128)(2,1)S(1)}, bf16[256,1536]{1,0:T(8,128)(2,1)S(1)}, u32[]{:S(2)}, u32[]{:S(2)}) collective-permute-start(bf16[256,1536]{1,0:T(8,128)(2,1)S(1)} %pad_maximum_fusion.4), channel_id=1, source_target_pairs={{0,2},{2,4},{4,6},{6,0},{1,3},{3,5},{5,7},{7,1},{8,10},{10,12},{12... | collective-permute-start | bytes 2359304 | tf_op jit(solution)/shard_map/ppermute | solution.py:199
  365.9 27.3 %collective-permute-start.20 = (bf16[256,1536]{1,0:T(8,128)(2,1)S(1)}, bf16[256,1536]{1,0:T(8,128)(2,1)S(1)}, u32[]{:S(2)}, u32[]{:S(2)}) collective-permute-start(bf16[256,1536]{1,0:T(8,128)(2,1)S(1)} %pad_maximum_fusion.5), channel_id=1, source_target_pairs={{0,6},{2,0},{4,2},{6,4},{1,7},{3,1},{5,3},{7,5},{8,14},{10,8},{12,... | collective-permute-start | bytes 2359304 | tf_op jit(solution)/shard_map/ppermute | solution.py:199
  386.9 6.1 %collective-permute-start.23 = (bf16[128,256]{1,0:T(8,128)(2,1)S(1)}, bf16[128,256]{1,0:T(8,128)(2,1)S(1)}, u32[]{:S(2)}, u32[]{:S(2)}) collective-permute-start(bf16[128,256]{1,0:T(8,128)(2,1)S(1)} %get-tuple-element.164), channel_id=1, source_target_pairs={{0,2},{2,4},{4,6},{6,0},{1,3},{3,5},{5,7},{7,1},{8,10},{10,12},{12... | collective-permute-start | bytes 196616 | tf_op jit(solution)/shard_map/ppermute | solution.py:199
  387.1 6.1 %collective-permute-start.25 = (bf16[128,256]{1,0:T(8,128)(2,1)S(1)}, bf16[128,256]{1,0:T(8,128)(2,1)S(1)}, u32[]{:S(2)}, u32[]{:S(2)}) collective-permute-start(bf16[128,256]{1,0:T(8,128)(2,1)S(1)} %get-tuple-element.165), channel_id=1, source_target_pairs={{0,6},{2,0},{4,2},{6,4},{1,7},{3,1},{5,3},{7,5},{8,14},{10,8},{12,... | collective-permute-start | bytes 196616 | tf_op jit(solution)/shard_map/ppermute | solution.py:199
  393.1 6.3 %collective-permute-start.24 = (bf16[128,512]{1,0:T(8,128)(2,1)S(1)}, bf16[128,512]{1,0:T(8,128)(2,1)S(1)}, u32[]{:S(2)}, u32[]{:S(2)}) collective-permute-start(bf16[128,512]{1,0:T(8,128)(2,1)S(1)} %pad_maximum_fusion.7), channel_id=1, source_target_pairs={{0,2},{2,4},{4,6},{6,0},{1,3},{3,5},{5,7},{7,1},{8,10},{10,12},{12... | collective-permute-start | bytes 393224 | tf_op jit(solution)/shard_map/ppermute | solution.py:199
  393.9 18.4 %collective-permute-start.21 = (bf16[128,1536]{1,0:T(8,128)(2,1)S(1)}, bf16[128,1536]{1,0:T(8,128)(2,1)S(1)}, u32[]{:S(2)}, u32[]{:S(2)}) collective-permute-start(bf16[128,1536]{1,0:T(8,128)(2,1)S(1)} %fusion.4), channel_id=1, source_target_pairs={{0,8},{8,0},{1,9},{9,1},{2,10},{10,2},{3,11},{11,3},{4,12},{12,4},... | collective-permute-start | bytes 1179656 | tf_op jit(solution)/shard_map/ppermute | solution.py:199
  395.2 5.8 %collective-permute-start.26 = (bf16[128,512]{1,0:T(8,128)(2,1)S(1)}, bf16[128,512]{1,0:T(8,128)(2,1)S(1)}, u32[]{:S(2)}, u32[]{:S(2)}) collective-permute-start(bf16[128,512]{1,0:T(8,128)(2,1)S(1)} %pad_maximum_fusion.8), channel_id=1, source_target_pairs={{0,6},{2,0},{4,2},{6,4},{1,7},{3,1},{5,3},{7,5},{8,14},{10,8},{12,... | collective-permute-start | bytes 393224 | tf_op jit(solution)/shard_map/ppermute | solution.py:199
  401.0 12.5 %copy-start.1 = (bf16[256,2048]{1,0:T(8,128)(2,1)S(1)}, bf16[256,2048]{1,0:T(8,128)(2,1)}, u32[]{:S(2)}) copy-start(bf16[256,2048]{1,0:T(8,128)(2,1)} %param.17) | copy-start | bytes 3145732
Sparse Core Ops, SparseCore 0:
  10.8 156.6 all-gather.2
